TPU v7x, 32 devices: a whole 2x2x4 slice. The times are simulated.
32 devices in a mesh: group: 2 (over y), frame: 4 (over z), space: 2 (over x), head: 2 (over core).
Axes of the slice: x: 2, y: 2, z: 4, core: 2. Of those that a mesh axis runs over, the one named last changes fastest.
Arguments:
- queries: bfloat16 [8, 8, 48, 3072], P(('group', 'frame'), 'space', None, 'head'), parts along dimension 0, may hold values from -8 to 8
- keys: bfloat16 [8, 8, 48, 3072], P(('group', 'frame'), 'space', None, 'head'), parts along dimension 0, may hold values from -8 to 8
- values: bfloat16 [8, 8, 48, 3072], P(('group', 'frame'), 'space', None, 'head'), parts along dimension 0, may hold values from -6 to 6
- flags: int32 [4, 4], replicated, may hold values from 0 to 1, as said below
- widths: int32 [4], replicated, may hold values from 0 to 8, as said below
Outputs:
- attended: bfloat16 [8, 8, 48, 3072], P(('group', 'frame'), 'space', None, 'head'), parts along dimension 0
There are 2 independent parts, one for each index of `group`. A program takes and returns all parts, laid end to end along the dimension named above; an argument that names none is the same for every part. Nothing has to cross between parts.
Inputs may be any that keep to these rules, and one draw needn't show every extreme that they name: flags[f, g] = 1 wherever |f - g| <= 1, and flags[0, 3] = flags[3, 0] = 0. widths[0] = 8, and widths never rise with the frame distance.
All inputs are finite; a program needn't handle non-finite values.
Results may differ from a plain program's by a relative error of at most 0.006.
Values may be sent and summed in bfloat16 or wider, within the bound.
No kernel may reach another device: no remote copies, remote signals or barrier semaphores. Data moves between devices by JAX's collectives and lax.ppermute only.
A program may use at most 128 MiB of HBM per device.

v0:
```python
import jax
import jax.numpy as jnp
from jax import lax
from jax.sharding import PartitionSpec as P

HEAD_DIM = 128


NEG_FILL = -1e30


def empty_state(leading, head_count, query_count):
    return (
        jnp.full(leading + (head_count, query_count), NEG_FILL, jnp.float32),
        jnp.zeros(leading + (head_count, query_count), jnp.float32),
        jnp.zeros(leading + (head_count, query_count, HEAD_DIM), jnp.float32),
    )


def block_update(state_old, query_heads, query_rows, reach_rows, key_block, key_rows):
    running_max, running_total, running_acc = state_old
    query_count, head_count, head_size = query_heads.shape
    key_count = key_rows.shape[0]
    score_scale = 1.0 / HEAD_DIM**0.5
    allowed = jnp.abs(query_rows[:, None] - key_rows[None, :]) <= reach_rows
    key_heads = key_block[0].reshape(key_count, head_count, head_size)
    value_heads = key_block[1].reshape(key_count, head_count, head_size)
    scores = (
        jnp.einsum("qhd,khd->hqk", query_heads, key_heads, preferred_element_type=jnp.float32)
        * score_scale
    )
    scores = jnp.where(allowed[None], scores, NEG_FILL)
    new_max = jnp.maximum(running_max, jnp.max(scores, axis=2))
    weights = jnp.where(allowed[None], jnp.exp(scores - new_max[:, :, None]), 0.0)
    rescale = jnp.exp(running_max - new_max)
    new_total = running_total * rescale + jnp.sum(weights, axis=2)
    new_acc = running_acc * rescale[:, :, None] + jnp.einsum(
        "hqk,khd->hqd",
        weights.astype(jnp.bfloat16),
        value_heads,
        preferred_element_type=jnp.float32,
    )
    return (new_max, new_total, new_acc)


def shards(queries, keys, values, flags, widths):
    frame_now = lax.axis_index("frame")
    head_query, head_key, head_value = (
        lax.all_to_all(queries, "space", split_axis=3, concat_axis=1, tiled=True),
        lax.all_to_all(keys, "space", split_axis=3, concat_axis=1, tiled=True),
        lax.all_to_all(values, "space", split_axis=3, concat_axis=1, tiled=True),
    )
    row_total = head_query.shape[1]
    columns = head_query.shape[2]
    features = head_query.shape[3]
    head_count = features // HEAD_DIM
    frame_tokens = row_total * columns
    key_rows = jnp.arange(frame_tokens, dtype=jnp.int32) // columns
    stacked = jnp.stack(
        [head_key.reshape(frame_tokens, features), head_value.reshape(frame_tokens, features)],
        axis=0,
    )[None]
    query_heads = head_query.reshape(frame_tokens, head_count, HEAD_DIM)
    flag_row = lax.dynamic_index_in_dim(flags, frame_now, 0, False)
    initial = empty_state((), head_count, frame_tokens)
    key_piece = lax.all_gather(stacked, "frame", axis=0, tiled=True)

    def advance(state_old, step_items):
        key_block, offset_now = step_items
        reach_rows = lax.dynamic_index_in_dim(widths, jnp.abs(frame_now - offset_now), 0, False)
        flag_now = lax.dynamic_index_in_dim(flag_row, offset_now, 0, False)
        state_new = lax.cond(
            flag_now > 0,
            lambda kept_state: block_update(
                kept_state, query_heads, key_rows, reach_rows, key_block, key_rows
            ),
            lambda kept_state: kept_state,
            state_old,
        )
        return (state_new, None)

    state_new, unused = lax.scan(
        advance, initial, (key_piece, jnp.arange(key_piece.shape[0], dtype=jnp.int32))
    )
    final_max, final_total, final_acc = state_new
    blended = final_acc / final_total[:, :, None]
    joined = jnp.transpose(blended, (1, 0, 2)).reshape(head_query.shape).astype(jnp.bfloat16)
    return lax.all_to_all(joined, "space", split_axis=1, concat_axis=3, tiled=True)


def solution(mesh):
    placed = (
        P(("group", "frame"), "space", None, "head"),
        P(("group", "frame"), "space", None, "head"),
        P(("group", "frame"), "space", None, "head"),
        P(),
        P(),
    )
    return jax.shard_map(
        shards,
        mesh=mesh,
        in_specs=placed,
        out_specs=P(("group", "frame"), "space", None, "head"),
        check_vma=False,
    )
```

profile of v0, /device:TPU:16, one launch (start us, length us, event | category | flops | bytes accessed | tf_op | source)
XLA Modules:
  0.0 200.1 jit_solution(7581698430664993695)
XLA Ops:
  6.5 2.6 %copy.41 = bf16[1,4,48,1536]{2,1,0,3:T(4,128)(2,1)S(1)} copy(bf16[1,4,48,1536]{3,2,1,0:T(8,128)(2,1)} %param.11) | data formatting | bytes 1179648 | tf_op args[2]
  9.1 3.4 %reshape.68 = bf16[2,2,73728]{2,1,0:T(2,128)(2,1)} reshape(bf16[1536,1,4,48]{3,2,1,0:T(4,128)(2,1)S(1)} %bitcast.61) | data formatting | bytes 1179648
  12.5 3.5 %all-to-all-start.1 = ((bf16[2,2,73728]{2,1,0:T(2,128)(2,1)}), bf16[2,2,73728]{2,1,0:T(2,128)(2,1)S(1)}, u32[]{:S(2)}, u32[]{:S(2)}) async-start(bf16[2,2,73728]{2,1,0:T(2,128)(2,1)} %reshape.68), calls=%async_computation.1 | async-start | bytes 1179648 | tf_op jit(solution)/shard_map/all_to_all | solution.py:51
  16.0 1.0 copy.38
  17.1 3.4 %reshape.70 = bf16[2,2,73728]{2,1,0:T(2,128)(2,1)} reshape(bf16[1536,1,4,48]{3,2,1,0:T(4,128)(2,1)S(1)} %bitcast.62) | data formatting | bytes 1179648
  20.5 4.5 %all-to-all-done.1 = bf16[2,2,73728]{2,1,0:T(2,128)(2,1)S(1)} async-done(((bf16[2,2,73728]{2,1,0:T(2,128)(2,1)}), bf16[2,2,73728]{2,1,0:T(2,128)(2,1)S(1)}, u32[]{:S(2)}, u32[]{:S(2)}) %all-to-all-start.1) | async-done | bytes 589856 | tf_op jit(solution)/shard_map/all_to_all | solution.py:51
  25.0 3.5 %all-to-all-start = ((bf16[2,2,73728]{2,1,0:T(2,128)(2,1)}), bf16[2,2,73728]{2,1,0:T(2,128)(2,1)S(1)}, u32[]{:S(2)}, u32[]{:S(2)}) async-start(bf16[2,2,73728]{2,1,0:T(2,128)(2,1)} %reshape.70), calls=%async_computation | async-start | bytes 1179648 | tf_op jit(solution)/shard_map/all_to_all | solution.py:50
  28.5 1.6 reshape.69
  30.1 1.3 copy.55
  31.5 5.0 %all-to-all-done = bf16[2,2,73728]{2,1,0:T(2,128)(2,1)S(1)} async-done(((bf16[2,2,73728]{2,1,0:T(2,128)(2,1)}), bf16[2,2,73728]{2,1,0:T(2,128)(2,1)S(1)}, u32[]{:S(2)}, u32[]{:S(2)}) %all-to-all-start) | async-done | bytes 589856 | tf_op jit(solution)/shard_map/all_to_all | solution.py:50
  36.5 1.6 reshape.71
  38.1 1.3 copy.54
  39.5 1.1 pad_maximum_fusion
  40.7 1.0 copy.44
  41.8 3.4 %reshape.72 = bf16[2,2,73728]{2,1,0:T(2,128)(2,1)} reshape(bf16[1536,1,4,48]{3,2,1,0:T(4,128)(2,1)S(1)} %bitcast.63) | data formatting | bytes 1179648
  45.2 3.7 %all-to-all-start.2 = ((bf16[2,2,73728]{2,1,0:T(2,128)(2,1)}), bf16[2,2,73728]{2,1,0:T(2,128)(2,1)S(1)}, u32[]{:S(2)}, u32[]{:S(2)}) async-start(bf16[2,2,73728]{2,1,0:T(2,128)(2,1)} %reshape.72), calls=%async_computation.2 | async-start | bytes 1179648 | tf_op jit(solution)/shard_map/all_to_all | solution.py:49
  48.9 6.9 %all-to-all-done.2 = bf16[2,2,73728]{2,1,0:T(2,128)(2,1)S(1)} async-done(((bf16[2,2,73728]{2,1,0:T(2,128)(2,1)}), bf16[2,2,73728]{2,1,0:T(2,128)(2,1)S(1)}, u32[]{:S(2)}, u32[]{:S(2)}) %all-to-all-start.2) | async-done | bytes 589856 | tf_op jit(solution)/shard_map/all_to_all | solution.py:49
  55.8 1.6 reshape.73
  57.4 0.8 copy.45
  58.2 0.7 reshape.64
  58.9 70.0 %all-gather.3.cloned.1.call-done = bf16[8,384,768]{2,1,0:T(8,128)(2,1)} async-done(((bf16[2,384,768]{2,1,0:T(8,128)(2,1)}), bf16[8,384,768]{2,1,0:T(8,128)(2,1)}) %all-gather.3.cloned.1.call-update) | async-done | bytes 4718608 | tf_op jit(solution)/shard_map/all_gather | solution.py:66
  128.9 6.6 %copy.46 = bf16[4,2,384,768]{2,3,1,0:T(8,128)(2,1)} copy(bf16[4,2,384,768]{3,2,1,0:T(8,128)(2,1)} %bitcast.64) | data formatting | bytes 9437184
  135.6 43.9 %while.15 = (s32[]{:T(128)}, f32[6,384]{1,0:T(8,128)S(1)}, f32[6,384]{1,0:T(8,128)S(1)}, f32[6,384,128]{2,1,0:T(8,128)S(1)}, s32[4]{0:T(128)S(1)}, /*index=5*/s3...) while((s32[]{:T(128)}, f32[6,384]{1,0:T(8,128)S(1)}, ...), condition=%wide.region_5.6_spmd.clone, body=%wide.region_0.5_spmd.clone.sunk | while | flops 465526272 | bytes 17858036 | solution.py:82
  135.7 0.6 dynamic_slice.35
  138.2 0.7 dynamic_slice.36
  139.5 7.1 %conditional.3 = ((f32[6,384]{1,0:T(8,128)S(1)}, f32[6,384]{1,0:T(8,128)S(1)}, f32[6,384,128]{2,1,0:T(8,128)S(1)})) conditional(s32[]{:T(128)} %bitcast.55, (f32[6,384]{1,0:T(8,128)S(1)}, f32[6,384]{1,0:T(8,128)S(1)}, f32[6,384,128]{2,1,0:T(8,128)S(1)}) %tuple.48, (s32[384]{0:T(512)S(1)}, s32[]{:T(128)}, s32[]{:T(128)}, s32[4]{0:T(128)S(1)}, ...), branch_computations={%region_1.1_spmd, %region_2.4_spmd.clone} | conditional | flops 465525888 | bytes 17853058 | solution.py:72
  140.2 0.6 dynamic_slice.30
  140.9 0.8 abs_compare_fusion
  141.8 1.4 constant_dynamic-slice_fusion.1
  143.1 0.9 fusion.2
  144.0 0.9 fusion.4
  144.9 1.7 fusion.12
  146.6 0.6 dynamic_slice.35
  149.2 0.7 dynamic_slice.36
  150.5 7.1 %conditional.3 = ((f32[6,384]{1,0:T(8,128)S(1)}, f32[6,384]{1,0:T(8,128)S(1)}, f32[6,384,128]{2,1,0:T(8,128)S(1)})) conditional(s32[]{:T(128)} %bitcast.55, (f32[6,384]{1,0:T(8,128)S(1)}, f32[6,384]{1,0:T(8,128)S(1)}, f32[6,384,128]{2,1,0:T(8,128)S(1)}) %tuple.48, (s32[384]{0:T(512)S(1)}, s32[]{:T(128)}, s32[]{:T(128)}, s32[4]{0:T(128)S(1)}, ...), branch_computations={%region_1.1_spmd, %region_2.4_spmd.clone} | conditional | flops 465525888 | bytes 17853058 | solution.py:72
  151.2 0.6 dynamic_slice.30
  151.9 0.8 abs_compare_fusion
  152.7 1.4 constant_dynamic-slice_fusion.1
  154.1 0.9 fusion.2
  155.0 0.9 fusion.4
  155.9 1.7 fusion.12
  157.6 0.6 dynamic_slice.35
  160.1 0.7 dynamic_slice.36
  161.5 7.1 %conditional.3 = ((f32[6,384]{1,0:T(8,128)S(1)}, f32[6,384]{1,0:T(8,128)S(1)}, f32[6,384,128]{2,1,0:T(8,128)S(1)})) conditional(s32[]{:T(128)} %bitcast.55, (f32[6,384]{1,0:T(8,128)S(1)}, f32[6,384]{1,0:T(8,128)S(1)}, f32[6,384,128]{2,1,0:T(8,128)S(1)}) %tuple.48, (s32[384]{0:T(512)S(1)}, s32[]{:T(128)}, s32[]{:T(128)}, s32[4]{0:T(128)S(1)}, ...), branch_computations={%region_1.1_spmd, %region_2.4_spmd.clone} | conditional | flops 465525888 | bytes 17853058 | solution.py:72
  162.1 0.6 dynamic_slice.30
  162.8 0.8 abs_compare_fusion
  163.7 1.4 constant_dynamic-slice_fusion.1
  165.1 0.9 fusion.2
  166.0 0.9 fusion.4
  166.8 1.7 fusion.12
  168.6 0.6 dynamic_slice.35
  171.1 0.7 dynamic_slice.36
  172.4 7.1 %conditional.3 = ((f32[6,384]{1,0:T(8,128)S(1)}, f32[6,384]{1,0:T(8,128)S(1)}, f32[6,384,128]{2,1,0:T(8,128)S(1)})) conditional(s32[]{:T(128)} %bitcast.55, (f32[6,384]{1,0:T(8,128)S(1)}, f32[6,384]{1,0:T(8,128)S(1)}, f32[6,384,128]{2,1,0:T(8,128)S(1)}) %tuple.48, (s32[384]{0:T(512)S(1)}, s32[]{:T(128)}, s32[]{:T(128)}, s32[4]{0:T(128)S(1)}, ...), branch_computations={%region_1.1_spmd, %region_2.4_spmd.clone} | conditional | flops 465525888 | bytes 17853058 | solution.py:72
  173.1 0.6 dynamic_slice.30
  173.8 0.8 abs_compare_fusion
  174.7 1.4 constant_dynamic-slice_fusion.1
  176.0 0.9 fusion.2
  176.9 0.9 fusion.4
  177.8 1.7 fusion.12
  179.5 0.4 fusion.19
  179.9 0.4 copy.48
  180.3 0.7 convert_element_type.30
  181.0 11.4 %all_to_all.63 = bf16[1,8,48,768]{3,2,0,1:T(8,128)(2,1)S(1)} all-to-all(bf16[1,8,48,768]{3,2,0,1:T(8,128)(2,1)S(1)} %bitcast.70), channel_id=1, replica_groups=mesh['group'=2,'frame'=4,'space'=2,'head'=2] {'space'}, dimensions={1} | all-to-all | bytes 1179648 | tf_op jit(solution)/shard_map/all_to_all | solution.py:88
  192.4 0.9 copy.56
  (46 shorter events, 1.0 us)
Async XLA Ops:
  6.5 42.4 %copy-start = (s32[4,4]{1,0:T(4,128)S(1)}, s32[4,4]{1,0:T(4,128)}, u32[]{:S(2)}) copy-start(s32[4,4]{1,0:T(4,128)} %param.12) | copy-start | bytes 196
  6.5 9.5 %copy-start.1 = (bf16[1,4,48,1536]{3,2,1,0:T(8,128)(2,1)S(1)}, bf16[1,4,48,1536]{3,2,1,0:T(8,128)(2,1)}, u32[]{:S(2)}) copy-start(bf16[1,4,48,1536]{3,2,1,0:T(8,128)(2,1)} %param.10) | copy-start | bytes 1769476
  12.5 12.4 %all-to-all-start.1 = ((bf16[2,2,73728]{2,1,0:T(2,128)(2,1)}), bf16[2,2,73728]{2,1,0:T(2,128)(2,1)S(1)}, u32[]{:S(2)}, u32[]{:S(2)}) async-start(bf16[2,2,73728]{2,1,0:T(2,128)(2,1)} %reshape.68), calls=%async_computation.1 | async-start | bytes 1179648 | tf_op jit(solution)/shard_map/all_to_all | solution.py:51
  25.0 11.6 %all-to-all-start = ((bf16[2,2,73728]{2,1,0:T(2,128)(2,1)}), bf16[2,2,73728]{2,1,0:T(2,128)(2,1)S(1)}, u32[]{:S(2)}, u32[]{:S(2)}) async-start(bf16[2,2,73728]{2,1,0:T(2,128)(2,1)} %reshape.70), calls=%async_computation | async-start | bytes 1179648 | tf_op jit(solution)/shard_map/all_to_all | solution.py:50
  28.5 100.4 %all-gather.3.cloned.1.call-start = ((), (), s32[]{:S(2)}) async-start(), calls=%async_computation.4 | async-start | bytes 5898240 | tf_op jit(solution)/shard_map/all_gather | solution.py:66
  38.1 2.6 %copy-start.2 = (bf16[1,4,48,1536]{3,2,1,0:T(8,128)(2,1)S(1)}, bf16[1,4,48,1536]{3,2,1,0:T(8,128)(2,1)}, u32[]{:S(2)}) copy-start(bf16[1,4,48,1536]{3,2,1,0:T(8,128)(2,1)} %param.9) | copy-start | bytes 1769476
  45.2 10.7 %all-to-all-start.2 = ((bf16[2,2,73728]{2,1,0:T(2,128)(2,1)}), bf16[2,2,73728]{2,1,0:T(2,128)(2,1)S(1)}, u32[]{:S(2)}, u32[]{:S(2)}) async-start(bf16[2,2,73728]{2,1,0:T(2,128)(2,1)} %reshape.72), calls=%async_computation.2 | async-start | bytes 1179648 | tf_op jit(solution)/shard_map/all_to_all | solution.py:49
  128.9 6.7 %copy-start.3 = (s32[4]{0:T(128)S(1)}, s32[4]{0:T(128)}, u32[]{:S(2)}) copy-start(s32[4]{0:T(128)} %param.13) | copy-start | bytes 52
Sparse Core Ops, SparseCore 0:
  40.8 88.0 all-gather.2
where the time goes:
time: 201 us; the launch traced here: 200 us
  waiting for transfers between devices  86.4 us (43%)
  local copies, waits for them, and re-layouts  45.4 us (23%)
  between operations  13.6 us (7%)
  loops' own time  13.4 us (7%)
  blocking collectives  11.4 us (6%)
  starting transfers between devices  10.8 us (5%)
  matrix products  10.3 us (5%)
  other arithmetic  8.87 us (4%)
    all_gather x1, waiting for transfers between devices, shards(): key_piece = lax.all_gather(stacked, 'frame', axis=0, tiled=True)  70 us
    unnamed x19, local copies, waits for them, and re-layouts  26.3 us
    all_to_all x1, blocking collectives, shards(): lax.all_to_all(joined, 'space', split_axis=1, concat_axis=3, tiled=True)  11.4 us
    another operation x1, loops' own time, shards(): lax.scan(advance, initial, (key_piece, jnp.arange(key_piece.shape[0], dty...  10.5 us
    all_to_all x1, waiting for transfers between devices, shards(): lax.all_to_all(queries, 'space', split_axis=3, concat_axis=1, tiled=True)  6.91 us
    dot_general x4, matrix products, block_update(): jnp.einsum('hqk,khd->hqd', weights.astype(jnp.bfloat16), value_heads, pre...  6.73 us
    slice x4, local copies, waits for them, and re-layouts, block_update(): value_heads = key_block[1].reshape(key_count, head_count, head_size)  5.48 us
    all_to_all x1, waiting for transfers between devices, shards(): lax.all_to_all(keys, 'space', split_axis=3, concat_axis=1, tiled=True)  5.02 us
  transfers between devices with their start and end apart: 4, of which 4 were waited for; matrix products, arithmetic and copies ran while one was open for 7% of the time, Pallas kernels for 0%

commit v1 on v0

v1 whole, which is shorter than its diff:
```python
import functools
import math

import jax
import jax.numpy as jnp
from jax import lax
from jax.experimental import pallas as pl
from jax.experimental.pallas import tpu as pltpu
from jax.sharding import PartitionSpec as P

HEAD_DIM = 128
NEG_FILL = -1e30
VMEM_LIMIT = 40 * 1024 * 1024


def pack_kernel(spaces, place_ref, q_ref, k_ref, v_ref, *rest):
    outs, sems = rest[:-1], rest[-1]
    width = outs[0].shape[-1]
    here = place_ref[1]
    copies = []
    for offset in range(spaces):
        column = pl.multiple_of(lax.rem(here + offset, spaces) * width, HEAD_DIM)
        sources = [k_ref, v_ref]
        targets = [outs[offset].at[0], outs[offset].at[1]]
        if offset > 0:
            sources.append(q_ref)
            targets.append(outs[spaces + offset - 1])
        for source, target in zip(sources, targets):
            copy = pltpu.make_async_copy(
                source.at[:, pl.ds(column, width)], target, sems.at[len(copies)]
            )
            copy.start()
            copies.append(copy)
    for copy in copies:
        copy.wait()


def pack(place, q, k, v, spaces):
    tokens, features = q.shape
    width = features // spaces
    shapes = [jax.ShapeDtypeStruct((2, tokens, width), q.dtype)] * spaces
    shapes += [jax.ShapeDtypeStruct((tokens, width), q.dtype)] * (spaces - 1)
    return pl.pallas_call(
        functools.partial(pack_kernel, spaces),
        grid_spec=pltpu.PrefetchScalarGridSpec(
            num_scalar_prefetch=1,
            grid=(1,),
            in_specs=[pl.BlockSpec(memory_space=pl.ANY)] * 3,
            out_specs=[pl.BlockSpec(memory_space=pl.ANY)] * len(shapes),
            scratch_shapes=[pltpu.SemaphoreType.DMA((3 * spaces - 1,))],
        ),
        out_shape=shapes,
        name="pack",
    )(place, q, k, v)


def attend_kernel(
    spaces, frames, columns, row_band, pieces, fresh, final,
    place_ref, flags_ref, widths_ref, *refs,
):
    refs = list(refs)
    queries = [refs.pop(0) for unused in range(spaces)]
    keyvals = [refs.pop(0) for unused in pieces]
    state_in = None if fresh else (refs.pop(0), refs.pop(0))
    outs = [refs.pop(0) for unused in range(spaces if final else 2)]
    top_ref, total_ref, acc_ref = refs
    tokens = queries[0].shape[0]
    frame_now, space_now = place_ref[0], place_ref[1]
    scale = math.log2(math.e) / math.sqrt(HEAD_DIM)

    def band(offset):
        return lax.rem(space_now - offset + spaces, spaces)

    query = jnp.concatenate([ref[...] for ref in queries], axis=0)
    count = spaces * tokens

    def scores_of(ref):
        return scale * lax.dot_general(
            query, ref[0], (((1,), (1,)), ((), ())), preferred_element_type=jnp.float32
        )

    def weighted(weights, ref):
        return jnp.dot(
            weights.astype(jnp.bfloat16), ref[1], preferred_element_type=jnp.float32
        )

    own = [n for n, (distance, offset) in enumerate(pieces) if distance == 0]
    if fresh:
        parts = [scores_of(keyvals[n]) for n in own]
        top = functools.reduce(
            jnp.maximum, [jnp.max(part, axis=1, keepdims=True) for part in parts]
        )
        weights = [jnp.exp2(part - top) for part in parts]
        top_ref[...] = top
        total_ref[...] = sum(jnp.sum(w, axis=1, keepdims=True) for w in weights)
        acc_ref[...] = sum(weighted(w, keyvals[n]) for w, n in zip(weights, own))
    else:
        acc_ref[...] = state_in[0][0]
        top_ref[...] = state_in[1][0, :, 0:1]
        total_ref[...] = state_in[1][0, :, 64:65]

    local = lax.broadcasted_iota(jnp.int32, (count, 1), 0)
    query_row = jnp.zeros((count, 1), jnp.int32)
    for offset in range(spaces):
        inside = (local >= offset * tokens) & (local < (offset + 1) * tokens)
        row = (local - offset * tokens) // columns + band(offset) * row_band
        query_row = jnp.where(inside, row, query_row)
    key_local = lax.broadcasted_iota(jnp.int32, (1, tokens), 1) // columns

    for n, (distance, offset) in enumerate(pieces):
        if distance == 0:
            continue
        key_frame = frame_now + distance
        known = (key_frame >= 0) & (key_frame < frames)
        safe = jnp.clip(key_frame, 0, frames - 1)
        reach = widths_ref[abs(distance)]
        asked = known & (flags_ref[frame_now, safe] > 0)

        @pl.when(asked)
        def _(n=n, offset=offset, reach=reach):
            key_row = key_local + band(offset) * row_band
            scores = scores_of(keyvals[n])
            scores = jnp.where(jnp.abs(query_row - key_row) <= reach, scores, NEG_FILL)
            old = top_ref[...]
            new = jnp.maximum(old, jnp.max(scores, axis=1, keepdims=True))
            weights = jnp.exp2(scores - new)
            fade = jnp.exp2(old - new)
            top_ref[...] = new
            total_ref[...] = total_ref[...] * fade + jnp.sum(weights, axis=1, keepdims=True)
            acc_ref[...] = acc_ref[...] * fade + weighted(weights, keyvals[n])

    if final:
        for offset in range(spaces):
            rows = pl.ds(offset * tokens, tokens)
            outs[offset][...] = (acc_ref[rows, :] / total_ref[rows, :]).astype(outs[offset].dtype)
    else:
        outs[0][0] = acc_ref[...]
        lane = lax.broadcasted_iota(jnp.int32, (count, HEAD_DIM), 1)
        outs[1][0] = jnp.where(lane < 64, top_ref[...], total_ref[...])


def attend(scalars, queries, keyvals, pieces, state, final, sizes):
    spaces, frames, columns, row_band, features = sizes
    tokens = queries[0].shape[0]
    width = features // spaces
    heads = width // HEAD_DIM
    count = spaces * tokens
    own_block = pl.BlockSpec((tokens, HEAD_DIM), lambda h, place, *_: (0, place[1] * heads + h))
    block = pl.BlockSpec((tokens, HEAD_DIM), lambda h, *_: (0, h))
    pair = pl.BlockSpec((2, tokens, HEAD_DIM), lambda h, *_: (0, 0, h))
    kept = pl.BlockSpec((1, count, HEAD_DIM), lambda h, *_: (h, 0, 0))
    in_specs = [own_block] + [block] * (spaces - 1) + [pair] * len(pieces)
    operands = list(queries) + list(keyvals)
    if state is not None:
        in_specs += [kept, kept]
        operands += list(state)
    if final:
        out_specs = [own_block] + [block] * (spaces - 1)
        out_shape = [jax.ShapeDtypeStruct((tokens, features), jnp.bfloat16)]
        out_shape += [jax.ShapeDtypeStruct((tokens, width), jnp.bfloat16)] * (spaces - 1)
    else:
        out_specs = [kept, kept]
        out_shape = [jax.ShapeDtypeStruct((heads, count, HEAD_DIM), jnp.float32)] * 2
    pairs = heads * count * tokens * len(pieces)
    return pl.pallas_call(
        functools.partial(
            attend_kernel, spaces, frames, columns, row_band, tuple(pieces), state is None, final
        ),
        grid_spec=pltpu.PrefetchScalarGridSpec(
            num_scalar_prefetch=3,
            grid=(heads,),
            in_specs=in_specs,
            out_specs=out_specs,
            scratch_shapes=[
                pltpu.VMEM((count, 1), jnp.float32),
                pltpu.VMEM((count, 1), jnp.float32),
                pltpu.VMEM((count, HEAD_DIM), jnp.float32),
            ],
        ),
        out_shape=out_shape,
        compiler_params=pltpu.CompilerParams(vmem_limit_bytes=VMEM_LIMIT),
        cost_estimate=pl.CostEstimate(
            flops=4 * pairs * HEAD_DIM,
            bytes_accessed=len(pieces) * 4 * tokens * width,
            transcendentals=pairs,
        ),
        name="attend_final" if final else "attend",
    )(*scalars, *operands)


def put_kernel(place_ref, piece_ref, whole_ref, out_ref):
    out_ref[...] = piece_ref[...]


def put(place, piece, whole, offset, spaces):
    tokens, width = piece.shape
    return pl.pallas_call(
        put_kernel,
        grid_spec=pltpu.PrefetchScalarGridSpec(
            num_scalar_prefetch=1,
            grid=(1,),
            in_specs=[
                pl.BlockSpec((tokens, width), lambda i, place: (0, 0)),
                pl.BlockSpec(memory_space=pl.ANY),
            ],
            out_specs=pl.BlockSpec(
                (tokens, width), lambda i, place: (0, lax.rem(place[1] + offset, spaces))
            ),
        ),
        out_shape=jax.ShapeDtypeStruct(whole.shape, whole.dtype),
        input_output_aliases={2: 0},
        name="put",
    )(place, piece, whole)


def shards(spaces, frames, queries, keys, values, flags, widths):
    unused, row_band, columns, features = queries.shape
    tokens = row_band * columns
    place = jnp.stack([lax.axis_index("frame"), lax.axis_index("space")]).astype(jnp.int32)
    scalars = (place, flags, widths)
    sizes = (spaces, frames, columns, row_band, features)
    q, k, v = (x.reshape(tokens, features) for x in (queries, keys, values))
    packed = pack(place, q, k, v, spaces)

    def along_space(x, offset):
        return lax.ppermute(x, "space", [(s, (s + offset) % spaces) for s in range(spaces)])

    def along_frame(x, step):
        return lax.ppermute(
            x, "frame", [(f, f + step) for f in range(frames) if 0 <= f + step < frames]
        )

    offsets = range(1, spaces)
    own = [packed[0]] + [along_space(packed[offset], offset) for offset in offsets]
    query_parts = [q] + [along_space(packed[spaces + offset - 1], offset) for offset in offsets]

    waves = [[(0, offset, x) for offset, x in enumerate(own)]]
    from_left, from_right = own, own
    for distance in range(1, frames - 1):
        from_left = [along_frame(x, 1) for x in from_left]
        from_right = [along_frame(x, -1) for x in from_right]
        wave = []
        for offset in range(spaces):
            wave.append((-distance, offset, from_left[offset]))
            wave.append((distance, offset, from_right[offset]))
        waves.append(wave)
    if len(waves) > 1:
        waves = [waves[0] + waves[1]] + waves[2:]

    state = None
    for n, wave in enumerate(waves):
        state = attend(
            scalars, query_parts, [x for d, o, x in wave], [(d, o) for d, o, x in wave],
            state, n == len(waves) - 1, sizes,
        )

    result = state[0]
    for offset in offsets:
        back = along_space(state[offset], -offset)
        result = put(place, back, result, offset, spaces)
    return result.reshape(queries.shape)


def solution(mesh):
    placed = P(("group", "frame"), "space", None, "head")
    return jax.shard_map(
        functools.partial(shards, mesh.shape["space"], mesh.shape["frame"]),
        mesh=mesh,
        in_specs=(placed, placed, placed, P(), P()),
        out_specs=placed,
        check_vma=False,
    )
```

time: 201 us -> 144 us (0.72)
  the two profiles are of different devices: /device:TPU:16 before, /device:TPU:14 now
where the time goes in v1:
time: 144 us; the launch traced here: 143 us
  Pallas kernels  87.6 us (61%)
  waiting for transfers between devices  27.8 us (19%)
  starting transfers between devices  25.2 us (18%)
  local copies, waits for them, and re-layouts  1.78 us (1%)
    pallas_call x1, Pallas kernels, pack(): pl.pallas_call(functools.partial(pack_kernel, spaces), grid_spec=pltpu.Pr...  46.6 us
    pallas_call x2, Pallas kernels, attend(): pl.pallas_call(functools.partial(attend_kernel, spaces, frames, columns,...  38.6 us
    ppermute x8, starting transfers between devices, along_frame(): lax.ppermute(x, 'frame', [(f, f + step) for f in range(frames) if 0 <= f...  23.5 us
    ppermute x3, waiting for transfers between devices, along_space(): lax.ppermute(x, 'space', [(s, (s + offset) % spaces) for s in range(space...  21.5 us
    ppermute x8, waiting for transfers between devices, along_frame(): lax.ppermute(x, 'frame', [(f, f + step) for f in range(frames) if 0 <= f...  6.38 us
  transfers between devices with their start and end apart: 11, of which 4 were waited for; matrix products, arithmetic and copies ran while one was open for 0% of the time, Pallas kernels for 18%

profile of v1, /device:TPU:14, one launch (start us, length us, event | category | flops | bytes accessed | tf_op | source)
XLA Modules:
  0.0 143.2 jit_solution(11152850698211323977)
XLA Ops:
  0.0 0.0 copy-start
  0.0 0.0 copy-start.2
  0.0 0.0 copy-start.3
  0.0 0.6 pad_add_fusion.place_ref
  0.6 0.0 copy-start.1
  0.6 46.6 %pack.1 = (bf16[2,192,768]{2,1,0:T(8,128)(2,1)}, bf16[2,192,768]{2,1,0:T(8,128)(2,1)}, bf16[192,768]{1,0:T(8,128)(2,1)}) custom-call(s32[2]{0:T(128)} %pad_add_fusion.place_ref, bf16[192,1536]{1,0:T(8,128)(2,1)} %bitcast.6, bf16[192,1536]{1,0:T(8,128)(2,1)} %bitcast.9, bf16[192,1536]{1,0:T(8,128)(2,1)} %bitcast.10), custom_call_target="tpu_custom_call" | custom-call | tf_op jit(solution)/shard_map/pack/pallas_call | solution.py:43
  47.3 0.6 collective-permute-start.5
  47.9 3.5 %collective-permute-start.1 = (bf16[2,192,768]{2,1,0:T(8,128)(2,1)}, bf16[2,192,768]{2,1,0:T(8,128)(2,1)S(1)}, u32[]{:S(2)}, u32[]{:S(2)}) collective-permute-start(bf16[2,192,768]{2,1,0:T(8,128)(2,1)} %get-tuple-element.13.refs_2_), channel_id=1, source_target_pairs={{0,4},{4,8},{8,12},{1,5},{5,9},{9,13},{2,6},{6,10},{10,14},{3,7},{... | collective-permute-start | bytes 1769480 | tf_op jit(solution)/shard_map/ppermute | solution.py:229
  51.3 2.4 %collective-permute-start.3 = (bf16[2,192,768]{2,1,0:T(8,128)(2,1)}, bf16[2,192,768]{2,1,0:T(8,128)(2,1)S(1)}, u32[]{:S(2)}, u32[]{:S(2)}) collective-permute-start(bf16[2,192,768]{2,1,0:T(8,128)(2,1)} %get-tuple-element.13.refs_2_), channel_id=1, source_target_pairs={{4,0},{8,4},{12,8},{5,1},{9,5},{13,9},{6,2},{10,6},{14,10},{7,3},{... | collective-permute-start | bytes 1769480 | tf_op jit(solution)/shard_map/ppermute | solution.py:229
  53.7 8.9 %collective-permute-done.5.refs_3_ = bf16[2,192,768]{2,1,0:T(8,128)(2,1)S(1)} collective-permute-done((bf16[2,192,768]{2,1,0:T(8,128)(2,1)}, bf16[2,192,768]{2,1,0:T(8,128)(2,1)S(1)}, u32[]{:S(2)}, u32[]{:S(2)}) %collective-permute-start.5) | collective-permute-done | bytes 589856 | tf_op jit(solution)/shard_map/ppermute | solution.py:226
  62.6 3.5 %collective-permute-start.6 = (bf16[2,192,768]{2,1,0:T(8,128)(2,1)S(1)}, bf16[2,192,768]{2,1,0:T(8,128)(2,1)S(1)}, u32[]{:S(2)}, u32[]{:S(2)}) collective-permute-start(bf16[2,192,768]{2,1,0:T(8,128)(2,1)S(1)} %collective-permute-done.5.refs_3_), channel_id=1, source_target_pairs={{0,4},{4,8},{8,12},{1,5},{5,9},{9,13},{2,6},{6,10},{10,14},{3,7},{... | collective-permute-start | bytes 1769480 | tf_op jit(solution)/shard_map/ppermute | solution.py:229
  66.1 2.4 %collective-permute-start.8 = (bf16[2,192,768]{2,1,0:T(8,128)(2,1)S(1)}, bf16[2,192,768]{2,1,0:T(8,128)(2,1)S(1)}, u32[]{:S(2)}, u32[]{:S(2)}) collective-permute-start(bf16[2,192,768]{2,1,0:T(8,128)(2,1)S(1)} %collective-permute-done.5.refs_3_), channel_id=1, source_target_pairs={{4,0},{8,4},{12,8},{5,1},{9,5},{13,9},{6,2},{10,6},{14,10},{7,3},{... | collective-permute-start | bytes 1769480 | tf_op jit(solution)/shard_map/ppermute | solution.py:229
  68.5 0.0 collective-permute-done.1.refs_4_
  68.5 3.5 %collective-permute-start.2 = (bf16[2,192,768]{2,1,0:T(8,128)(2,1)S(1)}, bf16[2,192,768]{2,1,0:T(8,128)(2,1)S(1)}, u32[]{:S(2)}, u32[]{:S(2)}) collective-permute-start(bf16[2,192,768]{2,1,0:T(8,128)(2,1)S(1)} %collective-permute-done.1.refs_4_), channel_id=1, source_target_pairs={{0,4},{4,8},{8,12},{1,5},{5,9},{9,13},{2,6},{6,10},{10,14},{3,7},{... | collective-permute-start | bytes 1769480 | tf_op jit(solution)/shard_map/ppermute | solution.py:229
  71.9 0.0 collective-permute-done.3.refs_5_
  72.0 2.4 %collective-permute-start.4 = (bf16[2,192,768]{2,1,0:T(8,128)(2,1)S(1)}, bf16[2,192,768]{2,1,0:T(8,128)(2,1)S(1)}, u32[]{:S(2)}, u32[]{:S(2)}) collective-permute-start(bf16[2,192,768]{2,1,0:T(8,128)(2,1)S(1)} %collective-permute-done.3.refs_5_), channel_id=1, source_target_pairs={{4,0},{8,4},{12,8},{5,1},{9,5},{13,9},{6,2},{10,6},{14,10},{7,3},{... | collective-permute-start | bytes 1769480 | tf_op jit(solution)/shard_map/ppermute | solution.py:229
  74.4 6.4 %collective-permute-done.6.refs_6_ = bf16[2,192,768]{2,1,0:T(8,128)(2,1)S(1)} collective-permute-done((bf16[2,192,768]{2,1,0:T(8,128)(2,1)S(1)}, bf16[2,192,768]{2,1,0:T(8,128)(2,1)S(1)}, u32[]{:S(2)}, u32[]{:S(2)}) %collective-permute-start.6) | collective-permute-done | bytes 589856 | tf_op jit(solution)/shard_map/ppermute | solution.py:229
  80.7 3.5 %collective-permute-start.7 = (bf16[2,192,768]{2,1,0:T(8,128)(2,1)S(1)}, bf16[2,192,768]{2,1,0:T(8,128)(2,1)S(1)}, u32[]{:S(2)}, u32[]{:S(2)}) collective-permute-start(bf16[2,192,768]{2,1,0:T(8,128)(2,1)S(1)} %collective-permute-done.6.refs_6_), channel_id=1, source_target_pairs={{0,4},{4,8},{8,12},{1,5},{5,9},{9,13},{2,6},{6,10},{10,14},{3,7},{... | collective-permute-start | bytes 1769480 | tf_op jit(solution)/shard_map/ppermute | solution.py:229
  84.2 0.0 collective-permute-done.8.refs_7_
  84.2 2.4 %collective-permute-start.9 = (bf16[2,192,768]{2,1,0:T(8,128)(2,1)S(1)}, bf16[2,192,768]{2,1,0:T(8,128)(2,1)S(1)}, u32[]{:S(2)}, u32[]{:S(2)}) collective-permute-start(bf16[2,192,768]{2,1,0:T(8,128)(2,1)S(1)} %collective-permute-done.8.refs_7_), channel_id=1, source_target_pairs={{4,0},{8,4},{12,8},{5,1},{9,5},{13,9},{6,2},{10,6},{14,10},{7,3},{... | collective-permute-start | bytes 1769480 | tf_op jit(solution)/shard_map/ppermute | solution.py:229
  86.6 0.6 collective-permute-start
  87.2 6.4 %collective-permute-done.refs_1_ = bf16[192,768]{1,0:T(8,128)(2,1)S(1)} collective-permute-done((bf16[192,768]{1,0:T(8,128)(2,1)}, bf16[192,768]{1,0:T(8,128)(2,1)S(1)}, u32[]{:S(2)}, u32[]{:S(2)}) %collective-permute-start) | collective-permute-done | bytes 294944 | tf_op jit(solution)/shard_map/ppermute | solution.py:226
  93.6 0.0 copy-done
  93.6 0.0 copy-done.2
  93.6 0.0 copy-done.3
  93.6 0.0 copy-done.1
  93.7 0.0 copy-start.4
  93.7 1.1 copy-done.4
  94.7 25.5 %attend.1 = (f32[6,384,128]{2,1,0:T(8,128)S(1)}, f32[6,384,128]{2,1,0:T(8,128)S(1)}) custom-call(s32[2]{0:T(128)S(1)} %copy-done.1, s32[4,4]{1,0:T(4,128)S(1)} %copy-done.2, s32[4]{0:T(128)S(1)} %copy-done.3, bf16[192,1536]{1,0:T(8,128)(2,1)S(1)} %bitcast.7, bf16[192,768]{1,0:T(8,128)(2,1)S(1)} %collective-permute-done.refs_1_, ...), custom_call_target="tpu_custom_call" | custom-call | flops 1358954496 | bytes 3538944 | tf_op jit(solution)/shard_map/attend/pallas_call | solution.py:165
  120.3 0.0 collective-permute-done.2.refs_2_
  120.3 0.0 collective-permute-done.4.refs_3_
  120.3 0.0 collective-permute-done.7.refs_4_
  120.3 0.0 collective-permute-done.9.refs_5_
  120.3 13.1 %attend_final.1 = (bf16[192,1536]{1,0:T(8,128)(2,1)}, bf16[192,768]{1,0:T(8,128)(2,1)S(1)}) custom-call(s32[2]{0:T(128)S(1)} %copy-done.1, s32[4,4]{1,0:T(4,128)S(1)} %copy-done.2, s32[4]{0:T(128)S(1)} %copy-done.3, bf16[192,1536]{1,0:T(8,128)(2,1)S(1)} %bitcast.8, bf16[192,768]{1,0:T(8,128)(2,1)S(1)} %collective-permute-done.refs_1_, ...), custom_call_target="tpu_custom_call" | custom-call | flops 905969664 | bytes 2359296 | tf_op jit(solution)/shard_map/attend_final/pallas_call | solution.py:165
  133.4 0.5 collective-permute-start.10
  133.9 6.2 %collective-permute-done.10.piece_ref = bf16[192,768]{1,0:T(8,128)(2,1)S(1)} collective-permute-done((bf16[192,768]{1,0:T(8,128)(2,1)S(1)}, bf16[192,768]{1,0:T(8,128)(2,1)S(1)}, u32[]{:S(2)}, u32[]{:S(2)}) %collective-permute-start.10) | collective-permute-done | bytes 294944 | tf_op jit(solution)/shard_map/ppermute | solution.py:226
  140.1 0.0 copy-start.5
  140.1 0.7 copy-done.5
  140.8 2.4 %put.1 = bf16[192,1536]{1,0:T(8,128)(2,1)} custom-call(s32[2]{0:T(128)} %pad_add_fusion.place_ref, bf16[192,768]{1,0:T(8,128)(2,1)} %copy-done.5, bf16[192,1536]{1,0:T(8,128)(2,1)} %get-tuple-element.18.whole_ref), custom_call_target="tpu_custom_call", output_to_operand_aliasing={{}: (2, {})} | custom-call | tf_op jit(solution)/shard_map/put/pallas_call | solution.py:197
Async XLA Ops:
  0.0 93.6 %copy-start = (bf16[1,4,48,1536]{3,2,1,0:T(8,128)(2,1)S(1)}, bf16[1,4,48,1536]{3,2,1,0:T(8,128)(2,1)}, u32[]{:S(2)}) copy-start(bf16[1,4,48,1536]{3,2,1,0:T(8,128)(2,1)} %param.5) | copy-start | bytes 1769476
  0.0 93.6 %copy-start.2 = (s32[4,4]{1,0:T(4,128)S(1)}, s32[4,4]{1,0:T(4,128)}, u32[]{:S(2)}) copy-start(s32[4,4]{1,0:T(4,128)} %flags_ref.3) | copy-start | bytes 196
  0.0 93.6 %copy-start.3 = (s32[4]{0:T(128)S(1)}, s32[4]{0:T(128)}, u32[]{:S(2)}) copy-start(s32[4]{0:T(128)} %widths_ref.3) | copy-start | bytes 52
  0.6 93.0 %copy-start.1 = (s32[2]{0:T(128)S(1)}, s32[2]{0:T(128)}, u32[]{:S(2)}) copy-start(s32[2]{0:T(128)} %pad_add_fusion.place_ref) | copy-start | bytes 28
  47.3 15.3 %collective-permute-start.5 = (bf16[2,192,768]{2,1,0:T(8,128)(2,1)}, bf16[2,192,768]{2,1,0:T(8,128)(2,1)S(1)}, u32[]{:S(2)}, u32[]{:S(2)}) collective-permute-start(bf16[2,192,768]{2,1,0:T(8,128)(2,1)} %get-tuple-element.14), channel_id=1, source_target_pairs={{0,2},{2,0},{1,3},{3,1},{4,6},{6,4},{5,7},{7,5},{8,10},{10,8},{9,1... | collective-permute-start | bytes 1769480 | tf_op jit(solution)/shard_map/ppermute | solution.py:226
  47.9 20.6 %collective-permute-start.1 = (bf16[2,192,768]{2,1,0:T(8,128)(2,1)}, bf16[2,192,768]{2,1,0:T(8,128)(2,1)S(1)}, u32[]{:S(2)}, u32[]{:S(2)}) collective-permute-start(bf16[2,192,768]{2,1,0:T(8,128)(2,1)} %get-tuple-element.13.refs_2_), channel_id=1, source_target_pairs={{0,4},{4,8},{8,12},{1,5},{5,9},{9,13},{2,6},{6,10},{10,14},{3,7},{... | collective-permute-start | bytes 1769480 | tf_op jit(solution)/shard_map/ppermute | solution.py:229
  51.3 20.6 %collective-permute-start.3 = (bf16[2,192,768]{2,1,0:T(8,128)(2,1)}, bf16[2,192,768]{2,1,0:T(8,128)(2,1)S(1)}, u32[]{:S(2)}, u32[]{:S(2)}) collective-permute-start(bf16[2,192,768]{2,1,0:T(8,128)(2,1)} %get-tuple-element.13.refs_2_), channel_id=1, source_target_pairs={{4,0},{8,4},{12,8},{5,1},{9,5},{13,9},{6,2},{10,6},{14,10},{7,3},{... | collective-permute-start | bytes 1769480 | tf_op jit(solution)/shard_map/ppermute | solution.py:229
  62.6 18.1 %collective-permute-start.6 = (bf16[2,192,768]{2,1,0:T(8,128)(2,1)S(1)}, bf16[2,192,768]{2,1,0:T(8,128)(2,1)S(1)}, u32[]{:S(2)}, u32[]{:S(2)}) collective-permute-start(bf16[2,192,768]{2,1,0:T(8,128)(2,1)S(1)} %collective-permute-done.5.refs_3_), channel_id=1, source_target_pairs={{0,4},{4,8},{8,12},{1,5},{5,9},{9,13},{2,6},{6,10},{10,14},{3,7},{... | collective-permute-start | bytes 1769480 | tf_op jit(solution)/shard_map/ppermute | solution.py:229
  66.1 18.2 %collective-permute-start.8 = (bf16[2,192,768]{2,1,0:T(8,128)(2,1)S(1)}, bf16[2,192,768]{2,1,0:T(8,128)(2,1)S(1)}, u32[]{:S(2)}, u32[]{:S(2)}) collective-permute-start(bf16[2,192,768]{2,1,0:T(8,128)(2,1)S(1)} %collective-permute-done.5.refs_3_), channel_id=1, source_target_pairs={{4,0},{8,4},{12,8},{5,1},{9,5},{13,9},{6,2},{10,6},{14,10},{7,3},{... | collective-permute-start | bytes 1769480 | tf_op jit(solution)/shard_map/ppermute | solution.py:229
  68.5 51.8 %collective-permute-start.2 = (bf16[2,192,768]{2,1,0:T(8,128)(2,1)S(1)}, bf16[2,192,768]{2,1,0:T(8,128)(2,1)S(1)}, u32[]{:S(2)}, u32[]{:S(2)}) collective-permute-start(bf16[2,192,768]{2,1,0:T(8,128)(2,1)S(1)} %collective-permute-done.1.refs_4_), channel_id=1, source_target_pairs={{0,4},{4,8},{8,12},{1,5},{5,9},{9,13},{2,6},{6,10},{10,14},{3,7},{... | collective-permute-start | bytes 1769480 | tf_op jit(solution)/shard_map/ppermute | solution.py:229
  72.0 48.3 %collective-permute-start.4 = (bf16[2,192,768]{2,1,0:T(8,128)(2,1)S(1)}, bf16[2,192,768]{2,1,0:T(8,128)(2,1)S(1)}, u32[]{:S(2)}, u32[]{:S(2)}) collective-permute-start(bf16[2,192,768]{2,1,0:T(8,128)(2,1)S(1)} %collective-permute-done.3.refs_5_), channel_id=1, source_target_pairs={{4,0},{8,4},{12,8},{5,1},{9,5},{13,9},{6,2},{10,6},{14,10},{7,3},{... | collective-permute-start | bytes 1769480 | tf_op jit(solution)/shard_map/ppermute | solution.py:229
  80.7 39.5 %collective-permute-start.7 = (bf16[2,192,768]{2,1,0:T(8,128)(2,1)S(1)}, bf16[2,192,768]{2,1,0:T(8,128)(2,1)S(1)}, u32[]{:S(2)}, u32[]{:S(2)}) collective-permute-start(bf16[2,192,768]{2,1,0:T(8,128)(2,1)S(1)} %collective-permute-done.6.refs_6_), channel_id=1, source_target_pairs={{0,4},{4,8},{8,12},{1,5},{5,9},{9,13},{2,6},{6,10},{10,14},{3,7},{... | collective-permute-start | bytes 1769480 | tf_op jit(solution)/shard_map/ppermute | solution.py:229
  84.2 36.1 %collective-permute-start.9 = (bf16[2,192,768]{2,1,0:T(8,128)(2,1)S(1)}, bf16[2,192,768]{2,1,0:T(8,128)(2,1)S(1)}, u32[]{:S(2)}, u32[]{:S(2)}) collective-permute-start(bf16[2,192,768]{2,1,0:T(8,128)(2,1)S(1)} %collective-permute-done.8.refs_7_), channel_id=1, source_target_pairs={{4,0},{8,4},{12,8},{5,1},{9,5},{13,9},{6,2},{10,6},{14,10},{7,3},{... | collective-permute-start | bytes 1769480 | tf_op jit(solution)/shard_map/ppermute | solution.py:229
  86.6 7.0 %collective-permute-start = (bf16[192,768]{1,0:T(8,128)(2,1)}, bf16[192,768]{1,0:T(8,128)(2,1)S(1)}, u32[]{:S(2)}, u32[]{:S(2)}) collective-permute-start(bf16[192,768]{1,0:T(8,128)(2,1)} %get-tuple-element.12), channel_id=1, source_target_pairs={{0,2},{2,0},{1,3},{3,1},{4,6},{6,4},{5,7},{7,5},{8,10},{10,8},{9,1... | collective-permute-start | bytes 884744 | tf_op jit(solution)/shard_map/ppermute | solution.py:226
  93.7 1.1 copy-start.4
  133.4 6.7 %collective-permute-start.10 = (bf16[192,768]{1,0:T(8,128)(2,1)S(1)}, bf16[192,768]{1,0:T(8,128)(2,1)S(1)}, u32[]{:S(2)}, u32[]{:S(2)}) collective-permute-start(bf16[192,768]{1,0:T(8,128)(2,1)S(1)} %get-tuple-element.17), channel_id=1, source_target_pairs={{0,2},{2,0},{1,3},{3,1},{4,6},{6,4},{5,7},{7,5},{8,10},{10,8},{9,1... | collective-permute-start | bytes 884744 | tf_op jit(solution)/shard_map/ppermute | solution.py:226
  140.1 0.7 copy-start.5

commit v2 on v1

v2 whole, which is shorter than its diff:
```python
import functools
import math

import jax
import jax.numpy as jnp
from jax import lax
from jax.experimental import pallas as pl
from jax.experimental.pallas import tpu as pltpu
from jax.sharding import PartitionSpec as P

HEAD_DIM = 128
NEG_FILL = -1e30
VMEM_LIMIT = 40 * 1024 * 1024
NT = (((1,), (1,)), ((), ()))
TN = (((0,), (0,)), ((), ()))


def pack_kernel(spaces, place_ref, q_ref, k_ref, v_ref, *outs):
    width = outs[0].shape[-1]
    here = place_ref[1]
    for offset in range(spaces):
        column = pl.multiple_of(lax.rem(here + offset, spaces) * width, HEAD_DIM)
        outs[offset][0] = k_ref[:, pl.ds(column, width)]
        outs[offset][1] = v_ref[:, pl.ds(column, width)]
        if offset > 0:
            outs[spaces + offset - 1][...] = q_ref[:, pl.ds(column, width)]


def pack(place, q, k, v, spaces):
    tokens, features = q.shape
    width = features // spaces
    shapes = [jax.ShapeDtypeStruct((2, tokens, width), q.dtype)] * spaces
    shapes += [jax.ShapeDtypeStruct((tokens, width), q.dtype)] * (spaces - 1)
    return pl.pallas_call(
        functools.partial(pack_kernel, spaces),
        in_specs=[pl.BlockSpec(memory_space=pltpu.SMEM)]
        + [pl.BlockSpec(memory_space=pltpu.VMEM)] * 3,
        out_specs=[pl.BlockSpec(memory_space=pltpu.VMEM)] * len(shapes),
        out_shape=shapes,
        compiler_params=pltpu.CompilerParams(vmem_limit_bytes=VMEM_LIMIT),
        name="pack",
    )(place, q, k, v)


def attend_kernel(
    spaces, frames, columns, row_band, groups, fresh, final,
    place_ref, flags_ref, widths_ref, *refs,
):
    refs = list(refs)
    queries = [refs.pop(0) for unused in range(spaces)]
    keyvals = [[refs.pop(0) for unused in range(spaces)] for unused in groups]
    state_in = None if fresh else (refs.pop(0), refs.pop(0))
    outs = [refs.pop(0) for unused in range(spaces if final else 2)]
    query_ref, key_ref, acc_ref, stat_ref = refs
    tokens = queries[0].shape[0]
    frame_now, space_now = place_ref[0], place_ref[1]
    scale = math.log2(math.e) / math.sqrt(HEAD_DIM)

    def first_row(offset):
        return lax.rem(space_now - offset + spaces, spaces) * row_band

    def asked_of(group):
        slot, hops = group
        side = 1 - 2 * lax.rem(frame_now + slot, 2)
        key_frame = frame_now + side * hops
        safe = jnp.clip(key_frame, 0, frames - 1)
        known = (key_frame >= 0) & (key_frame < frames)
        return known & (flags_ref[frame_now, safe] > 0)

    @pl.when(pl.program_id(0) == 0)
    def _():
        token = lax.broadcasted_iota(jnp.int32, (tokens, HEAD_DIM), 0)
        row = lax.broadcasted_iota(jnp.int32, (tokens, HEAD_DIM), 1)
        for offset in range(spaces):
            rows = pl.ds(offset * tokens, tokens)
            start = (row - first_row(offset)) * columns
            hit = (token >= start) & (token < start + columns)
            query_ref[rows, HEAD_DIM:] = jnp.where(hit, 1.0, 0.0).astype(query_ref.dtype)
            for n, group in enumerate(groups):
                if group[1] > 0:
                    reach = widths_ref[group[1]] * columns
                    near = (token >= start - reach) & (token < start + columns + reach)
                    key_ref[n, rows, HEAD_DIM:] = jnp.where(near, 0.0, NEG_FILL).astype(
                        key_ref.dtype
                    )

    for offset in range(spaces):
        query_ref[pl.ds(offset * tokens, tokens), :HEAD_DIM] = queries[offset][...]

    def step(scores, values, old):
        top = jnp.max(scores, axis=0, keepdims=True) * scale
        if old is not None:
            top = jnp.maximum(top, old[0])
        weights = jnp.exp2(scores * scale - top)
        total = jnp.sum(weights, axis=0, keepdims=True)
        acc = lax.dot_general(
            values, weights.astype(jnp.bfloat16), TN, preferred_element_type=jnp.float32
        )
        if old is not None:
            fade = jnp.exp2(old[0] - top)
            total = total + old[1] * fade
            acc = acc + acc_ref[...] * fade
        stat_ref[0:1, :] = top
        stat_ref[1:2, :] = total
        acc_ref[...] = acc

    if not fresh:
        acc_ref[...] = state_in[0][0]
        stat_ref[...] = state_in[1][0]

    for n, group in enumerate(groups):
        values = lambda n=n: jnp.concatenate([ref[1] for ref in keyvals[n]], axis=0)
        if group[1] == 0:
            keys = jnp.concatenate([ref[0] for ref in keyvals[n]], axis=0)
            scores = lax.dot_general(
                keys, query_ref[:, :HEAD_DIM], NT, preferred_element_type=jnp.float32
            )
            step(scores, values(), None)
            continue

        @pl.when(asked_of(group))
        def _(n=n, values=values):
            for offset in range(spaces):
                key_ref[n, pl.ds(offset * tokens, tokens), :HEAD_DIM] = keyvals[n][offset][0]
            scores = lax.dot_general(
                key_ref[n], query_ref[...], NT, preferred_element_type=jnp.float32
            )
            step(scores, values(), (stat_ref[0:1, :], stat_ref[1:2, :]))

    if final:
        result = jnp.transpose(acc_ref[...] / stat_ref[1:2, :])
        for offset in range(spaces):
            part = result[offset * tokens : (offset + 1) * tokens]
            outs[offset][...] = part.astype(outs[offset].dtype)
    else:
        outs[0][0] = acc_ref[...]
        outs[1][0] = stat_ref[...]


def attend(scalars, queries, groups, state, final, sizes):
    spaces, frames, columns, row_band, features = sizes
    tokens = queries[0].shape[0]
    width = features // spaces
    heads = width // HEAD_DIM
    count = spaces * tokens
    own_block = pl.BlockSpec((tokens, HEAD_DIM), lambda h, place, *_: (0, place[1] * heads + h))
    block = pl.BlockSpec((tokens, HEAD_DIM), lambda h, *_: (0, h))
    pair = pl.BlockSpec((2, tokens, HEAD_DIM), lambda h, *_: (0, 0, h))
    kept = [
        pl.BlockSpec((1, HEAD_DIM, count), lambda h, *_: (h, 0, 0)),
        pl.BlockSpec((1, 8, count), lambda h, *_: (h, 0, 0)),
    ]
    in_specs = [own_block] + [block] * (spaces - 1) + [pair] * (spaces * len(groups))
    operands = list(queries) + [x for slot, hops, pieces in groups for x in pieces]
    if state is not None:
        in_specs += kept
        operands += list(state)
    if final:
        out_specs = [own_block] + [block] * (spaces - 1)
        out_shape = [jax.ShapeDtypeStruct((tokens, features), jnp.bfloat16)]
        out_shape += [jax.ShapeDtypeStruct((tokens, width), jnp.bfloat16)] * (spaces - 1)
    else:
        out_specs = kept
        out_shape = [
            jax.ShapeDtypeStruct((heads, HEAD_DIM, count), jnp.float32),
            jax.ShapeDtypeStruct((heads, 8, count), jnp.float32),
        ]
    pairs = heads * count * count * len(groups)
    return pl.pallas_call(
        functools.partial(
            attend_kernel, spaces, frames, columns, row_band,
            tuple((slot, hops) for slot, hops, pieces in groups), state is None, final,
        ),
        grid_spec=pltpu.PrefetchScalarGridSpec(
            num_scalar_prefetch=3,
            grid=(heads,),
            in_specs=in_specs,
            out_specs=out_specs,
            scratch_shapes=[
                pltpu.VMEM((count, 2 * HEAD_DIM), jnp.bfloat16),
                pltpu.VMEM((len(groups), count, 2 * HEAD_DIM), jnp.bfloat16),
                pltpu.VMEM((HEAD_DIM, count), jnp.float32),
                pltpu.VMEM((8, count), jnp.float32),
            ],
        ),
        out_shape=out_shape,
        compiler_params=pltpu.CompilerParams(vmem_limit_bytes=VMEM_LIMIT),
        cost_estimate=pl.CostEstimate(
            flops=4 * pairs * HEAD_DIM,
            bytes_accessed=len(groups) * 4 * count * width,
            transcendentals=pairs,
        ),
        name="attend_final" if final else "attend",
    )(*scalars, *operands)


def put_kernel(spaces, offset, place_ref, piece_ref, whole_ref, out_ref, sem):
    width = piece_ref.shape[-1]
    column = pl.multiple_of(lax.rem(place_ref[1] + offset, spaces) * width, HEAD_DIM)
    copy = pltpu.make_async_copy(piece_ref, out_ref.at[:, pl.ds(column, width)], sem)
    copy.start()
    copy.wait()


def put(place, piece, whole, offset, spaces):
    return pl.pallas_call(
        functools.partial(put_kernel, spaces, offset),
        in_specs=[
            pl.BlockSpec(memory_space=pltpu.SMEM),
            pl.BlockSpec(memory_space=pltpu.VMEM),
            pl.BlockSpec(memory_space=pl.ANY),
        ],
        out_specs=pl.BlockSpec(memory_space=pl.ANY),
        out_shape=jax.ShapeDtypeStruct(whole.shape, whole.dtype),
        scratch_shapes=[pltpu.SemaphoreType.DMA],
        input_output_aliases={2: 0},
        name="put",
    )(place, piece, whole)


def shards(spaces, frames, queries, keys, values, flags, widths):
    unused, row_band, columns, features = queries.shape
    tokens = row_band * columns
    place = jnp.stack([lax.axis_index("frame"), lax.axis_index("space")]).astype(jnp.int32)
    scalars = (place, flags, widths)
    sizes = (spaces, frames, columns, row_band, features)
    q, k, v = (x.reshape(tokens, features) for x in (queries, keys, values))
    packed = pack(place, q, k, v, spaces)

    def along_space(x, offset):
        return lax.ppermute(x, "space", [(s, (s + offset) % spaces) for s in range(spaces)])

    def swap(x, slot, hops):
        pairs = []
        for f in range(frames):
            side = 1 if (f + slot) % 2 == 0 else -1
            source = f - side * (hops - 1)
            if 0 <= f + side < frames and 0 <= source < frames:
                pairs.append((f, f + side))
        return lax.ppermute(x, "frame", pairs)

    offsets = range(1, spaces)
    own = [packed[0]] + [along_space(packed[offset], offset) for offset in offsets]
    query_parts = [q] + [along_space(packed[spaces + offset - 1], offset) for offset in offsets]

    waves = [[(0, 0, own)]]
    carried = [own, own]
    for hops in range(1, frames - 1):
        carried = [
            [swap(x, 0, hops) for x in carried[1]],
            [swap(x, 1, hops) for x in carried[0]],
        ]
        waves.append([(0, hops, carried[0]), (1, hops, carried[1])])

    state = None
    for n, wave in enumerate(waves):
        state = attend(scalars, query_parts, wave, state, n == len(waves) - 1, sizes)

    result = state[0]
    for offset in offsets:
        back = along_space(state[offset], -offset)
        result = put(place, back, result, offset, spaces)
    return result.reshape(queries.shape)


def solution(mesh):
    placed = P(("group", "frame"), "space", None, "head")
    return jax.shard_map(
        functools.partial(shards, mesh.shape["space"], mesh.shape["frame"]),
        mesh=mesh,
        in_specs=(placed, placed, placed, P(), P()),
        out_specs=placed,
        check_vma=False,
    )
```

time: 144 us -> 78.6 us (0.55)
  the two profiles are of different devices: /device:TPU:14 before, /device:TPU:10 now
where the time goes in v2:
time: 78.6 us; the launch traced here: 78.3 us
  waiting for transfers between devices  31.7 us (40%)
  Pallas kernels  22.6 us (29%)
  starting transfers between devices  19.9 us (25%)
  local copies, waits for them, and re-layouts  3.92 us (5%)
    ppermute x3, waiting for transfers between devices, along_space(): lax.ppermute(x, 'space', [(s, (s + offset) % spaces) for s in range(space...  23.4 us
    pallas_call x3, Pallas kernels, attend(): pl.pallas_call(functools.partial(attend_kernel, spaces, frames, columns,...  20.2 us
    ppermute x8, starting transfers between devices, swap(): return lax.ppermute(x, 'frame', pairs)  18.2 us
    ppermute x8, waiting for transfers between devices, swap(): return lax.ppermute(x, 'frame', pairs)  8.28 us
    unnamed x14, local copies, waits for them, and re-layouts  3.92 us
    pallas_call x1, Pallas kernels, put(): pl.pallas_call(functools.partial(put_kernel, spaces, offset), in_specs=[p...  1.7 us
    ppermute x3, starting transfers between devices, along_space(): lax.ppermute(x, 'space', [(s, (s + offset) % spaces) for s in range(space...  1.68 us
  transfers between devices with their start and end apart: 11, of which 4 were waited for; matrix products, arithmetic and copies ran while one was open for 0% of the time, Pallas kernels for 17%

profile of v2, /device:TPU:10, one launch (start us, length us, event | category | flops | bytes accessed | tf_op | source)
XLA Modules:
  0.0 78.3 jit_solution(7197466960932756288)
XLA Ops:
  0.0 0.0 copy-start.3
  0.0 0.0 copy-start.5
  0.0 0.1 pad_add_fusion.place_ref
  0.1 0.0 copy-start.4
  0.1 0.0 copy-start
  0.1 1.1 %copy-done = bf16[1,4,48,1536]{3,2,1,0:T(8,128)(2,1)S(1)} copy-done((bf16[1,4,48,1536]{3,2,1,0:T(8,128)(2,1)S(1)}, bf16[1,4,48,1536]{3,2,1,0:T(8,128)(2,1)}, u32[]{:S(2)}) %copy-start) | copy-done | bytes 589848
  1.1 0.0 copy-start.1
  1.2 1.1 %copy-done.1 = bf16[1,4,48,1536]{3,2,1,0:T(8,128)(2,1)S(1)} copy-done((bf16[1,4,48,1536]{3,2,1,0:T(8,128)(2,1)S(1)}, bf16[1,4,48,1536]{3,2,1,0:T(8,128)(2,1)}, u32[]{:S(2)}) %copy-start.1) | copy-done | bytes 589848
  2.2 0.0 copy-start.2
  2.2 1.1 %copy-done.2 = bf16[1,4,48,1536]{3,2,1,0:T(8,128)(2,1)S(1)} copy-done((bf16[1,4,48,1536]{3,2,1,0:T(8,128)(2,1)S(1)}, bf16[1,4,48,1536]{3,2,1,0:T(8,128)(2,1)}, u32[]{:S(2)}) %copy-start.2) | copy-done | bytes 589848
  3.3 0.6 pack.1
  3.9 0.6 collective-permute-start.3
  4.5 3.5 %collective-permute-start.1 = (bf16[2,192,768]{2,1,0:T(8,128)(2,1)S(1)}, bf16[2,192,768]{2,1,0:T(8,128)(2,1)S(1)}, u32[]{:S(2)}, u32[]{:S(2)}) collective-permute-start(bf16[2,192,768]{2,1,0:T(8,128)(2,1)S(1)} %get-tuple-element.15.refs_2_), channel_id=1, source_target_pairs={{4,8},{8,4},{5,9},{9,5},{6,10},{10,6},{7,11},{11,7},{20,24},{24,20... | collective-permute-start | bytes 1769480 | tf_op jit(solution)/shard_map/ppermute | solution.py:240
  8.0 0.1 collective-permute-start.6
  8.1 11.0 %collective-permute-done.3.refs_3_ = bf16[2,192,768]{2,1,0:T(8,128)(2,1)S(1)} collective-permute-done((bf16[2,192,768]{2,1,0:T(8,128)(2,1)S(1)}, bf16[2,192,768]{2,1,0:T(8,128)(2,1)S(1)}, u32[]{:S(2)}, u32[]{:S(2)}) %collective-permute-start.3) | collective-permute-done | bytes 589856 | tf_op jit(solution)/shard_map/ppermute | solution.py:231
  19.1 3.5 %collective-permute-start.4 = (bf16[2,192,768]{2,1,0:T(8,128)(2,1)S(1)}, bf16[2,192,768]{2,1,0:T(8,128)(2,1)S(1)}, u32[]{:S(2)}, u32[]{:S(2)}) collective-permute-start(bf16[2,192,768]{2,1,0:T(8,128)(2,1)S(1)} %collective-permute-done.3.refs_3_), channel_id=1, source_target_pairs={{4,8},{8,4},{5,9},{9,5},{6,10},{10,6},{7,11},{11,7},{20,24},{24,20... | collective-permute-start | bytes 1769480 | tf_op jit(solution)/shard_map/ppermute | solution.py:240
  22.5 0.1 collective-permute-start.8
  22.6 0.0 collective-permute-done.1.refs_4_
  22.6 3.9 %collective-permute-start.2 = (bf16[2,192,768]{2,1,0:T(8,128)(2,1)S(1)}, bf16[2,192,768]{2,1,0:T(8,128)(2,1)S(1)}, u32[]{:S(2)}, u32[]{:S(2)}) collective-permute-start(bf16[2,192,768]{2,1,0:T(8,128)(2,1)S(1)} %collective-permute-done.1.refs_4_), channel_id=1, source_target_pairs={{4,0},{8,12},{5,1},{9,13},{6,2},{10,14},{7,3},{11,15},{20,16},{24,... | collective-permute-start | bytes 1769480 | tf_op jit(solution)/shard_map/ppermute | solution.py:240
  26.6 0.0 collective-permute-done.6.refs_2_
  26.6 2.4 %collective-permute-start.7 = (bf16[2,192,768]{2,1,0:T(8,128)(2,1)S(1)}, bf16[2,192,768]{2,1,0:T(8,128)(2,1)S(1)}, u32[]{:S(2)}, u32[]{:S(2)}) collective-permute-start(bf16[2,192,768]{2,1,0:T(8,128)(2,1)S(1)} %collective-permute-done.6.refs_2_), channel_id=1, source_target_pairs={{4,8},{8,4},{5,9},{9,5},{6,10},{10,6},{7,11},{11,7},{20,24},{24,20... | collective-permute-start | bytes 1769480 | tf_op jit(solution)/shard_map/ppermute | solution.py:240
  29.0 8.3 %collective-permute-done.4.refs_5_ = bf16[2,192,768]{2,1,0:T(8,128)(2,1)S(1)} collective-permute-done((bf16[2,192,768]{2,1,0:T(8,128)(2,1)S(1)}, bf16[2,192,768]{2,1,0:T(8,128)(2,1)S(1)}, u32[]{:S(2)}, u32[]{:S(2)}) %collective-permute-start.4) | collective-permute-done | bytes 589856 | tf_op jit(solution)/shard_map/ppermute | solution.py:240
  37.2 1.3 %collective-permute-start.5 = (bf16[2,192,768]{2,1,0:T(8,128)(2,1)S(1)}, bf16[2,192,768]{2,1,0:T(8,128)(2,1)S(1)}, u32[]{:S(2)}, u32[]{:S(2)}) collective-permute-start(bf16[2,192,768]{2,1,0:T(8,128)(2,1)S(1)} %collective-permute-done.4.refs_5_), channel_id=1, source_target_pairs={{4,0},{8,12},{5,1},{9,13},{6,2},{10,14},{7,3},{11,15},{20,16},{24,... | collective-permute-start | bytes 1769480 | tf_op jit(solution)/shard_map/ppermute | solution.py:240
  38.5 0.0 collective-permute-done.8.refs_3_
  38.5 3.5 %collective-permute-start.9 = (bf16[2,192,768]{2,1,0:T(8,128)(2,1)S(1)}, bf16[2,192,768]{2,1,0:T(8,128)(2,1)S(1)}, u32[]{:S(2)}, u32[]{:S(2)}) collective-permute-start(bf16[2,192,768]{2,1,0:T(8,128)(2,1)S(1)} %collective-permute-done.8.refs_3_), channel_id=1, source_target_pairs={{4,8},{8,4},{5,9},{9,5},{6,10},{10,6},{7,11},{11,7},{20,24},{24,20... | collective-permute-start | bytes 1769480 | tf_op jit(solution)/shard_map/ppermute | solution.py:240
  42.0 0.6 collective-permute-start
  42.6 6.2 %collective-permute-done.refs_1_ = bf16[192,768]{1,0:T(8,128)(2,1)S(1)} collective-permute-done((bf16[192,768]{1,0:T(8,128)(2,1)S(1)}, bf16[192,768]{1,0:T(8,128)(2,1)S(1)}, u32[]{:S(2)}, u32[]{:S(2)}) %collective-permute-start) | collective-permute-done | bytes 294944 | tf_op jit(solution)/shard_map/ppermute | solution.py:231
  48.8 0.0 copy-done.3
  48.8 0.0 copy-done.5
  48.8 4.6 %attend.2 = (f32[6,128,384]{2,1,0:T(8,128)S(1)}, f32[6,8,384]{2,1,0:T(8,128)S(1)}) custom-call(s32[2]{0:T(128)S(1)} %pad_add_fusion.place_ref, s32[4,4]{1,0:T(4,128)S(1)} %copy-done.3, s32[4]{0:T(128)S(1)} %copy-done.5, bf16[192,1536]{1,0:T(8,128)(2,1)S(1)} %bitcast.7, bf16[192,768]{1,0:T(8,128)(2,1)S(1)} %collective-permute-done.refs_1_, ...), custom_call_target="tpu_custom_call" | custom-call | flops 452984832 | bytes 1179648 | tf_op jit(solution)/shard_map/attend/pallas_call | solution.py:169
  53.4 8.9 %attend.3 = (f32[6,128,384]{2,1,0:T(8,128)S(1)}, f32[6,8,384]{2,1,0:T(8,128)S(1)}) custom-call(s32[2]{0:T(128)S(1)} %pad_add_fusion.place_ref, s32[4,4]{1,0:T(4,128)S(1)} %copy-done.3, s32[4]{0:T(128)S(1)} %copy-done.5, bf16[192,1536]{1,0:T(8,128)(2,1)S(1)} %bitcast.8, bf16[192,768]{1,0:T(8,128)(2,1)S(1)} %collective-permute-done.refs_1_, ...), custom_call_target="tpu_custom_call" | custom-call | flops 905969664 | bytes 2359296 | tf_op jit(solution)/shard_map/attend/pallas_call | solution.py:169
  62.3 0.0 collective-permute-done.2.refs_2_
  62.3 0.0 collective-permute-done.7.refs_4_
  62.3 0.0 collective-permute-done.5.refs_3_
  62.3 0.0 collective-permute-done.9.refs_5_
  62.3 0.0 copy-done.4
  62.3 6.8 %attend_final.1 = (bf16[192,1536]{1,0:T(8,128)(2,1)}, bf16[192,768]{1,0:T(8,128)(2,1)S(1)}) custom-call(s32[2]{0:T(128)S(1)} %pad_add_fusion.place_ref, s32[4,4]{1,0:T(4,128)S(1)} %copy-done.3, s32[4]{0:T(128)S(1)} %copy-done.5, bf16[192,1536]{1,0:T(8,128)(2,1)S(1)} %bitcast.9, bf16[192,768]{1,0:T(8,128)(2,1)S(1)} %collective-permute-done.refs_1_, ...), custom_call_target="tpu_custom_call" | custom-call | flops 905969664 | bytes 2359296 | tf_op jit(solution)/shard_map/attend_final/pallas_call | solution.py:169
  69.1 0.5 collective-permute-start.10
  69.6 6.2 %collective-permute-done.10.piece_ref = bf16[192,768]{1,0:T(8,128)(2,1)S(1)} collective-permute-done((bf16[192,768]{1,0:T(8,128)(2,1)S(1)}, bf16[192,768]{1,0:T(8,128)(2,1)S(1)}, u32[]{:S(2)}, u32[]{:S(2)}) %collective-permute-start.10) | collective-permute-done | bytes 294944 | tf_op jit(solution)/shard_map/ppermute | solution.py:231
  75.8 0.0 copy-start.6
  75.8 0.7 copy-done.6
  76.6 1.7 %put.1 = bf16[192,1536]{1,0:T(8,128)(2,1)} custom-call(s32[2]{0:T(128)} %copy-done.4, bf16[192,768]{1,0:T(8,128)(2,1)} %copy-done.6, bf16[192,1536]{1,0:T(8,128)(2,1)} %get-tuple-element.22.whole_ref), custom_call_target="tpu_custom_call", output_to_operand_aliasing={{}: (2, {})} | custom-call | tf_op jit(solution)/shard_map/put/pallas_call | solution.py:206
Async XLA Ops:
  0.0 48.8 %copy-start.3 = (s32[4,4]{1,0:T(4,128)S(1)}, s32[4,4]{1,0:T(4,128)}, u32[]{:S(2)}) copy-start(s32[4,4]{1,0:T(4,128)} %flags_ref.5) | copy-start | bytes 196
  0.0 48.8 %copy-start.5 = (s32[4]{0:T(128)S(1)}, s32[4]{0:T(128)}, u32[]{:S(2)}) copy-start(s32[4]{0:T(128)} %widths_ref.5) | copy-start | bytes 52
  0.1 62.3 %copy-start.4 = (s32[2]{0:T(128)}, s32[2]{0:T(128)S(1)}, u32[]{:S(2)}) copy-start(s32[2]{0:T(128)S(1)} %pad_add_fusion.place_ref) | copy-start | bytes 28
  0.1 1.1 %copy-start = (bf16[1,4,48,1536]{3,2,1,0:T(8,128)(2,1)S(1)}, bf16[1,4,48,1536]{3,2,1,0:T(8,128)(2,1)}, u32[]{:S(2)}) copy-start(bf16[1,4,48,1536]{3,2,1,0:T(8,128)(2,1)} %param.5) | copy-start | bytes 1769476
  1.1 1.1 %copy-start.1 = (bf16[1,4,48,1536]{3,2,1,0:T(8,128)(2,1)S(1)}, bf16[1,4,48,1536]{3,2,1,0:T(8,128)(2,1)}, u32[]{:S(2)}) copy-start(bf16[1,4,48,1536]{3,2,1,0:T(8,128)(2,1)} %param.6) | copy-start | bytes 1769476
  2.2 1.1 %copy-start.2 = (bf16[1,4,48,1536]{3,2,1,0:T(8,128)(2,1)S(1)}, bf16[1,4,48,1536]{3,2,1,0:T(8,128)(2,1)}, u32[]{:S(2)}) copy-start(bf16[1,4,48,1536]{3,2,1,0:T(8,128)(2,1)} %param.7) | copy-start | bytes 1769476
  3.9 15.1 %collective-permute-start.3 = (bf16[2,192,768]{2,1,0:T(8,128)(2,1)S(1)}, bf16[2,192,768]{2,1,0:T(8,128)(2,1)S(1)}, u32[]{:S(2)}, u32[]{:S(2)}) collective-permute-start(bf16[2,192,768]{2,1,0:T(8,128)(2,1)S(1)} %get-tuple-element.16), channel_id=1, source_target_pairs={{0,2},{2,0},{1,3},{3,1},{4,6},{6,4},{5,7},{7,5},{8,10},{10,8},{9,1... | collective-permute-start | bytes 1769480 | tf_op jit(solution)/shard_map/ppermute | solution.py:231
  4.5 18.1 %collective-permute-start.1 = (bf16[2,192,768]{2,1,0:T(8,128)(2,1)S(1)}, bf16[2,192,768]{2,1,0:T(8,128)(2,1)S(1)}, u32[]{:S(2)}, u32[]{:S(2)}) collective-permute-start(bf16[2,192,768]{2,1,0:T(8,128)(2,1)S(1)} %get-tuple-element.15.refs_2_), channel_id=1, source_target_pairs={{4,8},{8,4},{5,9},{9,5},{6,10},{10,6},{7,11},{11,7},{20,24},{24,20... | collective-permute-start | bytes 1769480 | tf_op jit(solution)/shard_map/ppermute | solution.py:240
  8.0 18.6 %collective-permute-start.6 = (bf16[2,192,768]{2,1,0:T(8,128)(2,1)S(1)}, bf16[2,192,768]{2,1,0:T(8,128)(2,1)S(1)}, u32[]{:S(2)}, u32[]{:S(2)}) collective-permute-start(bf16[2,192,768]{2,1,0:T(8,128)(2,1)S(1)} %get-tuple-element.15.refs_2_), channel_id=1, source_target_pairs={{0,4},{4,0},{8,12},{12,8},{1,5},{5,1},{9,13},{13,9},{2,6},{6,2},{1... | collective-permute-start | bytes 1769480 | tf_op jit(solution)/shard_map/ppermute | solution.py:240
  19.1 18.1 %collective-permute-start.4 = (bf16[2,192,768]{2,1,0:T(8,128)(2,1)S(1)}, bf16[2,192,768]{2,1,0:T(8,128)(2,1)S(1)}, u32[]{:S(2)}, u32[]{:S(2)}) collective-permute-start(bf16[2,192,768]{2,1,0:T(8,128)(2,1)S(1)} %collective-permute-done.3.refs_3_), channel_id=1, source_target_pairs={{4,8},{8,4},{5,9},{9,5},{6,10},{10,6},{7,11},{11,7},{20,24},{24,20... | collective-permute-start | bytes 1769480 | tf_op jit(solution)/shard_map/ppermute | solution.py:240
  22.5 16.0 %collective-permute-start.8 = (bf16[2,192,768]{2,1,0:T(8,128)(2,1)S(1)}, bf16[2,192,768]{2,1,0:T(8,128)(2,1)S(1)}, u32[]{:S(2)}, u32[]{:S(2)}) collective-permute-start(bf16[2,192,768]{2,1,0:T(8,128)(2,1)S(1)} %collective-permute-done.3.refs_3_), channel_id=1, source_target_pairs={{0,4},{4,0},{8,12},{12,8},{1,5},{5,1},{9,13},{13,9},{2,6},{6,2},{1... | collective-permute-start | bytes 1769480 | tf_op jit(solution)/shard_map/ppermute | solution.py:240
  22.6 39.7 %collective-permute-start.2 = (bf16[2,192,768]{2,1,0:T(8,128)(2,1)S(1)}, bf16[2,192,768]{2,1,0:T(8,128)(2,1)S(1)}, u32[]{:S(2)}, u32[]{:S(2)}) collective-permute-start(bf16[2,192,768]{2,1,0:T(8,128)(2,1)S(1)} %collective-permute-done.1.refs_4_), channel_id=1, source_target_pairs={{4,0},{8,12},{5,1},{9,13},{6,2},{10,14},{7,3},{11,15},{20,16},{24,... | collective-permute-start | bytes 1769480 | tf_op jit(solution)/shard_map/ppermute | solution.py:240
  26.6 35.7 %collective-permute-start.7 = (bf16[2,192,768]{2,1,0:T(8,128)(2,1)S(1)}, bf16[2,192,768]{2,1,0:T(8,128)(2,1)S(1)}, u32[]{:S(2)}, u32[]{:S(2)}) collective-permute-start(bf16[2,192,768]{2,1,0:T(8,128)(2,1)S(1)} %collective-permute-done.6.refs_2_), channel_id=1, source_target_pairs={{4,8},{8,4},{5,9},{9,5},{6,10},{10,6},{7,11},{11,7},{20,24},{24,20... | collective-permute-start | bytes 1769480 | tf_op jit(solution)/shard_map/ppermute | solution.py:240
  37.2 25.1 %collective-permute-start.5 = (bf16[2,192,768]{2,1,0:T(8,128)(2,1)S(1)}, bf16[2,192,768]{2,1,0:T(8,128)(2,1)S(1)}, u32[]{:S(2)}, u32[]{:S(2)}) collective-permute-start(bf16[2,192,768]{2,1,0:T(8,128)(2,1)S(1)} %collective-permute-done.4.refs_5_), channel_id=1, source_target_pairs={{4,0},{8,12},{5,1},{9,13},{6,2},{10,14},{7,3},{11,15},{20,16},{24,... | collective-permute-start | bytes 1769480 | tf_op jit(solution)/shard_map/ppermute | solution.py:240
  38.5 23.8 %collective-permute-start.9 = (bf16[2,192,768]{2,1,0:T(8,128)(2,1)S(1)}, bf16[2,192,768]{2,1,0:T(8,128)(2,1)S(1)}, u32[]{:S(2)}, u32[]{:S(2)}) collective-permute-start(bf16[2,192,768]{2,1,0:T(8,128)(2,1)S(1)} %collective-permute-done.8.refs_3_), channel_id=1, source_target_pairs={{4,8},{8,4},{5,9},{9,5},{6,10},{10,6},{7,11},{11,7},{20,24},{24,20... | collective-permute-start | bytes 1769480 | tf_op jit(solution)/shard_map/ppermute | solution.py:240
  42.0 6.8 %collective-permute-start = (bf16[192,768]{1,0:T(8,128)(2,1)S(1)}, bf16[192,768]{1,0:T(8,128)(2,1)S(1)}, u32[]{:S(2)}, u32[]{:S(2)}) collective-permute-start(bf16[192,768]{1,0:T(8,128)(2,1)S(1)} %get-tuple-element.14), channel_id=1, source_target_pairs={{0,2},{2,0},{1,3},{3,1},{4,6},{6,4},{5,7},{7,5},{8,10},{10,8},{9,1... | collective-permute-start | bytes 884744 | tf_op jit(solution)/shard_map/ppermute | solution.py:231
  69.1 6.7 %collective-permute-start.10 = (bf16[192,768]{1,0:T(8,128)(2,1)S(1)}, bf16[192,768]{1,0:T(8,128)(2,1)S(1)}, u32[]{:S(2)}, u32[]{:S(2)}) collective-permute-start(bf16[192,768]{1,0:T(8,128)(2,1)S(1)} %get-tuple-element.21), channel_id=1, source_target_pairs={{0,2},{2,0},{1,3},{3,1},{4,6},{6,4},{5,7},{7,5},{8,10},{10,8},{9,1... | collective-permute-start | bytes 884744 | tf_op jit(solution)/shard_map/ppermute | solution.py:231
  75.8 0.7 copy-start.6

commit v3 on v2

v3 whole, which is shorter than its diff:
```python
import functools
import math

import jax
import jax.numpy as jnp
from jax import lax
from jax.experimental import pallas as pl
from jax.experimental.pallas import tpu as pltpu
from jax.sharding import PartitionSpec as P

HEAD_DIM = 128
NEG_FILL = -1e30
VMEM_LIMIT = 40 * 1024 * 1024
NT = (((1,), (1,)), ((), ()))
TN = (((0,), (0,)), ((), ()))


def pack_kernel(spaces, jobs, place_ref, *refs):
    sems = refs[-1]
    here = place_ref[1]
    copies = []
    for n, (source, offset, first, width, target, row) in enumerate(jobs):
        share = refs[source].shape[-1] // spaces
        column = pl.multiple_of(lax.rem(here + offset, spaces) * share + first, HEAD_DIM)
        out = refs[target] if row is None else refs[target].at[row]
        copy = pltpu.make_async_copy(refs[source].at[:, pl.ds(column, width)], out, sems.at[n])
        copy.start()
        copies.append(copy)
    for copy in copies:
        copy.wait()


def pack(place, sources, blocks, after, spaces):
    tokens = sources[0].shape[0]
    several = len(sources) > 1
    jobs, shapes = [], []
    first_out = len(sources) + len(after)
    for n, (offset, first, width) in enumerate(blocks):
        lead = (len(sources),) if several else ()
        shapes.append(jax.ShapeDtypeStruct(lead + (tokens, width), sources[0].dtype))
        for row in range(len(sources)):
            jobs.append((row, offset, first, width, first_out + n, row if several else None))
    return pl.pallas_call(
        functools.partial(pack_kernel, spaces, tuple(jobs)),
        in_specs=[pl.BlockSpec(memory_space=pltpu.SMEM)]
        + [pl.BlockSpec(memory_space=pltpu.HBM)] * len(sources)
        + [pl.BlockSpec(memory_space=pl.ANY)] * len(after),
        out_specs=[pl.BlockSpec(memory_space=pltpu.VMEM)] * len(shapes),
        out_shape=shapes,
        scratch_shapes=[pltpu.SemaphoreType.DMA((len(jobs),))],
        compiler_params=pltpu.CompilerParams(vmem_limit_bytes=VMEM_LIMIT),
        name="pack",
    )(place, *sources, *after)


def tie(array, after):
    return pl.pallas_call(
        lambda array_ref, after_ref, out_ref: None,
        in_specs=[pl.BlockSpec(memory_space=pl.ANY)] * 2,
        out_specs=pl.BlockSpec(memory_space=pl.ANY),
        out_shape=jax.ShapeDtypeStruct(array.shape, array.dtype),
        input_output_aliases={0: 0},
        name="tie",
    )(array, after)


def attend_kernel(
    spaces, frames, columns, row_band, together, groups, fresh, final, kept_whole,
    place_ref, flags_ref, widths_ref, *refs,
):
    refs = list(refs)
    queries = [refs.pop(0) for unused in range(spaces)]
    keyvals = [[refs.pop(0) for unused in range(spaces)] for unused in groups]
    state_in = None if fresh else (refs.pop(0), refs.pop(0))
    if kept_whole:
        refs.pop(0)
    outs = [refs.pop(0) for unused in range(spaces if final else 2)]
    query_ref, key_ref, acc_ref, stat_ref = refs
    tokens = queries[0].shape[0]
    frame_now, space_now = place_ref[0], place_ref[1]
    scale = math.log2(math.e) / math.sqrt(HEAD_DIM)

    def first_row(offset):
        return lax.rem(space_now - offset + spaces, spaces) * row_band

    def asked_of(group):
        slot, hops = group
        side = 1 - 2 * lax.rem(frame_now + slot, 2)
        key_frame = frame_now + side * hops
        safe = jnp.clip(key_frame, 0, frames - 1)
        known = (key_frame >= 0) & (key_frame < frames)
        return known & (flags_ref[frame_now, safe] > 0)

    @pl.when(pl.program_id(0) == 0)
    def _():
        token = lax.broadcasted_iota(jnp.int32, (tokens, HEAD_DIM), 0)
        row = lax.broadcasted_iota(jnp.int32, (tokens, HEAD_DIM), 1)
        for offset in range(spaces):
            rows = pl.ds(offset * tokens, tokens)
            start = (row - first_row(offset)) * columns
            hit = (token >= start) & (token < start + columns)
            mark = jnp.where(hit, 1.0, 0.0).astype(query_ref.dtype)
            for h in range(together):
                query_ref[h, rows, HEAD_DIM:] = mark
            for n, group in enumerate(groups):
                if group[1] > 0:
                    reach = widths_ref[group[1]] * columns
                    near = (token >= start - reach) & (token < start + columns + reach)
                    fill = jnp.where(near, 0.0, NEG_FILL).astype(key_ref.dtype)
                    for h in range(together):
                        key_ref[n, h, rows, HEAD_DIM:] = fill

    def lanes(h):
        return pl.ds(h * HEAD_DIM, HEAD_DIM)

    for h in range(together):
        for offset in range(spaces):
            rows = pl.ds(offset * tokens, tokens)
            query_ref[h, rows, :HEAD_DIM] = queries[offset][:, lanes(h)]

    def step(h, scores, refs, old):
        top = jnp.max(scores, axis=0, keepdims=True) * scale
        if old:
            before = stat_ref[h, 0:1, :]
            top = jnp.maximum(top, before)
        weights = jnp.exp2(scores * scale - top)
        total = jnp.sum(weights, axis=0, keepdims=True)
        values = jnp.concatenate([ref[1, :, lanes(h)] for ref in refs], axis=0)
        acc = lax.dot_general(
            values, weights.astype(jnp.bfloat16), TN, preferred_element_type=jnp.float32
        )
        if old:
            fade = jnp.exp2(before - top)
            total = total + stat_ref[h, 1:2, :] * fade
            acc = acc + acc_ref[h] * fade
        stat_ref[h, 0:1, :] = top
        stat_ref[h, 1:2, :] = total
        acc_ref[h] = acc

    if not fresh:
        acc_ref[...] = state_in[0][...]
        stat_ref[...] = state_in[1][...]

    for n, group in enumerate(groups):
        if group[1] == 0:
            scores = []
            for h in range(together):
                keys = jnp.concatenate([ref[0, :, lanes(h)] for ref in keyvals[n]], axis=0)
                scores.append(
                    lax.dot_general(
                        keys, query_ref[h, :, :HEAD_DIM], NT, preferred_element_type=jnp.float32
                    )
                )
            for h in range(together):
                step(h, scores[h], keyvals[n], False)
            continue

        @pl.when(asked_of(group))
        def _(n=n):
            for h in range(together):
                for offset in range(spaces):
                    rows = pl.ds(offset * tokens, tokens)
                    key_ref[n, h, rows, :HEAD_DIM] = keyvals[n][offset][0, :, lanes(h)]
            scores = [
                lax.dot_general(
                    key_ref[n, h], query_ref[h], NT, preferred_element_type=jnp.float32
                )
                for h in range(together)
            ]
            for h in range(together):
                step(h, scores[h], keyvals[n], True)

    if final:
        for h in range(together):
            result = jnp.transpose(acc_ref[h] * (1.0 / stat_ref[h, 1:2, :]))
            for offset in range(spaces):
                part = result[offset * tokens : (offset + 1) * tokens]
                outs[offset][:, lanes(h)] = part.astype(outs[offset].dtype)
    else:
        outs[0][...] = acc_ref[...]
        outs[1][...] = stat_ref[...]


def attend(scalars, queries, groups, state, final, whole, chunk, sizes):
    spaces, frames, columns, row_band, features = sizes
    first, heads = chunk
    tokens = queries[0].shape[0]
    width = features // spaces
    all_heads = width // HEAD_DIM
    count = spaces * tokens
    together = 2 if all(x % 2 == 0 for x in (all_heads, first, heads)) else 1
    lanes = together * HEAD_DIM
    own_block = pl.BlockSpec(
        (tokens, lanes), lambda h, place, *_: (0, (place[1] * all_heads + first) // together + h)
    )

    def block(x):
        skip = first // together if x.shape[-1] == width else 0
        if len(x.shape) == 2:
            return pl.BlockSpec((tokens, lanes), lambda h, *_: (0, skip + h))
        return pl.BlockSpec((2, tokens, lanes), lambda h, *_: (0, 0, skip + h))

    kept = [
        pl.BlockSpec((together, HEAD_DIM, count), lambda h, *_: (h, 0, 0)),
        pl.BlockSpec((together, 8, count), lambda h, *_: (h, 0, 0)),
    ]
    operands = list(queries) + [x for slot, hops, pieces in groups for x in pieces]
    in_specs = [own_block] + [block(x) for x in operands[1:]]
    if state is not None:
        in_specs += kept
        operands += list(state)
    aliases = {}
    if final:
        mine = jax.ShapeDtypeStruct((tokens, features), jnp.bfloat16)
        theirs = jax.ShapeDtypeStruct((tokens, heads * HEAD_DIM), jnp.bfloat16)
        out_shape = [mine] + [theirs] * (spaces - 1)
        out_specs = [own_block] + [block(theirs)] * (spaces - 1)
        if heads == all_heads:
            out_specs = [own_block] + [pl.BlockSpec((tokens, lanes), lambda h, *_: (0, h))] * (
                spaces - 1
            )
        if whole is not None:
            aliases = {3 + len(operands): 0}
            in_specs.append(pl.BlockSpec(memory_space=pl.ANY))
            operands.append(whole)
    else:
        out_specs = kept
        out_shape = [
            jax.ShapeDtypeStruct((heads, HEAD_DIM, count), jnp.float32),
            jax.ShapeDtypeStruct((heads, 8, count), jnp.float32),
        ]
    pairs = heads * count * count * len(groups)
    return pl.pallas_call(
        functools.partial(
            attend_kernel, spaces, frames, columns, row_band, together,
            tuple((slot, hops) for slot, hops, pieces in groups),
            state is None, final, bool(aliases),
        ),
        grid_spec=pltpu.PrefetchScalarGridSpec(
            num_scalar_prefetch=3,
            grid=(heads // together,),
            in_specs=in_specs,
            out_specs=out_specs,
            scratch_shapes=[
                pltpu.VMEM((together, count, 2 * HEAD_DIM), jnp.bfloat16),
                pltpu.VMEM((len(groups), together, count, 2 * HEAD_DIM), jnp.bfloat16),
                pltpu.VMEM((together, HEAD_DIM, count), jnp.float32),
                pltpu.VMEM((together, 8, count), jnp.float32),
            ],
        ),
        out_shape=out_shape,
        input_output_aliases=aliases,
        compiler_params=pltpu.CompilerParams(vmem_limit_bytes=VMEM_LIMIT),
        cost_estimate=pl.CostEstimate(
            flops=4 * pairs * HEAD_DIM,
            bytes_accessed=len(groups) * 4 * count * heads * HEAD_DIM,
            transcendentals=pairs,
        ),
        name="attend_final" if final else "attend",
    )(*scalars, *operands)


def put_kernel(spaces, offset, first, place_ref, piece_ref, whole_ref, out_ref, sem):
    width = piece_ref.shape[-1]
    share = out_ref.shape[-1] // spaces
    column = pl.multiple_of(lax.rem(place_ref[1] + offset, spaces) * share + first, HEAD_DIM)
    copy = pltpu.make_async_copy(piece_ref, out_ref.at[:, pl.ds(column, width)], sem)
    copy.start()
    copy.wait()


def put(place, piece, whole, offset, first, spaces):
    return pl.pallas_call(
        functools.partial(put_kernel, spaces, offset, first),
        in_specs=[
            pl.BlockSpec(memory_space=pltpu.SMEM),
            pl.BlockSpec(memory_space=pltpu.VMEM),
            pl.BlockSpec(memory_space=pl.ANY),
        ],
        out_specs=pl.BlockSpec(memory_space=pl.ANY),
        out_shape=jax.ShapeDtypeStruct(whole.shape, whole.dtype),
        scratch_shapes=[pltpu.SemaphoreType.DMA],
        input_output_aliases={2: 0},
        name="put",
    )(place, piece, whole)


def shards(spaces, frames, queries, keys, values, flags, widths):
    unused, row_band, columns, features = queries.shape
    tokens = row_band * columns
    width = features // spaces
    heads = width // HEAD_DIM
    place = jnp.stack([lax.axis_index("frame"), lax.axis_index("space")]).astype(jnp.int32)
    scalars = (place, flags, widths)
    sizes = (spaces, frames, columns, row_band, features)
    q, k, v = (x.reshape(tokens, features) for x in (queries, keys, values))
    tail = max(heads // 3, 1)
    chunks = [(0, heads - tail), (heads - tail, tail)]
    offsets = range(1, spaces)

    def along_space(x, offset):
        return lax.ppermute(x, "space", [(s, (s + offset) % spaces) for s in range(spaces)])

    def swap(x, slot, hops):
        pairs = []
        for f in range(frames):
            side = 1 if (f + slot) % 2 == 0 else -1
            source = f - side * (hops - 1)
            if 0 <= f + side < frames and 0 <= source < frames:
                pairs.append((f, f + side))
        return lax.ppermute(x, "frame", pairs)

    mine = None
    partners = []
    arrived = []
    for first, number in chunks:
        blocks = [(offset, first * HEAD_DIM, number * HEAD_DIM) for offset in offsets]
        if mine is None:
            mine, *sends = pack(place, (k, v), [(0, 0, width)] + blocks, arrived, spaces)
        else:
            sends = pack(place, (k, v), blocks, arrived, spaces)
        arrived = [along_space(x, offset) for x, offset in zip(sends, offsets)]
        partners.append(arrived)
    sends = pack(place, (q,), [(offset, 0, width) for offset in offsets], arrived, spaces)
    query_parts = [q] + [along_space(x, offset) for x, offset in zip(sends, offsets)]

    carried = [[mine, mine]] + [[x, x] for x in partners]
    states = [None] * len(chunks)
    groups = [[(0, 0, [mine] + partners[c])] for c in range(len(chunks))]
    for hops in range(1, frames - 1):
        sent = []
        for c, (first_slot, second_slot) in enumerate(carried):
            over = [second_slot, first_slot]
            if c == 0:
                sent.append([swap(over[slot], slot, hops) for slot in range(2)])
                continue
            if c == len(chunks) and states[0] is not None:
                over = [[tie(x, states[0][1]) for x in xs] for xs in over]
            sent.append([[swap(x, slot, hops) for x in over[slot]] for slot in range(2)])
        carried = sent
        for c, chunk in enumerate(chunks):
            groups[c] += [
                (slot, hops, [carried[0][slot]] + carried[1 + c][slot]) for slot in range(2)
            ]
            if hops < frames - 2:
                states[c] = attend(
                    scalars, query_parts, groups[c], states[c], False, None, chunk, sizes
                )
                groups[c] = []

    result, returned = None, []
    for c, chunk in enumerate(chunks):
        result, *parts = attend(
            scalars, query_parts, groups[c], states[c], True, result, chunk, sizes
        )
        returned.append([along_space(x, -offset) for x, offset in zip(parts, offsets)])
    for (first, unused), parts in zip(chunks, returned):
        for offset, x in zip(offsets, parts):
            result = put(place, x, result, offset, first * HEAD_DIM, spaces)
    return result.reshape(queries.shape)


def solution(mesh):
    placed = P(("group", "frame"), "space", None, "head")
    return jax.shard_map(
        functools.partial(shards, mesh.shape["space"], mesh.shape["frame"]),
        mesh=mesh,
        in_specs=(placed, placed, placed, P(), P()),
        out_specs=placed,
        check_vma=False,
    )
```

time: 78.6 us -> 75.1 us (0.955)
  the two profiles are of different devices: /device:TPU:10 before, /device:TPU:8 now
where the time goes in v3:
time: 75.1 us; the launch traced here: 74.2 us
  starting transfers between devices  33.1 us (44%)
  Pallas kernels  20.9 us (28%)
  waiting for transfers between devices  13.1 us (17%)
  local copies, waits for them, and re-layouts  6.83 us (9%)
    ppermute x12, starting transfers between devices, swap(): return lax.ppermute(x, 'frame', pairs)  27.4 us
    pallas_call x4, Pallas kernels, attend(): pl.pallas_call(functools.partial(attend_kernel, spaces, frames, columns,...  15.8 us
    ppermute x5, waiting for transfers between devices, along_space(): lax.ppermute(x, 'space', [(s, (s + offset) % spaces) for s in range(space...  8.45 us
    unnamed x32, local copies, waits for them, and re-layouts  6.83 us
    ppermute x5, starting transfers between devices, along_space(): lax.ppermute(x, 'space', [(s, (s + offset) % spaces) for s in range(space...  5.68 us
    ppermute x12, waiting for transfers between devices, swap(): return lax.ppermute(x, 'frame', pairs)  4.63 us
    pallas_call x2, Pallas kernels, put(): pl.pallas_call(functools.partial(put_kernel, spaces, offset, first), in_s...  3.18 us
    pallas_call x3, Pallas kernels, pack(): pl.pallas_call(functools.partial(pack_kernel, spaces, tuple(jobs)), in_sp...  1.84 us
  transfers between devices with their start and end apart: 17, of which 7 were waited for; matrix products, arithmetic and copies ran while one was open for 0% of the time, Pallas kernels for 25%

profile of v3, /device:TPU:8, one launch (start us, length us, event | category | flops | bytes accessed | tf_op | source)
XLA Modules:
  0.0 74.2 jit_solution(11339384328150013434)
XLA Ops:
  0.0 0.1 pad_add_fusion.place_ref
  0.1 1.1 %copy-done.1 = bf16[1,4,48,1536]{3,2,1,0:T(8,128)(2,1)S(1)} copy-done((bf16[1,4,48,1536]{3,2,1,0:T(8,128)(2,1)S(1)}, bf16[1,4,48,1536]{3,2,1,0:T(8,128)(2,1)}, u32[]{:S(2)}) %copy-start.1) | copy-done | bytes 589848
  1.1 1.1 %copy-done.2 = bf16[1,4,48,1536]{3,2,1,0:T(8,128)(2,1)S(1)} copy-done((bf16[1,4,48,1536]{3,2,1,0:T(8,128)(2,1)S(1)}, bf16[1,4,48,1536]{3,2,1,0:T(8,128)(2,1)}, u32[]{:S(2)}) %copy-start.2) | copy-done | bytes 589848
  2.2 0.7 pack.3
  2.9 1.6 %collective-permute-start = (bf16[2,192,512]{2,1,0:T(8,128)(2,1)S(1)}, bf16[2,192,512]{2,1,0:T(8,128)(2,1)S(1)}, u32[]{:S(2)}, u32[]{:S(2)}) collective-permute-start(bf16[2,192,512]{2,1,0:T(8,128)(2,1)S(1)} %get-tuple-element.15), channel_id=1, source_target_pairs={{0,2},{2,0},{1,3},{3,1},{4,6},{6,4},{5,7},{7,5},{8,10},{10,8},{9,1... | collective-permute-start | bytes 1179656 | tf_op jit(solution)/shard_map/ppermute | solution.py:302
  4.4 3.6 %collective-permute-start.3 = (bf16[2,192,768]{2,1,0:T(8,128)(2,1)S(1)}, bf16[2,192,768]{2,1,0:T(8,128)(2,1)S(1)}, u32[]{:S(2)}, u32[]{:S(2)}) collective-permute-start(bf16[2,192,768]{2,1,0:T(8,128)(2,1)S(1)} %get-tuple-element.16.refs_2_), channel_id=1, source_target_pairs={{4,8},{8,4},{5,9},{9,5},{6,10},{10,6},{7,11},{11,7},{20,24},{24,20... | collective-permute-start | bytes 1769480 | tf_op jit(solution)/shard_map/ppermute | solution.py:311
  8.1 0.1 collective-permute-start.6
  8.1 5.7 %collective-permute-done.refs_2_.refs_3_ = bf16[2,192,512]{2,1,0:T(8,128)(2,1)S(1)} collective-permute-done((bf16[2,192,512]{2,1,0:T(8,128)(2,1)S(1)}, bf16[2,192,512]{2,1,0:T(8,128)(2,1)S(1)}, u32[]{:S(2)}, u32[]{:S(2)}) %collective-permute-start) | collective-permute-done | bytes 393248 | tf_op jit(solution)/shard_map/ppermute | solution.py:302
  13.8 0.6 pack.4
  14.4 1.6 %collective-permute-start.1 = (bf16[2,192,256]{2,1,0:T(8,128)(2,1)S(1)}, bf16[2,192,256]{2,1,0:T(8,128)(2,1)S(1)}, u32[]{:S(2)}, u32[]{:S(2)}) collective-permute-start(bf16[2,192,256]{2,1,0:T(8,128)(2,1)S(1)} %pack.4), channel_id=1, source_target_pairs={{0,2},{2,0},{1,3},{3,1},{4,6},{6,4},{5,7},{7,5},{8,10},{10,8},{9,1... | collective-permute-start | bytes 589832 | tf_op jit(solution)/shard_map/ppermute | solution.py:302
  16.0 3.5 %collective-permute-start.8 = (bf16[2,192,512]{2,1,0:T(8,128)(2,1)S(1)}, bf16[2,192,512]{2,1,0:T(8,128)(2,1)}, u32[]{:S(2)}, u32[]{:S(2)}) collective-permute-start(bf16[2,192,512]{2,1,0:T(8,128)(2,1)S(1)} %collective-permute-done.refs_2_.refs_3_), channel_id=1, source_target_pairs={{4,8},{8,4},{5,9},{9,5},{6,10},{10,6},{7,11},{11,7},{20,24},{24,20... | collective-permute-start | bytes 1179656 | tf_op jit(solution)/shard_map/ppermute | solution.py:311
  19.4 0.8 %collective-permute-done.1.refs_1_.refs_3_ = bf16[2,192,256]{2,1,0:T(8,128)(2,1)S(1)} collective-permute-done((bf16[2,192,256]{2,1,0:T(8,128)(2,1)S(1)}, bf16[2,192,256]{2,1,0:T(8,128)(2,1)S(1)}, u32[]{:S(2)}, u32[]{:S(2)}) %collective-permute-start.1) | collective-permute-done | bytes 196640 | tf_op jit(solution)/shard_map/ppermute | solution.py:302
  20.2 0.5 collective-permute-start.11
  20.8 1.5 %collective-permute-start.7 = (bf16[2,192,512]{2,1,0:T(8,128)(2,1)S(1)}, bf16[2,192,512]{2,1,0:T(8,128)(2,1)}, u32[]{:S(2)}, u32[]{:S(2)}) collective-permute-start(bf16[2,192,512]{2,1,0:T(8,128)(2,1)S(1)} %collective-permute-done.refs_2_.refs_3_), channel_id=1, source_target_pairs={{0,4},{4,0},{8,12},{12,8},{1,5},{5,1},{9,13},{13,9},{2,6},{6,2},{1... | collective-permute-start | bytes 1179656 | tf_op jit(solution)/shard_map/ppermute | solution.py:311
  22.3 0.4 collective-permute-done.3.refs_6_
  22.7 3.5 %collective-permute-start.5 = (bf16[2,192,256]{2,1,0:T(8,128)(2,1)S(1)}, bf16[2,192,256]{2,1,0:T(8,128)(2,1)S(1)}, u32[]{:S(2)}, u32[]{:S(2)}) collective-permute-start(bf16[2,192,256]{2,1,0:T(8,128)(2,1)S(1)} %collective-permute-done.1.refs_1_.refs_3_), channel_id=1, source_target_pairs={{4,8},{8,4},{5,9},{9,5},{6,10},{10,6},{7,11},{11,7},{20,24},{24,20... | collective-permute-start | bytes 589832 | tf_op jit(solution)/shard_map/ppermute | solution.py:311
  26.2 0.0 collective-permute-done.6.refs_4_
  26.2 1.3 %collective-permute-start.4 = (bf16[2,192,768]{2,1,0:T(8,128)(2,1)S(1)}, bf16[2,192,768]{2,1,0:T(8,128)(2,1)S(1)}, u32[]{:S(2)}, u32[]{:S(2)}) collective-permute-start(bf16[2,192,768]{2,1,0:T(8,128)(2,1)S(1)} %collective-permute-done.3.refs_6_), channel_id=1, source_target_pairs={{4,0},{8,12},{5,1},{9,13},{6,2},{10,14},{7,3},{11,15},{20,16},{24,... | collective-permute-start | bytes 1769480 | tf_op jit(solution)/shard_map/ppermute | solution.py:311
  27.5 1.0 %collective-permute-done.11.array_ref.refs_5_ = bf16[2,192,256]{2,1,0:T(8,128)(2,1)S(1)} collective-permute-done((bf16[2,192,256]{2,1,0:T(8,128)(2,1)S(1)}, bf16[2,192,256]{2,1,0:T(8,128)(2,1)S(1)}, u32[]{:S(2)}, u32[]{:S(2)}) %collective-permute-start.11) | collective-permute-done | bytes 196640 | tf_op jit(solution)/shard_map/ppermute | solution.py:311
  28.5 3.0 %collective-permute-start.10 = (bf16[2,192,768]{2,1,0:T(8,128)(2,1)S(1)}, bf16[2,192,768]{2,1,0:T(8,128)(2,1)S(1)}, u32[]{:S(2)}, u32[]{:S(2)}) collective-permute-start(bf16[2,192,768]{2,1,0:T(8,128)(2,1)S(1)} %collective-permute-done.6.refs_4_), channel_id=1, source_target_pairs={{4,8},{8,4},{5,9},{9,5},{6,10},{10,6},{7,11},{11,7},{20,24},{24,20... | collective-permute-start | bytes 1769480 | tf_op jit(solution)/shard_map/ppermute | solution.py:311
  31.6 0.0 copy-done
  31.6 0.0 copy-start.12
  31.6 0.0 copy-start.13
  31.6 0.6 pack.5
  32.2 3.2 %collective-permute-done.5.array_ref.refs_7_ = bf16[2,192,256]{2,1,0:T(8,128)(2,1)S(1)} collective-permute-done((bf16[2,192,256]{2,1,0:T(8,128)(2,1)S(1)}, bf16[2,192,256]{2,1,0:T(8,128)(2,1)S(1)}, u32[]{:S(2)}, u32[]{:S(2)}) %collective-permute-start.5) | collective-permute-done | bytes 196640 | tf_op jit(solution)/shard_map/ppermute | solution.py:311
  35.4 0.5 collective-permute-start.2
  35.9 0.0 collective-permute-done.8.refs_7_
  35.9 2.0 %collective-permute-start.13 = (bf16[2,192,512]{2,1,0:T(8,128)(2,1)}, bf16[2,192,512]{2,1,0:T(8,128)(2,1)}, u32[]{:S(2)}, u32[]{:S(2)}) collective-permute-start(bf16[2,192,512]{2,1,0:T(8,128)(2,1)} %collective-permute-done.8.refs_7_), channel_id=1, source_target_pairs={{4,0},{8,12},{5,1},{9,13},{6,2},{10,14},{7,3},{11,15},{20,16},{24,... | collective-permute-start | bytes 1179656 | tf_op jit(solution)/shard_map/ppermute | solution.py:311
  37.9 0.0 collective-permute-done.7.refs_5_
  37.9 3.5 %collective-permute-start.14 = (bf16[2,192,512]{2,1,0:T(8,128)(2,1)}, bf16[2,192,512]{2,1,0:T(8,128)(2,1)}, u32[]{:S(2)}, u32[]{:S(2)}) collective-permute-start(bf16[2,192,512]{2,1,0:T(8,128)(2,1)} %collective-permute-done.7.refs_5_), channel_id=1, source_target_pairs={{4,8},{8,4},{5,9},{9,5},{6,10},{10,6},{7,11},{11,7},{20,24},{24,20... | collective-permute-start | bytes 1179656 | tf_op jit(solution)/shard_map/ppermute | solution.py:311
  41.4 0.7 collective-permute-done.2.refs_1_
  42.1 0.0 copy-done.5
  42.1 0.0 copy-done.12
  42.1 0.0 copy-done.13
  42.1 2.9 %attend.3 = (f32[2,128,384]{2,1,0:T(8,128)S(1)}, f32[2,8,384]{2,1,0:T(8,128)S(1)}) custom-call(s32[2]{0:T(128)S(1)} %pad_add_fusion.place_ref, s32[4,4]{1,0:T(4,128)S(1)} %copy-done.12, s32[4]{0:T(128)S(1)} %copy-done.13, bf16[192,1536]{1,0:T(8,128)(2,1)S(1)} %bitcast.7, bf16[192,768]{1,0:T(8,128)(2,1)S(1)} %collective-permute-done.2.refs_1_, ...), custom_call_target="tpu_custom_call" | custom-call | flops 452984832 | bytes 1179648 | tf_op jit(solution)/shard_map/attend/pallas_call | solution.py:233
  45.0 0.0 copy-done.6
  45.0 0.0 copy-start.9
  45.1 0.8 %copy-done.9 = f32[2,128,384]{2,1,0:T(8,128)} copy-done((f32[2,128,384]{2,1,0:T(8,128)}, f32[2,128,384]{2,1,0:T(8,128)S(1)}, u32[]{:S(2)}) %copy-start.9) | copy-done | bytes 393240
  45.8 6.2 %attend.2 = (f32[4,128,384]{2,1,0:T(8,128)S(1)}, f32[4,8,384]{2,1,0:T(8,128)S(1)}) custom-call(s32[2]{0:T(128)S(1)} %pad_add_fusion.place_ref, s32[4,4]{1,0:T(4,128)S(1)} %copy-done.12, s32[4]{0:T(128)S(1)} %copy-done.13, bf16[192,1536]{1,0:T(8,128)(2,1)S(1)} %bitcast.8, bf16[192,768]{1,0:T(8,128)(2,1)S(1)} %collective-permute-done.2.refs_1_, ...), custom_call_target="tpu_custom_call" | custom-call | flops 905969664 | bytes 2359296 | tf_op jit(solution)/shard_map/attend/pallas_call | solution.py:233
  52.0 0.0 copy-start.3
  52.1 0.9 %copy-done.3 = f32[4,128,384]{2,1,0:T(8,128)} copy-done((f32[4,128,384]{2,1,0:T(8,128)}, f32[4,128,384]{2,1,0:T(8,128)S(1)}, u32[]{:S(2)}) %copy-start.3) | copy-done | bytes 786456
  52.9 0.6 copy-done.7
  53.6 1.4 %collective-permute-start.9 = (bf16[2,192,256]{2,1,0:T(8,128)(2,1)}, bf16[2,192,256]{2,1,0:T(8,128)(2,1)S(1)}, u32[]{:S(2)}, u32[]{:S(2)}) collective-permute-start(bf16[2,192,256]{2,1,0:T(8,128)(2,1)} %tie.2), channel_id=1, source_target_pairs={{4,0},{8,12},{5,1},{9,13},{6,2},{10,14},{7,3},{11,15},{20,16},{24,... | collective-permute-start | bytes 589832 | tf_op jit(solution)/shard_map/ppermute | solution.py:311
  55.0 0.0 collective-permute-done.4.refs_2_
  55.0 3.5 %collective-permute-start.12 = (bf16[2,192,256]{2,1,0:T(8,128)(2,1)}, bf16[2,192,256]{2,1,0:T(8,128)(2,1)S(1)}, u32[]{:S(2)}, u32[]{:S(2)}) collective-permute-start(bf16[2,192,256]{2,1,0:T(8,128)(2,1)} %tie.3), channel_id=1, source_target_pairs={{4,8},{8,4},{5,9},{9,5},{6,10},{10,6},{7,11},{11,7},{20,24},{24,20... | collective-permute-start | bytes 589832 | tf_op jit(solution)/shard_map/ppermute | solution.py:311
  58.5 0.0 collective-permute-done.10.refs_4_
  58.5 0.0 collective-permute-done.13.refs_3_
  58.5 0.0 collective-permute-done.14.refs_5_
  58.5 0.0 copy-done.8
  58.5 0.0 copy-start.4
  58.5 1.1 %copy-done.4 = f32[4,128,384]{2,1,0:T(8,128)S(1)} copy-done((f32[4,128,384]{2,1,0:T(8,128)S(1)}, f32[4,128,384]{2,1,0:T(8,128)}, u32[]{:S(2)}) %copy-start.4) | copy-done | bytes 786456
  59.7 4.4 %attend_final.2 = (bf16[192,1536]{1,0:T(8,128)(2,1)}, bf16[192,512]{1,0:T(8,128)(2,1)S(1)}) custom-call(s32[2]{0:T(128)S(1)} %pad_add_fusion.place_ref, s32[4,4]{1,0:T(4,128)S(1)} %copy-done.12, s32[4]{0:T(128)S(1)} %copy-done.13, bf16[192,1536]{1,0:T(8,128)(2,1)S(1)} %bitcast.9, bf16[192,768]{1,0:T(8,128)(2,1)S(1)} %collective-permute-done.2.refs_1_, ...), custom_call_target="tpu_custom_call" | custom-call | flops 603979776 | bytes 1572864 | tf_op jit(solution)/shard_map/attend_final/pallas_call | solution.py:233
  64.0 0.5 collective-permute-start.16
  64.6 0.0 collective-permute-done.9.refs_3_
  64.6 0.0 collective-permute-done.12.refs_5_
  64.6 0.0 copy-done.11
  64.6 2.3 %attend_final.3 = (bf16[192,1536]{1,0:T(8,128)(2,1)}, bf16[192,256]{1,0:T(8,128)(2,1)S(1)}) custom-call(s32[2]{0:T(128)S(1)} %pad_add_fusion.place_ref, s32[4,4]{1,0:T(4,128)S(1)} %copy-done.12, s32[4]{0:T(128)S(1)} %copy-done.13, bf16[192,1536]{1,0:T(8,128)(2,1)S(1)} %bitcast.10, ...), custom_call_target="tpu_custom_call", output_to_operand_aliasing={{0}: (11, {})} | custom-call | flops 301989888 | bytes 786432 | tf_op jit(solution)/shard_map/attend_final/pallas_call | solution.py:233
  66.9 1.5 %collective-permute-start.15 = (bf16[192,256]{1,0:T(8,128)(2,1)S(1)}, bf16[192,256]{1,0:T(8,128)(2,1)S(1)}, u32[]{:S(2)}, u32[]{:S(2)}) collective-permute-start(bf16[192,256]{1,0:T(8,128)(2,1)S(1)} %get-tuple-element.22), channel_id=1, source_target_pairs={{0,2},{2,0},{1,3},{3,1},{4,6},{6,4},{5,7},{7,5},{8,10},{10,8},{9,1... | collective-permute-start | bytes 294920 | tf_op jit(solution)/shard_map/ppermute | solution.py:302
  68.4 1.3 %collective-permute-done.16.piece_ref = bf16[192,512]{1,0:T(8,128)(2,1)S(1)} collective-permute-done((bf16[192,512]{1,0:T(8,128)(2,1)S(1)}, bf16[192,512]{1,0:T(8,128)(2,1)S(1)}, u32[]{:S(2)}, u32[]{:S(2)}) %collective-permute-start.16) | collective-permute-done | bytes 196640 | tf_op jit(solution)/shard_map/ppermute | solution.py:302
  69.7 0.7 copy-done.14
  70.4 1.6 %put.2.whole_ref = bf16[192,1536]{1,0:T(8,128)(2,1)} custom-call(s32[2]{0:T(128)} %copy-done.11, bf16[192,512]{1,0:T(8,128)(2,1)} %copy-done.14, bf16[192,1536]{1,0:T(8,128)(2,1)} %get-tuple-element.24.whole_ref), custom_call_target="tpu_custom_call", output_to_operand_aliasing={{}: (2, {})} | custom-call | tf_op jit(solution)/shard_map/put/pallas_call | solution.py:273
  72.0 0.0 collective-permute-done.15.piece_ref
  72.0 0.6 copy-done.15
  72.6 1.6 %put.3 = bf16[192,1536]{1,0:T(8,128)(2,1)} custom-call(s32[2]{0:T(128)} %copy-done.11, bf16[192,256]{1,0:T(8,128)(2,1)} %copy-done.15, bf16[192,1536]{1,0:T(8,128)(2,1)} %put.2.whole_ref), custom_call_target="tpu_custom_call", output_to_operand_aliasing={{}: (2, {})} | custom-call | tf_op jit(solution)/shard_map/put/pallas_call | solution.py:273
  (14 shorter events, 0.0 us)
Async XLA Ops:
  0.1 64.5 %copy-start.11 = (s32[2]{0:T(128)}, s32[2]{0:T(128)S(1)}, u32[]{:S(2)}) copy-start(s32[2]{0:T(128)S(1)} %pad_add_fusion.place_ref) | copy-start | bytes 28
  0.1 1.1 %copy-start.1 = (bf16[1,4,48,1536]{3,2,1,0:T(8,128)(2,1)S(1)}, bf16[1,4,48,1536]{3,2,1,0:T(8,128)(2,1)}, u32[]{:S(2)}) copy-start(bf16[1,4,48,1536]{3,2,1,0:T(8,128)(2,1)} %param.6) | copy-start | bytes 1769476
  1.1 1.1 %copy-start.2 = (bf16[1,4,48,1536]{3,2,1,0:T(8,128)(2,1)S(1)}, bf16[1,4,48,1536]{3,2,1,0:T(8,128)(2,1)}, u32[]{:S(2)}) copy-start(bf16[1,4,48,1536]{3,2,1,0:T(8,128)(2,1)} %param.7) | copy-start | bytes 1769476
  2.9 10.9 %collective-permute-start = (bf16[2,192,512]{2,1,0:T(8,128)(2,1)S(1)}, bf16[2,192,512]{2,1,0:T(8,128)(2,1)S(1)}, u32[]{:S(2)}, u32[]{:S(2)}) collective-permute-start(bf16[2,192,512]{2,1,0:T(8,128)(2,1)S(1)} %get-tuple-element.15), channel_id=1, source_target_pairs={{0,2},{2,0},{1,3},{3,1},{4,6},{6,4},{5,7},{7,5},{8,10},{10,8},{9,1... | collective-permute-start | bytes 1179656 | tf_op jit(solution)/shard_map/ppermute | solution.py:302
  4.4 27.1 %copy-start = (bf16[1,4,48,1536]{3,2,1,0:T(8,128)(2,1)S(1)}, bf16[1,4,48,1536]{3,2,1,0:T(8,128)(2,1)}, u32[]{:S(2)}) copy-start(bf16[1,4,48,1536]{3,2,1,0:T(8,128)(2,1)} %param.5) | copy-start | bytes 1769476
  4.4 18.3 %collective-permute-start.3 = (bf16[2,192,768]{2,1,0:T(8,128)(2,1)S(1)}, bf16[2,192,768]{2,1,0:T(8,128)(2,1)S(1)}, u32[]{:S(2)}, u32[]{:S(2)}) collective-permute-start(bf16[2,192,768]{2,1,0:T(8,128)(2,1)S(1)} %get-tuple-element.16.refs_2_), channel_id=1, source_target_pairs={{4,8},{8,4},{5,9},{9,5},{6,10},{10,6},{7,11},{11,7},{20,24},{24,20... | collective-permute-start | bytes 1769480 | tf_op jit(solution)/shard_map/ppermute | solution.py:311
  8.1 18.1 %collective-permute-start.6 = (bf16[2,192,768]{2,1,0:T(8,128)(2,1)S(1)}, bf16[2,192,768]{2,1,0:T(8,128)(2,1)S(1)}, u32[]{:S(2)}, u32[]{:S(2)}) collective-permute-start(bf16[2,192,768]{2,1,0:T(8,128)(2,1)S(1)} %get-tuple-element.16.refs_2_), channel_id=1, source_target_pairs={{0,4},{4,0},{8,12},{12,8},{1,5},{5,1},{9,13},{13,9},{2,6},{6,2},{1... | collective-permute-start | bytes 1769480 | tf_op jit(solution)/shard_map/ppermute | solution.py:311
  14.4 5.8 %collective-permute-start.1 = (bf16[2,192,256]{2,1,0:T(8,128)(2,1)S(1)}, bf16[2,192,256]{2,1,0:T(8,128)(2,1)S(1)}, u32[]{:S(2)}, u32[]{:S(2)}) collective-permute-start(bf16[2,192,256]{2,1,0:T(8,128)(2,1)S(1)} %pack.4), channel_id=1, source_target_pairs={{0,2},{2,0},{1,3},{3,1},{4,6},{6,4},{5,7},{7,5},{8,10},{10,8},{9,1... | collective-permute-start | bytes 589832 | tf_op jit(solution)/shard_map/ppermute | solution.py:302
  16.0 19.9 %collective-permute-start.8 = (bf16[2,192,512]{2,1,0:T(8,128)(2,1)S(1)}, bf16[2,192,512]{2,1,0:T(8,128)(2,1)}, u32[]{:S(2)}, u32[]{:S(2)}) collective-permute-start(bf16[2,192,512]{2,1,0:T(8,128)(2,1)S(1)} %collective-permute-done.refs_2_.refs_3_), channel_id=1, source_target_pairs={{4,8},{8,4},{5,9},{9,5},{6,10},{10,6},{7,11},{11,7},{20,24},{24,20... | collective-permute-start | bytes 1179656 | tf_op jit(solution)/shard_map/ppermute | solution.py:311
  20.2 8.3 %collective-permute-start.11 = (bf16[2,192,256]{2,1,0:T(8,128)(2,1)S(1)}, bf16[2,192,256]{2,1,0:T(8,128)(2,1)S(1)}, u32[]{:S(2)}, u32[]{:S(2)}) collective-permute-start(bf16[2,192,256]{2,1,0:T(8,128)(2,1)S(1)} %collective-permute-done.1.refs_1_.refs_3_), channel_id=1, source_target_pairs={{0,4},{4,0},{8,12},{12,8},{1,5},{5,1},{9,13},{13,9},{2,6},{6,2},{1... | collective-permute-start | bytes 589832 | tf_op jit(solution)/shard_map/ppermute | solution.py:311
  20.8 17.2 %collective-permute-start.7 = (bf16[2,192,512]{2,1,0:T(8,128)(2,1)S(1)}, bf16[2,192,512]{2,1,0:T(8,128)(2,1)}, u32[]{:S(2)}, u32[]{:S(2)}) collective-permute-start(bf16[2,192,512]{2,1,0:T(8,128)(2,1)S(1)} %collective-permute-done.refs_2_.refs_3_), channel_id=1, source_target_pairs={{0,4},{4,0},{8,12},{12,8},{1,5},{5,1},{9,13},{13,9},{2,6},{6,2},{1... | collective-permute-start | bytes 1179656 | tf_op jit(solution)/shard_map/ppermute | solution.py:311
  22.7 12.6 %collective-permute-start.5 = (bf16[2,192,256]{2,1,0:T(8,128)(2,1)S(1)}, bf16[2,192,256]{2,1,0:T(8,128)(2,1)S(1)}, u32[]{:S(2)}, u32[]{:S(2)}) collective-permute-start(bf16[2,192,256]{2,1,0:T(8,128)(2,1)S(1)} %collective-permute-done.1.refs_1_.refs_3_), channel_id=1, source_target_pairs={{4,8},{8,4},{5,9},{9,5},{6,10},{10,6},{7,11},{11,7},{20,24},{24,20... | collective-permute-start | bytes 589832 | tf_op jit(solution)/shard_map/ppermute | solution.py:311
  26.2 28.8 %collective-permute-start.4 = (bf16[2,192,768]{2,1,0:T(8,128)(2,1)S(1)}, bf16[2,192,768]{2,1,0:T(8,128)(2,1)S(1)}, u32[]{:S(2)}, u32[]{:S(2)}) collective-permute-start(bf16[2,192,768]{2,1,0:T(8,128)(2,1)S(1)} %collective-permute-done.3.refs_6_), channel_id=1, source_target_pairs={{4,0},{8,12},{5,1},{9,13},{6,2},{10,14},{7,3},{11,15},{20,16},{24,... | collective-permute-start | bytes 1769480 | tf_op jit(solution)/shard_map/ppermute | solution.py:311
  28.5 13.5 %copy-start.5 = (bf16[2,192,256]{2,1,0:T(8,128)(2,1)}, bf16[2,192,256]{2,1,0:T(8,128)(2,1)S(1)}, u32[]{:S(2)}) copy-start(bf16[2,192,256]{2,1,0:T(8,128)(2,1)S(1)} %collective-permute-done.11.array_ref.refs_5_) | copy-start | bytes 589828
  28.5 30.0 %collective-permute-start.10 = (bf16[2,192,768]{2,1,0:T(8,128)(2,1)S(1)}, bf16[2,192,768]{2,1,0:T(8,128)(2,1)S(1)}, u32[]{:S(2)}, u32[]{:S(2)}) collective-permute-start(bf16[2,192,768]{2,1,0:T(8,128)(2,1)S(1)} %collective-permute-done.6.refs_4_), channel_id=1, source_target_pairs={{4,8},{8,4},{5,9},{9,5},{6,10},{10,6},{7,11},{11,7},{20,24},{24,20... | collective-permute-start | bytes 1769480 | tf_op jit(solution)/shard_map/ppermute | solution.py:311
  31.6 10.5 %copy-start.12 = (s32[4,4]{1,0:T(4,128)S(1)}, s32[4,4]{1,0:T(4,128)}, u32[]{:S(2)}) copy-start(s32[4,4]{1,0:T(4,128)} %flags_ref.7) | copy-start | bytes 196
  31.6 10.5 %copy-start.13 = (s32[4]{0:T(128)S(1)}, s32[4]{0:T(128)}, u32[]{:S(2)}) copy-start(s32[4]{0:T(128)} %widths_ref.7) | copy-start | bytes 52
  35.3 9.7 %copy-start.6 = (bf16[2,192,256]{2,1,0:T(8,128)(2,1)}, bf16[2,192,256]{2,1,0:T(8,128)(2,1)S(1)}, u32[]{:S(2)}) copy-start(bf16[2,192,256]{2,1,0:T(8,128)(2,1)S(1)} %collective-permute-done.5.array_ref.refs_7_) | copy-start | bytes 589828
  35.4 6.7 %collective-permute-start.2 = (bf16[192,768]{1,0:T(8,128)(2,1)S(1)}, bf16[192,768]{1,0:T(8,128)(2,1)S(1)}, u32[]{:S(2)}, u32[]{:S(2)}) collective-permute-start(bf16[192,768]{1,0:T(8,128)(2,1)S(1)} %pack.5), channel_id=1, source_target_pairs={{0,2},{2,0},{1,3},{3,1},{4,6},{6,4},{5,7},{7,5},{8,10},{10,8},{9,1... | collective-permute-start | bytes 884744 | tf_op jit(solution)/shard_map/ppermute | solution.py:302
  35.9 22.6 %collective-permute-start.13 = (bf16[2,192,512]{2,1,0:T(8,128)(2,1)}, bf16[2,192,512]{2,1,0:T(8,128)(2,1)}, u32[]{:S(2)}, u32[]{:S(2)}) collective-permute-start(bf16[2,192,512]{2,1,0:T(8,128)(2,1)} %collective-permute-done.8.refs_7_), channel_id=1, source_target_pairs={{4,0},{8,12},{5,1},{9,13},{6,2},{10,14},{7,3},{11,15},{20,16},{24,... | collective-permute-start | bytes 1179656 | tf_op jit(solution)/shard_map/ppermute | solution.py:311
  37.9 20.6 %collective-permute-start.14 = (bf16[2,192,512]{2,1,0:T(8,128)(2,1)}, bf16[2,192,512]{2,1,0:T(8,128)(2,1)}, u32[]{:S(2)}, u32[]{:S(2)}) collective-permute-start(bf16[2,192,512]{2,1,0:T(8,128)(2,1)} %collective-permute-done.7.refs_5_), channel_id=1, source_target_pairs={{4,8},{8,4},{5,9},{9,5},{6,10},{10,6},{7,11},{11,7},{20,24},{24,20... | collective-permute-start | bytes 1179656 | tf_op jit(solution)/shard_map/ppermute | solution.py:311
  45.0 0.8 %copy-start.9 = (f32[2,128,384]{2,1,0:T(8,128)}, f32[2,128,384]{2,1,0:T(8,128)S(1)}, u32[]{:S(2)}) copy-start(f32[2,128,384]{2,1,0:T(8,128)S(1)} %get-tuple-element.18.refs_6_) | copy-start | bytes 1179652
  52.0 0.9 %copy-start.3 = (f32[4,128,384]{2,1,0:T(8,128)}, f32[4,128,384]{2,1,0:T(8,128)S(1)}, u32[]{:S(2)}) copy-start(f32[4,128,384]{2,1,0:T(8,128)S(1)} %get-tuple-element.20.refs_6_) | copy-start | bytes 2359300
  52.9 0.6 copy-start.7
  53.5 5.0 %copy-start.8 = (f32[4,8,384]{2,1,0:T(8,128)S(1)}, f32[4,8,384]{2,1,0:T(8,128)}, u32[]{:S(2)}) copy-start(f32[4,8,384]{2,1,0:T(8,128)} %copy-done.7) | copy-start | bytes 147460
  53.6 11.0 %collective-permute-start.9 = (bf16[2,192,256]{2,1,0:T(8,128)(2,1)}, bf16[2,192,256]{2,1,0:T(8,128)(2,1)S(1)}, u32[]{:S(2)}, u32[]{:S(2)}) collective-permute-start(bf16[2,192,256]{2,1,0:T(8,128)(2,1)} %tie.2), channel_id=1, source_target_pairs={{4,0},{8,12},{5,1},{9,13},{6,2},{10,14},{7,3},{11,15},{20,16},{24,... | collective-permute-start | bytes 589832 | tf_op jit(solution)/shard_map/ppermute | solution.py:311
  55.0 9.6 %collective-permute-start.12 = (bf16[2,192,256]{2,1,0:T(8,128)(2,1)}, bf16[2,192,256]{2,1,0:T(8,128)(2,1)S(1)}, u32[]{:S(2)}, u32[]{:S(2)}) collective-permute-start(bf16[2,192,256]{2,1,0:T(8,128)(2,1)} %tie.3), channel_id=1, source_target_pairs={{4,8},{8,4},{5,9},{9,5},{6,10},{10,6},{7,11},{11,7},{20,24},{24,20... | collective-permute-start | bytes 589832 | tf_op jit(solution)/shard_map/ppermute | solution.py:311
  58.5 1.1 %copy-start.4 = (f32[4,128,384]{2,1,0:T(8,128)S(1)}, f32[4,128,384]{2,1,0:T(8,128)}, u32[]{:S(2)}) copy-start(f32[4,128,384]{2,1,0:T(8,128)} %copy-done.3) | copy-start | bytes 2359300
  59.7 4.9 %copy-start.10 = (f32[2,128,384]{2,1,0:T(8,128)S(1)}, f32[2,128,384]{2,1,0:T(8,128)}, u32[]{:S(2)}) copy-start(f32[2,128,384]{2,1,0:T(8,128)} %copy-done.9) | copy-start | bytes 1179652
  64.0 5.7 %collective-permute-start.16 = (bf16[192,512]{1,0:T(8,128)(2,1)S(1)}, bf16[192,512]{1,0:T(8,128)(2,1)S(1)}, u32[]{:S(2)}, u32[]{:S(2)}) collective-permute-start(bf16[192,512]{1,0:T(8,128)(2,1)S(1)} %get-tuple-element.23), channel_id=1, source_target_pairs={{0,2},{2,0},{1,3},{3,1},{4,6},{6,4},{5,7},{7,5},{8,10},{10,8},{9,1... | collective-permute-start | bytes 589832 | tf_op jit(solution)/shard_map/ppermute | solution.py:302
  66.9 5.1 %collective-permute-start.15 = (bf16[192,256]{1,0:T(8,128)(2,1)S(1)}, bf16[192,256]{1,0:T(8,128)(2,1)S(1)}, u32[]{:S(2)}, u32[]{:S(2)}) collective-permute-start(bf16[192,256]{1,0:T(8,128)(2,1)S(1)} %get-tuple-element.22), channel_id=1, source_target_pairs={{0,2},{2,0},{1,3},{3,1},{4,6},{6,4},{5,7},{7,5},{8,10},{10,8},{9,1... | collective-permute-start | bytes 294920 | tf_op jit(solution)/shard_map/ppermute | solution.py:302
  69.7 0.7 copy-start.14
  72.0 0.6 copy-start.15

commit v4 on v3

v4 whole, which is shorter than its diff:
```python
import functools
import math

import jax
import jax.numpy as jnp
from jax import lax
from jax.experimental import pallas as pl
from jax.experimental.pallas import tpu as pltpu
from jax.sharding import PartitionSpec as P

HEAD_DIM = 128
NEG_FILL = -1e30
VMEM_LIMIT = 16 * 1024 * 1024
SMALL_LIMIT = 2 * 1024 * 1024
STAGED_LIMIT = 60 * 1024 * 1024
NT = (((1,), (1,)), ((), ()))
TN = (((0,), (0,)), ((), ()))


def pack_kernel(spaces, jobs, staged, place_ref, *refs):
    refs = list(refs)
    halfway = refs[len(refs) - len(jobs) - 1 : -1] if staged else []
    sems = refs[-1]
    here = place_ref[1]

    def target_of(job):
        return refs[job[4]] if job[5] is None else refs[job[4]].at[job[5]]

    copies = []
    for n, job in enumerate(jobs):
        source, offset, first, width = job[:4]
        share = refs[source].shape[-1] // spaces
        column = pl.multiple_of(lax.rem(here + offset, spaces) * share + first, HEAD_DIM)
        out = halfway[n] if staged else target_of(job)
        copy = pltpu.make_async_copy(refs[source].at[:, pl.ds(column, width)], out, sems.at[n])
        copy.start()
        copies.append(copy)
    if staged:
        seconds = []
        for n, job in enumerate(jobs):
            copies[n].wait()
            copy = pltpu.make_async_copy(halfway[n], target_of(job), sems.at[len(jobs) + n])
            copy.start()
            seconds.append(copy)
        copies = seconds
    for copy in copies:
        copy.wait()


def pack(place, sources, blocks, after, spaces, staged):
    tokens = sources[0].shape[0]
    several = len(sources) > 1
    jobs, shapes = [], []
    first_out = len(sources) + len(after)
    for n, (offset, first, width) in enumerate(blocks):
        lead = (len(sources),) if several else ()
        shapes.append(jax.ShapeDtypeStruct(lead + (tokens, width), sources[0].dtype))
        for row in range(len(sources)):
            jobs.append((row, offset, first, width, first_out + n, row if several else None))
    halfway = [pltpu.VMEM((tokens, job[3]), sources[0].dtype) for job in jobs]
    space = pl.ANY if staged else pltpu.VMEM
    return pl.pallas_call(
        functools.partial(pack_kernel, spaces, tuple(jobs), staged),
        in_specs=[pl.BlockSpec(memory_space=pltpu.SMEM)]
        + [pl.BlockSpec(memory_space=pl.ANY)] * first_out,
        out_specs=[pl.BlockSpec(memory_space=space)] * len(shapes),
        out_shape=shapes,
        scratch_shapes=(halfway if staged else []) + [pltpu.SemaphoreType.DMA((2 * len(jobs),))],
        compiler_params=pltpu.CompilerParams(
            vmem_limit_bytes=STAGED_LIMIT if staged else SMALL_LIMIT
        ),
        name="pack",
    )(place, *sources, *after)


def tie(array, after):
    return pl.pallas_call(
        lambda *refs: None,
        in_specs=[pl.BlockSpec(memory_space=pl.ANY)] * (1 + len(after)),
        out_specs=pl.BlockSpec(memory_space=pl.ANY),
        out_shape=jax.ShapeDtypeStruct(array.shape, array.dtype),
        input_output_aliases={0: 0},
        compiler_params=pltpu.CompilerParams(vmem_limit_bytes=SMALL_LIMIT),
        name="tie",
    )(array, *after)


def attend_kernel(
    spaces, frames, columns, row_band, heads, together, groups, skips, fresh, final,
    place_ref, flags_ref, widths_ref, *refs,
):
    refs = list(refs)
    queries = [refs.pop(0) for unused in range(spaces)]
    keyvals = [[refs.pop(0) for unused in range(spaces)] for unused in groups]
    state_in = None if fresh else (refs.pop(0), refs.pop(0))
    outs = [refs.pop(0) for unused in range(spaces if final else 2)]
    query_ref, key_ref = refs[:2]
    acc_ref, stat_ref = refs[2:] if final else outs
    query_skips, piece_skips = skips
    tokens = queries[0].shape[0]
    frame_now, space_now = place_ref[0], place_ref[1]
    scale = math.log2(math.e) / math.sqrt(HEAD_DIM)
    own_column = space_now * (queries[0].shape[-1] // spaces)

    def first_row(offset):
        return lax.rem(space_now - offset + spaces, spaces) * row_band

    def asked_of(group):
        slot, hops = group
        side = 1 - 2 * lax.rem(frame_now + slot, 2)
        key_frame = frame_now + side * hops
        safe = jnp.clip(key_frame, 0, frames - 1)
        known = (key_frame >= 0) & (key_frame < frames)
        return known & (flags_ref[frame_now, safe] > 0)

    token = lax.broadcasted_iota(jnp.int32, (tokens, HEAD_DIM), 0)
    row = lax.broadcasted_iota(jnp.int32, (tokens, HEAD_DIM), 1)
    for offset in range(spaces):
        rows = pl.ds(offset * tokens, tokens)
        start = (row - first_row(offset)) * columns
        hit = (token >= start) & (token < start + columns)
        mark = jnp.where(hit, 1.0, 0.0).astype(query_ref.dtype)
        for t in range(together):
            query_ref[t, rows, HEAD_DIM:] = mark
        for n, group in enumerate(groups):
            if group[1] > 0:

                @pl.when(asked_of(group))
                def _(n=n, group=group, start=start, rows=rows):
                    reach = widths_ref[group[1]] * columns
                    near = (token >= start - reach) & (token < start + columns + reach)
                    fill = jnp.where(near, 0.0, NEG_FILL).astype(key_ref.dtype)
                    for t in range(together):
                        key_ref[n, t, rows, HEAD_DIM:] = fill

    def attend_heads(turn, carry):
        head = turn * together
        slot_of = (lambda t: t) if final else (lambda t: head + t)

        def lanes(t, skip):
            return pl.ds(pl.multiple_of((head + t) * HEAD_DIM + skip, HEAD_DIM), HEAD_DIM)

        def step(t, scores, n, old):
            h = slot_of(t)
            top = jnp.max(scores, axis=0, keepdims=True) * scale
            if old:
                before = stat_ref[h, 0:1, :]
                top = jnp.maximum(top, before)
            weights = jnp.exp2(scores * scale - top)
            total = jnp.sum(weights, axis=0, keepdims=True)
            values = jnp.concatenate(
                [ref[1, :, lanes(t, skip)] for ref, skip in zip(keyvals[n], piece_skips[n])],
                axis=0,
            )
            acc = lax.dot_general(
                values, weights.astype(jnp.bfloat16), TN, preferred_element_type=jnp.float32
            )
            if old:
                fade = jnp.exp2(before - top)
                total = total + stat_ref[h, 1:2, :] * fade
                acc = acc + acc_ref[h] * fade
            stat_ref[h, 0:1, :] = top
            stat_ref[h, 1:2, :] = total
            acc_ref[h] = acc

        for t in range(together):
            for offset in range(spaces):
                skip = query_skips[offset] + (own_column if offset == 0 else 0)
                query_ref[t, pl.ds(offset * tokens, tokens), :HEAD_DIM] = queries[offset][
                    :, lanes(t, skip)
                ]
            if not fresh:
                acc_ref[slot_of(t)] = state_in[0][head + t]
                stat_ref[slot_of(t)] = state_in[1][head + t]

        for n, group in enumerate(groups):
            if group[1] == 0:
                scores = []
                for t in range(together):
                    keys = jnp.concatenate(
                        [
                            ref[0, :, lanes(t, skip)]
                            for ref, skip in zip(keyvals[n], piece_skips[n])
                        ],
                        axis=0,
                    )
                    scores.append(
                        lax.dot_general(
                            keys, query_ref[t, :, :HEAD_DIM], NT,
                            preferred_element_type=jnp.float32,
                        )
                    )
                for t in range(together):
                    step(t, scores[t], n, False)
                continue

            @pl.when(asked_of(group))
            def _(n=n):
                for t in range(together):
                    for offset in range(spaces):
                        rows = pl.ds(offset * tokens, tokens)
                        key_ref[n, t, rows, :HEAD_DIM] = keyvals[n][offset][
                            0, :, lanes(t, piece_skips[n][offset])
                        ]
                scores = [
                    lax.dot_general(
                        key_ref[n, t], query_ref[t], NT, preferred_element_type=jnp.float32
                    )
                    for t in range(together)
                ]
                for t in range(together):
                    step(t, scores[t], n, True)

        if final:
            for t in range(together):
                result = jnp.transpose(acc_ref[t] * (1.0 / stat_ref[t, 1:2, :]))
                for offset in range(spaces):
                    part = result[offset * tokens : (offset + 1) * tokens]
                    outs[offset][:, lanes(t, 0)] = part.astype(outs[offset].dtype)
        return carry

    lax.fori_loop(0, heads // together, attend_heads, 0)


def attend(scalars, queries, groups, state, final, chunk, sizes):
    spaces, frames, columns, row_band, features = sizes
    first, heads = chunk
    tokens = queries[0].shape[0]
    width = features // spaces
    count = spaces * tokens
    together = 2 if heads % 2 == 0 else 1

    def skip_of(x):
        return first * HEAD_DIM if x.shape[-1] != heads * HEAD_DIM else 0

    skips = (
        tuple(skip_of(x) for x in queries),
        tuple(tuple(skip_of(x) for x in pieces) for slot, hops, pieces in groups),
    )
    operands = list(queries) + [x for slot, hops, pieces in groups for x in pieces]
    if state is not None:
        operands += list(state)
    state_shape = [(heads, HEAD_DIM, count), (heads, 8, count)]
    if final:
        out_shape = [jax.ShapeDtypeStruct((tokens, heads * HEAD_DIM), jnp.bfloat16)] * spaces
    else:
        out_shape = [jax.ShapeDtypeStruct(shape, jnp.float32) for shape in state_shape]
    scratch = [
        pltpu.VMEM((together, count, 2 * HEAD_DIM), jnp.bfloat16),
        pltpu.VMEM((len(groups), together, count, 2 * HEAD_DIM), jnp.bfloat16),
    ]
    if final:
        scratch += [pltpu.VMEM((together,) + shape[1:], jnp.float32) for shape in state_shape]
    pairs = heads * count * count * len(groups)
    return pl.pallas_call(
        functools.partial(
            attend_kernel, spaces, frames, columns, row_band, heads, together,
            tuple((slot, hops) for slot, hops, pieces in groups), skips, state is None, final,
        ),
        in_specs=[pl.BlockSpec(memory_space=pltpu.SMEM)] * 3
        + [pl.BlockSpec(memory_space=pltpu.VMEM)] * len(operands),
        out_specs=[pl.BlockSpec(memory_space=pltpu.VMEM)] * len(out_shape),
        out_shape=out_shape,
        scratch_shapes=scratch,
        compiler_params=pltpu.CompilerParams(vmem_limit_bytes=VMEM_LIMIT),
        cost_estimate=pl.CostEstimate(
            flops=4 * pairs * HEAD_DIM,
            bytes_accessed=len(groups) * 4 * count * heads * HEAD_DIM,
            transcendentals=pairs,
        ),
        name="attend_final" if final else "attend",
    )(*scalars, *operands)


def put_kernel(spaces, places, kept, place_ref, *refs):
    pieces, out_ref, sems = refs[: len(places)], refs[-2], refs[-1]
    share = out_ref.shape[-1] // spaces
    copies = []
    for n, (offset, first) in enumerate(places):
        column = pl.multiple_of(lax.rem(place_ref[1] + offset, spaces) * share + first, HEAD_DIM)
        width = pieces[n].shape[-1]
        copy = pltpu.make_async_copy(pieces[n], out_ref.at[:, pl.ds(column, width)], sems.at[n])
        copy.start()
        copies.append(copy)
    for copy in copies:
        copy.wait()


def put(place, pieces, places, whole, shape, spaces):
    kept = [] if whole is None else [whole]
    return pl.pallas_call(
        functools.partial(put_kernel, spaces, tuple(places), len(kept)),
        in_specs=[pl.BlockSpec(memory_space=pltpu.SMEM)]
        + [pl.BlockSpec(memory_space=pltpu.VMEM)] * len(pieces)
        + [pl.BlockSpec(memory_space=pl.ANY)] * len(kept),
        out_specs=pl.BlockSpec(memory_space=pl.ANY),
        out_shape=jax.ShapeDtypeStruct(shape, pieces[0].dtype),
        scratch_shapes=[pltpu.SemaphoreType.DMA((len(pieces),))],
        input_output_aliases={1 + len(pieces): 0} if kept else {},
        compiler_params=pltpu.CompilerParams(vmem_limit_bytes=SMALL_LIMIT),
        name="put",
    )(place, *pieces, *kept)


def shards(spaces, frames, queries, keys, values, flags, widths):
    unused, row_band, columns, features = queries.shape
    tokens = row_band * columns
    width = features // spaces
    heads = width // HEAD_DIM
    place = jnp.stack([lax.axis_index("frame"), lax.axis_index("space")]).astype(jnp.int32)
    scalars = (place, flags, widths)
    sizes = (spaces, frames, columns, row_band, features)
    q, k, v = (x.reshape(tokens, features) for x in (queries, keys, values))
    tail = max(heads // 3, 1)
    chunks = [(0, heads - tail), (heads - tail, tail)]
    offsets = range(1, spaces)

    def along_space(x, offset):
        return lax.ppermute(x, "space", [(s, (s + offset) % spaces) for s in range(spaces)])

    def swap(x, slot, hops):
        pairs = []
        for f in range(frames):
            side = 1 if (f + slot) % 2 == 0 else -1
            source = f - side * (hops - 1)
            if 0 <= f + side < frames and 0 <= source < frames:
                pairs.append((f, f + side))
        return lax.ppermute(x, "frame", pairs)

    mine, queries_back, partners, arrived = None, None, [], []
    for first, number in chunks:
        blocks = [(offset, first * HEAD_DIM, number * HEAD_DIM) for offset in offsets]
        if mine is None:
            mine, *sends = pack(place, (k, v), [(0, 0, width)] + blocks, (), spaces, True)
        else:
            sends = pack(place, (k, v), blocks, arrived, spaces, False)
        arrived = [along_space(x, offset) for x, offset in zip(sends, offsets)]
        partners.append(arrived)
        if queries_back is None:
            sends = pack(place, (q,), [(o, 0, width) for o in offsets], arrived, spaces, False)
            arrived = [along_space(x, offset) for x, offset in zip(sends, offsets)]
            queries_back = arrived
    query_parts = [q] + queries_back

    carried = [[mine, mine]] + [[x, x] for x in partners]
    states = [None] * len(chunks)
    groups = [[(0, 0, [mine] + partners[c])] for c in range(len(chunks))]
    for hops in range(1, frames - 1):
        sent = []
        for c, (first_slot, second_slot) in enumerate(carried):
            over = [second_slot, first_slot]
            if c == 0:
                sent.append([swap(over[slot], slot, hops) for slot in range(2)])
                continue
            if c == len(chunks) and states[0] is not None:
                over = [[tie(x, [state[1] for state in states]) for x in xs] for xs in over]
            sent.append([[swap(x, slot, hops) for x in over[slot]] for slot in range(2)])
        carried = sent
        for c, chunk in enumerate(chunks):
            groups[c] += [
                (slot, hops, [carried[0][slot]] + carried[1 + c][slot]) for slot in range(2)
            ]
            if hops < frames - 2:
                states[c] = attend(
                    scalars, query_parts, groups[c], states[c], False, chunk, sizes
                )
                groups[c] = []

    own, returned = [], []
    for c, chunk in enumerate(chunks):
        kept, *parts = attend(scalars, query_parts, groups[c], states[c], True, chunk, sizes)
        own.append((kept, (0, chunk[0] * HEAD_DIM)))
        for offset, x in zip(offsets, parts):
            returned.append((along_space(x, -offset), (offset, chunk[0] * HEAD_DIM)))
    late = len(returned) - len(offsets)
    result = None
    for batch in (own + returned[:late], returned[late:]):
        pieces, places = zip(*batch)
        result = put(place, pieces, places, result, q.shape, spaces)
    return result.reshape(queries.shape)


def solution(mesh):
    placed = P(("group", "frame"), "space", None, "head")
    return jax.shard_map(
        functools.partial(shards, mesh.shape["space"], mesh.shape["frame"]),
        mesh=mesh,
        in_specs=(placed, placed, placed, P(), P()),
        out_specs=placed,
        check_vma=False,
    )
```

time: 75.1 us -> 77.7 us (1.035)
  the two profiles are of different devices: /device:TPU:8 before, /device:TPU:0 now
where the time goes in v4:
time: 77.7 us; the launch traced here: 77 us
  starting transfers between devices  40.5 us (52%)
  waiting for transfers between devices  21.3 us (27%)
  Pallas kernels  14.2 us (18%)
    ppermute x12, starting transfers between devices, swap(): return lax.ppermute(x, 'frame', pairs)  33 us
    ppermute x5, waiting for transfers between devices, along_space(): lax.ppermute(x, 'space', [(s, (s + offset) % spaces) for s in range(space...  13.3 us
    ppermute x12, waiting for transfers between devices, swap(): return lax.ppermute(x, 'frame', pairs)  8 us
    pallas_call x4, Pallas kernels, attend(): pl.pallas_call(functools.partial(attend_kernel, spaces, frames, columns,...  7.7 us
    ppermute x5, starting transfers between devices, along_space(): lax.ppermute(x, 'space', [(s, (s + offset) % spaces) for s in range(space...  7.5 us
    pallas_call x3, Pallas kernels, pack(): pl.pallas_call(functools.partial(pack_kernel, spaces, tuple(jobs), staged...  3.96 us
    pallas_call x2, Pallas kernels, put(): pl.pallas_call(functools.partial(put_kernel, spaces, tuple(places), len(k...  2.54 us
  transfers between devices with their start and end apart: 17, of which 6 were waited for; matrix products, arithmetic and copies ran while one was open for 0% of the time, Pallas kernels for 13%

profile of v4, /device:TPU:0, one launch (start us, length us, event | category | flops | bytes accessed | tf_op | source)
XLA Modules:
  0.0 77.0 jit_solution(16500874195467913013)
XLA Ops:
  0.0 0.6 pad_add_fusion.place_ref
  0.6 0.0 copy-start
  0.6 2.8 %pack.3 = (bf16[2,192,768]{2,1,0:T(8,128)(2,1)}, bf16[2,192,512]{2,1,0:T(8,128)(2,1)}) custom-call(s32[2]{0:T(128)} %pad_add_fusion.place_ref, bf16[192,1536]{1,0:T(8,128)(2,1)} %bitcast.11, bf16[192,1536]{1,0:T(8,128)(2,1)} %bitcast.13), custom_call_target="tpu_custom_call" | custom-call | tf_op jit(solution)/shard_map/pack/pallas_call | solution.py:62
  3.4 3.0 %collective-permute-start = (bf16[2,192,512]{2,1,0:T(8,128)(2,1)}, bf16[2,192,512]{2,1,0:T(8,128)(2,1)S(1)}, u32[]{:S(2)}, u32[]{:S(2)}) collective-permute-start(bf16[2,192,512]{2,1,0:T(8,128)(2,1)} %get-tuple-element.15), channel_id=1, source_target_pairs={{0,2},{2,0},{1,3},{3,1},{4,6},{6,4},{5,7},{7,5},{8,10},{10,8},{9,1... | collective-permute-start | bytes 1179656 | tf_op jit(solution)/shard_map/ppermute | solution.py:319
  6.4 0.0 copy-start.4
  6.4 1.6 %collective-permute-start.6 = (bf16[2,192,768]{2,1,0:T(8,128)(2,1)}, bf16[2,192,768]{2,1,0:T(8,128)(2,1)S(1)}, u32[]{:S(2)}, u32[]{:S(2)}) collective-permute-start(bf16[2,192,768]{2,1,0:T(8,128)(2,1)} %get-tuple-element.16.refs_2_), channel_id=1, source_target_pairs={{0,4},{4,0},{8,12},{12,8},{1,5},{5,1},{9,13},{13,9},{2,6},{6,2},{1... | collective-permute-start | bytes 1769480 | tf_op jit(solution)/shard_map/ppermute | solution.py:328
  8.0 0.7 collective-permute-start.2
  8.7 7.1 %collective-permute-done.refs_1_.refs_3_ = bf16[2,192,512]{2,1,0:T(8,128)(2,1)S(1)} collective-permute-done((bf16[2,192,512]{2,1,0:T(8,128)(2,1)}, bf16[2,192,512]{2,1,0:T(8,128)(2,1)S(1)}, u32[]{:S(2)}, u32[]{:S(2)}) %collective-permute-start) | collective-permute-done | bytes 393248 | tf_op jit(solution)/shard_map/ppermute | solution.py:319
  15.7 0.0 copy-done
  15.7 0.0 copy-done.4
  15.7 0.0 copy-start.1
  15.8 0.0 copy-start.2
  15.8 0.6 pack.4
  16.4 0.0 copy-start.3
  16.4 0.0 copy-start.5
  16.4 0.0 copy-start.6
  16.4 1.8 %collective-permute-start.1 = (bf16[192,768]{1,0:T(8,128)(2,1)S(1)}, bf16[192,768]{1,0:T(8,128)(2,1)S(1)}, u32[]{:S(2)}, u32[]{:S(2)}) collective-permute-start(bf16[192,768]{1,0:T(8,128)(2,1)S(1)} %pack.4), channel_id=1, source_target_pairs={{0,2},{2,0},{1,3},{3,1},{4,6},{6,4},{5,7},{7,5},{8,10},{10,8},{9,1... | collective-permute-start | bytes 884744 | tf_op jit(solution)/shard_map/ppermute | solution.py:319
  18.2 0.7 collective-permute-start.8
  18.9 4.4 %collective-permute-start.7 = (bf16[2,192,512]{2,1,0:T(8,128)(2,1)S(1)}, bf16[2,192,512]{2,1,0:T(8,128)(2,1)S(1)}, u32[]{:S(2)}, u32[]{:S(2)}) collective-permute-start(bf16[2,192,512]{2,1,0:T(8,128)(2,1)S(1)} %collective-permute-done.refs_1_.refs_3_), channel_id=1, source_target_pairs={{0,4},{4,0},{8,12},{12,8},{1,5},{5,1},{9,13},{13,9},{2,6},{6,2},{1... | collective-permute-start | bytes 1179656 | tf_op jit(solution)/shard_map/ppermute | solution.py:328
  23.3 1.3 %collective-permute-done.1.refs_2_.refs_1_ = bf16[192,768]{1,0:T(8,128)(2,1)S(1)} collective-permute-done((bf16[192,768]{1,0:T(8,128)(2,1)S(1)}, bf16[192,768]{1,0:T(8,128)(2,1)S(1)}, u32[]{:S(2)}, u32[]{:S(2)}) %collective-permute-start.1) | collective-permute-done | bytes 294944 | tf_op jit(solution)/shard_map/ppermute | solution.py:319
  24.7 0.0 copy-done.1
  24.7 0.0 copy-done.2
  24.7 0.6 pack.5
  25.3 1.5 %collective-permute-start.4 = (bf16[2,192,256]{2,1,0:T(8,128)(2,1)S(1)}, bf16[2,192,256]{2,1,0:T(8,128)(2,1)S(1)}, u32[]{:S(2)}, u32[]{:S(2)}) collective-permute-start(bf16[2,192,256]{2,1,0:T(8,128)(2,1)S(1)} %pack.5), channel_id=1, source_target_pairs={{0,2},{2,0},{1,3},{3,1},{4,6},{6,4},{5,7},{7,5},{8,10},{10,8},{9,1... | collective-permute-start | bytes 589832 | tf_op jit(solution)/shard_map/ppermute | solution.py:319
  26.8 0.0 collective-permute-done.6.refs_4_
  26.8 0.7 collective-permute-start.11
  27.5 0.0 collective-permute-done.2.refs_6_
  27.5 1.3 %collective-permute-start.3 = (bf16[2,192,768]{2,1,0:T(8,128)(2,1)S(1)}, bf16[2,192,768]{2,1,0:T(8,128)(2,1)S(1)}, u32[]{:S(2)}, u32[]{:S(2)}) collective-permute-start(bf16[2,192,768]{2,1,0:T(8,128)(2,1)S(1)} %collective-permute-done.2.refs_6_), channel_id=1, source_target_pairs={{4,0},{8,12},{5,1},{9,13},{6,2},{10,14},{7,3},{11,15},{20,16},{24,... | collective-permute-start | bytes 1769480 | tf_op jit(solution)/shard_map/ppermute | solution.py:328
  28.8 2.2 %collective-permute-done.4.refs_3_ = bf16[2,192,256]{2,1,0:T(8,128)(2,1)S(1)} collective-permute-done((bf16[2,192,256]{2,1,0:T(8,128)(2,1)S(1)}, bf16[2,192,256]{2,1,0:T(8,128)(2,1)S(1)}, u32[]{:S(2)}, u32[]{:S(2)}) %collective-permute-start.4) | collective-permute-done | bytes 196640 | tf_op jit(solution)/shard_map/ppermute | solution.py:319
  31.0 0.7 collective-permute-start.5
  31.7 0.0 collective-permute-done.8.refs_7_
  31.7 1.3 %collective-permute-start.14 = (bf16[2,192,512]{2,1,0:T(8,128)(2,1)S(1)}, bf16[2,192,512]{2,1,0:T(8,128)(2,1)S(1)}, u32[]{:S(2)}, u32[]{:S(2)}) collective-permute-start(bf16[2,192,512]{2,1,0:T(8,128)(2,1)S(1)} %collective-permute-done.8.refs_7_), channel_id=1, source_target_pairs={{4,0},{8,12},{5,1},{9,13},{6,2},{10,14},{7,3},{11,15},{20,16},{24,... | collective-permute-start | bytes 1179656 | tf_op jit(solution)/shard_map/ppermute | solution.py:328
  33.0 0.0 collective-permute-done.7.refs_5_
  33.0 0.7 collective-permute-start.15
  33.7 0.0 collective-permute-done.5.refs_7_.refs_0_
  33.7 19.1 %collective-permute-start.9 = (bf16[2,192,256]{2,1,0:T(8,128)(2,1)S(1)}, bf16[2,192,256]{2,1,0:T(8,128)(2,1)S(1)}, u32[]{:S(2)}, u32[]{:S(2)}) collective-permute-start(bf16[2,192,256]{2,1,0:T(8,128)(2,1)S(1)} %collective-permute-done.4.refs_3_), channel_id=1, source_target_pairs={{0,4},{4,0},{8,12},{12,8},{1,5},{5,1},{9,13},{13,9},{2,6},{6,2},{1... | collective-permute-start | bytes 589832 | tf_op jit(solution)/shard_map/ppermute | solution.py:328
  52.8 0.0 copy-done.3
  52.8 0.0 copy-done.5
  52.8 0.0 copy-done.6
  52.8 3.6 %attend.2 = (f32[4,128,384]{2,1,0:T(8,128)S(1)}, f32[4,8,384]{2,1,0:T(8,128)S(1)}) custom-call(s32[2]{0:T(128)S(1)} %copy-done.4, s32[4,4]{1,0:T(4,128)S(1)} %copy-done.5, s32[4]{0:T(128)S(1)} %copy-done.6, bf16[192,1536]{1,0:T(8,128)(2,1)S(1)} %bitcast.7, bf16[192,768]{1,0:T(8,128)(2,1)S(1)} %collective-permute-done.1.refs_2_.refs_1_, ...), custom_call_target="tpu_custom_call" | custom-call | flops 905969664 | bytes 2359296 | tf_op jit(solution)/shard_map/attend/pallas_call | solution.py:255
  56.4 0.3 collective-permute-done.9.refs_5_.refs_0_
  56.7 2.1 %attend.3 = (f32[2,128,384]{2,1,0:T(8,128)S(1)}, f32[2,8,384]{2,1,0:T(8,128)S(1)}) custom-call(s32[2]{0:T(128)S(1)} %copy-done.4, s32[4,4]{1,0:T(4,128)S(1)} %copy-done.5, s32[4]{0:T(128)S(1)} %copy-done.6, bf16[192,1536]{1,0:T(8,128)(2,1)S(1)} %bitcast.8, bf16[192,768]{1,0:T(8,128)(2,1)S(1)} %collective-permute-done.1.refs_2_.refs_1_, ...), custom_call_target="tpu_custom_call" | custom-call | flops 452984832 | bytes 1179648 | tf_op jit(solution)/shard_map/attend/pallas_call | solution.py:255
  58.9 0.7 collective-permute-start.12
  59.6 0.0 collective-permute-done.11.refs_4_
  59.6 1.3 %collective-permute-start.10 = (bf16[2,192,256]{2,1,0:T(8,128)(2,1)S(1)}, bf16[2,192,256]{2,1,0:T(8,128)(2,1)S(1)}, u32[]{:S(2)}, u32[]{:S(2)}) collective-permute-start(bf16[2,192,256]{2,1,0:T(8,128)(2,1)S(1)} %tie.2), channel_id=1, source_target_pairs={{4,0},{8,12},{5,1},{9,13},{6,2},{10,14},{7,3},{11,15},{20,16},{24,... | collective-permute-start | bytes 589832 | tf_op jit(solution)/shard_map/ppermute | solution.py:328
  60.9 0.0 collective-permute-done.3.refs_2_
  60.9 0.0 collective-permute-done.14.refs_3_
  60.9 0.0 collective-permute-done.15.refs_5_
  60.9 1.1 %attend_final.3 = (bf16[192,512]{1,0:T(8,128)(2,1)S(1)}, bf16[192,512]{1,0:T(8,128)(2,1)S(1)}) custom-call(s32[2]{0:T(128)S(1)} %copy-done.4, s32[4,4]{1,0:T(4,128)S(1)} %copy-done.5, s32[4]{0:T(128)S(1)} %copy-done.6, bf16[192,1536]{1,0:T(8,128)(2,1)S(1)} %bitcast.9, bf16[192,768]{1,0:T(8,128)(2,1)S(1)} %collective-permute-done.1.refs_2_.refs_1_, ...), custom_call_target="tpu_custom_call" | custom-call | flops 603979776 | bytes 1572864 | tf_op jit(solution)/shard_map/attend_final/pallas_call | solution.py:255
  62.0 0.6 collective-permute-start.16
  62.6 0.0 collective-permute-done.12.refs_5_
  62.6 7.6 %collective-permute-done.10.refs_3_ = bf16[2,192,256]{2,1,0:T(8,128)(2,1)S(1)} collective-permute-done((bf16[2,192,256]{2,1,0:T(8,128)(2,1)S(1)}, bf16[2,192,256]{2,1,0:T(8,128)(2,1)S(1)}, u32[]{:S(2)}, u32[]{:S(2)}) %collective-permute-start.10) | collective-permute-done | bytes 196640 | tf_op jit(solution)/shard_map/ppermute | solution.py:328
  70.3 0.9 %attend_final.2 = (bf16[192,256]{1,0:T(8,128)(2,1)S(1)}, bf16[192,256]{1,0:T(8,128)(2,1)S(1)}) custom-call(s32[2]{0:T(128)S(1)} %copy-done.4, s32[4,4]{1,0:T(4,128)S(1)} %copy-done.5, s32[4]{0:T(128)S(1)} %copy-done.6, bf16[192,1536]{1,0:T(8,128)(2,1)S(1)} %bitcast.10, bf16[192,768]{1,0:T(8,128)(2,1)S(1)} %collective-permute-done.1.refs_2_.refs_1_, ...), custom_call_target="tpu_custom_call" | custom-call | flops 301989888 | bytes 786432 | tf_op jit(solution)/shard_map/attend_final/pallas_call | solution.py:255
  71.1 0.6 collective-permute-start.13
  71.7 0.0 collective-permute-done.16.refs_2_
  71.7 1.3 %put.2.refs_1_ = bf16[192,1536]{1,0:T(8,128)(2,1)} custom-call(s32[2]{0:T(128)S(1)} %copy-done.4, bf16[192,512]{1,0:T(8,128)(2,1)S(1)} %get-tuple-element.22.refs_0_, bf16[192,256]{1,0:T(8,128)(2,1)S(1)} %get-tuple-element.23.refs_1_, bf16[192,512]{1,0:T(8,128)(2,1)S(1)} %collective-permute-done.16.refs_2_), custom_call_target="tpu_custom_call" | custom-call | tf_op jit(solution)/shard_map/put/pallas_call | solution.py:291
  73.1 2.7 %collective-permute-done.13.refs_0_ = bf16[192,256]{1,0:T(8,128)(2,1)S(1)} collective-permute-done((bf16[192,256]{1,0:T(8,128)(2,1)S(1)}, bf16[192,256]{1,0:T(8,128)(2,1)S(1)}, u32[]{:S(2)}, u32[]{:S(2)}) %collective-permute-start.13) | collective-permute-done | bytes 98336 | tf_op jit(solution)/shard_map/ppermute | solution.py:319
  75.8 1.2 %put.3 = bf16[192,1536]{1,0:T(8,128)(2,1)} custom-call(s32[2]{0:T(128)S(1)} %copy-done.4, bf16[192,256]{1,0:T(8,128)(2,1)S(1)} %collective-permute-done.13.refs_0_, bf16[192,1536]{1,0:T(8,128)(2,1)} %put.2.refs_1_), custom_call_target="tpu_custom_call", output_to_operand_aliasing={{}: (2, {})} | custom-call | tf_op jit(solution)/shard_map/put/pallas_call | solution.py:291
  (2 shorter events, 0.0 us)
Async XLA Ops:
  0.6 15.1 %copy-start = (bf16[1,4,48,1536]{3,2,1,0:T(8,128)(2,1)S(1)}, bf16[1,4,48,1536]{3,2,1,0:T(8,128)(2,1)}, u32[]{:S(2)}) copy-start(bf16[1,4,48,1536]{3,2,1,0:T(8,128)(2,1)} %param.5) | copy-start | bytes 1769476
  3.4 12.3 %collective-permute-start = (bf16[2,192,512]{2,1,0:T(8,128)(2,1)}, bf16[2,192,512]{2,1,0:T(8,128)(2,1)S(1)}, u32[]{:S(2)}, u32[]{:S(2)}) collective-permute-start(bf16[2,192,512]{2,1,0:T(8,128)(2,1)} %get-tuple-element.15), channel_id=1, source_target_pairs={{0,2},{2,0},{1,3},{3,1},{4,6},{6,4},{5,7},{7,5},{8,10},{10,8},{9,1... | collective-permute-start | bytes 1179656 | tf_op jit(solution)/shard_map/ppermute | solution.py:319
  6.4 9.3 %copy-start.4 = (s32[2]{0:T(128)S(1)}, s32[2]{0:T(128)}, u32[]{:S(2)}) copy-start(s32[2]{0:T(128)} %pad_add_fusion.place_ref) | copy-start | bytes 28
  6.4 20.3 %collective-permute-start.6 = (bf16[2,192,768]{2,1,0:T(8,128)(2,1)}, bf16[2,192,768]{2,1,0:T(8,128)(2,1)S(1)}, u32[]{:S(2)}, u32[]{:S(2)}) collective-permute-start(bf16[2,192,768]{2,1,0:T(8,128)(2,1)} %get-tuple-element.16.refs_2_), channel_id=1, source_target_pairs={{0,4},{4,0},{8,12},{12,8},{1,5},{5,1},{9,13},{13,9},{2,6},{6,2},{1... | collective-permute-start | bytes 1769480 | tf_op jit(solution)/shard_map/ppermute | solution.py:328
  8.0 19.5 %collective-permute-start.2 = (bf16[2,192,768]{2,1,0:T(8,128)(2,1)}, bf16[2,192,768]{2,1,0:T(8,128)(2,1)S(1)}, u32[]{:S(2)}, u32[]{:S(2)}) collective-permute-start(bf16[2,192,768]{2,1,0:T(8,128)(2,1)} %get-tuple-element.16.refs_2_), channel_id=1, source_target_pairs={{4,8},{8,4},{5,9},{9,5},{6,10},{10,6},{7,11},{11,7},{20,24},{24,20... | collective-permute-start | bytes 1769480 | tf_op jit(solution)/shard_map/ppermute | solution.py:328
  15.7 8.9 %copy-start.1 = (bf16[1,4,48,1536]{3,2,1,0:T(8,128)(2,1)S(1)}, bf16[1,4,48,1536]{3,2,1,0:T(8,128)(2,1)}, u32[]{:S(2)}) copy-start(bf16[1,4,48,1536]{3,2,1,0:T(8,128)(2,1)} %param.6) | copy-start | bytes 1769476
  15.8 8.9 %copy-start.2 = (bf16[1,4,48,1536]{3,2,1,0:T(8,128)(2,1)S(1)}, bf16[1,4,48,1536]{3,2,1,0:T(8,128)(2,1)}, u32[]{:S(2)}) copy-start(bf16[1,4,48,1536]{3,2,1,0:T(8,128)(2,1)} %param.7) | copy-start | bytes 1769476
  16.4 36.4 %copy-start.3 = (bf16[2,192,768]{2,1,0:T(8,128)(2,1)S(1)}, bf16[2,192,768]{2,1,0:T(8,128)(2,1)}, u32[]{:S(2)}) copy-start(bf16[2,192,768]{2,1,0:T(8,128)(2,1)} %get-tuple-element.16.refs_2_) | copy-start | bytes 1769476
  16.4 36.4 %copy-start.5 = (s32[4,4]{1,0:T(4,128)S(1)}, s32[4,4]{1,0:T(4,128)}, u32[]{:S(2)}) copy-start(s32[4,4]{1,0:T(4,128)} %flags_ref.7) | copy-start | bytes 196
  16.4 36.4 %copy-start.6 = (s32[4]{0:T(128)S(1)}, s32[4]{0:T(128)}, u32[]{:S(2)}) copy-start(s32[4]{0:T(128)} %widths_ref.7) | copy-start | bytes 52
  16.4 8.3 %collective-permute-start.1 = (bf16[192,768]{1,0:T(8,128)(2,1)S(1)}, bf16[192,768]{1,0:T(8,128)(2,1)S(1)}, u32[]{:S(2)}, u32[]{:S(2)}) collective-permute-start(bf16[192,768]{1,0:T(8,128)(2,1)S(1)} %pack.4), channel_id=1, source_target_pairs={{0,2},{2,0},{1,3},{3,1},{4,6},{6,4},{5,7},{7,5},{8,10},{10,8},{9,1... | collective-permute-start | bytes 884744 | tf_op jit(solution)/shard_map/ppermute | solution.py:319
  18.2 13.5 %collective-permute-start.8 = (bf16[2,192,512]{2,1,0:T(8,128)(2,1)S(1)}, bf16[2,192,512]{2,1,0:T(8,128)(2,1)S(1)}, u32[]{:S(2)}, u32[]{:S(2)}) collective-permute-start(bf16[2,192,512]{2,1,0:T(8,128)(2,1)S(1)} %collective-permute-done.refs_1_.refs_3_), channel_id=1, source_target_pairs={{4,8},{8,4},{5,9},{9,5},{6,10},{10,6},{7,11},{11,7},{20,24},{24,20... | collective-permute-start | bytes 1179656 | tf_op jit(solution)/shard_map/ppermute | solution.py:328
  18.9 14.1 %collective-permute-start.7 = (bf16[2,192,512]{2,1,0:T(8,128)(2,1)S(1)}, bf16[2,192,512]{2,1,0:T(8,128)(2,1)S(1)}, u32[]{:S(2)}, u32[]{:S(2)}) collective-permute-start(bf16[2,192,512]{2,1,0:T(8,128)(2,1)S(1)} %collective-permute-done.refs_1_.refs_3_), channel_id=1, source_target_pairs={{0,4},{4,0},{8,12},{12,8},{1,5},{5,1},{9,13},{13,9},{2,6},{6,2},{1... | collective-permute-start | bytes 1179656 | tf_op jit(solution)/shard_map/ppermute | solution.py:328
  25.3 5.7 %collective-permute-start.4 = (bf16[2,192,256]{2,1,0:T(8,128)(2,1)S(1)}, bf16[2,192,256]{2,1,0:T(8,128)(2,1)S(1)}, u32[]{:S(2)}, u32[]{:S(2)}) collective-permute-start(bf16[2,192,256]{2,1,0:T(8,128)(2,1)S(1)} %pack.5), channel_id=1, source_target_pairs={{0,2},{2,0},{1,3},{3,1},{4,6},{6,4},{5,7},{7,5},{8,10},{10,8},{9,1... | collective-permute-start | bytes 589832 | tf_op jit(solution)/shard_map/ppermute | solution.py:319
  26.8 32.8 %collective-permute-start.11 = (bf16[2,192,768]{2,1,0:T(8,128)(2,1)S(1)}, bf16[2,192,768]{2,1,0:T(8,128)(2,1)S(1)}, u32[]{:S(2)}, u32[]{:S(2)}) collective-permute-start(bf16[2,192,768]{2,1,0:T(8,128)(2,1)S(1)} %collective-permute-done.6.refs_4_), channel_id=1, source_target_pairs={{4,8},{8,4},{5,9},{9,5},{6,10},{10,6},{7,11},{11,7},{20,24},{24,20... | collective-permute-start | bytes 1769480 | tf_op jit(solution)/shard_map/ppermute | solution.py:328
  27.5 33.4 %collective-permute-start.3 = (bf16[2,192,768]{2,1,0:T(8,128)(2,1)S(1)}, bf16[2,192,768]{2,1,0:T(8,128)(2,1)S(1)}, u32[]{:S(2)}, u32[]{:S(2)}) collective-permute-start(bf16[2,192,768]{2,1,0:T(8,128)(2,1)S(1)} %collective-permute-done.2.refs_6_), channel_id=1, source_target_pairs={{4,0},{8,12},{5,1},{9,13},{6,2},{10,14},{7,3},{11,15},{20,16},{24,... | collective-permute-start | bytes 1769480 | tf_op jit(solution)/shard_map/ppermute | solution.py:328
  31.0 2.7 %collective-permute-start.5 = (bf16[2,192,256]{2,1,0:T(8,128)(2,1)S(1)}, bf16[2,192,256]{2,1,0:T(8,128)(2,1)S(1)}, u32[]{:S(2)}, u32[]{:S(2)}) collective-permute-start(bf16[2,192,256]{2,1,0:T(8,128)(2,1)S(1)} %collective-permute-done.4.refs_3_), channel_id=1, source_target_pairs={{4,8},{8,4},{5,9},{9,5},{6,10},{10,6},{7,11},{11,7},{20,24},{24,20... | collective-permute-start | bytes 589832 | tf_op jit(solution)/shard_map/ppermute | solution.py:328
  31.7 29.2 %collective-permute-start.14 = (bf16[2,192,512]{2,1,0:T(8,128)(2,1)S(1)}, bf16[2,192,512]{2,1,0:T(8,128)(2,1)S(1)}, u32[]{:S(2)}, u32[]{:S(2)}) collective-permute-start(bf16[2,192,512]{2,1,0:T(8,128)(2,1)S(1)} %collective-permute-done.8.refs_7_), channel_id=1, source_target_pairs={{4,0},{8,12},{5,1},{9,13},{6,2},{10,14},{7,3},{11,15},{20,16},{24,... | collective-permute-start | bytes 1179656 | tf_op jit(solution)/shard_map/ppermute | solution.py:328
  33.0 27.9 %collective-permute-start.15 = (bf16[2,192,512]{2,1,0:T(8,128)(2,1)S(1)}, bf16[2,192,512]{2,1,0:T(8,128)(2,1)S(1)}, u32[]{:S(2)}, u32[]{:S(2)}) collective-permute-start(bf16[2,192,512]{2,1,0:T(8,128)(2,1)S(1)} %collective-permute-done.7.refs_5_), channel_id=1, source_target_pairs={{4,8},{8,4},{5,9},{9,5},{6,10},{10,6},{7,11},{11,7},{20,24},{24,20... | collective-permute-start | bytes 1179656 | tf_op jit(solution)/shard_map/ppermute | solution.py:328
  33.7 23.0 %collective-permute-start.9 = (bf16[2,192,256]{2,1,0:T(8,128)(2,1)S(1)}, bf16[2,192,256]{2,1,0:T(8,128)(2,1)S(1)}, u32[]{:S(2)}, u32[]{:S(2)}) collective-permute-start(bf16[2,192,256]{2,1,0:T(8,128)(2,1)S(1)} %collective-permute-done.4.refs_3_), channel_id=1, source_target_pairs={{0,4},{4,0},{8,12},{12,8},{1,5},{5,1},{9,13},{13,9},{2,6},{6,2},{1... | collective-permute-start | bytes 589832 | tf_op jit(solution)/shard_map/ppermute | solution.py:328
  58.9 3.7 %collective-permute-start.12 = (bf16[2,192,256]{2,1,0:T(8,128)(2,1)S(1)}, bf16[2,192,256]{2,1,0:T(8,128)(2,1)S(1)}, u32[]{:S(2)}, u32[]{:S(2)}) collective-permute-start(bf16[2,192,256]{2,1,0:T(8,128)(2,1)S(1)} %tie.3), channel_id=1, source_target_pairs={{4,8},{8,4},{5,9},{9,5},{6,10},{10,6},{7,11},{11,7},{20,24},{24,20... | collective-permute-start | bytes 589832 | tf_op jit(solution)/shard_map/ppermute | solution.py:328
  59.6 10.7 %collective-permute-start.10 = (bf16[2,192,256]{2,1,0:T(8,128)(2,1)S(1)}, bf16[2,192,256]{2,1,0:T(8,128)(2,1)S(1)}, u32[]{:S(2)}, u32[]{:S(2)}) collective-permute-start(bf16[2,192,256]{2,1,0:T(8,128)(2,1)S(1)} %tie.2), channel_id=1, source_target_pairs={{4,0},{8,12},{5,1},{9,13},{6,2},{10,14},{7,3},{11,15},{20,16},{24,... | collective-permute-start | bytes 589832 | tf_op jit(solution)/shard_map/ppermute | solution.py:328
  62.0 9.7 %collective-permute-start.16 = (bf16[192,512]{1,0:T(8,128)(2,1)S(1)}, bf16[192,512]{1,0:T(8,128)(2,1)S(1)}, u32[]{:S(2)}, u32[]{:S(2)}) collective-permute-start(bf16[192,512]{1,0:T(8,128)(2,1)S(1)} %get-tuple-element.24), channel_id=1, source_target_pairs={{0,2},{2,0},{1,3},{3,1},{4,6},{6,4},{5,7},{7,5},{8,10},{10,8},{9,1... | collective-permute-start | bytes 589832 | tf_op jit(solution)/shard_map/ppermute | solution.py:319
  71.1 4.7 %collective-permute-start.13 = (bf16[192,256]{1,0:T(8,128)(2,1)S(1)}, bf16[192,256]{1,0:T(8,128)(2,1)S(1)}, u32[]{:S(2)}, u32[]{:S(2)}) collective-permute-start(bf16[192,256]{1,0:T(8,128)(2,1)S(1)} %get-tuple-element.20), channel_id=1, source_target_pairs={{0,2},{2,0},{1,3},{3,1},{4,6},{6,4},{5,7},{7,5},{8,10},{10,8},{9,1... | collective-permute-start | bytes 294920 | tf_op jit(solution)/shard_map/ppermute | solution.py:319

commit v5 on v4

--- a/solution.py
+++ b/solution.py
@@ -13,41 +13,43 @@
 VMEM_LIMIT = 16 * 1024 * 1024
 SMALL_LIMIT = 2 * 1024 * 1024
 STAGED_LIMIT = 60 * 1024 * 1024
+ROW_GROUPS = 4
 NT = (((1,), (1,)), ((), ()))
 TN = (((0,), (0,)), ((), ()))
 
 
-def pack_kernel(spaces, jobs, staged, place_ref, *refs):
+def pack_kernel(spaces, jobs, staged, *refs):
     refs = list(refs)
     halfway = refs[len(refs) - len(jobs) - 1 : -1] if staged else []
     sems = refs[-1]
-    here = place_ref[1]
-
-    def target_of(job):
-        return refs[job[4]] if job[5] is None else refs[job[4]].at[job[5]]
-
-    copies = []
-    for n, job in enumerate(jobs):
-        source, offset, first, width = job[:4]
+    here = lax.axis_index("space")
+    tokens = refs[0].shape[0]
+    groups = ROW_GROUPS if staged else 1
+    first_copies, second_copies = [], []
+    for n, (source, offset, first, width, target, row) in enumerate(jobs):
         share = refs[source].shape[-1] // spaces
         column = pl.multiple_of(lax.rem(here + offset, spaces) * share + first, HEAD_DIM)
-        out = halfway[n] if staged else target_of(job)
-        copy = pltpu.make_async_copy(refs[source].at[:, pl.ds(column, width)], out, sems.at[n])
-        copy.start()
-        copies.append(copy)
-    if staged:
-        seconds = []
-        for n, job in enumerate(jobs):
-            copies[n].wait()
-            copy = pltpu.make_async_copy(halfway[n], target_of(job), sems.at[len(jobs) + n])
+        out = refs[target] if row is None else refs[target].at[row]
+        for g in range(groups):
+            rows = pl.ds(g * (tokens // groups), tokens // groups)
+            origin = refs[source].at[rows, pl.ds(column, width)]
+            stop = halfway[n].at[rows] if staged else out.at[rows]
+            copy = pltpu.make_async_copy(origin, stop, sems.at[0, n * groups + g])
             copy.start()
-            seconds.append(copy)
-        copies = seconds
-    for copy in copies:
+            first_copies.append(copy)
+            if staged:
+                second_copies.append(
+                    pltpu.make_async_copy(stop, out.at[rows], sems.at[1, n * groups + g])
+                )
+    for n, copy in enumerate(first_copies):
         copy.wait()
-
-
-def pack(place, sources, blocks, after, spaces, staged):
+        if staged:
+            second_copies[n].start()
+    for copy in second_copies:
+        copy.wait()
+
+
+def pack(sources, blocks, after, spaces, staged):
     tokens = sources[0].shape[0]
     several = len(sources) > 1
     jobs, shapes = [], []
@@ -61,28 +63,28 @@
     space = pl.ANY if staged else pltpu.VMEM
     return pl.pallas_call(
         functools.partial(pack_kernel, spaces, tuple(jobs), staged),
-        in_specs=[pl.BlockSpec(memory_space=pltpu.SMEM)]
-        + [pl.BlockSpec(memory_space=pl.ANY)] * first_out,
+        in_specs=[pl.BlockSpec(memory_space=pl.ANY)] * first_out,
         out_specs=[pl.BlockSpec(memory_space=space)] * len(shapes),
         out_shape=shapes,
-        scratch_shapes=(halfway if staged else []) + [pltpu.SemaphoreType.DMA((2 * len(jobs),))],
+        scratch_shapes=(halfway if staged else [])
+        + [pltpu.SemaphoreType.DMA((2, ROW_GROUPS * len(jobs)))],
         compiler_params=pltpu.CompilerParams(
             vmem_limit_bytes=STAGED_LIMIT if staged else SMALL_LIMIT
         ),
         name="pack",
-    )(place, *sources, *after)
-
-
-def tie(array, after):
+    )(*sources, *after)
+
+
+def tie(arrays, after):
     return pl.pallas_call(
         lambda *refs: None,
-        in_specs=[pl.BlockSpec(memory_space=pl.ANY)] * (1 + len(after)),
-        out_specs=pl.BlockSpec(memory_space=pl.ANY),
-        out_shape=jax.ShapeDtypeStruct(array.shape, array.dtype),
-        input_output_aliases={0: 0},
+        in_specs=[pl.BlockSpec(memory_space=pl.ANY)] * (len(arrays) + len(after)),
+        out_specs=[pl.BlockSpec(memory_space=pl.ANY)] * len(arrays),
+        out_shape=[jax.ShapeDtypeStruct(x.shape, x.dtype) for x in arrays],
+        input_output_aliases={n: n for n in range(len(arrays))},
         compiler_params=pltpu.CompilerParams(vmem_limit_bytes=SMALL_LIMIT),
         name="tie",
-    )(array, *after)
+    )(*arrays, *after)
 
 
 def attend_kernel(
@@ -228,7 +230,7 @@
     tokens = queries[0].shape[0]
     width = features // spaces
     count = spaces * tokens
-    together = 2 if heads % 2 == 0 else 1
+    together = next(n for n in (3, 2, 1) if heads % n == 0)
 
     def skip_of(x):
         return first * HEAD_DIM if x.shape[-1] != heads * HEAD_DIM else 0
@@ -311,8 +313,8 @@
     scalars = (place, flags, widths)
     sizes = (spaces, frames, columns, row_band, features)
     q, k, v = (x.reshape(tokens, features) for x in (queries, keys, values))
-    tail = max(heads // 3, 1)
-    chunks = [(0, heads - tail), (heads - tail, tail)]
+    half = heads - heads // 2
+    chunks = [(0, half), (half, heads - half)]
     offsets = range(1, spaces)
 
     def along_space(x, offset):
@@ -327,48 +329,68 @@
                 pairs.append((f, f + side))
         return lax.ppermute(x, "frame", pairs)
 
-    mine, queries_back, partners, arrived = None, None, [], []
-    for first, number in chunks:
+    partners, arrived = [], []
+    for c, (first, number) in enumerate(chunks):
         blocks = [(offset, first * HEAD_DIM, number * HEAD_DIM) for offset in offsets]
-        if mine is None:
-            mine, *sends = pack(place, (k, v), [(0, 0, width)] + blocks, (), spaces, True)
+        if c == 0:
+            mine, *sends = pack((k, v), [(0, 0, width)] + blocks, (), spaces, True)
         else:
-            sends = pack(place, (k, v), blocks, arrived, spaces, False)
+            sends = pack((k, v), blocks, arrived, spaces, False)
         arrived = [along_space(x, offset) for x, offset in zip(sends, offsets)]
         partners.append(arrived)
-        if queries_back is None:
-            sends = pack(place, (q,), [(o, 0, width) for o in offsets], arrived, spaces, False)
-            arrived = [along_space(x, offset) for x, offset in zip(sends, offsets)]
-            queries_back = arrived
-    query_parts = [q] + queries_back
-
-    carried = [[mine, mine]] + [[x, x] for x in partners]
+    sends = pack((q,), [(offset, 0, width) for offset in offsets], arrived, spaces, False)
+    query_parts = [q] + [along_space(x, offset) for x, offset in zip(sends, offsets)]
+
+    def tied(lists, after):
+        flat = list(tie([x for xs in lists for x in xs], after))
+        return [[flat.pop(0) for unused in xs] for xs in lists]
+
     states = [None] * len(chunks)
-    groups = [[(0, 0, [mine] + partners[c])] for c in range(len(chunks))]
+    own_now = [[mine], [mine]]
+    own_next = [[swap(x, slot, 1) for x in own_now[slot]] for slot in range(2)]
+    first_next = [[swap(x, slot, 1) for x in partners[0]] for slot in range(2)]
+    *first_next, partners[1] = tied(first_next + [partners[1]], sends)
+    second_next = [[swap(x, slot, 1) for x in partners[1]] for slot in range(2)]
+    groups = [[(0, 0, [mine] + xs)] for xs in partners]
     for hops in range(1, frames - 1):
-        sent = []
-        for c, (first_slot, second_slot) in enumerate(carried):
-            over = [second_slot, first_slot]
-            if c == 0:
-                sent.append([swap(over[slot], slot, hops) for slot in range(2)])
-                continue
-            if c == len(chunks) and states[0] is not None:
-                over = [[tie(x, [state[1] for state in states]) for x in xs] for xs in over]
-            sent.append([[swap(x, slot, hops) for x in over[slot]] for slot in range(2)])
-        carried = sent
-        for c, chunk in enumerate(chunks):
-            groups[c] += [
-                (slot, hops, [carried[0][slot]] + carried[1 + c][slot]) for slot in range(2)
+        if hops > 1:
+            own_now, first_now, second_now = own_next, first_next, second_next
+            own_next = early
+            lists = tied(first_now + second_now, [states[0][1]])
+            first_now, second_now = lists[:2], lists[2:]
+            first_next = [[swap(x, slot, hops) for x in first_now[1 - slot]] for slot in range(2)]
+            groups[1] = [
+                (slot, hops - 1, own_now[slot] + second_now[slot]) for slot in range(2)
             ]
-            if hops < frames - 2:
-                states[c] = attend(
-                    scalars, query_parts, groups[c], states[c], False, chunk, sizes
-                )
-                groups[c] = []
+            if hops == 2:
+                groups[1].insert(0, (0, 0, [mine] + partners[1]))
+            states[1] = attend(
+                scalars, query_parts, groups[1], states[1], False, chunks[1], sizes
+            )
+            lists = tied(second_now + own_next, [states[1][1]])
+            second_now, own_next = lists[:2], lists[2:]
+            second_next = [
+                [swap(x, slot, hops) for x in second_now[1 - slot]] for slot in range(2)
+            ]
+        if hops < frames - 2:
+            early = [[swap(x, slot, hops + 1) for x in own_next[1 - slot]] for slot in range(2)]
+            if hops > 1:
+                groups[0] = []
+            groups[0] += [(slot, hops, own_next[slot] + first_next[slot]) for slot in range(2)]
+            states[0] = attend(
+                scalars, query_parts, groups[0], states[0], False, chunks[0], sizes
+            )
+    last = frames - 2
+    finals = [
+        [(slot, last, own_next[slot] + xs[slot]) for slot in range(2)]
+        for xs in (first_next, second_next)
+    ]
+    if last == 1:
+        finals = [own + final for own, final in zip(groups, finals)]
 
     own, returned = [], []
     for c, chunk in enumerate(chunks):
-        kept, *parts = attend(scalars, query_parts, groups[c], states[c], True, chunk, sizes)
+        kept, *parts = attend(scalars, query_parts, finals[c], states[c], True, chunk, sizes)
         own.append((kept, (0, chunk[0] * HEAD_DIM)))
         for offset, x in zip(offsets, parts):
             returned.append((along_space(x, -offset), (offset, chunk[0] * HEAD_DIM)))

time: 77.7 us -> 74.4 us (0.958)
  the two profiles are of different devices: /device:TPU:0 before, /device:TPU:8 now
where the time goes in v5:
time: 74.4 us; the launch traced here: 73.9 us
  starting transfers between devices  30.1 us (40%)
  waiting for transfers between devices  22.7 us (31%)
  Pallas kernels  18.1 us (24%)
  local copies, waits for them, and re-layouts  2.7 us (4%)
    ppermute x12, starting transfers between devices, swap(): return lax.ppermute(x, 'frame', pairs)  23.3 us
    ppermute x12, waiting for transfers between devices, swap(): return lax.ppermute(x, 'frame', pairs)  12.9 us
    pallas_call x4, Pallas kernels, attend(): pl.pallas_call(functools.partial(attend_kernel, spaces, frames, columns,...  12.3 us
    ppermute x5, waiting for transfers between devices, along_space(): lax.ppermute(x, 'space', [(s, (s + offset) % spaces) for s in range(space...  9.79 us
    ppermute x5, starting transfers between devices, along_space(): lax.ppermute(x, 'space', [(s, (s + offset) % spaces) for s in range(space...  6.82 us
    pallas_call x3, Pallas kernels, pack(): pl.pallas_call(functools.partial(pack_kernel, spaces, tuple(jobs), staged...  3.27 us
    unnamed x16, local copies, waits for them, and re-layouts  2.7 us
    pallas_call x2, Pallas kernels, put(): pl.pallas_call(functools.partial(put_kernel, spaces, tuple(places), len(k...  2.55 us
  transfers between devices with their start and end apart: 17, of which 7 were waited for; matrix products, arithmetic and copies ran while one was open for 0% of the time, Pallas kernels for 20%

profile of v5, /device:TPU:8, one launch (start us, length us, event | category | flops | bytes accessed | tf_op | source)
XLA Modules:
  0.0 73.9 jit_solution(519392511634358353)
XLA Ops:
  0.0 0.0 copy-start.2
  0.0 0.0 copy-start.3
  0.0 2.2 %pack.3 = (bf16[2,192,768]{2,1,0:T(8,128)(2,1)}, bf16[2,192,384]{2,1,0:T(8,128)(2,1)}) custom-call(bf16[192,1536]{1,0:T(8,128)(2,1)} %bitcast.11, bf16[192,1536]{1,0:T(8,128)(2,1)} %bitcast.13), custom_call_target="tpu_custom_call" | custom-call | tf_op jit(solution)/shard_map/pack/pallas_call | solution.py:64
  2.2 0.1 collective-permute-start.7
  2.3 5.0 %collective-permute-start.8 = (bf16[2,192,768]{2,1,0:T(8,128)(2,1)}, bf16[2,192,768]{2,1,0:T(8,128)(2,1)}, u32[]{:S(2)}, u32[]{:S(2)}) collective-permute-start(bf16[2,192,768]{2,1,0:T(8,128)(2,1)} %get-tuple-element.30.refs_2_), channel_id=1, source_target_pairs={{4,8},{8,4},{5,9},{9,5},{6,10},{10,6},{7,11},{11,7},{20,24},{24,20... | collective-permute-start | bytes 1769480 | tf_op jit(solution)/shard_map/ppermute | solution.py:330
  7.4 0.0 copy-start
  7.4 1.6 %collective-permute-start = (bf16[2,192,384]{2,1,0:T(8,128)(2,1)}, bf16[2,192,384]{2,1,0:T(8,128)(2,1)S(1)}, u32[]{:S(2)}, u32[]{:S(2)}) collective-permute-start(bf16[2,192,384]{2,1,0:T(8,128)(2,1)} %get-tuple-element.26), channel_id=1, source_target_pairs={{0,2},{2,0},{1,3},{3,1},{4,6},{6,4},{5,7},{7,5},{8,10},{10,8},{9,1... | collective-permute-start | bytes 884744 | tf_op jit(solution)/shard_map/ppermute | solution.py:321
  8.9 6.9 %collective-permute-done.refs_2_.refs_3_ = bf16[2,192,384]{2,1,0:T(8,128)(2,1)S(1)} collective-permute-done((bf16[2,192,384]{2,1,0:T(8,128)(2,1)}, bf16[2,192,384]{2,1,0:T(8,128)(2,1)S(1)}, u32[]{:S(2)}, u32[]{:S(2)}) %collective-permute-start) | collective-permute-done | bytes 294944 | tf_op jit(solution)/shard_map/ppermute | solution.py:321
  15.8 0.0 copy-done.2
  15.9 0.0 copy-done.3
  15.9 0.0 copy-start.4
  15.9 0.2 pack.4
  16.1 1.6 %collective-permute-start.1 = (bf16[2,192,384]{2,1,0:T(8,128)(2,1)S(1)}, bf16[2,192,384]{2,1,0:T(8,128)(2,1)S(1)}, u32[]{:S(2)}, u32[]{:S(2)}) collective-permute-start(bf16[2,192,384]{2,1,0:T(8,128)(2,1)S(1)} %pack.4), channel_id=1, source_target_pairs={{0,2},{2,0},{1,3},{3,1},{4,6},{6,4},{5,7},{7,5},{8,10},{10,8},{9,1... | collective-permute-start | bytes 884744 | tf_op jit(solution)/shard_map/ppermute | solution.py:321
  17.6 0.0 collective-permute-start.3
  17.6 0.0 copy-done.4
  17.6 2.2 %collective-permute-start.4 = (bf16[2,192,384]{2,1,0:T(8,128)(2,1)S(1)}, bf16[2,192,384]{2,1,0:T(8,128)(2,1)S(1)}, u32[]{:S(2)}, u32[]{:S(2)}) collective-permute-start(bf16[2,192,384]{2,1,0:T(8,128)(2,1)S(1)} %collective-permute-done.refs_2_.refs_3_), channel_id=1, source_target_pairs={{4,8},{8,4},{5,9},{9,5},{6,10},{10,6},{7,11},{11,7},{20,24},{24,20... | collective-permute-start | bytes 884744 | tf_op jit(solution)/shard_map/ppermute | solution.py:330
  19.8 0.0 collective-permute-done.7.refs_4_
  19.8 3.6 %collective-permute-start.10 = (bf16[2,192,768]{2,1,0:T(8,128)(2,1)}, bf16[2,192,768]{2,1,0:T(8,128)(2,1)S(1)}, u32[]{:S(2)}, u32[]{:S(2)}) collective-permute-start(bf16[2,192,768]{2,1,0:T(8,128)(2,1)} %collective-permute-done.7.refs_4_), channel_id=1, source_target_pairs={{4,8},{8,4},{5,9},{9,5},{6,10},{10,6},{7,11},{11,7},{20,24},{24,20... | collective-permute-start | bytes 1769480 | tf_op jit(solution)/shard_map/ppermute | solution.py:330
  23.5 0.0 collective-permute-done.8.refs_6_
  23.5 1.3 %collective-permute-start.9 = (bf16[2,192,768]{2,1,0:T(8,128)(2,1)}, bf16[2,192,768]{2,1,0:T(8,128)(2,1)S(1)}, u32[]{:S(2)}, u32[]{:S(2)}) collective-permute-start(bf16[2,192,768]{2,1,0:T(8,128)(2,1)} %collective-permute-done.8.refs_6_), channel_id=1, source_target_pairs={{4,0},{8,12},{5,1},{9,13},{6,2},{10,14},{7,3},{11,15},{20,16},{24,... | collective-permute-start | bytes 1769480 | tf_op jit(solution)/shard_map/ppermute | solution.py:330
  24.8 0.0 collective-permute-done.1.refs_1_.refs_2_
  24.8 0.0 copy-done
  24.8 0.8 %pack.5.refs_3_ = bf16[192,768]{1,0:T(8,128)(2,1)} custom-call(bf16[192,1536]{1,0:T(8,128)(2,1)S(1)} %bitcast.6, bf16[2,192,384]{2,1,0:T(8,128)(2,1)S(1)} %collective-permute-done.1.refs_1_.refs_2_), custom_call_target="tpu_custom_call" | custom-call | tf_op jit(solution)/shard_map/pack/pallas_call | solution.py:64
  25.7 0.6 collective-permute-start.2
  26.3 0.0 collective-permute-done.3.refs_0_
  26.3 3.1 %collective-permute-done.4.refs_1_ = bf16[2,192,384]{2,1,0:T(8,128)(2,1)S(1)} collective-permute-done((bf16[2,192,384]{2,1,0:T(8,128)(2,1)S(1)}, bf16[2,192,384]{2,1,0:T(8,128)(2,1)S(1)}, u32[]{:S(2)}, u32[]{:S(2)}) %collective-permute-start.4) | collective-permute-done | bytes 294944 | tf_op jit(solution)/shard_map/ppermute | solution.py:330
  29.4 0.0 collective-permute-start.5
  29.5 2.6 %collective-permute-start.6 = (bf16[2,192,384]{2,1,0:T(8,128)(2,1)S(1)}, bf16[2,192,384]{2,1,0:T(8,128)(2,1)S(1)}, u32[]{:S(2)}, u32[]{:S(2)}) collective-permute-start(bf16[2,192,384]{2,1,0:T(8,128)(2,1)S(1)} %get-tuple-element.29.refs_3_), channel_id=1, source_target_pairs={{4,8},{8,4},{5,9},{9,5},{6,10},{10,6},{7,11},{11,7},{20,24},{24,20... | collective-permute-start | bytes 884744 | tf_op jit(solution)/shard_map/ppermute | solution.py:330
  32.0 0.1 pad_add_fusion.place_ref
  32.1 0.0 copy-start.6
  32.1 0.6 collective-permute-done.2.refs_1_
  32.7 0.0 copy-start.7
  32.7 0.1 copy-done.6
  32.8 0.5 copy-done.7
  33.4 0.0 copy-start.1
  33.4 1.1 %copy-done.1 = bf16[2,192,768]{2,1,0:T(8,128)(2,1)S(1)} copy-done((bf16[2,192,768]{2,1,0:T(8,128)(2,1)S(1)}, bf16[2,192,768]{2,1,0:T(8,128)(2,1)}, u32[]{:S(2)}) %copy-start.1) | copy-done | bytes 589848
  34.4 0.0 copy-start.5
  34.4 1.0 %copy-done.5 = bf16[2,192,384]{2,1,0:T(8,128)(2,1)S(1)} copy-done((bf16[2,192,384]{2,1,0:T(8,128)(2,1)S(1)}, bf16[2,192,384]{2,1,0:T(8,128)(2,1)}, u32[]{:S(2)}) %copy-start.5) | copy-done | bytes 294936
  35.4 4.2 %attend.2 = (f32[3,128,384]{2,1,0:T(8,128)S(1)}, f32[3,8,384]{2,1,0:T(8,128)S(1)}) custom-call(s32[2]{0:T(128)S(1)} %pad_add_fusion.place_ref, s32[4,4]{1,0:T(4,128)S(1)} %copy-done.6, s32[4]{0:T(128)S(1)} %copy-done.7, bf16[192,1536]{1,0:T(8,128)(2,1)S(1)} %bitcast.7, bf16[192,768]{1,0:T(8,128)(2,1)S(1)} %collective-permute-done.2.refs_1_, ...), custom_call_target="tpu_custom_call" | custom-call | flops 679477248 | bytes 1769472 | tf_op jit(solution)/shard_map/attend/pallas_call | solution.py:257
  39.6 2.3 %collective-permute-done.5.refs_2_ = bf16[2,192,384]{2,1,0:T(8,128)(2,1)S(1)} collective-permute-done((bf16[2,192,384]{2,1,0:T(8,128)(2,1)S(1)}, bf16[2,192,384]{2,1,0:T(8,128)(2,1)S(1)}, u32[]{:S(2)}, u32[]{:S(2)}) %collective-permute-start.5) | collective-permute-done | bytes 294944 | tf_op jit(solution)/shard_map/ppermute | solution.py:330
  41.9 4.0 %collective-permute-done.6.refs_3_ = bf16[2,192,384]{2,1,0:T(8,128)(2,1)S(1)} collective-permute-done((bf16[2,192,384]{2,1,0:T(8,128)(2,1)S(1)}, bf16[2,192,384]{2,1,0:T(8,128)(2,1)S(1)}, u32[]{:S(2)}, u32[]{:S(2)}) %collective-permute-start.6) | collective-permute-done | bytes 294944 | tf_op jit(solution)/shard_map/ppermute | solution.py:330
  45.9 1.3 %collective-permute-start.14 = (bf16[2,192,384]{2,1,0:T(8,128)(2,1)S(1)}, bf16[2,192,384]{2,1,0:T(8,128)(2,1)S(1)}, u32[]{:S(2)}, u32[]{:S(2)}) collective-permute-start(bf16[2,192,384]{2,1,0:T(8,128)(2,1)S(1)} %get-tuple-element.41), channel_id=1, source_target_pairs={{4,0},{8,12},{5,1},{9,13},{6,2},{10,14},{7,3},{11,15},{20,16},{24,... | collective-permute-start | bytes 884744 | tf_op jit(solution)/shard_map/ppermute | solution.py:330
  47.2 3.6 %collective-permute-start.15 = (bf16[2,192,384]{2,1,0:T(8,128)(2,1)S(1)}, bf16[2,192,384]{2,1,0:T(8,128)(2,1)S(1)}, u32[]{:S(2)}, u32[]{:S(2)}) collective-permute-start(bf16[2,192,384]{2,1,0:T(8,128)(2,1)S(1)} %get-tuple-element.42), channel_id=1, source_target_pairs={{4,8},{8,4},{5,9},{9,5},{6,10},{10,6},{7,11},{11,7},{20,24},{24,20... | collective-permute-start | bytes 884744 | tf_op jit(solution)/shard_map/ppermute | solution.py:330
  50.8 4.2 %attend.3 = (f32[3,128,384]{2,1,0:T(8,128)S(1)}, f32[3,8,384]{2,1,0:T(8,128)S(1)}) custom-call(s32[2]{0:T(128)S(1)} %pad_add_fusion.place_ref, s32[4,4]{1,0:T(4,128)S(1)} %copy-done.6, s32[4]{0:T(128)S(1)} %copy-done.7, bf16[192,1536]{1,0:T(8,128)(2,1)S(1)} %bitcast.8, bf16[192,768]{1,0:T(8,128)(2,1)S(1)} %collective-permute-done.2.refs_1_, ...), custom_call_target="tpu_custom_call" | custom-call | flops 679477248 | bytes 1769472 | tf_op jit(solution)/shard_map/attend/pallas_call | solution.py:257
  55.1 0.0 collective-permute-done.10.refs_3_
  55.1 0.0 collective-permute-done.9.refs_2_
  55.1 1.3 %collective-permute-start.11 = (bf16[2,192,384]{2,1,0:T(8,128)(2,1)S(1)}, bf16[2,192,384]{2,1,0:T(8,128)(2,1)S(1)}, u32[]{:S(2)}, u32[]{:S(2)}) collective-permute-start(bf16[2,192,384]{2,1,0:T(8,128)(2,1)S(1)} %get-tuple-element.36), channel_id=1, source_target_pairs={{4,0},{8,12},{5,1},{9,13},{6,2},{10,14},{7,3},{11,15},{20,16},{24,... | collective-permute-start | bytes 884744 | tf_op jit(solution)/shard_map/ppermute | solution.py:330
  56.4 2.2 %collective-permute-start.12 = (bf16[2,192,384]{2,1,0:T(8,128)(2,1)S(1)}, bf16[2,192,384]{2,1,0:T(8,128)(2,1)S(1)}, u32[]{:S(2)}, u32[]{:S(2)}) collective-permute-start(bf16[2,192,384]{2,1,0:T(8,128)(2,1)S(1)} %get-tuple-element.38), channel_id=1, source_target_pairs={{4,8},{8,4},{5,9},{9,5},{6,10},{10,6},{7,11},{11,7},{20,24},{24,20... | collective-permute-start | bytes 884744 | tf_op jit(solution)/shard_map/ppermute | solution.py:330
  58.6 0.0 collective-permute-done.14.refs_3_
  58.6 0.0 collective-permute-done.15.refs_5_
  58.7 1.9 %attend_final.3 = (bf16[192,384]{1,0:T(8,128)(2,1)S(1)}, bf16[192,384]{1,0:T(8,128)(2,1)S(1)}) custom-call(s32[2]{0:T(128)S(1)} %pad_add_fusion.place_ref, s32[4,4]{1,0:T(4,128)S(1)} %copy-done.6, s32[4]{0:T(128)S(1)} %copy-done.7, bf16[192,1536]{1,0:T(8,128)(2,1)S(1)} %bitcast.9, bf16[192,768]{1,0:T(8,128)(2,1)S(1)} %collective-permute-done.2.refs_1_, ...), custom_call_target="tpu_custom_call" | custom-call | flops 452984832 | bytes 1179648 | tf_op jit(solution)/shard_map/attend_final/pallas_call | solution.py:257
  60.6 1.6 %collective-permute-start.16 = (bf16[192,384]{1,0:T(8,128)(2,1)S(1)}, bf16[192,384]{1,0:T(8,128)(2,1)S(1)}, u32[]{:S(2)}, u32[]{:S(2)}) collective-permute-start(bf16[192,384]{1,0:T(8,128)(2,1)S(1)} %get-tuple-element.46), channel_id=1, source_target_pairs={{0,2},{2,0},{1,3},{3,1},{4,6},{6,4},{5,7},{7,5},{8,10},{10,8},{9,1... | collective-permute-start | bytes 442376 | tf_op jit(solution)/shard_map/ppermute | solution.py:321
  62.1 0.0 collective-permute-done.11.refs_3_
  62.1 3.5 %collective-permute-done.12.refs_5_ = bf16[2,192,384]{2,1,0:T(8,128)(2,1)S(1)} collective-permute-done((bf16[2,192,384]{2,1,0:T(8,128)(2,1)S(1)}, bf16[2,192,384]{2,1,0:T(8,128)(2,1)S(1)}, u32[]{:S(2)}, u32[]{:S(2)}) %collective-permute-start.12) | collective-permute-done | bytes 294944 | tf_op jit(solution)/shard_map/ppermute | solution.py:330
  65.6 1.9 %attend_final.2 = (bf16[192,384]{1,0:T(8,128)(2,1)S(1)}, bf16[192,384]{1,0:T(8,128)(2,1)S(1)}) custom-call(s32[2]{0:T(128)S(1)} %pad_add_fusion.place_ref, s32[4,4]{1,0:T(4,128)S(1)} %copy-done.6, s32[4]{0:T(128)S(1)} %copy-done.7, bf16[192,1536]{1,0:T(8,128)(2,1)S(1)} %bitcast.10, bf16[192,768]{1,0:T(8,128)(2,1)S(1)} %collective-permute-done.2.refs_1_, ...), custom_call_target="tpu_custom_call" | custom-call | flops 452984832 | bytes 1179648 | tf_op jit(solution)/shard_map/attend_final/pallas_call | solution.py:257
  67.5 1.6 %collective-permute-start.13 = (bf16[192,384]{1,0:T(8,128)(2,1)S(1)}, bf16[192,384]{1,0:T(8,128)(2,1)S(1)}, u32[]{:S(2)}, u32[]{:S(2)}) collective-permute-start(bf16[192,384]{1,0:T(8,128)(2,1)S(1)} %get-tuple-element.40), channel_id=1, source_target_pairs={{0,2},{2,0},{1,3},{3,1},{4,6},{6,4},{5,7},{7,5},{8,10},{10,8},{9,1... | collective-permute-start | bytes 442376 | tf_op jit(solution)/shard_map/ppermute | solution.py:321
  69.1 0.0 collective-permute-done.16.refs_2_
  69.1 1.3 %put.2.refs_1_ = bf16[192,1536]{1,0:T(8,128)(2,1)} custom-call(s32[2]{0:T(128)S(1)} %pad_add_fusion.place_ref, bf16[192,384]{1,0:T(8,128)(2,1)S(1)} %get-tuple-element.44.refs_0_, bf16[192,384]{1,0:T(8,128)(2,1)S(1)} %get-tuple-element.45.refs_1_, bf16[192,384]{1,0:T(8,128)(2,1)S(1)} %collective-permute-done.16.refs_2_), custom_call_target="tpu_custom_call" | custom-call | tf_op jit(solution)/shard_map/put/pallas_call | solution.py:293
  70.4 2.3 %collective-permute-done.13.refs_0_ = bf16[192,384]{1,0:T(8,128)(2,1)S(1)} collective-permute-done((bf16[192,384]{1,0:T(8,128)(2,1)S(1)}, bf16[192,384]{1,0:T(8,128)(2,1)S(1)}, u32[]{:S(2)}, u32[]{:S(2)}) %collective-permute-start.13) | collective-permute-done | bytes 147488 | tf_op jit(solution)/shard_map/ppermute | solution.py:321
  72.7 1.2 %put.3 = bf16[192,1536]{1,0:T(8,128)(2,1)} custom-call(s32[2]{0:T(128)S(1)} %pad_add_fusion.place_ref, bf16[192,384]{1,0:T(8,128)(2,1)S(1)} %collective-permute-done.13.refs_0_, bf16[192,1536]{1,0:T(8,128)(2,1)} %put.2.refs_1_), custom_call_target="tpu_custom_call", output_to_operand_aliasing={{}: (2, {})} | custom-call | tf_op jit(solution)/shard_map/put/pallas_call | solution.py:293
  (3 shorter events, 0.0 us)
Async XLA Ops:
  0.0 15.8 %copy-start.2 = (bf16[1,4,48,1536]{3,2,1,0:T(8,128)(2,1)S(1)}, bf16[1,4,48,1536]{3,2,1,0:T(8,128)(2,1)}, u32[]{:S(2)}) copy-start(bf16[1,4,48,1536]{3,2,1,0:T(8,128)(2,1)} %param.6) | copy-start | bytes 1769476
  0.0 15.8 %copy-start.3 = (bf16[1,4,48,1536]{3,2,1,0:T(8,128)(2,1)S(1)}, bf16[1,4,48,1536]{3,2,1,0:T(8,128)(2,1)}, u32[]{:S(2)}) copy-start(bf16[1,4,48,1536]{3,2,1,0:T(8,128)(2,1)} %param.7) | copy-start | bytes 1769476
  2.2 17.6 %collective-permute-start.7 = (bf16[2,192,768]{2,1,0:T(8,128)(2,1)}, bf16[2,192,768]{2,1,0:T(8,128)(2,1)}, u32[]{:S(2)}, u32[]{:S(2)}) collective-permute-start(bf16[2,192,768]{2,1,0:T(8,128)(2,1)} %get-tuple-element.30.refs_2_), channel_id=1, source_target_pairs={{0,4},{4,0},{8,12},{12,8},{1,5},{5,1},{9,13},{13,9},{2,6},{6,2},{1... | collective-permute-start | bytes 1769480 | tf_op jit(solution)/shard_map/ppermute | solution.py:330
  2.3 21.1 %collective-permute-start.8 = (bf16[2,192,768]{2,1,0:T(8,128)(2,1)}, bf16[2,192,768]{2,1,0:T(8,128)(2,1)}, u32[]{:S(2)}, u32[]{:S(2)}) collective-permute-start(bf16[2,192,768]{2,1,0:T(8,128)(2,1)} %get-tuple-element.30.refs_2_), channel_id=1, source_target_pairs={{4,8},{8,4},{5,9},{9,5},{6,10},{10,6},{7,11},{11,7},{20,24},{24,20... | collective-permute-start | bytes 1769480 | tf_op jit(solution)/shard_map/ppermute | solution.py:330
  7.4 17.5 %copy-start = (bf16[1,4,48,1536]{3,2,1,0:T(8,128)(2,1)S(1)}, bf16[1,4,48,1536]{3,2,1,0:T(8,128)(2,1)}, u32[]{:S(2)}) copy-start(bf16[1,4,48,1536]{3,2,1,0:T(8,128)(2,1)} %param.5) | copy-start | bytes 1769476
  7.4 8.5 %collective-permute-start = (bf16[2,192,384]{2,1,0:T(8,128)(2,1)}, bf16[2,192,384]{2,1,0:T(8,128)(2,1)S(1)}, u32[]{:S(2)}, u32[]{:S(2)}) collective-permute-start(bf16[2,192,384]{2,1,0:T(8,128)(2,1)} %get-tuple-element.26), channel_id=1, source_target_pairs={{0,2},{2,0},{1,3},{3,1},{4,6},{6,4},{5,7},{7,5},{8,10},{10,8},{9,1... | collective-permute-start | bytes 884744 | tf_op jit(solution)/shard_map/ppermute | solution.py:321
  15.9 1.8 %copy-start.4 = (bf16[2,192,384]{2,1,0:T(8,128)(2,1)}, bf16[2,192,384]{2,1,0:T(8,128)(2,1)S(1)}, u32[]{:S(2)}) copy-start(bf16[2,192,384]{2,1,0:T(8,128)(2,1)S(1)} %collective-permute-done.refs_2_.refs_3_) | copy-start | bytes 884740
  16.1 8.8 %collective-permute-start.1 = (bf16[2,192,384]{2,1,0:T(8,128)(2,1)S(1)}, bf16[2,192,384]{2,1,0:T(8,128)(2,1)S(1)}, u32[]{:S(2)}, u32[]{:S(2)}) collective-permute-start(bf16[2,192,384]{2,1,0:T(8,128)(2,1)S(1)} %pack.4), channel_id=1, source_target_pairs={{0,2},{2,0},{1,3},{3,1},{4,6},{6,4},{5,7},{7,5},{8,10},{10,8},{9,1... | collective-permute-start | bytes 884744 | tf_op jit(solution)/shard_map/ppermute | solution.py:321
  17.6 8.7 %collective-permute-start.3 = (bf16[2,192,384]{2,1,0:T(8,128)(2,1)S(1)}, bf16[2,192,384]{2,1,0:T(8,128)(2,1)S(1)}, u32[]{:S(2)}, u32[]{:S(2)}) collective-permute-start(bf16[2,192,384]{2,1,0:T(8,128)(2,1)S(1)} %collective-permute-done.refs_2_.refs_3_), channel_id=1, source_target_pairs={{0,4},{4,0},{8,12},{12,8},{1,5},{5,1},{9,13},{13,9},{2,6},{6,2},{1... | collective-permute-start | bytes 884744 | tf_op jit(solution)/shard_map/ppermute | solution.py:330
  17.6 11.8 %collective-permute-start.4 = (bf16[2,192,384]{2,1,0:T(8,128)(2,1)S(1)}, bf16[2,192,384]{2,1,0:T(8,128)(2,1)S(1)}, u32[]{:S(2)}, u32[]{:S(2)}) collective-permute-start(bf16[2,192,384]{2,1,0:T(8,128)(2,1)S(1)} %collective-permute-done.refs_2_.refs_3_), channel_id=1, source_target_pairs={{4,8},{8,4},{5,9},{9,5},{6,10},{10,6},{7,11},{11,7},{20,24},{24,20... | collective-permute-start | bytes 884744 | tf_op jit(solution)/shard_map/ppermute | solution.py:330
  19.8 35.3 %collective-permute-start.10 = (bf16[2,192,768]{2,1,0:T(8,128)(2,1)}, bf16[2,192,768]{2,1,0:T(8,128)(2,1)S(1)}, u32[]{:S(2)}, u32[]{:S(2)}) collective-permute-start(bf16[2,192,768]{2,1,0:T(8,128)(2,1)} %collective-permute-done.7.refs_4_), channel_id=1, source_target_pairs={{4,8},{8,4},{5,9},{9,5},{6,10},{10,6},{7,11},{11,7},{20,24},{24,20... | collective-permute-start | bytes 1769480 | tf_op jit(solution)/shard_map/ppermute | solution.py:330
  23.5 31.6 %collective-permute-start.9 = (bf16[2,192,768]{2,1,0:T(8,128)(2,1)}, bf16[2,192,768]{2,1,0:T(8,128)(2,1)S(1)}, u32[]{:S(2)}, u32[]{:S(2)}) collective-permute-start(bf16[2,192,768]{2,1,0:T(8,128)(2,1)} %collective-permute-done.8.refs_6_), channel_id=1, source_target_pairs={{4,0},{8,12},{5,1},{9,13},{6,2},{10,14},{7,3},{11,15},{20,16},{24,... | collective-permute-start | bytes 1769480 | tf_op jit(solution)/shard_map/ppermute | solution.py:330
  25.7 7.0 %collective-permute-start.2 = (bf16[192,768]{1,0:T(8,128)(2,1)}, bf16[192,768]{1,0:T(8,128)(2,1)S(1)}, u32[]{:S(2)}, u32[]{:S(2)}) collective-permute-start(bf16[192,768]{1,0:T(8,128)(2,1)} %pack.5.refs_3_), channel_id=1, source_target_pairs={{0,2},{2,0},{1,3},{3,1},{4,6},{6,4},{5,7},{7,5},{8,10},{10,8},{9,1... | collective-permute-start | bytes 884744 | tf_op jit(solution)/shard_map/ppermute | solution.py:321
  29.4 12.5 %collective-permute-start.5 = (bf16[2,192,384]{2,1,0:T(8,128)(2,1)S(1)}, bf16[2,192,384]{2,1,0:T(8,128)(2,1)S(1)}, u32[]{:S(2)}, u32[]{:S(2)}) collective-permute-start(bf16[2,192,384]{2,1,0:T(8,128)(2,1)S(1)} %get-tuple-element.29.refs_3_), channel_id=1, source_target_pairs={{0,4},{4,0},{8,12},{12,8},{1,5},{5,1},{9,13},{13,9},{2,6},{6,2},{1... | collective-permute-start | bytes 884744 | tf_op jit(solution)/shard_map/ppermute | solution.py:330
  29.5 16.4 %collective-permute-start.6 = (bf16[2,192,384]{2,1,0:T(8,128)(2,1)S(1)}, bf16[2,192,384]{2,1,0:T(8,128)(2,1)S(1)}, u32[]{:S(2)}, u32[]{:S(2)}) collective-permute-start(bf16[2,192,384]{2,1,0:T(8,128)(2,1)S(1)} %get-tuple-element.29.refs_3_), channel_id=1, source_target_pairs={{4,8},{8,4},{5,9},{9,5},{6,10},{10,6},{7,11},{11,7},{20,24},{24,20... | collective-permute-start | bytes 884744 | tf_op jit(solution)/shard_map/ppermute | solution.py:330
  32.1 0.7 copy-start.6
  32.7 0.7 copy-start.7
  33.4 1.1 %copy-start.1 = (bf16[2,192,768]{2,1,0:T(8,128)(2,1)S(1)}, bf16[2,192,768]{2,1,0:T(8,128)(2,1)}, u32[]{:S(2)}) copy-start(bf16[2,192,768]{2,1,0:T(8,128)(2,1)} %get-tuple-element.30.refs_2_) | copy-start | bytes 1769476
  34.4 1.0 %copy-start.5 = (bf16[2,192,384]{2,1,0:T(8,128)(2,1)S(1)}, bf16[2,192,384]{2,1,0:T(8,128)(2,1)}, u32[]{:S(2)}) copy-start(bf16[2,192,384]{2,1,0:T(8,128)(2,1)} %copy-done.4) | copy-start | bytes 884740
  45.9 12.7 %collective-permute-start.14 = (bf16[2,192,384]{2,1,0:T(8,128)(2,1)S(1)}, bf16[2,192,384]{2,1,0:T(8,128)(2,1)S(1)}, u32[]{:S(2)}, u32[]{:S(2)}) collective-permute-start(bf16[2,192,384]{2,1,0:T(8,128)(2,1)S(1)} %get-tuple-element.41), channel_id=1, source_target_pairs={{4,0},{8,12},{5,1},{9,13},{6,2},{10,14},{7,3},{11,15},{20,16},{24,... | collective-permute-start | bytes 884744 | tf_op jit(solution)/shard_map/ppermute | solution.py:330
  47.2 11.4 %collective-permute-start.15 = (bf16[2,192,384]{2,1,0:T(8,128)(2,1)S(1)}, bf16[2,192,384]{2,1,0:T(8,128)(2,1)S(1)}, u32[]{:S(2)}, u32[]{:S(2)}) collective-permute-start(bf16[2,192,384]{2,1,0:T(8,128)(2,1)S(1)} %get-tuple-element.42), channel_id=1, source_target_pairs={{4,8},{8,4},{5,9},{9,5},{6,10},{10,6},{7,11},{11,7},{20,24},{24,20... | collective-permute-start | bytes 884744 | tf_op jit(solution)/shard_map/ppermute | solution.py:330
  55.1 7.0 %collective-permute-start.11 = (bf16[2,192,384]{2,1,0:T(8,128)(2,1)S(1)}, bf16[2,192,384]{2,1,0:T(8,128)(2,1)S(1)}, u32[]{:S(2)}, u32[]{:S(2)}) collective-permute-start(bf16[2,192,384]{2,1,0:T(8,128)(2,1)S(1)} %get-tuple-element.36), channel_id=1, source_target_pairs={{4,0},{8,12},{5,1},{9,13},{6,2},{10,14},{7,3},{11,15},{20,16},{24,... | collective-permute-start | bytes 884744 | tf_op jit(solution)/shard_map/ppermute | solution.py:330
  56.4 9.2 %collective-permute-start.12 = (bf16[2,192,384]{2,1,0:T(8,128)(2,1)S(1)}, bf16[2,192,384]{2,1,0:T(8,128)(2,1)S(1)}, u32[]{:S(2)}, u32[]{:S(2)}) collective-permute-start(bf16[2,192,384]{2,1,0:T(8,128)(2,1)S(1)} %get-tuple-element.38), channel_id=1, source_target_pairs={{4,8},{8,4},{5,9},{9,5},{6,10},{10,6},{7,11},{11,7},{20,24},{24,20... | collective-permute-start | bytes 884744 | tf_op jit(solution)/shard_map/ppermute | solution.py:330
  60.6 8.5 %collective-permute-start.16 = (bf16[192,384]{1,0:T(8,128)(2,1)S(1)}, bf16[192,384]{1,0:T(8,128)(2,1)S(1)}, u32[]{:S(2)}, u32[]{:S(2)}) collective-permute-start(bf16[192,384]{1,0:T(8,128)(2,1)S(1)} %get-tuple-element.46), channel_id=1, source_target_pairs={{0,2},{2,0},{1,3},{3,1},{4,6},{6,4},{5,7},{7,5},{8,10},{10,8},{9,1... | collective-permute-start | bytes 442376 | tf_op jit(solution)/shard_map/ppermute | solution.py:321
  67.5 5.2 %collective-permute-start.13 = (bf16[192,384]{1,0:T(8,128)(2,1)S(1)}, bf16[192,384]{1,0:T(8,128)(2,1)S(1)}, u32[]{:S(2)}, u32[]{:S(2)}) collective-permute-start(bf16[192,384]{1,0:T(8,128)(2,1)S(1)} %get-tuple-element.40), channel_id=1, source_target_pairs={{0,2},{2,0},{1,3},{3,1},{4,6},{6,4},{5,7},{7,5},{8,10},{10,8},{9,1... | collective-permute-start | bytes 442376 | tf_op jit(solution)/shard_map/ppermute | solution.py:321

commit v6 on v5

--- a/solution.py
+++ b/solution.py
@@ -93,12 +93,12 @@
 ):
     refs = list(refs)
     queries = [refs.pop(0) for unused in range(spaces)]
-    keyvals = [[refs.pop(0) for unused in range(spaces)] for unused in groups]
+    arrays = 1 + max(piece[0] for group in groups for piece in group[2])
+    keyvals = [refs.pop(0) for unused in range(arrays)]
     state_in = None if fresh else (refs.pop(0), refs.pop(0))
     outs = [refs.pop(0) for unused in range(spaces if final else 2)]
     query_ref, key_ref = refs[:2]
     acc_ref, stat_ref = refs[2:] if final else outs
-    query_skips, piece_skips = skips
     tokens = queries[0].shape[0]
     frame_now, space_now = place_ref[0], place_ref[1]
     scale = math.log2(math.e) / math.sqrt(HEAD_DIM)
@@ -108,7 +108,7 @@
         return lax.rem(space_now - offset + spaces, spaces) * row_band
 
     def asked_of(group):
-        slot, hops = group
+        slot, hops = group[:2]
         side = 1 - 2 * lax.rem(frame_now + slot, 2)
         key_frame = frame_now + side * hops
         safe = jnp.clip(key_frame, 0, frames - 1)
@@ -117,32 +117,33 @@
 
     token = lax.broadcasted_iota(jnp.int32, (tokens, HEAD_DIM), 0)
     row = lax.broadcasted_iota(jnp.int32, (tokens, HEAD_DIM), 1)
-    for offset in range(spaces):
-        rows = pl.ds(offset * tokens, tokens)
-        start = (row - first_row(offset)) * columns
+    starts = [(row - first_row(offset)) * columns for offset in range(spaces)]
+    for offset, start in enumerate(starts):
         hit = (token >= start) & (token < start + columns)
         mark = jnp.where(hit, 1.0, 0.0).astype(query_ref.dtype)
         for t in range(together):
-            query_ref[t, rows, HEAD_DIM:] = mark
-        for n, group in enumerate(groups):
-            if group[1] > 0:
-
-                @pl.when(asked_of(group))
-                def _(n=n, group=group, start=start, rows=rows):
-                    reach = widths_ref[group[1]] * columns
+            query_ref[t, pl.ds(offset * tokens, tokens), HEAD_DIM:] = mark
+    for n, group in enumerate(groups):
+        if group[1] > 0:
+
+            @pl.when(asked_of(group))
+            def _(n=n, group=group):
+                reach = widths_ref[group[1]] * columns
+                for m, (unused, unused, offset) in enumerate(group[2]):
+                    start = starts[offset]
                     near = (token >= start - reach) & (token < start + columns + reach)
                     fill = jnp.where(near, 0.0, NEG_FILL).astype(key_ref.dtype)
                     for t in range(together):
-                        key_ref[n, t, rows, HEAD_DIM:] = fill
+                        key_ref[n, t, pl.ds(m * tokens, tokens), HEAD_DIM:] = fill
 
     def attend_heads(turn, carry):
         head = turn * together
         slot_of = (lambda t: t) if final else (lambda t: head + t)
 
-        def lanes(t, skip):
+        def lanes(t, skip=0):
             return pl.ds(pl.multiple_of((head + t) * HEAD_DIM + skip, HEAD_DIM), HEAD_DIM)
 
-        def step(t, scores, n, old):
+        def step(t, scores, pieces, old):
             h = slot_of(t)
             top = jnp.max(scores, axis=0, keepdims=True) * scale
             if old:
@@ -150,10 +151,7 @@
                 top = jnp.maximum(top, before)
             weights = jnp.exp2(scores * scale - top)
             total = jnp.sum(weights, axis=0, keepdims=True)
-            values = jnp.concatenate(
-                [ref[1, :, lanes(t, skip)] for ref, skip in zip(keyvals[n], piece_skips[n])],
-                axis=0,
-            )
+            values = jnp.concatenate([keyvals[i][r + 1, :, lanes(t)] for i, r, o in pieces], axis=0)
             acc = lax.dot_general(
                 values, weights.astype(jnp.bfloat16), TN, preferred_element_type=jnp.float32
             )
@@ -167,7 +165,7 @@
 
         for t in range(together):
             for offset in range(spaces):
-                skip = query_skips[offset] + (own_column if offset == 0 else 0)
+                skip = skips[offset] + (own_column if offset == 0 else 0)
                 query_ref[t, pl.ds(offset * tokens, tokens), :HEAD_DIM] = queries[offset][
                     :, lanes(t, skip)
                 ]
@@ -175,16 +173,12 @@
                 acc_ref[slot_of(t)] = state_in[0][head + t]
                 stat_ref[slot_of(t)] = state_in[1][head + t]
 
-        for n, group in enumerate(groups):
-            if group[1] == 0:
+        for n, (slot, hops, pieces) in enumerate(groups):
+            if hops == 0:
                 scores = []
                 for t in range(together):
                     keys = jnp.concatenate(
-                        [
-                            ref[0, :, lanes(t, skip)]
-                            for ref, skip in zip(keyvals[n], piece_skips[n])
-                        ],
-                        axis=0,
+                        [keyvals[i][r, :, lanes(t)] for i, r, o in pieces], axis=0
                     )
                     scores.append(
                         lax.dot_general(
@@ -193,32 +187,32 @@
                         )
                     )
                 for t in range(together):
-                    step(t, scores[t], n, False)
+                    step(t, scores[t], pieces, False)
                 continue
 
-            @pl.when(asked_of(group))
-            def _(n=n):
+            @pl.when(asked_of(groups[n]))
+            def _(n=n, pieces=pieces):
+                many = pl.ds(0, len(pieces) * tokens)
                 for t in range(together):
-                    for offset in range(spaces):
-                        rows = pl.ds(offset * tokens, tokens)
-                        key_ref[n, t, rows, :HEAD_DIM] = keyvals[n][offset][
-                            0, :, lanes(t, piece_skips[n][offset])
+                    for m, (i, r, unused) in enumerate(pieces):
+                        key_ref[n, t, pl.ds(m * tokens, tokens), :HEAD_DIM] = keyvals[i][
+                            r, :, lanes(t)
                         ]
                 scores = [
                     lax.dot_general(
-                        key_ref[n, t], query_ref[t], NT, preferred_element_type=jnp.float32
+                        key_ref[n, t, many], query_ref[t], NT, preferred_element_type=jnp.float32
                     )
                     for t in range(together)
                 ]
                 for t in range(together):
-                    step(t, scores[t], n, True)
+                    step(t, scores[t], pieces, True)
 
         if final:
             for t in range(together):
                 result = jnp.transpose(acc_ref[t] * (1.0 / stat_ref[t, 1:2, :]))
                 for offset in range(spaces):
                     part = result[offset * tokens : (offset + 1) * tokens]
-                    outs[offset][:, lanes(t, 0)] = part.astype(outs[offset].dtype)
+                    outs[offset][:, lanes(t)] = part.astype(outs[offset].dtype)
         return carry
 
     lax.fori_loop(0, heads // together, attend_heads, 0)
@@ -228,20 +222,19 @@
     spaces, frames, columns, row_band, features = sizes
     first, heads = chunk
     tokens = queries[0].shape[0]
-    width = features // spaces
     count = spaces * tokens
     together = next(n for n in (3, 2, 1) if heads % n == 0)
-
-    def skip_of(x):
-        return first * HEAD_DIM if x.shape[-1] != heads * HEAD_DIM else 0
-
-    skips = (
-        tuple(skip_of(x) for x in queries),
-        tuple(tuple(skip_of(x) for x in pieces) for slot, hops, pieces in groups),
-    )
-    operands = list(queries) + [x for slot, hops, pieces in groups for x in pieces]
-    if state is not None:
-        operands += list(state)
+    arrays, numbered = [], []
+    for slot, hops, pieces in groups:
+        listed = []
+        for array, row, offset in pieces:
+            known = [n for n, x in enumerate(arrays) if x is array]
+            if not known:
+                known = [len(arrays)]
+                arrays.append(array)
+            listed.append((known[0], row, offset))
+        numbered.append((slot, hops, tuple(listed)))
+    operands = list(queries) + arrays + (list(state) if state is not None else [])
     state_shape = [(heads, HEAD_DIM, count), (heads, 8, count)]
     if final:
         out_shape = [jax.ShapeDtypeStruct((tokens, heads * HEAD_DIM), jnp.bfloat16)] * spaces
@@ -253,11 +246,11 @@
     ]
     if final:
         scratch += [pltpu.VMEM((together,) + shape[1:], jnp.float32) for shape in state_shape]
-    pairs = heads * count * count * len(groups)
+    pairs = heads * count * tokens * sum(len(pieces) for slot, hops, pieces in groups)
     return pl.pallas_call(
         functools.partial(
             attend_kernel, spaces, frames, columns, row_band, heads, together,
-            tuple((slot, hops) for slot, hops, pieces in groups), skips, state is None, final,
+            tuple(numbered), (first * HEAD_DIM,) * spaces, state is None, final,
         ),
         in_specs=[pl.BlockSpec(memory_space=pltpu.SMEM)] * 3
         + [pl.BlockSpec(memory_space=pltpu.VMEM)] * len(operands),
@@ -267,11 +260,29 @@
         compiler_params=pltpu.CompilerParams(vmem_limit_bytes=VMEM_LIMIT),
         cost_estimate=pl.CostEstimate(
             flops=4 * pairs * HEAD_DIM,
-            bytes_accessed=len(groups) * 4 * count * heads * HEAD_DIM,
+            bytes_accessed=8 * count * heads * HEAD_DIM,
             transcendentals=pairs,
         ),
         name="attend_final" if final else "attend",
     )(*scalars, *operands)
+
+
+def join_kernel(parts, *refs):
+    for n, rows in enumerate(parts):
+        refs[-1][pl.ds(sum(parts[:n]), rows)] = refs[n][...]
+
+
+def join(arrays):
+    parts = tuple(x.shape[0] for x in arrays)
+    shape = (sum(parts),) + arrays[0].shape[1:]
+    return pl.pallas_call(
+        functools.partial(join_kernel, parts),
+        in_specs=[pl.BlockSpec(memory_space=pltpu.VMEM)] * len(arrays),
+        out_specs=pl.BlockSpec(memory_space=pltpu.VMEM),
+        out_shape=jax.ShapeDtypeStruct(shape, arrays[0].dtype),
+        compiler_params=pltpu.CompilerParams(vmem_limit_bytes=SMALL_LIMIT),
+        name="join",
+    )(*arrays)
 
 
 def put_kernel(spaces, places, kept, place_ref, *refs):
@@ -320,20 +331,25 @@
     def along_space(x, offset):
         return lax.ppermute(x, "space", [(s, (s + offset) % spaces) for s in range(spaces)])
 
-    def swap(x, slot, hops):
+    def swap(x, slot):
         pairs = []
         for f in range(frames):
             side = 1 if (f + slot) % 2 == 0 else -1
-            source = f - side * (hops - 1)
-            if 0 <= f + side < frames and 0 <= source < frames:
+            if 0 <= f + side < frames:
                 pairs.append((f, f + side))
         return lax.ppermute(x, "frame", pairs)
 
-    partners, arrived = [], []
+    def swap_both(xs):
+        second = swap(xs[1], 1)
+        return [swap(xs[0], 0), second]
+
+    own, partners, arrived = [], [], []
     for c, (first, number) in enumerate(chunks):
         blocks = [(offset, first * HEAD_DIM, number * HEAD_DIM) for offset in offsets]
         if c == 0:
-            mine, *sends = pack((k, v), [(0, 0, width)] + blocks, (), spaces, True)
+            mine = [(0, f * HEAD_DIM, n * HEAD_DIM) for f, n in chunks]
+            packed = pack((k, v), blocks + mine, (), spaces, True)
+            sends, own = packed[: len(blocks)], packed[len(blocks) :]
         else:
             sends = pack((k, v), blocks, arrived, spaces, False)
         arrived = [along_space(x, offset) for x, offset in zip(sends, offsets)]
@@ -341,56 +357,58 @@
     sends = pack((q,), [(offset, 0, width) for offset in offsets], arrived, spaces, False)
     query_parts = [q] + [along_space(x, offset) for x, offset in zip(sends, offsets)]
 
-    def tied(lists, after):
-        flat = list(tie([x for xs in lists for x in xs], after))
-        return [[flat.pop(0) for unused in xs] for xs in lists]
-
-    states = [None] * len(chunks)
-    own_now = [[mine], [mine]]
-    own_next = [[swap(x, slot, 1) for x in own_now[slot]] for slot in range(2)]
-    first_next = [[swap(x, slot, 1) for x in partners[0]] for slot in range(2)]
-    *first_next, partners[1] = tied(first_next + [partners[1]], sends)
-    second_next = [[swap(x, slot, 1) for x in partners[1]] for slot in range(2)]
-    groups = [[(0, 0, [mine] + xs)] for xs in partners]
-    for hops in range(1, frames - 1):
-        if hops > 1:
-            own_now, first_now, second_now = own_next, first_next, second_next
-            own_next = early
-            lists = tied(first_now + second_now, [states[0][1]])
-            first_now, second_now = lists[:2], lists[2:]
-            first_next = [[swap(x, slot, hops) for x in first_now[1 - slot]] for slot in range(2)]
-            groups[1] = [
-                (slot, hops - 1, own_now[slot] + second_now[slot]) for slot in range(2)
-            ]
-            if hops == 2:
-                groups[1].insert(0, (0, 0, [mine] + partners[1]))
-            states[1] = attend(
-                scalars, query_parts, groups[1], states[1], False, chunks[1], sizes
-            )
-            lists = tied(second_now + own_next, [states[1][1]])
-            second_now, own_next = lists[:2], lists[2:]
-            second_next = [
-                [swap(x, slot, hops) for x in second_now[1 - slot]] for slot in range(2)
-            ]
-        if hops < frames - 2:
-            early = [[swap(x, slot, hops + 1) for x in own_next[1 - slot]] for slot in range(2)]
-            if hops > 1:
-                groups[0] = []
-            groups[0] += [(slot, hops, own_next[slot] + first_next[slot]) for slot in range(2)]
-            states[0] = attend(
-                scalars, query_parts, groups[0], states[0], False, chunks[0], sizes
-            )
     last = frames - 2
-    finals = [
-        [(slot, last, own_next[slot] + xs[slot]) for slot in range(2)]
-        for xs in (first_next, second_next)
-    ]
-    if last == 1:
-        finals = [own + final for own, final in zip(groups, finals)]
+    behind = 2 * len(offsets)
+
+    def own_band(message, hops):
+        return [(slot, hops, [(x, x.shape[0] - 2, 0)]) for slot, x in enumerate(message)]
+
+    def partner_bands(message, hops):
+        return [
+            (slot, hops, [(x, 2 * (o - 1), o) for o in offsets]) for slot, x in enumerate(message)
+        ]
+
+    firsts = [swap_both([x, x]) for x in own]
+    seconds = []
+    for c in range(len(chunks)):
+        ready = [join(partners[c] + [firsts[c][1 - slot]]) for slot in range(2)]
+        seconds.append(swap_both(ready))
+    messages, states, ends = seconds, [None] * len(chunks), [None] * len(chunks)
+    for hops in range(2, frames):
+        following = []
+        for c, chunk in enumerate(chunks):
+            came = messages[c]
+            if c > 0:
+                came = list(tie(came, [states[c - 1][1]]))
+            if hops == last:
+                sent = [came[1 - slot][:behind] for slot in range(2)]
+            else:
+                sent = [came[1 - slot] for slot in range(2)]
+            if hops <= last:
+                following.append(swap_both(sent))
+                groups = [
+                    (slot, hops - 1, a + b)
+                    for (slot, unused, a), (unused, unused, b) in zip(
+                        own_band(firsts[c], 1), partner_bands(came, 1)
+                    )
+                ]
+                if hops == 2:
+                    own_frame = [(own[c], 0, 0)]
+                    own_frame += [(x, 0, o) for x, o in zip(partners[c], offsets)]
+                    groups.insert(0, (0, 0, own_frame))
+                else:
+                    groups = partner_bands(came, hops - 1)
+                groups += own_band(came, hops)
+                states[c] = attend(
+                    scalars, query_parts, groups, states[c], False, chunk, sizes
+                )
+            else:
+                ends[c] = partner_bands(came, last)
+        messages = following
 
     own, returned = [], []
     for c, chunk in enumerate(chunks):
-        kept, *parts = attend(scalars, query_parts, finals[c], states[c], True, chunk, sizes)
+        kept, *parts = attend(scalars, query_parts, ends[c], states[c], True, chunk, sizes)
         own.append((kept, (0, chunk[0] * HEAD_DIM)))
         for offset, x in zip(offsets, parts):
             returned.append((along_space(x, -offset), (offset, chunk[0] * HEAD_DIM)))

time: 74.4 us -> 71.2 us (0.957)
  the two profiles are of different devices: /device:TPU:8 before, /device:TPU:0 now
where the time goes in v6:
time: 71.2 us; the launch traced here: 70.6 us
  starting transfers between devices  38.3 us (54%)
  Pallas kernels  18.8 us (26%)
  waiting for transfers between devices  9.8 us (14%)
  local copies, waits for them, and re-layouts  3.4 us (5%)
    ppermute x12, starting transfers between devices, swap(): return lax.ppermute(x, 'frame', pairs)  30.7 us
    pallas_call x4, Pallas kernels, attend(): pl.pallas_call(functools.partial(attend_kernel, spaces, frames, columns,...  10.3 us
    ppermute x5, starting transfers between devices, along_space(): lax.ppermute(x, 'space', [(s, (s + offset) % spaces) for s in range(space...  7.57 us
    ppermute x12, waiting for transfers between devices, swap(): return lax.ppermute(x, 'frame', pairs)  6.98 us
    pallas_call x3, Pallas kernels, pack(): pl.pallas_call(functools.partial(pack_kernel, spaces, tuple(jobs), staged...  3.25 us
    ppermute x5, waiting for transfers between devices, along_space(): lax.ppermute(x, 'space', [(s, (s + offset) % spaces) for s in range(space...  2.83 us
    pallas_call x4, Pallas kernels, join(): pl.pallas_call(functools.partial(join_kernel, parts), in_specs=[pl.BlockS...  2.75 us
    pallas_call x2, Pallas kernels, put(): pl.pallas_call(functools.partial(put_kernel, spaces, tuple(places), len(k...  2.55 us
  transfers between devices with their start and end apart: 17, of which 5 were waited for; matrix products, arithmetic and copies ran while one was open for 3% of the time, Pallas kernels for 22%

profile of v6, /device:TPU:0, one launch (start us, length us, event | category | flops | bytes accessed | tf_op | source)
XLA Modules:
  0.0 70.6 jit_solution(15200801055671798548)
XLA Ops:
  0.0 2.3 %pack.3 = (bf16[2,192,384]{2,1,0:T(8,128)(2,1)}, bf16[2,192,384]{2,1,0:T(8,128)(2,1)}, bf16[2,192,384]{2,1,0:T(8,128)(2,1)}) custom-call(bf16[192,1536]{1,0:T(8,128)(2,1)} %bitcast.11, bf16[192,1536]{1,0:T(8,128)(2,1)} %bitcast.13), custom_call_target="tpu_custom_call" | custom-call | tf_op jit(solution)/shard_map/pack/pallas_call | solution.py:64
  2.3 3.0 %collective-permute-start = (bf16[2,192,384]{2,1,0:T(8,128)(2,1)}, bf16[2,192,384]{2,1,0:T(8,128)(2,1)S(1)}, u32[]{:S(2)}, u32[]{:S(2)}) collective-permute-start(bf16[2,192,384]{2,1,0:T(8,128)(2,1)} %get-tuple-element.20), channel_id=1, source_target_pairs={{0,2},{2,0},{1,3},{3,1},{4,6},{6,4},{5,7},{7,5},{8,10},{10,8},{9,1... | collective-permute-start | bytes 884744 | tf_op jit(solution)/shard_map/ppermute | solution.py:332
  5.3 1.6 %collective-permute-start.7 = (bf16[2,192,384]{2,1,0:T(8,128)(2,1)}, bf16[2,192,384]{2,1,0:T(8,128)(2,1)S(1)}, u32[]{:S(2)}, u32[]{:S(2)}) collective-permute-start(bf16[2,192,384]{2,1,0:T(8,128)(2,1)} %get-tuple-element.22.refs_2_), channel_id=1, source_target_pairs={{0,4},{4,0},{8,12},{12,8},{1,5},{5,1},{9,13},{13,9},{2,6},{6,2},{1... | collective-permute-start | bytes 884744 | tf_op jit(solution)/shard_map/ppermute | solution.py:340
  6.9 0.7 collective-permute-start.8
  7.5 0.0 copy-start.11
  7.5 4.4 %collective-permute-start.5 = (bf16[2,192,384]{2,1,0:T(8,128)(2,1)}, bf16[2,192,384]{2,1,0:T(8,128)(2,1)S(1)}, u32[]{:S(2)}, u32[]{:S(2)}) collective-permute-start(bf16[2,192,384]{2,1,0:T(8,128)(2,1)} %get-tuple-element.21.refs_2_), channel_id=1, source_target_pairs={{0,4},{4,0},{8,12},{12,8},{1,5},{5,1},{9,13},{13,9},{2,6},{6,2},{1... | collective-permute-start | bytes 884744 | tf_op jit(solution)/shard_map/ppermute | solution.py:340
  12.0 0.5 collective-permute-done.refs_2_.refs_0_.refs_3_
  12.5 0.0 copy-done.1
  12.5 0.0 copy-done.2
  12.5 0.2 pack.4
  12.7 1.8 %collective-permute-start.1 = (bf16[2,192,384]{2,1,0:T(8,128)(2,1)S(1)}, bf16[2,192,384]{2,1,0:T(8,128)(2,1)S(1)}, u32[]{:S(2)}, u32[]{:S(2)}) collective-permute-start(bf16[2,192,384]{2,1,0:T(8,128)(2,1)S(1)} %pack.4), channel_id=1, source_target_pairs={{0,2},{2,0},{1,3},{3,1},{4,6},{6,4},{5,7},{7,5},{8,10},{10,8},{9,1... | collective-permute-start | bytes 884744 | tf_op jit(solution)/shard_map/ppermute | solution.py:332
  14.5 0.0 copy-done.11
  14.5 0.7 collective-permute-start.3
  15.2 0.2 collective-permute-done.7.refs_1_.refs_4_
  15.4 0.9 %join.7 = bf16[4,192,384]{2,1,0:T(8,128)(2,1)} custom-call(bf16[2,192,384]{2,1,0:T(8,128)(2,1)S(1)} %collective-permute-done.refs_2_.refs_0_.refs_3_, bf16[2,192,384]{2,1,0:T(8,128)(2,1)S(1)} %collective-permute-done.7.refs_1_.refs_4_), custom_call_target="tpu_custom_call" | custom-call | tf_op jit(solution)/shard_map/join/pallas_call | solution.py:278
  16.4 0.0 copy-done.5
  16.4 1.5 %collective-permute-start.10 = (bf16[4,192,384]{2,1,0:T(8,128)(2,1)}, bf16[4,192,384]{2,1,0:T(8,128)(2,1)}, u32[]{:S(2)}, u32[]{:S(2)}) collective-permute-start(bf16[4,192,384]{2,1,0:T(8,128)(2,1)} %join.7), channel_id=1, source_target_pairs={{4,8},{8,4},{5,9},{9,5},{6,10},{10,6},{7,11},{11,7},{20,24},{24,20... | collective-permute-start | bytes 1769480 | tf_op jit(solution)/shard_map/ppermute | solution.py:340
  17.8 0.0 collective-permute-done.8.refs_1_.refs_6_
  17.8 0.9 %join.6 = bf16[4,192,384]{2,1,0:T(8,128)(2,1)} custom-call(bf16[2,192,384]{2,1,0:T(8,128)(2,1)S(1)} %collective-permute-done.refs_2_.refs_0_.refs_3_, bf16[2,192,384]{2,1,0:T(8,128)(2,1)S(1)} %collective-permute-done.8.refs_1_.refs_6_), custom_call_target="tpu_custom_call" | custom-call | tf_op jit(solution)/shard_map/join/pallas_call | solution.py:278
  18.7 0.0 copy-done.7
  18.7 5.0 %collective-permute-start.9 = (bf16[4,192,384]{2,1,0:T(8,128)(2,1)}, bf16[4,192,384]{2,1,0:T(8,128)(2,1)}, u32[]{:S(2)}, u32[]{:S(2)}) collective-permute-start(bf16[4,192,384]{2,1,0:T(8,128)(2,1)} %join.6), channel_id=1, source_target_pairs={{0,4},{4,0},{8,12},{12,8},{1,5},{5,1},{9,13},{13,9},{2,6},{6,2},{1... | collective-permute-start | bytes 1769480 | tf_op jit(solution)/shard_map/ppermute | solution.py:340
  23.8 0.0 collective-permute-done.5.refs_1_.refs_4_
  23.8 0.0 collective-permute-done.1.refs_1_.refs_0_.refs_3_
  23.8 0.1 join.5
  23.8 0.0 copy-start
  23.9 0.8 %collective-permute-start.6 = (bf16[4,192,384]{2,1,0:T(8,128)(2,1)S(1)}, bf16[4,192,384]{2,1,0:T(8,128)(2,1)S(1)}, u32[]{:S(2)}, u32[]{:S(2)}) collective-permute-start(bf16[4,192,384]{2,1,0:T(8,128)(2,1)S(1)} %join.5), channel_id=1, source_target_pairs={{4,8},{8,4},{5,9},{9,5},{6,10},{10,6},{7,11},{11,7},{20,24},{24,20... | collective-permute-start | bytes 1769480 | tf_op jit(solution)/shard_map/ppermute | solution.py:340
  24.7 0.0 collective-permute-done.3.refs_1_.refs_6_
  24.7 0.9 %join.4 = bf16[4,192,384]{2,1,0:T(8,128)(2,1)} custom-call(bf16[2,192,384]{2,1,0:T(8,128)(2,1)S(1)} %collective-permute-done.1.refs_1_.refs_0_.refs_3_, bf16[2,192,384]{2,1,0:T(8,128)(2,1)S(1)} %collective-permute-done.3.refs_1_.refs_6_), custom_call_target="tpu_custom_call" | custom-call | tf_op jit(solution)/shard_map/join/pallas_call | solution.py:278
  25.6 0.7 copy-done.3
  26.3 2.8 %collective-permute-start.4 = (bf16[4,192,384]{2,1,0:T(8,128)(2,1)}, bf16[4,192,384]{2,1,0:T(8,128)(2,1)S(1)}, u32[]{:S(2)}, u32[]{:S(2)}) collective-permute-start(bf16[4,192,384]{2,1,0:T(8,128)(2,1)} %join.4), channel_id=1, source_target_pairs={{0,4},{4,0},{8,12},{12,8},{1,5},{5,1},{9,13},{13,9},{2,6},{6,2},{1... | collective-permute-start | bytes 1769480 | tf_op jit(solution)/shard_map/ppermute | solution.py:340
  29.1 0.0 copy-done
  29.1 0.8 %pack.5 = bf16[192,768]{1,0:T(8,128)(2,1)} custom-call(bf16[192,1536]{1,0:T(8,128)(2,1)S(1)} %bitcast.6, bf16[2,192,384]{2,1,0:T(8,128)(2,1)S(1)} %collective-permute-done.1.refs_1_.refs_0_.refs_3_), custom_call_target="tpu_custom_call" | custom-call | tf_op jit(solution)/shard_map/pack/pallas_call | solution.py:64
  29.9 0.6 collective-permute-start.2
  30.5 0.0 collective-permute-done.10.refs_7_
  30.5 1.0 %slice.16 = bf16[2,192,384]{2,1,0:T(8,128)(2,1)S(1)} slice(bf16[4,192,384]{2,1,0:T(8,128)(2,1)} %collective-permute-done.10.refs_7_), slice={[0:2], [0:192], [0:384]} | slice | bytes 589824 | tf_op jit(solution)/shard_map/slice | solution.py:384
  31.5 0.0 copy-start.6
  31.6 9.8 %collective-permute-start.14 = (bf16[2,192,384]{2,1,0:T(8,128)(2,1)S(1)}, bf16[2,192,384]{2,1,0:T(8,128)(2,1)S(1)}, u32[]{:S(2)}, u32[]{:S(2)}) collective-permute-start(bf16[2,192,384]{2,1,0:T(8,128)(2,1)S(1)} %slice.16), channel_id=1, source_target_pairs={{0,4},{4,0},{8,12},{12,8},{1,5},{5,1},{9,13},{13,9},{2,6},{6,2},{1... | collective-permute-start | bytes 884744 | tf_op jit(solution)/shard_map/ppermute | solution.py:340
  41.3 0.0 collective-permute-done.9.refs_5_
  41.3 1.0 %slice.17 = bf16[2,192,384]{2,1,0:T(8,128)(2,1)S(1)} slice(bf16[4,192,384]{2,1,0:T(8,128)(2,1)} %collective-permute-done.9.refs_5_), slice={[0:2], [0:192], [0:384]} | slice | bytes 589824 | tf_op jit(solution)/shard_map/slice | solution.py:384
  42.3 0.7 collective-permute-start.15
  43.0 0.0 copy-start.9
  43.0 0.0 copy-start.10
  43.0 0.1 pad_add_fusion.place_ref
  43.1 0.0 collective-permute-done.2.refs_1_
  43.1 0.0 copy-done.6
  43.1 0.6 copy-done.9
  43.7 3.9 %attend.2 = (f32[3,128,384]{2,1,0:T(8,128)S(1)}, f32[3,8,384]{2,1,0:T(8,128)S(1)}) custom-call(s32[2]{0:T(128)S(1)} %pad_add_fusion.place_ref, s32[4,4]{1,0:T(4,128)S(1)} %copy-done.9, s32[4]{0:T(128)S(1)} %copy-done.10, bf16[192,1536]{1,0:T(8,128)(2,1)S(1)} %bitcast.7, bf16[192,768]{1,0:T(8,128)(2,1)S(1)} %collective-permute-done.2.refs_1_, ...), custom_call_target="tpu_custom_call" | custom-call | flops 905969664 | bytes 1179648 | tf_op jit(solution)/shard_map/attend/pallas_call | solution.py:250
  47.6 0.0 collective-permute-done.6.refs_1_
  47.6 3.2 %collective-permute-done.4.refs_0_ = bf16[4,192,384]{2,1,0:T(8,128)(2,1)S(1)} collective-permute-done((bf16[4,192,384]{2,1,0:T(8,128)(2,1)}, bf16[4,192,384]{2,1,0:T(8,128)(2,1)S(1)}, u32[]{:S(2)}, u32[]{:S(2)}) %collective-permute-start.4) | collective-permute-done | bytes 589856 | tf_op jit(solution)/shard_map/ppermute | solution.py:340
  50.9 2.1 %collective-permute-start.11 = (bf16[2,192,384]{2,1,0:T(8,128)(2,1)S(1)}, bf16[2,192,384]{2,1,0:T(8,128)(2,1)S(1)}, u32[]{:S(2)}, u32[]{:S(2)}) collective-permute-start(bf16[2,192,384]{2,1,0:T(8,128)(2,1)S(1)} %slice.12), channel_id=1, source_target_pairs={{0,4},{4,0},{8,12},{12,8},{1,5},{5,1},{9,13},{13,9},{2,6},{6,2},{1... | collective-permute-start | bytes 884744 | tf_op jit(solution)/shard_map/ppermute | solution.py:340
  53.0 0.7 collective-permute-start.12
  53.7 3.5 %collective-permute-done.14.refs_2_ = bf16[2,192,384]{2,1,0:T(8,128)(2,1)S(1)} collective-permute-done((bf16[2,192,384]{2,1,0:T(8,128)(2,1)S(1)}, bf16[2,192,384]{2,1,0:T(8,128)(2,1)S(1)}, u32[]{:S(2)}, u32[]{:S(2)}) %collective-permute-start.14) | collective-permute-done | bytes 294944 | tf_op jit(solution)/shard_map/ppermute | solution.py:340
  57.2 0.0 collective-permute-done.15.refs_3_
  57.2 1.6 %attend_final.3 = (bf16[192,384]{1,0:T(8,128)(2,1)S(1)}, bf16[192,384]{1,0:T(8,128)(2,1)S(1)}) custom-call(s32[2]{0:T(128)S(1)} %pad_add_fusion.place_ref, s32[4,4]{1,0:T(4,128)S(1)} %copy-done.9, s32[4]{0:T(128)S(1)} %copy-done.10, bf16[192,1536]{1,0:T(8,128)(2,1)S(1)} %bitcast.8, bf16[192,768]{1,0:T(8,128)(2,1)S(1)} %collective-permute-done.2.refs_1_, ...), custom_call_target="tpu_custom_call" | custom-call | flops 226492416 | bytes 1179648 | tf_op jit(solution)/shard_map/attend_final/pallas_call | solution.py:250
  58.8 0.6 collective-permute-start.16
  59.4 3.2 %attend.3 = (f32[3,128,384]{2,1,0:T(8,128)S(1)}, f32[3,8,384]{2,1,0:T(8,128)S(1)}) custom-call(s32[2]{0:T(128)S(1)} %pad_add_fusion.place_ref, s32[4,4]{1,0:T(4,128)S(1)} %copy-done.9, s32[4]{0:T(128)S(1)} %copy-done.10, bf16[192,1536]{1,0:T(8,128)(2,1)S(1)} %bitcast.9, bf16[192,768]{1,0:T(8,128)(2,1)S(1)} %collective-permute-done.2.refs_1_, ...), custom_call_target="tpu_custom_call" | custom-call | flops 905969664 | bytes 1179648 | tf_op jit(solution)/shard_map/attend/pallas_call | solution.py:250
  62.6 0.0 collective-permute-done.11.refs_0_
  62.6 0.0 collective-permute-done.12.refs_1_
  62.7 1.6 %attend_final.2 = (bf16[192,384]{1,0:T(8,128)(2,1)S(1)}, bf16[192,384]{1,0:T(8,128)(2,1)S(1)}) custom-call(s32[2]{0:T(128)S(1)} %pad_add_fusion.place_ref, s32[4,4]{1,0:T(4,128)S(1)} %copy-done.9, s32[4]{0:T(128)S(1)} %copy-done.10, bf16[192,1536]{1,0:T(8,128)(2,1)S(1)} %bitcast.10, bf16[192,768]{1,0:T(8,128)(2,1)S(1)} %collective-permute-done.2.refs_1_, ...), custom_call_target="tpu_custom_call" | custom-call | flops 226492416 | bytes 1179648 | tf_op jit(solution)/shard_map/attend_final/pallas_call | solution.py:250
  64.2 1.6 %collective-permute-start.13 = (bf16[192,384]{1,0:T(8,128)(2,1)S(1)}, bf16[192,384]{1,0:T(8,128)(2,1)S(1)}, u32[]{:S(2)}, u32[]{:S(2)}) collective-permute-start(bf16[192,384]{1,0:T(8,128)(2,1)S(1)} %get-tuple-element.30), channel_id=1, source_target_pairs={{0,2},{2,0},{1,3},{3,1},{4,6},{6,4},{5,7},{7,5},{8,10},{10,8},{9,1... | collective-permute-start | bytes 442376 | tf_op jit(solution)/shard_map/ppermute | solution.py:332
  65.8 0.0 collective-permute-done.16.refs_2_
  65.8 1.3 %put.2.refs_1_ = bf16[192,1536]{1,0:T(8,128)(2,1)} custom-call(s32[2]{0:T(128)S(1)} %pad_add_fusion.place_ref, bf16[192,384]{1,0:T(8,128)(2,1)S(1)} %get-tuple-element.32.refs_0_, bf16[192,384]{1,0:T(8,128)(2,1)S(1)} %get-tuple-element.33.refs_1_, bf16[192,384]{1,0:T(8,128)(2,1)S(1)} %collective-permute-done.16.refs_2_), custom_call_target="tpu_custom_call" | custom-call | tf_op jit(solution)/shard_map/put/pallas_call | solution.py:304
  67.1 2.3 %collective-permute-done.13.refs_0_ = bf16[192,384]{1,0:T(8,128)(2,1)S(1)} collective-permute-done((bf16[192,384]{1,0:T(8,128)(2,1)S(1)}, bf16[192,384]{1,0:T(8,128)(2,1)S(1)}, u32[]{:S(2)}, u32[]{:S(2)}) %collective-permute-start.13) | collective-permute-done | bytes 147488 | tf_op jit(solution)/shard_map/ppermute | solution.py:332
  69.4 1.2 %put.3 = bf16[192,1536]{1,0:T(8,128)(2,1)} custom-call(s32[2]{0:T(128)S(1)} %pad_add_fusion.place_ref, bf16[192,384]{1,0:T(8,128)(2,1)S(1)} %collective-permute-done.13.refs_0_, bf16[192,1536]{1,0:T(8,128)(2,1)} %put.2.refs_1_), custom_call_target="tpu_custom_call", output_to_operand_aliasing={{}: (2, {})} | custom-call | tf_op jit(solution)/shard_map/put/pallas_call | solution.py:304
  (18 shorter events, 0.1 us)
Async XLA Ops:
  0.0 12.5 %copy-start.1 = (bf16[1,4,48,1536]{3,2,1,0:T(8,128)(2,1)S(1)}, bf16[1,4,48,1536]{3,2,1,0:T(8,128)(2,1)}, u32[]{:S(2)}) copy-start(bf16[1,4,48,1536]{3,2,1,0:T(8,128)(2,1)} %param.6) | copy-start | bytes 1769476
  0.0 12.5 %copy-start.2 = (bf16[1,4,48,1536]{3,2,1,0:T(8,128)(2,1)S(1)}, bf16[1,4,48,1536]{3,2,1,0:T(8,128)(2,1)}, u32[]{:S(2)}) copy-start(bf16[1,4,48,1536]{3,2,1,0:T(8,128)(2,1)} %param.7) | copy-start | bytes 1769476
  2.3 10.2 %collective-permute-start = (bf16[2,192,384]{2,1,0:T(8,128)(2,1)}, bf16[2,192,384]{2,1,0:T(8,128)(2,1)S(1)}, u32[]{:S(2)}, u32[]{:S(2)}) collective-permute-start(bf16[2,192,384]{2,1,0:T(8,128)(2,1)} %get-tuple-element.20), channel_id=1, source_target_pairs={{0,2},{2,0},{1,3},{3,1},{4,6},{6,4},{5,7},{7,5},{8,10},{10,8},{9,1... | collective-permute-start | bytes 884744 | tf_op jit(solution)/shard_map/ppermute | solution.py:332
  5.3 10.1 %collective-permute-start.7 = (bf16[2,192,384]{2,1,0:T(8,128)(2,1)}, bf16[2,192,384]{2,1,0:T(8,128)(2,1)S(1)}, u32[]{:S(2)}, u32[]{:S(2)}) collective-permute-start(bf16[2,192,384]{2,1,0:T(8,128)(2,1)} %get-tuple-element.22.refs_2_), channel_id=1, source_target_pairs={{0,4},{4,0},{8,12},{12,8},{1,5},{5,1},{9,13},{13,9},{2,6},{6,2},{1... | collective-permute-start | bytes 884744 | tf_op jit(solution)/shard_map/ppermute | solution.py:340
  6.9 11.0 %collective-permute-start.8 = (bf16[2,192,384]{2,1,0:T(8,128)(2,1)}, bf16[2,192,384]{2,1,0:T(8,128)(2,1)S(1)}, u32[]{:S(2)}, u32[]{:S(2)}) collective-permute-start(bf16[2,192,384]{2,1,0:T(8,128)(2,1)} %get-tuple-element.22.refs_2_), channel_id=1, source_target_pairs={{4,8},{8,4},{5,9},{9,5},{6,10},{10,6},{7,11},{11,7},{20,24},{24,20... | collective-permute-start | bytes 884744 | tf_op jit(solution)/shard_map/ppermute | solution.py:340
  7.5 7.0 %copy-start.11 = (bf16[2,192,384]{2,1,0:T(8,128)(2,1)S(1)}, bf16[2,192,384]{2,1,0:T(8,128)(2,1)}, u32[]{:S(2)}) copy-start(bf16[2,192,384]{2,1,0:T(8,128)(2,1)} %get-tuple-element.21.refs_2_) | copy-start | bytes 884740
  7.5 16.2 %collective-permute-start.5 = (bf16[2,192,384]{2,1,0:T(8,128)(2,1)}, bf16[2,192,384]{2,1,0:T(8,128)(2,1)S(1)}, u32[]{:S(2)}, u32[]{:S(2)}) collective-permute-start(bf16[2,192,384]{2,1,0:T(8,128)(2,1)} %get-tuple-element.21.refs_2_), channel_id=1, source_target_pairs={{0,4},{4,0},{8,12},{12,8},{1,5},{5,1},{9,13},{13,9},{2,6},{6,2},{1... | collective-permute-start | bytes 884744 | tf_op jit(solution)/shard_map/ppermute | solution.py:340
  12.7 11.1 %collective-permute-start.1 = (bf16[2,192,384]{2,1,0:T(8,128)(2,1)S(1)}, bf16[2,192,384]{2,1,0:T(8,128)(2,1)S(1)}, u32[]{:S(2)}, u32[]{:S(2)}) collective-permute-start(bf16[2,192,384]{2,1,0:T(8,128)(2,1)S(1)} %pack.4), channel_id=1, source_target_pairs={{0,2},{2,0},{1,3},{3,1},{4,6},{6,4},{5,7},{7,5},{8,10},{10,8},{9,1... | collective-permute-start | bytes 884744 | tf_op jit(solution)/shard_map/ppermute | solution.py:332
  14.5 10.2 %collective-permute-start.3 = (bf16[2,192,384]{2,1,0:T(8,128)(2,1)S(1)}, bf16[2,192,384]{2,1,0:T(8,128)(2,1)S(1)}, u32[]{:S(2)}, u32[]{:S(2)}) collective-permute-start(bf16[2,192,384]{2,1,0:T(8,128)(2,1)S(1)} %copy-done.11), channel_id=1, source_target_pairs={{4,8},{8,4},{5,9},{9,5},{6,10},{10,6},{7,11},{11,7},{20,24},{24,20... | collective-permute-start | bytes 884744 | tf_op jit(solution)/shard_map/ppermute | solution.py:340
  15.4 0.9 %copy-start.5 = (bf16[2,192,384]{2,1,0:T(8,128)(2,1)}, bf16[2,192,384]{2,1,0:T(8,128)(2,1)S(1)}, u32[]{:S(2)}) copy-start(bf16[2,192,384]{2,1,0:T(8,128)(2,1)S(1)} %collective-permute-done.7.refs_1_.refs_4_) | copy-start | bytes 884740
  16.4 14.1 %collective-permute-start.10 = (bf16[4,192,384]{2,1,0:T(8,128)(2,1)}, bf16[4,192,384]{2,1,0:T(8,128)(2,1)}, u32[]{:S(2)}, u32[]{:S(2)}) collective-permute-start(bf16[4,192,384]{2,1,0:T(8,128)(2,1)} %join.7), channel_id=1, source_target_pairs={{4,8},{8,4},{5,9},{9,5},{6,10},{10,6},{7,11},{11,7},{20,24},{24,20... | collective-permute-start | bytes 1769480 | tf_op jit(solution)/shard_map/ppermute | solution.py:340
  17.8 0.9 %copy-start.7 = (bf16[2,192,384]{2,1,0:T(8,128)(2,1)}, bf16[2,192,384]{2,1,0:T(8,128)(2,1)S(1)}, u32[]{:S(2)}) copy-start(bf16[2,192,384]{2,1,0:T(8,128)(2,1)S(1)} %collective-permute-done.8.refs_1_.refs_6_) | copy-start | bytes 884740
  18.7 22.6 %collective-permute-start.9 = (bf16[4,192,384]{2,1,0:T(8,128)(2,1)}, bf16[4,192,384]{2,1,0:T(8,128)(2,1)}, u32[]{:S(2)}, u32[]{:S(2)}) collective-permute-start(bf16[4,192,384]{2,1,0:T(8,128)(2,1)} %join.6), channel_id=1, source_target_pairs={{0,4},{4,0},{8,12},{12,8},{1,5},{5,1},{9,13},{13,9},{2,6},{6,2},{1... | collective-permute-start | bytes 1769480 | tf_op jit(solution)/shard_map/ppermute | solution.py:340
  23.8 5.2 %copy-start = (bf16[1,4,48,1536]{3,2,1,0:T(8,128)(2,1)S(1)}, bf16[1,4,48,1536]{3,2,1,0:T(8,128)(2,1)}, u32[]{:S(2)}) copy-start(bf16[1,4,48,1536]{3,2,1,0:T(8,128)(2,1)} %param.5) | copy-start | bytes 1769476
  23.9 23.8 %collective-permute-start.6 = (bf16[4,192,384]{2,1,0:T(8,128)(2,1)S(1)}, bf16[4,192,384]{2,1,0:T(8,128)(2,1)S(1)}, u32[]{:S(2)}, u32[]{:S(2)}) collective-permute-start(bf16[4,192,384]{2,1,0:T(8,128)(2,1)S(1)} %join.5), channel_id=1, source_target_pairs={{4,8},{8,4},{5,9},{9,5},{6,10},{10,6},{7,11},{11,7},{20,24},{24,20... | collective-permute-start | bytes 1769480 | tf_op jit(solution)/shard_map/ppermute | solution.py:340
  25.6 0.7 copy-start.3
  26.3 24.6 %collective-permute-start.4 = (bf16[4,192,384]{2,1,0:T(8,128)(2,1)}, bf16[4,192,384]{2,1,0:T(8,128)(2,1)S(1)}, u32[]{:S(2)}, u32[]{:S(2)}) collective-permute-start(bf16[4,192,384]{2,1,0:T(8,128)(2,1)} %join.4), channel_id=1, source_target_pairs={{0,4},{4,0},{8,12},{12,8},{1,5},{5,1},{9,13},{13,9},{2,6},{6,2},{1... | collective-permute-start | bytes 1769480 | tf_op jit(solution)/shard_map/ppermute | solution.py:340
  29.9 13.2 %collective-permute-start.2 = (bf16[192,768]{1,0:T(8,128)(2,1)}, bf16[192,768]{1,0:T(8,128)(2,1)S(1)}, u32[]{:S(2)}, u32[]{:S(2)}) collective-permute-start(bf16[192,768]{1,0:T(8,128)(2,1)} %pack.5), channel_id=1, source_target_pairs={{0,2},{2,0},{1,3},{3,1},{4,6},{6,4},{5,7},{7,5},{8,10},{10,8},{9,1... | collective-permute-start | bytes 884744 | tf_op jit(solution)/shard_map/ppermute | solution.py:332
  30.5 12.6 %copy-start.13 = (bf16[2,192,384]{2,1,0:T(8,128)(2,1)S(1)}, bf16[2,192,384]{2,1,0:T(8,128)(2,1)}, u32[]{:S(2)}) copy-start(bf16[2,192,384]{2,1,0:T(8,128)(2,1)} %get-tuple-element.22.refs_2_) | copy-start | bytes 884740
  31.5 11.6 %copy-start.6 = (bf16[2,192,384]{2,1,0:T(8,128)(2,1)S(1)}, bf16[2,192,384]{2,1,0:T(8,128)(2,1)}, u32[]{:S(2)}) copy-start(bf16[2,192,384]{2,1,0:T(8,128)(2,1)} %copy-done.5) | copy-start | bytes 884740
  31.5 11.6 %copy-start.8 = (bf16[2,192,384]{2,1,0:T(8,128)(2,1)S(1)}, bf16[2,192,384]{2,1,0:T(8,128)(2,1)}, u32[]{:S(2)}) copy-start(bf16[2,192,384]{2,1,0:T(8,128)(2,1)} %copy-done.7) | copy-start | bytes 884740
  31.6 25.6 %collective-permute-start.14 = (bf16[2,192,384]{2,1,0:T(8,128)(2,1)S(1)}, bf16[2,192,384]{2,1,0:T(8,128)(2,1)S(1)}, u32[]{:S(2)}, u32[]{:S(2)}) collective-permute-start(bf16[2,192,384]{2,1,0:T(8,128)(2,1)S(1)} %slice.16), channel_id=1, source_target_pairs={{0,4},{4,0},{8,12},{12,8},{1,5},{5,1},{9,13},{13,9},{2,6},{6,2},{1... | collective-permute-start | bytes 884744 | tf_op jit(solution)/shard_map/ppermute | solution.py:340
  42.3 14.9 %collective-permute-start.15 = (bf16[2,192,384]{2,1,0:T(8,128)(2,1)S(1)}, bf16[2,192,384]{2,1,0:T(8,128)(2,1)S(1)}, u32[]{:S(2)}, u32[]{:S(2)}) collective-permute-start(bf16[2,192,384]{2,1,0:T(8,128)(2,1)S(1)} %slice.17), channel_id=1, source_target_pairs={{4,8},{8,4},{5,9},{9,5},{6,10},{10,6},{7,11},{11,7},{20,24},{24,20... | collective-permute-start | bytes 884744 | tf_op jit(solution)/shard_map/ppermute | solution.py:340
  43.0 0.7 copy-start.9
  43.0 0.7 copy-start.10
  50.9 11.7 %collective-permute-start.11 = (bf16[2,192,384]{2,1,0:T(8,128)(2,1)S(1)}, bf16[2,192,384]{2,1,0:T(8,128)(2,1)S(1)}, u32[]{:S(2)}, u32[]{:S(2)}) collective-permute-start(bf16[2,192,384]{2,1,0:T(8,128)(2,1)S(1)} %slice.12), channel_id=1, source_target_pairs={{0,4},{4,0},{8,12},{12,8},{1,5},{5,1},{9,13},{13,9},{2,6},{6,2},{1... | collective-permute-start | bytes 884744 | tf_op jit(solution)/shard_map/ppermute | solution.py:340
  53.0 9.6 %collective-permute-start.12 = (bf16[2,192,384]{2,1,0:T(8,128)(2,1)S(1)}, bf16[2,192,384]{2,1,0:T(8,128)(2,1)S(1)}, u32[]{:S(2)}, u32[]{:S(2)}) collective-permute-start(bf16[2,192,384]{2,1,0:T(8,128)(2,1)S(1)} %slice.13), channel_id=1, source_target_pairs={{4,8},{8,4},{5,9},{9,5},{6,10},{10,6},{7,11},{11,7},{20,24},{24,20... | collective-permute-start | bytes 884744 | tf_op jit(solution)/shard_map/ppermute | solution.py:340
  57.2 2.2 %copy-start.4 = (bf16[2,192,384]{2,1,0:T(8,128)(2,1)S(1)}, bf16[2,192,384]{2,1,0:T(8,128)(2,1)}, u32[]{:S(2)}) copy-start(bf16[2,192,384]{2,1,0:T(8,128)(2,1)} %copy-done.3) | copy-start | bytes 884740
  57.2 2.2 %copy-start.12 = (bf16[2,192,384]{2,1,0:T(8,128)(2,1)S(1)}, bf16[2,192,384]{2,1,0:T(8,128)(2,1)}, u32[]{:S(2)}) copy-start(bf16[2,192,384]{2,1,0:T(8,128)(2,1)} %get-tuple-element.21.refs_2_) | copy-start | bytes 884740
  58.8 7.0 %collective-permute-start.16 = (bf16[192,384]{1,0:T(8,128)(2,1)S(1)}, bf16[192,384]{1,0:T(8,128)(2,1)S(1)}, u32[]{:S(2)}, u32[]{:S(2)}) collective-permute-start(bf16[192,384]{1,0:T(8,128)(2,1)S(1)} %get-tuple-element.34), channel_id=1, source_target_pairs={{0,2},{2,0},{1,3},{3,1},{4,6},{6,4},{5,7},{7,5},{8,10},{10,8},{9,1... | collective-permute-start | bytes 442376 | tf_op jit(solution)/shard_map/ppermute | solution.py:332
  64.2 5.2 %collective-permute-start.13 = (bf16[192,384]{1,0:T(8,128)(2,1)S(1)}, bf16[192,384]{1,0:T(8,128)(2,1)S(1)}, u32[]{:S(2)}, u32[]{:S(2)}) collective-permute-start(bf16[192,384]{1,0:T(8,128)(2,1)S(1)} %get-tuple-element.30), channel_id=1, source_target_pairs={{0,2},{2,0},{1,3},{3,1},{4,6},{6,4},{5,7},{7,5},{8,10},{10,8},{9,1... | collective-permute-start | bytes 442376 | tf_op jit(solution)/shard_map/ppermute | solution.py:332

commit v7 on v6

--- a/solution.py
+++ b/solution.py
@@ -89,7 +89,7 @@
 
 def attend_kernel(
     spaces, frames, columns, row_band, heads, together, groups, skips, fresh, final,
-    place_ref, flags_ref, widths_ref, *refs,
+    flags_ref, widths_ref, *refs,
 ):
     refs = list(refs)
     queries = [refs.pop(0) for unused in range(spaces)]
@@ -100,7 +100,7 @@
     query_ref, key_ref = refs[:2]
     acc_ref, stat_ref = refs[2:] if final else outs
     tokens = queries[0].shape[0]
-    frame_now, space_now = place_ref[0], place_ref[1]
+    frame_now, space_now = lax.axis_index("frame"), lax.axis_index("space")
     scale = math.log2(math.e) / math.sqrt(HEAD_DIM)
     own_column = space_now * (queries[0].shape[-1] // spaces)
 
@@ -252,7 +252,7 @@
             attend_kernel, spaces, frames, columns, row_band, heads, together,
             tuple(numbered), (first * HEAD_DIM,) * spaces, state is None, final,
         ),
-        in_specs=[pl.BlockSpec(memory_space=pltpu.SMEM)] * 3
+        in_specs=[pl.BlockSpec(memory_space=pltpu.SMEM)] * 2
         + [pl.BlockSpec(memory_space=pltpu.VMEM)] * len(operands),
         out_specs=[pl.BlockSpec(memory_space=pltpu.VMEM)] * len(out_shape),
         out_shape=out_shape,
@@ -285,12 +285,13 @@
     )(*arrays)
 
 
-def put_kernel(spaces, places, kept, place_ref, *refs):
+def put_kernel(spaces, places, *refs):
     pieces, out_ref, sems = refs[: len(places)], refs[-2], refs[-1]
     share = out_ref.shape[-1] // spaces
+    here = lax.axis_index("space")
     copies = []
     for n, (offset, first) in enumerate(places):
-        column = pl.multiple_of(lax.rem(place_ref[1] + offset, spaces) * share + first, HEAD_DIM)
+        column = pl.multiple_of(lax.rem(here + offset, spaces) * share + first, HEAD_DIM)
         width = pieces[n].shape[-1]
         copy = pltpu.make_async_copy(pieces[n], out_ref.at[:, pl.ds(column, width)], sems.at[n])
         copy.start()
@@ -299,20 +300,19 @@
         copy.wait()
 
 
-def put(place, pieces, places, whole, shape, spaces):
+def put(pieces, places, whole, shape, spaces):
     kept = [] if whole is None else [whole]
     return pl.pallas_call(
-        functools.partial(put_kernel, spaces, tuple(places), len(kept)),
-        in_specs=[pl.BlockSpec(memory_space=pltpu.SMEM)]
-        + [pl.BlockSpec(memory_space=pltpu.VMEM)] * len(pieces)
+        functools.partial(put_kernel, spaces, tuple(places)),
+        in_specs=[pl.BlockSpec(memory_space=pltpu.VMEM)] * len(pieces)
         + [pl.BlockSpec(memory_space=pl.ANY)] * len(kept),
         out_specs=pl.BlockSpec(memory_space=pl.ANY),
         out_shape=jax.ShapeDtypeStruct(shape, pieces[0].dtype),
         scratch_shapes=[pltpu.SemaphoreType.DMA((len(pieces),))],
-        input_output_aliases={1 + len(pieces): 0} if kept else {},
+        input_output_aliases={len(pieces): 0} if kept else {},
         compiler_params=pltpu.CompilerParams(vmem_limit_bytes=SMALL_LIMIT),
         name="put",
-    )(place, *pieces, *kept)
+    )(*pieces, *kept)
 
 
 def shards(spaces, frames, queries, keys, values, flags, widths):
@@ -320,8 +320,7 @@
     tokens = row_band * columns
     width = features // spaces
     heads = width // HEAD_DIM
-    place = jnp.stack([lax.axis_index("frame"), lax.axis_index("space")]).astype(jnp.int32)
-    scalars = (place, flags, widths)
+    scalars = (flags, widths)
     sizes = (spaces, frames, columns, row_band, features)
     q, k, v = (x.reshape(tokens, features) for x in (queries, keys, values))
     half = heads - heads // 2
@@ -356,6 +355,7 @@
         partners.append(arrived)
     sends = pack((q,), [(offset, 0, width) for offset in offsets], arrived, spaces, False)
     query_parts = [q] + [along_space(x, offset) for x, offset in zip(sends, offsets)]
+    partners[1] = list(tie(partners[1], sends))
 
     last = frames - 2
     behind = 2 * len(offsets)
@@ -373,38 +373,27 @@
     for c in range(len(chunks)):
         ready = [join(partners[c] + [firsts[c][1 - slot]]) for slot in range(2)]
         seconds.append(swap_both(ready))
-    messages, states, ends = seconds, [None] * len(chunks), [None] * len(chunks)
-    for hops in range(2, frames):
+    states = []
+    for c, chunk in enumerate(chunks):
+        pieces = [(own[c], 0, 0)] + [(x, 0, o) for x, o in zip(partners[c], offsets)]
+        groups = [(0, 0, pieces)] + own_band(firsts[c], 1)
+        states.append(attend(scalars, query_parts, groups, None, False, chunk, sizes))
+
+    messages = seconds
+    for hops in range(2, frames - 1):
         following = []
         for c, chunk in enumerate(chunks):
-            came = messages[c]
-            if c > 0:
-                came = list(tie(came, [states[c - 1][1]]))
-            if hops == last:
-                sent = [came[1 - slot][:behind] for slot in range(2)]
-            else:
-                sent = [came[1 - slot] for slot in range(2)]
-            if hops <= last:
-                following.append(swap_both(sent))
-                groups = [
-                    (slot, hops - 1, a + b)
-                    for (slot, unused, a), (unused, unused, b) in zip(
-                        own_band(firsts[c], 1), partner_bands(came, 1)
-                    )
-                ]
-                if hops == 2:
-                    own_frame = [(own[c], 0, 0)]
-                    own_frame += [(x, 0, o) for x, o in zip(partners[c], offsets)]
-                    groups.insert(0, (0, 0, own_frame))
-                else:
-                    groups = partner_bands(came, hops - 1)
-                groups += own_band(came, hops)
-                states[c] = attend(
-                    scalars, query_parts, groups, states[c], False, chunk, sizes
-                )
-            else:
-                ends[c] = partner_bands(came, last)
+            after = [state[1] for state in (states if c == 0 else states[:c])]
+            came = list(tie(messages[c], after))
+            rows = behind if hops == last else behind + 2
+            following.append(swap_both([came[1 - slot][:rows] for slot in range(2)]))
+            groups = partner_bands(came, hops - 1) + own_band(came, hops)
+            states[c] = attend(scalars, query_parts, groups, states[c], False, chunk, sizes)
         messages = following
+    ends = []
+    for message in messages:
+        came = list(tie(message, [state[1] for state in states]))
+        ends.append(partner_bands(came, last))
 
     own, returned = [], []
     for c, chunk in enumerate(chunks):
@@ -416,7 +405,7 @@
     result = None
     for batch in (own + returned[:late], returned[late:]):
         pieces, places = zip(*batch)
-        result = put(place, pieces, places, result, q.shape, spaces)
+        result = put(pieces, places, result, q.shape, spaces)
     return result.reshape(queries.shape)
 
 

time: 71.2 us -> 70.8 us (level)
  waiting for transfers between devices: 9.8 us -> 17.3 us
  local copies, waits for them, and re-layouts: 3.4 us -> 0.16 us
  Pallas kernels: 18.8 us -> 15.9 us
  starting transfers between devices: 38.3 us -> 37 us
    ppermute x5, waiting for transfers between devices: 2.83 us -> 12.2 us  [along_space(): lax.ppermute(x, 'space', [(s, (s + offset) % spaces) for s in range(space...]
    pallas_call x4, Pallas kernels: 2.75 us -> 0.21 us  [join(): pl.pallas_call(functools.partial(join_kernel, parts), in_specs=[pl.BlockS...]
    slice x4, local copies, waits for them, and re-layouts: 2.09 us -> 0.12 us  [shards(): following.append(swap_both([came[1 - slot][:rows] for slot in range(2)]))]
    ppermute x12, waiting for transfers between devices: 6.98 us -> 5.04 us  [swap(): return lax.ppermute(x, 'frame', pairs)]
    pallas_call x4 -> x6, Pallas kernels: 10.3 us -> 11.7 us  [attend(): pl.pallas_call(functools.partial(attend_kernel, spaces, frames, columns,...]
    unnamed x28 -> x14, local copies, waits for them, and re-layouts: 1.31 us -> 0.03 us
    pallas_call x2, Pallas kernels: 2.55 us -> 1.45 us  [put(): pl.pallas_call(functools.partial(put_kernel, spaces, tuple(places)), in_s...]
    ppermute x5, starting transfers between devices: 7.57 us -> 6.61 us  [along_space(): lax.ppermute(x, 'space', [(s, (s + offset) % spaces) for s in range(space...]
  transfers between devices with their start and end apart: 17 -> 17, of which waited for: 5 -> 9; matrix products, arithmetic and copies ran while one was open for 3% -> 0% of each run, Pallas kernels for 22% -> 18%
where the time goes in v7:
time: 70.8 us; the launch traced here: 70.5 us
  starting transfers between devices  37 us (52%)
  waiting for transfers between devices  17.3 us (24%)
  Pallas kernels  15.9 us (22%)
    ppermute x12, starting transfers between devices, swap(): return lax.ppermute(x, 'frame', pairs)  30.4 us
    ppermute x5, waiting for transfers between devices, along_space(): lax.ppermute(x, 'space', [(s, (s + offset) % spaces) for s in range(space...  12.2 us
    pallas_call x6, Pallas kernels, attend(): pl.pallas_call(functools.partial(attend_kernel, spaces, frames, columns,...  11.7 us
    ppermute x5, starting transfers between devices, along_space(): lax.ppermute(x, 'space', [(s, (s + offset) % spaces) for s in range(space...  6.61 us
    ppermute x12, waiting for transfers between devices, swap(): return lax.ppermute(x, 'frame', pairs)  5.04 us
    pallas_call x3, Pallas kernels, pack(): pl.pallas_call(functools.partial(pack_kernel, spaces, tuple(jobs), staged...  2.54 us
    pallas_call x2, Pallas kernels, put(): pl.pallas_call(functools.partial(put_kernel, spaces, tuple(places)), in_s...  1.45 us
  transfers between devices with their start and end apart: 17, of which 9 were waited for; matrix products, arithmetic and copies ran while one was open for 0% of the time, Pallas kernels for 18%

profile of v7, /device:TPU:0, one launch (start us, length us, event | category | flops | bytes accessed | tf_op | source)
XLA Modules:
  0.0 70.5 jit_solution(3274317521777834725)
XLA Ops:
  0.0 0.0 copy-start.1
  0.0 0.0 copy-start.2
  0.0 2.3 %pack.3 = (bf16[2,192,384]{2,1,0:T(8,128)(2,1)}, bf16[2,192,384]{2,1,0:T(8,128)(2,1)}, bf16[2,192,384]{2,1,0:T(8,128)(2,1)}) custom-call(bf16[192,1536]{1,0:T(8,128)(2,1)} %bitcast.11, bf16[192,1536]{1,0:T(8,128)(2,1)} %bitcast.13), custom_call_target="tpu_custom_call" | custom-call | tf_op jit(solution)/shard_map/pack/pallas_call | solution.py:64
  2.3 3.0 %collective-permute-start = (bf16[2,192,384]{2,1,0:T(8,128)(2,1)}, bf16[2,192,384]{2,1,0:T(8,128)(2,1)S(1)}, u32[]{:S(2)}, u32[]{:S(2)}) collective-permute-start(bf16[2,192,384]{2,1,0:T(8,128)(2,1)} %get-tuple-element.28), channel_id=1, source_target_pairs={{0,2},{2,0},{1,3},{3,1},{4,6},{6,4},{5,7},{7,5},{8,10},{10,8},{9,1... | collective-permute-start | bytes 884744 | tf_op jit(solution)/shard_map/ppermute | solution.py:331
  5.3 0.0 copy-start.3
  5.3 0.8 %collective-permute-start.7 = (bf16[2,192,384]{2,1,0:T(8,128)(2,1)}, bf16[2,192,384]{2,1,0:T(8,128)(2,1)S(1)}, u32[]{:S(2)}, u32[]{:S(2)}) collective-permute-start(bf16[2,192,384]{2,1,0:T(8,128)(2,1)} %get-tuple-element.30.refs_2_), channel_id=1, source_target_pairs={{4,8},{8,4},{5,9},{9,5},{6,10},{10,6},{7,11},{11,7},{20,24},{24,20... | collective-permute-start | bytes 884744 | tf_op jit(solution)/shard_map/ppermute | solution.py:339
  6.1 4.4 %collective-permute-start.9 = (bf16[2,192,384]{2,1,0:T(8,128)(2,1)}, bf16[2,192,384]{2,1,0:T(8,128)(2,1)S(1)}, u32[]{:S(2)}, u32[]{:S(2)}) collective-permute-start(bf16[2,192,384]{2,1,0:T(8,128)(2,1)} %get-tuple-element.30.refs_2_), channel_id=1, source_target_pairs={{0,4},{4,0},{8,12},{12,8},{1,5},{5,1},{9,13},{13,9},{2,6},{6,2},{1... | collective-permute-start | bytes 884744 | tf_op jit(solution)/shard_map/ppermute | solution.py:339
  10.5 2.0 %collective-permute-done.refs_2_.refs_0_.refs_3_ = bf16[2,192,384]{2,1,0:T(8,128)(2,1)S(1)} collective-permute-done((bf16[2,192,384]{2,1,0:T(8,128)(2,1)}, bf16[2,192,384]{2,1,0:T(8,128)(2,1)S(1)}, u32[]{:S(2)}, u32[]{:S(2)}) %collective-permute-start) | collective-permute-done | bytes 294944 | tf_op jit(solution)/shard_map/ppermute | solution.py:331
  12.5 0.0 copy-done.1
  12.5 0.0 copy-done.2
  12.5 0.2 pack.4
  12.7 1.8 %collective-permute-start.1 = (bf16[2,192,384]{2,1,0:T(8,128)(2,1)S(1)}, bf16[2,192,384]{2,1,0:T(8,128)(2,1)S(1)}, u32[]{:S(2)}, u32[]{:S(2)}) collective-permute-start(bf16[2,192,384]{2,1,0:T(8,128)(2,1)S(1)} %pack.4), channel_id=1, source_target_pairs={{0,2},{2,0},{1,3},{3,1},{4,6},{6,4},{5,7},{7,5},{8,10},{10,8},{9,1... | collective-permute-start | bytes 884744 | tf_op jit(solution)/shard_map/ppermute | solution.py:331
  14.5 0.0 copy-done.3
  14.5 0.7 collective-permute-start.3
  15.2 4.4 %collective-permute-start.5 = (bf16[2,192,384]{2,1,0:T(8,128)(2,1)S(1)}, bf16[2,192,384]{2,1,0:T(8,128)(2,1)S(1)}, u32[]{:S(2)}, u32[]{:S(2)}) collective-permute-start(bf16[2,192,384]{2,1,0:T(8,128)(2,1)S(1)} %copy-done.3), channel_id=1, source_target_pairs={{0,4},{4,0},{8,12},{12,8},{1,5},{5,1},{9,13},{13,9},{2,6},{6,2},{1... | collective-permute-start | bytes 884744 | tf_op jit(solution)/shard_map/ppermute | solution.py:339
  19.6 0.0 collective-permute-done.7.refs_1_.refs_5_
  19.6 0.1 join.6
  19.7 0.0 copy-start
  19.7 0.1 collective-permute-start.8
  19.8 0.0 collective-permute-done.9.refs_1_.refs_4_
  19.8 0.1 join.7
  19.8 0.8 %collective-permute-start.10 = (bf16[4,192,384]{2,1,0:T(8,128)(2,1)S(1)}, bf16[4,192,384]{2,1,0:T(8,128)(2,1)S(1)}, u32[]{:S(2)}, u32[]{:S(2)}) collective-permute-start(bf16[4,192,384]{2,1,0:T(8,128)(2,1)S(1)} %join.7), channel_id=1, source_target_pairs={{4,8},{8,4},{5,9},{9,5},{6,10},{10,6},{7,11},{11,7},{20,24},{24,20... | collective-permute-start | bytes 1769480 | tf_op jit(solution)/shard_map/ppermute | solution.py:339
  20.7 0.3 collective-permute-done.1.refs_1_.refs_0_
  21.0 0.0 copy-done
  21.0 0.1 pack.5.refs_1_
  21.1 0.0 collective-permute-done.3.refs_1_.refs_5_
  21.1 0.1 join.4
  21.1 0.0 copy-start.4
  21.1 0.0 copy-start.5
  21.2 0.0 copy-start.6
  21.2 6.0 %collective-permute-start.4 = (bf16[4,192,384]{2,1,0:T(8,128)(2,1)S(1)}, bf16[4,192,384]{2,1,0:T(8,128)(2,1)S(1)}, u32[]{:S(2)}, u32[]{:S(2)}) collective-permute-start(bf16[4,192,384]{2,1,0:T(8,128)(2,1)S(1)} %join.4), channel_id=1, source_target_pairs={{0,4},{4,0},{8,12},{12,8},{1,5},{5,1},{9,13},{13,9},{2,6},{6,2},{1... | collective-permute-start | bytes 1769480 | tf_op jit(solution)/shard_map/ppermute | solution.py:339
  27.2 0.4 collective-permute-done.5.refs_1_.refs_4_
  27.5 0.1 join.5
  27.6 0.7 collective-permute-start.6
  28.3 0.6 collective-permute-start.2
  28.9 6.2 %collective-permute-done.2.refs_1_ = bf16[192,768]{1,0:T(8,128)(2,1)S(1)} collective-permute-done((bf16[192,768]{1,0:T(8,128)(2,1)S(1)}, bf16[192,768]{1,0:T(8,128)(2,1)S(1)}, u32[]{:S(2)}, u32[]{:S(2)}) %collective-permute-start.2) | collective-permute-done | bytes 294944 | tf_op jit(solution)/shard_map/ppermute | solution.py:331
  35.1 0.0 copy-done.4
  35.1 0.0 copy-done.5
  35.1 0.0 copy-done.6
  35.1 2.2 %attend.4 = (f32[3,128,384]{2,1,0:T(8,128)S(1)}, f32[3,8,384]{2,1,0:T(8,128)S(1)}) custom-call(s32[4,4]{1,0:T(4,128)S(1)} %copy-done.5, s32[4]{0:T(128)S(1)} %copy-done.6, bf16[192,1536]{1,0:T(8,128)(2,1)S(1)} %bitcast.5, bf16[192,768]{1,0:T(8,128)(2,1)S(1)} %collective-permute-done.2.refs_1_, bf16[2,192,384]{2,1,0:T(8,128)(2,1)S(1)} %copy-done.4, ...), custom_call_target="tpu_custom_call" | custom-call | flops 452984832 | bytes 1179648 | tf_op jit(solution)/shard_map/attend/pallas_call | solution.py:250
  37.3 2.3 %attend.5 = (f32[3,128,384]{2,1,0:T(8,128)S(1)}, f32[3,8,384]{2,1,0:T(8,128)S(1)}) custom-call(s32[4,4]{1,0:T(4,128)S(1)} %copy-done.5, s32[4]{0:T(128)S(1)} %copy-done.6, bf16[192,1536]{1,0:T(8,128)(2,1)S(1)} %bitcast.6, bf16[192,768]{1,0:T(8,128)(2,1)S(1)} %collective-permute-done.2.refs_1_, bf16[2,192,384]{2,1,0:T(8,128)(2,1)S(1)} %copy-done.3, ...), custom_call_target="tpu_custom_call" | custom-call | flops 452984832 | bytes 1179648 | tf_op jit(solution)/shard_map/attend/pallas_call | solution.py:250
  39.6 0.6 collective-permute-done.8.refs_0_
  40.2 0.0 collective-permute-done.10.refs_1_
  40.3 0.7 collective-permute-start.15
  41.0 7.3 %collective-permute-start.14 = (bf16[2,192,384]{2,1,0:T(8,128)(2,1)S(1)}, bf16[2,192,384]{2,1,0:T(8,128)(2,1)S(1)}, u32[]{:S(2)}, u32[]{:S(2)}) collective-permute-start(bf16[2,192,384]{2,1,0:T(8,128)(2,1)S(1)} %slice.14), channel_id=1, source_target_pairs={{0,4},{4,0},{8,12},{12,8},{1,5},{5,1},{9,13},{13,9},{2,6},{6,2},{1... | collective-permute-start | bytes 884744 | tf_op jit(solution)/shard_map/ppermute | solution.py:339
  48.2 2.0 %attend.6 = (f32[3,128,384]{2,1,0:T(8,128)S(1)}, f32[3,8,384]{2,1,0:T(8,128)S(1)}) custom-call(s32[4,4]{1,0:T(4,128)S(1)} %copy-done.5, s32[4]{0:T(128)S(1)} %copy-done.6, bf16[192,1536]{1,0:T(8,128)(2,1)S(1)} %bitcast.7, bf16[192,768]{1,0:T(8,128)(2,1)S(1)} %collective-permute-done.2.refs_1_, bf16[4,192,384]{2,1,0:T(8,128)(2,1)S(1)} %get-tuple-element.33.refs_2_, ...), custom_call_target="tpu_custom_call" | custom-call | flops 452984832 | bytes 1179648 | tf_op jit(solution)/shard_map/attend/pallas_call | solution.py:250
  50.3 2.5 %collective-permute-done.4.refs_0_ = bf16[4,192,384]{2,1,0:T(8,128)(2,1)S(1)} collective-permute-done((bf16[4,192,384]{2,1,0:T(8,128)(2,1)S(1)}, bf16[4,192,384]{2,1,0:T(8,128)(2,1)S(1)}, u32[]{:S(2)}, u32[]{:S(2)}) %collective-permute-start.4) | collective-permute-done | bytes 589856 | tf_op jit(solution)/shard_map/ppermute | solution.py:339
  52.8 0.0 collective-permute-done.6.refs_1_
  52.9 0.7 collective-permute-start.12
  53.6 3.8 %collective-permute-start.11 = (bf16[2,192,384]{2,1,0:T(8,128)(2,1)S(1)}, bf16[2,192,384]{2,1,0:T(8,128)(2,1)S(1)}, u32[]{:S(2)}, u32[]{:S(2)}) collective-permute-start(bf16[2,192,384]{2,1,0:T(8,128)(2,1)S(1)} %slice.12), channel_id=1, source_target_pairs={{0,4},{4,0},{8,12},{12,8},{1,5},{5,1},{9,13},{13,9},{2,6},{6,2},{1... | collective-permute-start | bytes 884744 | tf_op jit(solution)/shard_map/ppermute | solution.py:339
  57.4 2.1 %attend.7 = (f32[3,128,384]{2,1,0:T(8,128)S(1)}, f32[3,8,384]{2,1,0:T(8,128)S(1)}) custom-call(s32[4,4]{1,0:T(4,128)S(1)} %copy-done.5, s32[4]{0:T(128)S(1)} %copy-done.6, bf16[192,1536]{1,0:T(8,128)(2,1)S(1)} %bitcast.8, bf16[192,768]{1,0:T(8,128)(2,1)S(1)} %collective-permute-done.2.refs_1_, bf16[4,192,384]{2,1,0:T(8,128)(2,1)S(1)} %get-tuple-element.38.refs_2_, ...), custom_call_target="tpu_custom_call" | custom-call | flops 452984832 | bytes 1179648 | tf_op jit(solution)/shard_map/attend/pallas_call | solution.py:250
  59.4 0.0 collective-permute-done.15.refs_1_
  59.4 0.0 collective-permute-done.14.refs_0_
  59.5 1.6 %attend_final.3 = (bf16[192,384]{1,0:T(8,128)(2,1)S(1)}, bf16[192,384]{1,0:T(8,128)(2,1)S(1)}) custom-call(s32[4,4]{1,0:T(4,128)S(1)} %copy-done.5, s32[4]{0:T(128)S(1)} %copy-done.6, bf16[192,1536]{1,0:T(8,128)(2,1)S(1)} %bitcast.9, bf16[192,768]{1,0:T(8,128)(2,1)S(1)} %collective-permute-done.2.refs_1_, ...), custom_call_target="tpu_custom_call" | custom-call | flops 226492416 | bytes 1179648 | tf_op jit(solution)/shard_map/attend_final/pallas_call | solution.py:250
  61.0 0.6 collective-permute-start.16
  61.6 0.0 collective-permute-done.12.refs_1_
  61.6 1.5 %collective-permute-done.11.refs_0_ = bf16[2,192,384]{2,1,0:T(8,128)(2,1)S(1)} collective-permute-done((bf16[2,192,384]{2,1,0:T(8,128)(2,1)S(1)}, bf16[2,192,384]{2,1,0:T(8,128)(2,1)S(1)}, u32[]{:S(2)}, u32[]{:S(2)}) %collective-permute-start.11) | collective-permute-done | bytes 294944 | tf_op jit(solution)/shard_map/ppermute | solution.py:339
  63.1 1.5 %attend_final.2 = (bf16[192,384]{1,0:T(8,128)(2,1)S(1)}, bf16[192,384]{1,0:T(8,128)(2,1)S(1)}) custom-call(s32[4,4]{1,0:T(4,128)S(1)} %copy-done.5, s32[4]{0:T(128)S(1)} %copy-done.6, bf16[192,1536]{1,0:T(8,128)(2,1)S(1)} %bitcast.10, bf16[192,768]{1,0:T(8,128)(2,1)S(1)} %collective-permute-done.2.refs_1_, ...), custom_call_target="tpu_custom_call" | custom-call | flops 226492416 | bytes 1179648 | tf_op jit(solution)/shard_map/attend_final/pallas_call | solution.py:250
  64.7 0.6 collective-permute-start.13
  65.3 2.2 %collective-permute-done.16.refs_2_ = bf16[192,384]{1,0:T(8,128)(2,1)S(1)} collective-permute-done((bf16[192,384]{1,0:T(8,128)(2,1)S(1)}, bf16[192,384]{1,0:T(8,128)(2,1)S(1)}, u32[]{:S(2)}, u32[]{:S(2)}) %collective-permute-start.16) | collective-permute-done | bytes 147488 | tf_op jit(solution)/shard_map/ppermute | solution.py:331
  67.4 0.8 %put.2.refs_1_ = bf16[192,1536]{1,0:T(8,128)(2,1)} custom-call(bf16[192,384]{1,0:T(8,128)(2,1)S(1)} %get-tuple-element.48.refs_0_, bf16[192,384]{1,0:T(8,128)(2,1)S(1)} %get-tuple-element.49.refs_1_, bf16[192,384]{1,0:T(8,128)(2,1)S(1)} %collective-permute-done.16.refs_2_), custom_call_target="tpu_custom_call" | custom-call | tf_op jit(solution)/shard_map/put/pallas_call | solution.py:305
  68.2 1.7 %collective-permute-done.13.refs_0_ = bf16[192,384]{1,0:T(8,128)(2,1)S(1)} collective-permute-done((bf16[192,384]{1,0:T(8,128)(2,1)S(1)}, bf16[192,384]{1,0:T(8,128)(2,1)S(1)}, u32[]{:S(2)}, u32[]{:S(2)}) %collective-permute-start.13) | collective-permute-done | bytes 147488 | tf_op jit(solution)/shard_map/ppermute | solution.py:331
  69.9 0.7 put.3
  (9 shorter events, 0.1 us)
Async XLA Ops:
  0.0 12.5 %copy-start.1 = (bf16[1,4,48,1536]{3,2,1,0:T(8,128)(2,1)S(1)}, bf16[1,4,48,1536]{3,2,1,0:T(8,128)(2,1)}, u32[]{:S(2)}) copy-start(bf16[1,4,48,1536]{3,2,1,0:T(8,128)(2,1)} %param.6) | copy-start | bytes 1769476
  0.0 12.5 %copy-start.2 = (bf16[1,4,48,1536]{3,2,1,0:T(8,128)(2,1)S(1)}, bf16[1,4,48,1536]{3,2,1,0:T(8,128)(2,1)}, u32[]{:S(2)}) copy-start(bf16[1,4,48,1536]{3,2,1,0:T(8,128)(2,1)} %param.7) | copy-start | bytes 1769476
  2.3 10.2 %collective-permute-start = (bf16[2,192,384]{2,1,0:T(8,128)(2,1)}, bf16[2,192,384]{2,1,0:T(8,128)(2,1)S(1)}, u32[]{:S(2)}, u32[]{:S(2)}) collective-permute-start(bf16[2,192,384]{2,1,0:T(8,128)(2,1)} %get-tuple-element.28), channel_id=1, source_target_pairs={{0,2},{2,0},{1,3},{3,1},{4,6},{6,4},{5,7},{7,5},{8,10},{10,8},{9,1... | collective-permute-start | bytes 884744 | tf_op jit(solution)/shard_map/ppermute | solution.py:331
  5.3 9.2 %copy-start.3 = (bf16[2,192,384]{2,1,0:T(8,128)(2,1)S(1)}, bf16[2,192,384]{2,1,0:T(8,128)(2,1)}, u32[]{:S(2)}) copy-start(bf16[2,192,384]{2,1,0:T(8,128)(2,1)} %get-tuple-element.29.refs_2_) | copy-start | bytes 884740
  5.3 14.3 %collective-permute-start.7 = (bf16[2,192,384]{2,1,0:T(8,128)(2,1)}, bf16[2,192,384]{2,1,0:T(8,128)(2,1)S(1)}, u32[]{:S(2)}, u32[]{:S(2)}) collective-permute-start(bf16[2,192,384]{2,1,0:T(8,128)(2,1)} %get-tuple-element.30.refs_2_), channel_id=1, source_target_pairs={{4,8},{8,4},{5,9},{9,5},{6,10},{10,6},{7,11},{11,7},{20,24},{24,20... | collective-permute-start | bytes 884744 | tf_op jit(solution)/shard_map/ppermute | solution.py:339
  6.1 13.7 %collective-permute-start.9 = (bf16[2,192,384]{2,1,0:T(8,128)(2,1)}, bf16[2,192,384]{2,1,0:T(8,128)(2,1)S(1)}, u32[]{:S(2)}, u32[]{:S(2)}) collective-permute-start(bf16[2,192,384]{2,1,0:T(8,128)(2,1)} %get-tuple-element.30.refs_2_), channel_id=1, source_target_pairs={{0,4},{4,0},{8,12},{12,8},{1,5},{5,1},{9,13},{13,9},{2,6},{6,2},{1... | collective-permute-start | bytes 884744 | tf_op jit(solution)/shard_map/ppermute | solution.py:339
  12.7 8.3 %collective-permute-start.1 = (bf16[2,192,384]{2,1,0:T(8,128)(2,1)S(1)}, bf16[2,192,384]{2,1,0:T(8,128)(2,1)S(1)}, u32[]{:S(2)}, u32[]{:S(2)}) collective-permute-start(bf16[2,192,384]{2,1,0:T(8,128)(2,1)S(1)} %pack.4), channel_id=1, source_target_pairs={{0,2},{2,0},{1,3},{3,1},{4,6},{6,4},{5,7},{7,5},{8,10},{10,8},{9,1... | collective-permute-start | bytes 884744 | tf_op jit(solution)/shard_map/ppermute | solution.py:331
  14.5 6.6 %collective-permute-start.3 = (bf16[2,192,384]{2,1,0:T(8,128)(2,1)S(1)}, bf16[2,192,384]{2,1,0:T(8,128)(2,1)S(1)}, u32[]{:S(2)}, u32[]{:S(2)}) collective-permute-start(bf16[2,192,384]{2,1,0:T(8,128)(2,1)S(1)} %copy-done.3), channel_id=1, source_target_pairs={{4,8},{8,4},{5,9},{9,5},{6,10},{10,6},{7,11},{11,7},{20,24},{24,20... | collective-permute-start | bytes 884744 | tf_op jit(solution)/shard_map/ppermute | solution.py:339
  15.2 12.4 %collective-permute-start.5 = (bf16[2,192,384]{2,1,0:T(8,128)(2,1)S(1)}, bf16[2,192,384]{2,1,0:T(8,128)(2,1)S(1)}, u32[]{:S(2)}, u32[]{:S(2)}) collective-permute-start(bf16[2,192,384]{2,1,0:T(8,128)(2,1)S(1)} %copy-done.3), channel_id=1, source_target_pairs={{0,4},{4,0},{8,12},{12,8},{1,5},{5,1},{9,13},{13,9},{2,6},{6,2},{1... | collective-permute-start | bytes 884744 | tf_op jit(solution)/shard_map/ppermute | solution.py:339
  19.7 1.3 %copy-start = (bf16[1,4,48,1536]{3,2,1,0:T(8,128)(2,1)S(1)}, bf16[1,4,48,1536]{3,2,1,0:T(8,128)(2,1)}, u32[]{:S(2)}) copy-start(bf16[1,4,48,1536]{3,2,1,0:T(8,128)(2,1)} %param.5) | copy-start | bytes 1769476
  19.7 20.5 %collective-permute-start.8 = (bf16[4,192,384]{2,1,0:T(8,128)(2,1)S(1)}, bf16[4,192,384]{2,1,0:T(8,128)(2,1)S(1)}, u32[]{:S(2)}, u32[]{:S(2)}) collective-permute-start(bf16[4,192,384]{2,1,0:T(8,128)(2,1)S(1)} %join.6), channel_id=1, source_target_pairs={{0,4},{4,0},{8,12},{12,8},{1,5},{5,1},{9,13},{13,9},{2,6},{6,2},{1... | collective-permute-start | bytes 1769480 | tf_op jit(solution)/shard_map/ppermute | solution.py:339
  19.8 20.3 %collective-permute-start.10 = (bf16[4,192,384]{2,1,0:T(8,128)(2,1)S(1)}, bf16[4,192,384]{2,1,0:T(8,128)(2,1)S(1)}, u32[]{:S(2)}, u32[]{:S(2)}) collective-permute-start(bf16[4,192,384]{2,1,0:T(8,128)(2,1)S(1)} %join.7), channel_id=1, source_target_pairs={{4,8},{8,4},{5,9},{9,5},{6,10},{10,6},{7,11},{11,7},{20,24},{24,20... | collective-permute-start | bytes 1769480 | tf_op jit(solution)/shard_map/ppermute | solution.py:339
  21.1 14.0 %copy-start.4 = (bf16[2,192,384]{2,1,0:T(8,128)(2,1)S(1)}, bf16[2,192,384]{2,1,0:T(8,128)(2,1)}, u32[]{:S(2)}) copy-start(bf16[2,192,384]{2,1,0:T(8,128)(2,1)} %get-tuple-element.30.refs_2_) | copy-start | bytes 884740
  21.1 14.0 %copy-start.5 = (s32[4,4]{1,0:T(4,128)S(1)}, s32[4,4]{1,0:T(4,128)}, u32[]{:S(2)}) copy-start(s32[4,4]{1,0:T(4,128)} %flags_ref.11) | copy-start | bytes 196
  21.2 13.9 %copy-start.6 = (s32[4]{0:T(128)S(1)}, s32[4]{0:T(128)}, u32[]{:S(2)}) copy-start(s32[4]{0:T(128)} %widths_ref.11) | copy-start | bytes 52
  21.2 31.7 %collective-permute-start.4 = (bf16[4,192,384]{2,1,0:T(8,128)(2,1)S(1)}, bf16[4,192,384]{2,1,0:T(8,128)(2,1)S(1)}, u32[]{:S(2)}, u32[]{:S(2)}) collective-permute-start(bf16[4,192,384]{2,1,0:T(8,128)(2,1)S(1)} %join.4), channel_id=1, source_target_pairs={{0,4},{4,0},{8,12},{12,8},{1,5},{5,1},{9,13},{13,9},{2,6},{6,2},{1... | collective-permute-start | bytes 1769480 | tf_op jit(solution)/shard_map/ppermute | solution.py:339
  27.6 25.2 %collective-permute-start.6 = (bf16[4,192,384]{2,1,0:T(8,128)(2,1)S(1)}, bf16[4,192,384]{2,1,0:T(8,128)(2,1)S(1)}, u32[]{:S(2)}, u32[]{:S(2)}) collective-permute-start(bf16[4,192,384]{2,1,0:T(8,128)(2,1)S(1)} %join.5), channel_id=1, source_target_pairs={{4,8},{8,4},{5,9},{9,5},{6,10},{10,6},{7,11},{11,7},{20,24},{24,20... | collective-permute-start | bytes 1769480 | tf_op jit(solution)/shard_map/ppermute | solution.py:339
  28.3 6.8 %collective-permute-start.2 = (bf16[192,768]{1,0:T(8,128)(2,1)S(1)}, bf16[192,768]{1,0:T(8,128)(2,1)S(1)}, u32[]{:S(2)}, u32[]{:S(2)}) collective-permute-start(bf16[192,768]{1,0:T(8,128)(2,1)S(1)} %pack.5.refs_1_), channel_id=1, source_target_pairs={{0,2},{2,0},{1,3},{3,1},{4,6},{6,4},{5,7},{7,5},{8,10},{10,8},{9,1... | collective-permute-start | bytes 884744 | tf_op jit(solution)/shard_map/ppermute | solution.py:331
  40.3 19.2 %collective-permute-start.15 = (bf16[2,192,384]{2,1,0:T(8,128)(2,1)S(1)}, bf16[2,192,384]{2,1,0:T(8,128)(2,1)S(1)}, u32[]{:S(2)}, u32[]{:S(2)}) collective-permute-start(bf16[2,192,384]{2,1,0:T(8,128)(2,1)S(1)} %slice.15), channel_id=1, source_target_pairs={{4,8},{8,4},{5,9},{9,5},{6,10},{10,6},{7,11},{11,7},{20,24},{24,20... | collective-permute-start | bytes 884744 | tf_op jit(solution)/shard_map/ppermute | solution.py:339
  41.0 18.5 %collective-permute-start.14 = (bf16[2,192,384]{2,1,0:T(8,128)(2,1)S(1)}, bf16[2,192,384]{2,1,0:T(8,128)(2,1)S(1)}, u32[]{:S(2)}, u32[]{:S(2)}) collective-permute-start(bf16[2,192,384]{2,1,0:T(8,128)(2,1)S(1)} %slice.14), channel_id=1, source_target_pairs={{0,4},{4,0},{8,12},{12,8},{1,5},{5,1},{9,13},{13,9},{2,6},{6,2},{1... | collective-permute-start | bytes 884744 | tf_op jit(solution)/shard_map/ppermute | solution.py:339
  52.9 8.7 %collective-permute-start.12 = (bf16[2,192,384]{2,1,0:T(8,128)(2,1)S(1)}, bf16[2,192,384]{2,1,0:T(8,128)(2,1)S(1)}, u32[]{:S(2)}, u32[]{:S(2)}) collective-permute-start(bf16[2,192,384]{2,1,0:T(8,128)(2,1)S(1)} %slice.13), channel_id=1, source_target_pairs={{4,8},{8,4},{5,9},{9,5},{6,10},{10,6},{7,11},{11,7},{20,24},{24,20... | collective-permute-start | bytes 884744 | tf_op jit(solution)/shard_map/ppermute | solution.py:339
  53.6 9.5 %collective-permute-start.11 = (bf16[2,192,384]{2,1,0:T(8,128)(2,1)S(1)}, bf16[2,192,384]{2,1,0:T(8,128)(2,1)S(1)}, u32[]{:S(2)}, u32[]{:S(2)}) collective-permute-start(bf16[2,192,384]{2,1,0:T(8,128)(2,1)S(1)} %slice.12), channel_id=1, source_target_pairs={{0,4},{4,0},{8,12},{12,8},{1,5},{5,1},{9,13},{13,9},{2,6},{6,2},{1... | collective-permute-start | bytes 884744 | tf_op jit(solution)/shard_map/ppermute | solution.py:339
  61.0 6.4 %collective-permute-start.16 = (bf16[192,384]{1,0:T(8,128)(2,1)S(1)}, bf16[192,384]{1,0:T(8,128)(2,1)S(1)}, u32[]{:S(2)}, u32[]{:S(2)}) collective-permute-start(bf16[192,384]{1,0:T(8,128)(2,1)S(1)} %get-tuple-element.50), channel_id=1, source_target_pairs={{0,2},{2,0},{1,3},{3,1},{4,6},{6,4},{5,7},{7,5},{8,10},{10,8},{9,1... | collective-permute-start | bytes 442376 | tf_op jit(solution)/shard_map/ppermute | solution.py:331
  64.7 5.2 %collective-permute-start.13 = (bf16[192,384]{1,0:T(8,128)(2,1)S(1)}, bf16[192,384]{1,0:T(8,128)(2,1)S(1)}, u32[]{:S(2)}, u32[]{:S(2)}) collective-permute-start(bf16[192,384]{1,0:T(8,128)(2,1)S(1)} %get-tuple-element.44), channel_id=1, source_target_pairs={{0,2},{2,0},{1,3},{3,1},{4,6},{6,4},{5,7},{7,5},{8,10},{10,8},{9,1... | collective-permute-start | bytes 442376 | tf_op jit(solution)/shard_map/ppermute | solution.py:331

commit v8 on v7

--- a/solution.py
+++ b/solution.py
@@ -97,6 +97,7 @@
     keyvals = [refs.pop(0) for unused in range(arrays)]
     state_in = None if fresh else (refs.pop(0), refs.pop(0))
     outs = [refs.pop(0) for unused in range(spaces if final else 2)]
+    query_skip, array_skips = skips
     query_ref, key_ref = refs[:2]
     acc_ref, stat_ref = refs[2:] if final else outs
     tokens = queries[0].shape[0]
@@ -151,7 +152,9 @@
                 top = jnp.maximum(top, before)
             weights = jnp.exp2(scores * scale - top)
             total = jnp.sum(weights, axis=0, keepdims=True)
-            values = jnp.concatenate([keyvals[i][r + 1, :, lanes(t)] for i, r, o in pieces], axis=0)
+            values = jnp.concatenate(
+                [keyvals[i][r + 1, :, lanes(t, array_skips[i])] for i, r, o in pieces], axis=0
+            )
             acc = lax.dot_general(
                 values, weights.astype(jnp.bfloat16), TN, preferred_element_type=jnp.float32
             )
@@ -165,7 +168,7 @@
 
         for t in range(together):
             for offset in range(spaces):
-                skip = skips[offset] + (own_column if offset == 0 else 0)
+                skip = query_skip + (own_column if offset == 0 else 0)
                 query_ref[t, pl.ds(offset * tokens, tokens), :HEAD_DIM] = queries[offset][
                     :, lanes(t, skip)
                 ]
@@ -178,7 +181,7 @@
                 scores = []
                 for t in range(together):
                     keys = jnp.concatenate(
-                        [keyvals[i][r, :, lanes(t)] for i, r, o in pieces], axis=0
+                        [keyvals[i][r, :, lanes(t, array_skips[i])] for i, r, o in pieces], axis=0
                     )
                     scores.append(
                         lax.dot_general(
@@ -196,7 +199,7 @@
                 for t in range(together):
                     for m, (i, r, unused) in enumerate(pieces):
                         key_ref[n, t, pl.ds(m * tokens, tokens), :HEAD_DIM] = keyvals[i][
-                            r, :, lanes(t)
+                            r, :, lanes(t, array_skips[i])
                         ]
                 scores = [
                     lax.dot_general(
@@ -234,6 +237,10 @@
                 arrays.append(array)
             listed.append((known[0], row, offset))
         numbered.append((slot, hops, tuple(listed)))
+    skips = (
+        first * HEAD_DIM,
+        tuple(first * HEAD_DIM if x.shape[-1] != heads * HEAD_DIM else 0 for x in arrays),
+    )
     operands = list(queries) + arrays + (list(state) if state is not None else [])
     state_shape = [(heads, HEAD_DIM, count), (heads, 8, count)]
     if final:
@@ -250,7 +257,7 @@
     return pl.pallas_call(
         functools.partial(
             attend_kernel, spaces, frames, columns, row_band, heads, together,
-            tuple(numbered), (first * HEAD_DIM,) * spaces, state is None, final,
+            tuple(numbered), skips, state is None, final,
         ),
         in_specs=[pl.BlockSpec(memory_space=pltpu.SMEM)] * 2
         + [pl.BlockSpec(memory_space=pltpu.VMEM)] * len(operands),
@@ -267,19 +274,32 @@
     )(*scalars, *operands)
 
 
-def join_kernel(parts, *refs):
-    for n, rows in enumerate(parts):
-        refs[-1][pl.ds(sum(parts[:n]), rows)] = refs[n][...]
-
-
-def join(arrays):
-    parts = tuple(x.shape[0] for x in arrays)
-    shape = (sum(parts),) + arrays[0].shape[1:]
+def join_kernel(first, parts, *refs):
+    arrays, outs = refs[: -len(parts)], refs[-len(parts) :]
+    for out_ref, part in zip(outs, parts):
+        row, width = 0, out_ref.shape[-1]
+        for n in part:
+            rows = arrays[n].shape[0]
+            skip = first if arrays[n].shape[-1] != width else 0
+            out_ref[pl.ds(row, rows)] = arrays[n][:, :, pl.ds(skip, width)]
+            row += rows
+
+
+def join(arrays, parts, chunk):
+    first, heads = chunk
+    tokens = arrays[0].shape[1]
+
+    def rows(part):
+        return sum(arrays[n].shape[0] for n in part)
+
     return pl.pallas_call(
-        functools.partial(join_kernel, parts),
+        functools.partial(join_kernel, first * HEAD_DIM, parts),
         in_specs=[pl.BlockSpec(memory_space=pltpu.VMEM)] * len(arrays),
-        out_specs=pl.BlockSpec(memory_space=pltpu.VMEM),
-        out_shape=jax.ShapeDtypeStruct(shape, arrays[0].dtype),
+        out_specs=[pl.BlockSpec(memory_space=pltpu.VMEM)] * len(parts),
+        out_shape=[
+            jax.ShapeDtypeStruct((rows(part), tokens, heads * HEAD_DIM), arrays[0].dtype)
+            for part in parts
+        ],
         compiler_params=pltpu.CompilerParams(vmem_limit_bytes=SMALL_LIMIT),
         name="join",
     )(*arrays)
@@ -342,18 +362,16 @@
         second = swap(xs[1], 1)
         return [swap(xs[0], 0), second]
 
-    own, partners, arrived = [], [], []
-    for c, (first, number) in enumerate(chunks):
-        blocks = [(offset, first * HEAD_DIM, number * HEAD_DIM) for offset in offsets]
-        if c == 0:
-            mine = [(0, f * HEAD_DIM, n * HEAD_DIM) for f, n in chunks]
-            packed = pack((k, v), blocks + mine, (), spaces, True)
-            sends, own = packed[: len(blocks)], packed[len(blocks) :]
-        else:
-            sends = pack((k, v), blocks, arrived, spaces, False)
-        arrived = [along_space(x, offset) for x, offset in zip(sends, offsets)]
-        partners.append(arrived)
-    sends = pack((q,), [(offset, 0, width) for offset in offsets], arrived, spaces, False)
+    blocks = [
+        [(offset, first * HEAD_DIM, number * HEAD_DIM) for offset in offsets]
+        for first, number in chunks
+    ]
+    *sends, own = pack((k, v), blocks[0] + [(0, 0, width)], (), spaces, True)
+    partners = [[along_space(x, offset) for x, offset in zip(sends, offsets)]]
+    firsts = swap_both([own, own])
+    sends = pack((k, v), blocks[1], partners[0] + firsts, spaces, False)
+    partners.append([along_space(x, offset) for x, offset in zip(sends, offsets)])
+    sends = pack((q,), [(offset, 0, width) for offset in offsets], partners[1], spaces, False)
     query_parts = [q] + [along_space(x, offset) for x, offset in zip(sends, offsets)]
     partners[1] = list(tie(partners[1], sends))
 
@@ -368,22 +386,22 @@
             (slot, hops, [(x, 2 * (o - 1), o) for o in offsets]) for slot, x in enumerate(message)
         ]
 
-    firsts = [swap_both([x, x]) for x in own]
     seconds = []
-    for c in range(len(chunks)):
-        ready = [join(partners[c] + [firsts[c][1 - slot]]) for slot in range(2)]
-        seconds.append(swap_both(ready))
+    for c, chunk in enumerate(chunks):
+        shared = tuple(range(len(offsets)))
+        parts = tuple(shared + (len(offsets) + 1 - slot,) for slot in range(2))
+        seconds.append(swap_both(join(partners[c] + firsts, parts, chunk)))
     states = []
     for c, chunk in enumerate(chunks):
-        pieces = [(own[c], 0, 0)] + [(x, 0, o) for x, o in zip(partners[c], offsets)]
-        groups = [(0, 0, pieces)] + own_band(firsts[c], 1)
+        pieces = [(own, 0, 0)] + [(x, 0, o) for x, o in zip(partners[c], offsets)]
+        groups = [(0, 0, pieces)] + own_band(firsts, 1)
         states.append(attend(scalars, query_parts, groups, None, False, chunk, sizes))
 
     messages = seconds
     for hops in range(2, frames - 1):
         following = []
         for c, chunk in enumerate(chunks):
-            after = [state[1] for state in (states if c == 0 else states[:c])]
+            after = [state[1] for state in states[: c + 1]]
             came = list(tie(messages[c], after))
             rows = behind if hops == last else behind + 2
             following.append(swap_both([came[1 - slot][:rows] for slot in range(2)]))
@@ -395,15 +413,15 @@
         came = list(tie(message, [state[1] for state in states]))
         ends.append(partner_bands(came, last))
 
-    own, returned = [], []
+    kept, returned = [], []
     for c, chunk in enumerate(chunks):
-        kept, *parts = attend(scalars, query_parts, ends[c], states[c], True, chunk, sizes)
-        own.append((kept, (0, chunk[0] * HEAD_DIM)))
+        mine, *parts = attend(scalars, query_parts, ends[c], states[c], True, chunk, sizes)
+        kept.append((mine, (0, chunk[0] * HEAD_DIM)))
         for offset, x in zip(offsets, parts):
             returned.append((along_space(x, -offset), (offset, chunk[0] * HEAD_DIM)))
     late = len(returned) - len(offsets)
     result = None
-    for batch in (own + returned[:late], returned[late:]):
+    for batch in (kept + returned[:late], returned[late:]):
         pieces, places = zip(*batch)
         result = put(pieces, places, result, q.shape, spaces)
     return result.reshape(queries.shape)

time: 70.8 us -> 71.7 us (1.013)
  waiting for transfers between devices: 17.3 us -> 24.8 us
  starting transfers between devices: 37 us -> 30.3 us
    ppermute x5, waiting for transfers between devices: 12.2 us -> 19.2 us  [along_space(): lax.ppermute(x, 'space', [(s, (s + offset) % spaces) for s in range(space...]
    ppermute x12 -> x10, starting transfers between devices: 30.4 us -> 24 us  [swap(): return lax.ppermute(x, 'frame', pairs)]
    ppermute x12 -> x10, waiting for transfers between devices: 5.04 us -> 5.62 us  [swap(): return lax.ppermute(x, 'frame', pairs)]
  transfers between devices with their start and end apart: 17 -> 15, of which waited for: 9 -> 8; matrix products, arithmetic and copies ran while one was open for 0% -> 0% of each run, Pallas kernels for 18% -> 18%
where the time goes in v8:
time: 71.7 us; the launch traced here: 71.5 us
  starting transfers between devices  30.3 us (42%)
  waiting for transfers between devices  24.8 us (35%)
  Pallas kernels  15.9 us (22%)
    ppermute x10, starting transfers between devices, swap(): return lax.ppermute(x, 'frame', pairs)  24 us
    ppermute x5, waiting for transfers between devices, along_space(): lax.ppermute(x, 'space', [(s, (s + offset) % spaces) for s in range(space...  19.2 us
    pallas_call x6, Pallas kernels, attend(): pl.pallas_call(functools.partial(attend_kernel, spaces, frames, columns,...  11.7 us
    ppermute x5, starting transfers between devices, along_space(): lax.ppermute(x, 'space', [(s, (s + offset) % spaces) for s in range(space...  6.33 us
    ppermute x10, waiting for transfers between devices, swap(): return lax.ppermute(x, 'frame', pairs)  5.62 us
    pallas_call x3, Pallas kernels, pack(): pl.pallas_call(functools.partial(pack_kernel, spaces, tuple(jobs), staged...  2.53 us
    pallas_call x2, Pallas kernels, put(): pl.pallas_call(functools.partial(put_kernel, spaces, tuple(places)), in_s...  1.45 us
  transfers between devices with their start and end apart: 15, of which 8 were waited for; matrix products, arithmetic and copies ran while one was open for 0% of the time, Pallas kernels for 18%

profile of v8, /device:TPU:0, one launch (start us, length us, event | category | flops | bytes accessed | tf_op | source)
XLA Modules:
  0.0 71.5 jit_solution(1303364593494272642)
XLA Ops:
  0.0 0.0 copy-start.1
  0.0 0.0 copy-start.2
  0.0 2.3 %pack.3 = (bf16[2,192,384]{2,1,0:T(8,128)(2,1)}, bf16[2,192,768]{2,1,0:T(8,128)(2,1)}) custom-call(bf16[192,1536]{1,0:T(8,128)(2,1)} %bitcast.11, bf16[192,1536]{1,0:T(8,128)(2,1)} %bitcast.13), custom_call_target="tpu_custom_call" | custom-call | tf_op jit(solution)/shard_map/pack/pallas_call | solution.py:64
  2.3 0.7 collective-permute-start.2
  3.0 5.9 %collective-permute-start.1 = (bf16[2,192,768]{2,1,0:T(8,128)(2,1)}, bf16[2,192,768]{2,1,0:T(8,128)(2,1)S(1)}, u32[]{:S(2)}, u32[]{:S(2)}) collective-permute-start(bf16[2,192,768]{2,1,0:T(8,128)(2,1)} %get-tuple-element.32.refs_2_), channel_id=1, source_target_pairs={{0,4},{4,0},{8,12},{12,8},{1,5},{5,1},{9,13},{13,9},{2,6},{6,2},{1... | collective-permute-start | bytes 1769480 | tf_op jit(solution)/shard_map/ppermute | solution.py:359
  8.9 1.5 %collective-permute-start = (bf16[2,192,384]{2,1,0:T(8,128)(2,1)}, bf16[2,192,384]{2,1,0:T(8,128)(2,1)S(1)}, u32[]{:S(2)}, u32[]{:S(2)}) collective-permute-start(bf16[2,192,384]{2,1,0:T(8,128)(2,1)} %get-tuple-element.31), channel_id=1, source_target_pairs={{0,2},{2,0},{1,3},{3,1},{4,6},{6,4},{5,7},{7,5},{8,10},{10,8},{9,1... | collective-permute-start | bytes 884744 | tf_op jit(solution)/shard_map/ppermute | solution.py:351
  10.3 6.9 %collective-permute-done.refs_2_.refs_0_.refs_3_ = bf16[2,192,384]{2,1,0:T(8,128)(2,1)S(1)} collective-permute-done((bf16[2,192,384]{2,1,0:T(8,128)(2,1)}, bf16[2,192,384]{2,1,0:T(8,128)(2,1)S(1)}, u32[]{:S(2)}, u32[]{:S(2)}) %collective-permute-start) | collective-permute-done | bytes 294944 | tf_op jit(solution)/shard_map/ppermute | solution.py:351
  17.3 0.0 collective-permute-done.2.refs_4_.refs_2_.refs_5_
  17.3 4.9 %collective-permute-done.1.refs_3_.refs_1_.refs_4_ = bf16[2,192,768]{2,1,0:T(8,128)(2,1)S(1)} collective-permute-done((bf16[2,192,768]{2,1,0:T(8,128)(2,1)}, bf16[2,192,768]{2,1,0:T(8,128)(2,1)S(1)}, u32[]{:S(2)}, u32[]{:S(2)}) %collective-permute-start.1) | collective-permute-done | bytes 589856 | tf_op jit(solution)/shard_map/ppermute | solution.py:359
  22.1 0.0 copy-done.1
  22.1 0.0 copy-done.2
  22.1 0.2 pack.4
  22.3 0.0 copy-start
  22.3 1.6 %collective-permute-start.3 = (bf16[2,192,384]{2,1,0:T(8,128)(2,1)S(1)}, bf16[2,192,384]{2,1,0:T(8,128)(2,1)S(1)}, u32[]{:S(2)}, u32[]{:S(2)}) collective-permute-start(bf16[2,192,384]{2,1,0:T(8,128)(2,1)S(1)} %pack.4), channel_id=1, source_target_pairs={{0,2},{2,0},{1,3},{3,1},{4,6},{6,4},{5,7},{7,5},{8,10},{10,8},{9,1... | collective-permute-start | bytes 884744 | tf_op jit(solution)/shard_map/ppermute | solution.py:351
  23.9 0.1 join.3
  24.0 1.8 %collective-permute-start.7 = (bf16[4,192,384]{2,1,0:T(8,128)(2,1)S(1)}, bf16[4,192,384]{2,1,0:T(8,128)(2,1)S(1)}, u32[]{:S(2)}, u32[]{:S(2)}) collective-permute-start(bf16[4,192,384]{2,1,0:T(8,128)(2,1)S(1)} %get-tuple-element.35), channel_id=1, source_target_pairs={{0,4},{4,0},{8,12},{12,8},{1,5},{5,1},{9,13},{13,9},{2,6},{6,2},{1... | collective-permute-start | bytes 1769480 | tf_op jit(solution)/shard_map/ppermute | solution.py:359
  25.8 0.7 collective-permute-start.8
  26.5 3.8 %collective-permute-done.3.refs_1_.refs_0_ = bf16[2,192,384]{2,1,0:T(8,128)(2,1)S(1)} collective-permute-done((bf16[2,192,384]{2,1,0:T(8,128)(2,1)S(1)}, bf16[2,192,384]{2,1,0:T(8,128)(2,1)S(1)}, u32[]{:S(2)}, u32[]{:S(2)}) %collective-permute-start.3) | collective-permute-done | bytes 294944 | tf_op jit(solution)/shard_map/ppermute | solution.py:351
  30.3 0.0 copy-done
  30.3 0.1 pack.5.refs_1_
  30.4 0.0 copy-start.3
  30.4 0.1 join.2
  30.5 0.0 copy-start.4
  30.5 0.0 copy-start.5
  30.5 1.5 %collective-permute-start.5 = (bf16[4,192,384]{2,1,0:T(8,128)(2,1)S(1)}, bf16[4,192,384]{2,1,0:T(8,128)(2,1)S(1)}, u32[]{:S(2)}, u32[]{:S(2)}) collective-permute-start(bf16[4,192,384]{2,1,0:T(8,128)(2,1)S(1)} %get-tuple-element.33), channel_id=1, source_target_pairs={{0,4},{4,0},{8,12},{12,8},{1,5},{5,1},{9,13},{13,9},{2,6},{6,2},{1... | collective-permute-start | bytes 1769480 | tf_op jit(solution)/shard_map/ppermute | solution.py:359
  32.0 0.7 collective-permute-start.6
  32.7 1.6 %collective-permute-start.4 = (bf16[192,768]{1,0:T(8,128)(2,1)S(1)}, bf16[192,768]{1,0:T(8,128)(2,1)S(1)}, u32[]{:S(2)}, u32[]{:S(2)}) collective-permute-start(bf16[192,768]{1,0:T(8,128)(2,1)S(1)} %pack.5.refs_1_), channel_id=1, source_target_pairs={{0,2},{2,0},{1,3},{3,1},{4,6},{6,4},{5,7},{7,5},{8,10},{10,8},{9,1... | collective-permute-start | bytes 884744 | tf_op jit(solution)/shard_map/ppermute | solution.py:351
  34.3 5.2 %collective-permute-done.4.refs_1_ = bf16[192,768]{1,0:T(8,128)(2,1)S(1)} collective-permute-done((bf16[192,768]{1,0:T(8,128)(2,1)S(1)}, bf16[192,768]{1,0:T(8,128)(2,1)S(1)}, u32[]{:S(2)}, u32[]{:S(2)}) %collective-permute-start.4) | collective-permute-done | bytes 294944 | tf_op jit(solution)/shard_map/ppermute | solution.py:351
  39.5 0.0 copy-done.3
  39.5 0.0 copy-done.4
  39.5 0.0 copy-done.5
  39.5 2.2 %attend.4 = (f32[3,128,384]{2,1,0:T(8,128)S(1)}, f32[3,8,384]{2,1,0:T(8,128)S(1)}) custom-call(s32[4,4]{1,0:T(4,128)S(1)} %copy-done.4, s32[4]{0:T(128)S(1)} %copy-done.5, bf16[192,1536]{1,0:T(8,128)(2,1)S(1)} %bitcast.5, bf16[192,768]{1,0:T(8,128)(2,1)S(1)} %collective-permute-done.4.refs_1_, bf16[2,192,768]{2,1,0:T(8,128)(2,1)S(1)} %copy-done.3, ...), custom_call_target="tpu_custom_call" | custom-call | flops 452984832 | bytes 1179648 | tf_op jit(solution)/shard_map/attend/pallas_call | solution.py:257
  41.7 0.0 collective-permute-done.7.refs_0_
  41.8 0.0 collective-permute-done.8.refs_1_
  41.9 0.7 collective-permute-start.13
  42.5 5.8 %collective-permute-start.12 = (bf16[2,192,384]{2,1,0:T(8,128)(2,1)S(1)}, bf16[2,192,384]{2,1,0:T(8,128)(2,1)S(1)}, u32[]{:S(2)}, u32[]{:S(2)}) collective-permute-start(bf16[2,192,384]{2,1,0:T(8,128)(2,1)S(1)} %slice.14), channel_id=1, source_target_pairs={{0,4},{4,0},{8,12},{12,8},{1,5},{5,1},{9,13},{13,9},{2,6},{6,2},{1... | collective-permute-start | bytes 884744 | tf_op jit(solution)/shard_map/ppermute | solution.py:359
  48.3 2.2 %attend.6 = (f32[3,128,384]{2,1,0:T(8,128)S(1)}, f32[3,8,384]{2,1,0:T(8,128)S(1)}) custom-call(s32[4,4]{1,0:T(4,128)S(1)} %copy-done.4, s32[4]{0:T(128)S(1)} %copy-done.5, bf16[192,1536]{1,0:T(8,128)(2,1)S(1)} %bitcast.6, bf16[192,768]{1,0:T(8,128)(2,1)S(1)} %collective-permute-done.4.refs_1_, bf16[2,192,768]{2,1,0:T(8,128)(2,1)S(1)} %copy-done.3, ...), custom_call_target="tpu_custom_call" | custom-call | flops 452984832 | bytes 1179648 | tf_op jit(solution)/shard_map/attend/pallas_call | solution.py:257
  50.6 2.1 %attend.5 = (f32[3,128,384]{2,1,0:T(8,128)S(1)}, f32[3,8,384]{2,1,0:T(8,128)S(1)}) custom-call(s32[4,4]{1,0:T(4,128)S(1)} %copy-done.4, s32[4]{0:T(128)S(1)} %copy-done.5, bf16[192,1536]{1,0:T(8,128)(2,1)S(1)} %bitcast.7, bf16[192,768]{1,0:T(8,128)(2,1)S(1)} %collective-permute-done.4.refs_1_, bf16[4,192,384]{2,1,0:T(8,128)(2,1)S(1)} %get-tuple-element.38.refs_2_, ...), custom_call_target="tpu_custom_call" | custom-call | flops 452984832 | bytes 1179648 | tf_op jit(solution)/shard_map/attend/pallas_call | solution.py:257
  52.6 0.3 collective-permute-done.5.refs_0_
  52.9 0.0 collective-permute-done.6.refs_1_
  53.0 0.7 collective-permute-start.10
  53.7 5.6 %collective-permute-start.9 = (bf16[2,192,384]{2,1,0:T(8,128)(2,1)S(1)}, bf16[2,192,384]{2,1,0:T(8,128)(2,1)S(1)}, u32[]{:S(2)}, u32[]{:S(2)}) collective-permute-start(bf16[2,192,384]{2,1,0:T(8,128)(2,1)S(1)} %slice.12), channel_id=1, source_target_pairs={{0,4},{4,0},{8,12},{12,8},{1,5},{5,1},{9,13},{13,9},{2,6},{6,2},{1... | collective-permute-start | bytes 884744 | tf_op jit(solution)/shard_map/ppermute | solution.py:359
  59.4 2.1 %attend.7 = (f32[3,128,384]{2,1,0:T(8,128)S(1)}, f32[3,8,384]{2,1,0:T(8,128)S(1)}) custom-call(s32[4,4]{1,0:T(4,128)S(1)} %copy-done.4, s32[4]{0:T(128)S(1)} %copy-done.5, bf16[192,1536]{1,0:T(8,128)(2,1)S(1)} %bitcast.8, bf16[192,768]{1,0:T(8,128)(2,1)S(1)} %collective-permute-done.4.refs_1_, bf16[4,192,384]{2,1,0:T(8,128)(2,1)S(1)} %get-tuple-element.44.refs_2_, ...), custom_call_target="tpu_custom_call" | custom-call | flops 452984832 | bytes 1179648 | tf_op jit(solution)/shard_map/attend/pallas_call | solution.py:257
  61.4 0.0 collective-permute-done.13.refs_1_
  61.5 0.0 collective-permute-done.12.refs_0_
  61.5 1.5 %attend_final.3 = (bf16[192,384]{1,0:T(8,128)(2,1)S(1)}, bf16[192,384]{1,0:T(8,128)(2,1)S(1)}) custom-call(s32[4,4]{1,0:T(4,128)S(1)} %copy-done.4, s32[4]{0:T(128)S(1)} %copy-done.5, bf16[192,1536]{1,0:T(8,128)(2,1)S(1)} %bitcast.9, bf16[192,768]{1,0:T(8,128)(2,1)S(1)} %collective-permute-done.4.refs_1_, ...), custom_call_target="tpu_custom_call" | custom-call | flops 226492416 | bytes 1179648 | tf_op jit(solution)/shard_map/attend_final/pallas_call | solution.py:257
  63.0 0.6 collective-permute-start.14
  63.6 0.0 collective-permute-done.10.refs_1_
  63.6 0.4 collective-permute-done.9.refs_0_
  64.1 1.6 %attend_final.2 = (bf16[192,384]{1,0:T(8,128)(2,1)S(1)}, bf16[192,384]{1,0:T(8,128)(2,1)S(1)}) custom-call(s32[4,4]{1,0:T(4,128)S(1)} %copy-done.4, s32[4]{0:T(128)S(1)} %copy-done.5, bf16[192,1536]{1,0:T(8,128)(2,1)S(1)} %bitcast.10, bf16[192,768]{1,0:T(8,128)(2,1)S(1)} %collective-permute-done.4.refs_1_, ...), custom_call_target="tpu_custom_call" | custom-call | flops 226492416 | bytes 1179648 | tf_op jit(solution)/shard_map/attend_final/pallas_call | solution.py:257
  65.6 1.1 %collective-permute-start.11 = (bf16[192,384]{1,0:T(8,128)(2,1)S(1)}, bf16[192,384]{1,0:T(8,128)(2,1)S(1)}, u32[]{:S(2)}, u32[]{:S(2)}) collective-permute-start(bf16[192,384]{1,0:T(8,128)(2,1)S(1)} %get-tuple-element.50), channel_id=1, source_target_pairs={{0,2},{2,0},{1,3},{3,1},{4,6},{6,4},{5,7},{7,5},{8,10},{10,8},{9,1... | collective-permute-start | bytes 442376 | tf_op jit(solution)/shard_map/ppermute | solution.py:351
  66.8 1.5 %collective-permute-done.14.refs_2_ = bf16[192,384]{1,0:T(8,128)(2,1)S(1)} collective-permute-done((bf16[192,384]{1,0:T(8,128)(2,1)S(1)}, bf16[192,384]{1,0:T(8,128)(2,1)S(1)}, u32[]{:S(2)}, u32[]{:S(2)}) %collective-permute-start.14) | collective-permute-done | bytes 147488 | tf_op jit(solution)/shard_map/ppermute | solution.py:351
  68.2 0.8 %put.2.refs_1_ = bf16[192,1536]{1,0:T(8,128)(2,1)} custom-call(bf16[192,384]{1,0:T(8,128)(2,1)S(1)} %get-tuple-element.54.refs_0_, bf16[192,384]{1,0:T(8,128)(2,1)S(1)} %get-tuple-element.55.refs_1_, bf16[192,384]{1,0:T(8,128)(2,1)S(1)} %collective-permute-done.14.refs_2_), custom_call_target="tpu_custom_call" | custom-call | tf_op jit(solution)/shard_map/put/pallas_call | solution.py:325
  69.0 1.8 %collective-permute-done.11.refs_0_ = bf16[192,384]{1,0:T(8,128)(2,1)S(1)} collective-permute-done((bf16[192,384]{1,0:T(8,128)(2,1)S(1)}, bf16[192,384]{1,0:T(8,128)(2,1)S(1)}, u32[]{:S(2)}, u32[]{:S(2)}) %collective-permute-start.11) | collective-permute-done | bytes 147488 | tf_op jit(solution)/shard_map/ppermute | solution.py:351
  70.8 0.7 put.3
  (9 shorter events, 0.1 us)
Async XLA Ops:
  0.0 22.1 %copy-start.1 = (bf16[1,4,48,1536]{3,2,1,0:T(8,128)(2,1)S(1)}, bf16[1,4,48,1536]{3,2,1,0:T(8,128)(2,1)}, u32[]{:S(2)}) copy-start(bf16[1,4,48,1536]{3,2,1,0:T(8,128)(2,1)} %param.6) | copy-start | bytes 1769476
  0.0 22.1 %copy-start.2 = (bf16[1,4,48,1536]{3,2,1,0:T(8,128)(2,1)S(1)}, bf16[1,4,48,1536]{3,2,1,0:T(8,128)(2,1)}, u32[]{:S(2)}) copy-start(bf16[1,4,48,1536]{3,2,1,0:T(8,128)(2,1)} %param.7) | copy-start | bytes 1769476
  2.3 15.0 %collective-permute-start.2 = (bf16[2,192,768]{2,1,0:T(8,128)(2,1)}, bf16[2,192,768]{2,1,0:T(8,128)(2,1)S(1)}, u32[]{:S(2)}, u32[]{:S(2)}) collective-permute-start(bf16[2,192,768]{2,1,0:T(8,128)(2,1)} %get-tuple-element.32.refs_2_), channel_id=1, source_target_pairs={{4,8},{8,4},{5,9},{9,5},{6,10},{10,6},{7,11},{11,7},{20,24},{24,20... | collective-permute-start | bytes 1769480 | tf_op jit(solution)/shard_map/ppermute | solution.py:359
  3.0 19.1 %collective-permute-start.1 = (bf16[2,192,768]{2,1,0:T(8,128)(2,1)}, bf16[2,192,768]{2,1,0:T(8,128)(2,1)S(1)}, u32[]{:S(2)}, u32[]{:S(2)}) collective-permute-start(bf16[2,192,768]{2,1,0:T(8,128)(2,1)} %get-tuple-element.32.refs_2_), channel_id=1, source_target_pairs={{0,4},{4,0},{8,12},{12,8},{1,5},{5,1},{9,13},{13,9},{2,6},{6,2},{1... | collective-permute-start | bytes 1769480 | tf_op jit(solution)/shard_map/ppermute | solution.py:359
  8.9 8.4 %collective-permute-start = (bf16[2,192,384]{2,1,0:T(8,128)(2,1)}, bf16[2,192,384]{2,1,0:T(8,128)(2,1)S(1)}, u32[]{:S(2)}, u32[]{:S(2)}) collective-permute-start(bf16[2,192,384]{2,1,0:T(8,128)(2,1)} %get-tuple-element.31), channel_id=1, source_target_pairs={{0,2},{2,0},{1,3},{3,1},{4,6},{6,4},{5,7},{7,5},{8,10},{10,8},{9,1... | collective-permute-start | bytes 884744 | tf_op jit(solution)/shard_map/ppermute | solution.py:351
  22.3 8.0 %copy-start = (bf16[1,4,48,1536]{3,2,1,0:T(8,128)(2,1)S(1)}, bf16[1,4,48,1536]{3,2,1,0:T(8,128)(2,1)}, u32[]{:S(2)}) copy-start(bf16[1,4,48,1536]{3,2,1,0:T(8,128)(2,1)} %param.5) | copy-start | bytes 1769476
  22.3 7.9 %collective-permute-start.3 = (bf16[2,192,384]{2,1,0:T(8,128)(2,1)S(1)}, bf16[2,192,384]{2,1,0:T(8,128)(2,1)S(1)}, u32[]{:S(2)}, u32[]{:S(2)}) collective-permute-start(bf16[2,192,384]{2,1,0:T(8,128)(2,1)S(1)} %pack.4), channel_id=1, source_target_pairs={{0,2},{2,0},{1,3},{3,1},{4,6},{6,4},{5,7},{7,5},{8,10},{10,8},{9,1... | collective-permute-start | bytes 884744 | tf_op jit(solution)/shard_map/ppermute | solution.py:351
  24.0 17.8 %collective-permute-start.7 = (bf16[4,192,384]{2,1,0:T(8,128)(2,1)S(1)}, bf16[4,192,384]{2,1,0:T(8,128)(2,1)S(1)}, u32[]{:S(2)}, u32[]{:S(2)}) collective-permute-start(bf16[4,192,384]{2,1,0:T(8,128)(2,1)S(1)} %get-tuple-element.35), channel_id=1, source_target_pairs={{0,4},{4,0},{8,12},{12,8},{1,5},{5,1},{9,13},{13,9},{2,6},{6,2},{1... | collective-permute-start | bytes 1769480 | tf_op jit(solution)/shard_map/ppermute | solution.py:359
  25.8 16.0 %collective-permute-start.8 = (bf16[4,192,384]{2,1,0:T(8,128)(2,1)S(1)}, bf16[4,192,384]{2,1,0:T(8,128)(2,1)S(1)}, u32[]{:S(2)}, u32[]{:S(2)}) collective-permute-start(bf16[4,192,384]{2,1,0:T(8,128)(2,1)S(1)} %get-tuple-element.36), channel_id=1, source_target_pairs={{4,8},{8,4},{5,9},{9,5},{6,10},{10,6},{7,11},{11,7},{20,24},{24,20... | collective-permute-start | bytes 1769480 | tf_op jit(solution)/shard_map/ppermute | solution.py:359
  30.4 9.1 %copy-start.3 = (bf16[2,192,768]{2,1,0:T(8,128)(2,1)S(1)}, bf16[2,192,768]{2,1,0:T(8,128)(2,1)}, u32[]{:S(2)}) copy-start(bf16[2,192,768]{2,1,0:T(8,128)(2,1)} %get-tuple-element.32.refs_2_) | copy-start | bytes 1769476
  30.5 9.0 %copy-start.4 = (s32[4,4]{1,0:T(4,128)S(1)}, s32[4,4]{1,0:T(4,128)}, u32[]{:S(2)}) copy-start(s32[4,4]{1,0:T(4,128)} %flags_ref.11) | copy-start | bytes 196
  30.5 9.0 %copy-start.5 = (s32[4]{0:T(128)S(1)}, s32[4]{0:T(128)}, u32[]{:S(2)}) copy-start(s32[4]{0:T(128)} %widths_ref.11) | copy-start | bytes 52
  30.5 22.4 %collective-permute-start.5 = (bf16[4,192,384]{2,1,0:T(8,128)(2,1)S(1)}, bf16[4,192,384]{2,1,0:T(8,128)(2,1)S(1)}, u32[]{:S(2)}, u32[]{:S(2)}) collective-permute-start(bf16[4,192,384]{2,1,0:T(8,128)(2,1)S(1)} %get-tuple-element.33), channel_id=1, source_target_pairs={{0,4},{4,0},{8,12},{12,8},{1,5},{5,1},{9,13},{13,9},{2,6},{6,2},{1... | collective-permute-start | bytes 1769480 | tf_op jit(solution)/shard_map/ppermute | solution.py:359
  32.0 20.9 %collective-permute-start.6 = (bf16[4,192,384]{2,1,0:T(8,128)(2,1)S(1)}, bf16[4,192,384]{2,1,0:T(8,128)(2,1)S(1)}, u32[]{:S(2)}, u32[]{:S(2)}) collective-permute-start(bf16[4,192,384]{2,1,0:T(8,128)(2,1)S(1)} %get-tuple-element.34), channel_id=1, source_target_pairs={{4,8},{8,4},{5,9},{9,5},{6,10},{10,6},{7,11},{11,7},{20,24},{24,20... | collective-permute-start | bytes 1769480 | tf_op jit(solution)/shard_map/ppermute | solution.py:359
  32.7 6.8 %collective-permute-start.4 = (bf16[192,768]{1,0:T(8,128)(2,1)S(1)}, bf16[192,768]{1,0:T(8,128)(2,1)S(1)}, u32[]{:S(2)}, u32[]{:S(2)}) collective-permute-start(bf16[192,768]{1,0:T(8,128)(2,1)S(1)} %pack.5.refs_1_), channel_id=1, source_target_pairs={{0,2},{2,0},{1,3},{3,1},{4,6},{6,4},{5,7},{7,5},{8,10},{10,8},{9,1... | collective-permute-start | bytes 884744 | tf_op jit(solution)/shard_map/ppermute | solution.py:351
  41.9 19.6 %collective-permute-start.13 = (bf16[2,192,384]{2,1,0:T(8,128)(2,1)S(1)}, bf16[2,192,384]{2,1,0:T(8,128)(2,1)S(1)}, u32[]{:S(2)}, u32[]{:S(2)}) collective-permute-start(bf16[2,192,384]{2,1,0:T(8,128)(2,1)S(1)} %slice.15), channel_id=1, source_target_pairs={{4,8},{8,4},{5,9},{9,5},{6,10},{10,6},{7,11},{11,7},{20,24},{24,20... | collective-permute-start | bytes 884744 | tf_op jit(solution)/shard_map/ppermute | solution.py:359
  42.5 18.9 %collective-permute-start.12 = (bf16[2,192,384]{2,1,0:T(8,128)(2,1)S(1)}, bf16[2,192,384]{2,1,0:T(8,128)(2,1)S(1)}, u32[]{:S(2)}, u32[]{:S(2)}) collective-permute-start(bf16[2,192,384]{2,1,0:T(8,128)(2,1)S(1)} %slice.14), channel_id=1, source_target_pairs={{0,4},{4,0},{8,12},{12,8},{1,5},{5,1},{9,13},{13,9},{2,6},{6,2},{1... | collective-permute-start | bytes 884744 | tf_op jit(solution)/shard_map/ppermute | solution.py:359
  53.0 10.6 %collective-permute-start.10 = (bf16[2,192,384]{2,1,0:T(8,128)(2,1)S(1)}, bf16[2,192,384]{2,1,0:T(8,128)(2,1)S(1)}, u32[]{:S(2)}, u32[]{:S(2)}) collective-permute-start(bf16[2,192,384]{2,1,0:T(8,128)(2,1)S(1)} %slice.13), channel_id=1, source_target_pairs={{4,8},{8,4},{5,9},{9,5},{6,10},{10,6},{7,11},{11,7},{20,24},{24,20... | collective-permute-start | bytes 884744 | tf_op jit(solution)/shard_map/ppermute | solution.py:359
  53.7 10.4 %collective-permute-start.9 = (bf16[2,192,384]{2,1,0:T(8,128)(2,1)S(1)}, bf16[2,192,384]{2,1,0:T(8,128)(2,1)S(1)}, u32[]{:S(2)}, u32[]{:S(2)}) collective-permute-start(bf16[2,192,384]{2,1,0:T(8,128)(2,1)S(1)} %slice.12), channel_id=1, source_target_pairs={{0,4},{4,0},{8,12},{12,8},{1,5},{5,1},{9,13},{13,9},{2,6},{6,2},{1... | collective-permute-start | bytes 884744 | tf_op jit(solution)/shard_map/ppermute | solution.py:359
  63.0 5.2 %collective-permute-start.14 = (bf16[192,384]{1,0:T(8,128)(2,1)S(1)}, bf16[192,384]{1,0:T(8,128)(2,1)S(1)}, u32[]{:S(2)}, u32[]{:S(2)}) collective-permute-start(bf16[192,384]{1,0:T(8,128)(2,1)S(1)} %get-tuple-element.56), channel_id=1, source_target_pairs={{0,2},{2,0},{1,3},{3,1},{4,6},{6,4},{5,7},{7,5},{8,10},{10,8},{9,1... | collective-permute-start | bytes 442376 | tf_op jit(solution)/shard_map/ppermute | solution.py:351
  65.6 5.2 %collective-permute-start.11 = (bf16[192,384]{1,0:T(8,128)(2,1)S(1)}, bf16[192,384]{1,0:T(8,128)(2,1)S(1)}, u32[]{:S(2)}, u32[]{:S(2)}) collective-permute-start(bf16[192,384]{1,0:T(8,128)(2,1)S(1)} %get-tuple-element.50), channel_id=1, source_target_pairs={{0,2},{2,0},{1,3},{3,1},{4,6},{6,4},{5,7},{7,5},{8,10},{10,8},{9,1... | collective-permute-start | bytes 442376 | tf_op jit(solution)/shard_map/ppermute | solution.py:351

commit v9 on v7

--- a/solution.py
+++ b/solution.py
@@ -268,18 +268,27 @@
 
 
 def join_kernel(parts, *refs):
-    for n, rows in enumerate(parts):
-        refs[-1][pl.ds(sum(parts[:n]), rows)] = refs[n][...]
-
-
-def join(arrays):
-    parts = tuple(x.shape[0] for x in arrays)
-    shape = (sum(parts),) + arrays[0].shape[1:]
+    arrays, outs = refs[: -len(parts)], refs[-len(parts) :]
+    for out_ref, part in zip(outs, parts):
+        row = 0
+        for n in part:
+            rows = arrays[n].shape[0]
+            out_ref[pl.ds(row, rows)] = arrays[n][...]
+            row += rows
+
+
+def join(arrays, parts):
+    def rows(part):
+        return sum(arrays[n].shape[0] for n in part)
+
     return pl.pallas_call(
         functools.partial(join_kernel, parts),
         in_specs=[pl.BlockSpec(memory_space=pltpu.VMEM)] * len(arrays),
-        out_specs=pl.BlockSpec(memory_space=pltpu.VMEM),
-        out_shape=jax.ShapeDtypeStruct(shape, arrays[0].dtype),
+        out_specs=[pl.BlockSpec(memory_space=pltpu.VMEM)] * len(parts),
+        out_shape=[
+            jax.ShapeDtypeStruct((rows(part),) + arrays[0].shape[1:], arrays[0].dtype)
+            for part in parts
+        ],
         compiler_params=pltpu.CompilerParams(vmem_limit_bytes=SMALL_LIMIT),
         name="join",
     )(*arrays)
@@ -371,8 +380,9 @@
     firsts = [swap_both([x, x]) for x in own]
     seconds = []
     for c in range(len(chunks)):
-        ready = [join(partners[c] + [firsts[c][1 - slot]]) for slot in range(2)]
-        seconds.append(swap_both(ready))
+        shared = tuple(range(len(offsets)))
+        parts = tuple(shared + (len(offsets) + 1 - slot,) for slot in range(2))
+        seconds.append(swap_both(join(partners[c] + firsts[c], parts)))
     states = []
     for c, chunk in enumerate(chunks):
         pieces = [(own[c], 0, 0)] + [(x, 0, o) for x, o in zip(partners[c], offsets)]
@@ -383,8 +393,8 @@
     for hops in range(2, frames - 1):
         following = []
         for c, chunk in enumerate(chunks):
-            after = [state[1] for state in (states if c == 0 else states[:c])]
-            came = list(tie(messages[c], after))
+            after = [state[1] for state in states[: c + 1]]
+            came = list(tie(messages[c][::-1], after))[::-1]
             rows = behind if hops == last else behind + 2
             following.append(swap_both([came[1 - slot][:rows] for slot in range(2)]))
             groups = partner_bands(came, hops - 1) + own_band(came, hops)

time: 70.8 us -> 70.5 us (level)
  waiting for transfers between devices: 17.3 us -> 23.6 us
  starting transfers between devices: 37 us -> 32.5 us
  Pallas kernels: 15.9 us -> 13.4 us
    ppermute x12, waiting for transfers between devices: 5.04 us -> 11.7 us  [swap(): return lax.ppermute(x, 'frame', pairs)]
    ppermute x12, starting transfers between devices: 30.4 us -> 26 us  [swap(): return lax.ppermute(x, 'frame', pairs)]
    pallas_call x6, Pallas kernels: 11.7 us -> 9.17 us  [attend(): pl.pallas_call(functools.partial(attend_kernel, spaces, frames, columns,...]
  transfers between devices with their start and end apart: 17 -> 17, of which waited for: 9 -> 8; matrix products, arithmetic and copies ran while one was open for 0% -> 0% of each run, Pallas kernels for 18% -> 15%
where the time goes in v9:
time: 70.5 us; the launch traced here: 69.9 us
  starting transfers between devices  32.5 us (46%)
  waiting for transfers between devices  23.6 us (33%)
  Pallas kernels  13.4 us (19%)
    ppermute x12, starting transfers between devices, swap(): return lax.ppermute(x, 'frame', pairs)  26 us
    ppermute x5, waiting for transfers between devices, along_space(): lax.ppermute(x, 'space', [(s, (s + offset) % spaces) for s in range(space...  12 us
    ppermute x12, waiting for transfers between devices, swap(): return lax.ppermute(x, 'frame', pairs)  11.7 us
    pallas_call x6, Pallas kernels, attend(): pl.pallas_call(functools.partial(attend_kernel, spaces, frames, columns,...  9.17 us
    ppermute x5, starting transfers between devices, along_space(): lax.ppermute(x, 'space', [(s, (s + offset) % spaces) for s in range(space...  6.54 us
    pallas_call x3, Pallas kernels, pack(): pl.pallas_call(functools.partial(pack_kernel, spaces, tuple(jobs), staged...  2.55 us
    pallas_call x2, Pallas kernels, put(): pl.pallas_call(functools.partial(put_kernel, spaces, tuple(places)), in_s...  1.45 us
  transfers between devices with their start and end apart: 17, of which 8 were waited for; matrix products, arithmetic and copies ran while one was open for 0% of the time, Pallas kernels for 15%

profile of v9, /device:TPU:0, one launch (start us, length us, event | category | flops | bytes accessed | tf_op | source)
XLA Modules:
  0.0 69.9 jit_solution(5323343758220231434)
XLA Ops:
  0.0 0.0 copy-start.1
  0.0 0.0 copy-start.2
  0.0 2.3 %pack.3 = (bf16[2,192,384]{2,1,0:T(8,128)(2,1)}, bf16[2,192,384]{2,1,0:T(8,128)(2,1)}, bf16[2,192,384]{2,1,0:T(8,128)(2,1)}) custom-call(bf16[192,1536]{1,0:T(8,128)(2,1)} %bitcast.11, bf16[192,1536]{1,0:T(8,128)(2,1)} %bitcast.13), custom_call_target="tpu_custom_call" | custom-call | tf_op jit(solution)/shard_map/pack/pallas_call | solution.py:64
  2.3 3.0 %collective-permute-start = (bf16[2,192,384]{2,1,0:T(8,128)(2,1)}, bf16[2,192,384]{2,1,0:T(8,128)(2,1)S(1)}, u32[]{:S(2)}, u32[]{:S(2)}) collective-permute-start(bf16[2,192,384]{2,1,0:T(8,128)(2,1)} %get-tuple-element.32), channel_id=1, source_target_pairs={{0,2},{2,0},{1,3},{3,1},{4,6},{6,4},{5,7},{7,5},{8,10},{10,8},{9,1... | collective-permute-start | bytes 884744 | tf_op jit(solution)/shard_map/ppermute | solution.py:340
  5.3 0.0 copy-start.3
  5.3 0.8 %collective-permute-start.8 = (bf16[2,192,384]{2,1,0:T(8,128)(2,1)}, bf16[2,192,384]{2,1,0:T(8,128)(2,1)S(1)}, u32[]{:S(2)}, u32[]{:S(2)}) collective-permute-start(bf16[2,192,384]{2,1,0:T(8,128)(2,1)} %get-tuple-element.36.refs_2_), channel_id=1, source_target_pairs={{4,8},{8,4},{5,9},{9,5},{6,10},{10,6},{7,11},{11,7},{20,24},{24,20... | collective-permute-start | bytes 884744 | tf_op jit(solution)/shard_map/ppermute | solution.py:348
  6.1 4.4 %collective-permute-start.7 = (bf16[2,192,384]{2,1,0:T(8,128)(2,1)}, bf16[2,192,384]{2,1,0:T(8,128)(2,1)S(1)}, u32[]{:S(2)}, u32[]{:S(2)}) collective-permute-start(bf16[2,192,384]{2,1,0:T(8,128)(2,1)} %get-tuple-element.36.refs_2_), channel_id=1, source_target_pairs={{0,4},{4,0},{8,12},{12,8},{1,5},{5,1},{9,13},{13,9},{2,6},{6,2},{1... | collective-permute-start | bytes 884744 | tf_op jit(solution)/shard_map/ppermute | solution.py:348
  10.5 2.0 %collective-permute-done.refs_2_.refs_0_.refs_3_ = bf16[2,192,384]{2,1,0:T(8,128)(2,1)S(1)} collective-permute-done((bf16[2,192,384]{2,1,0:T(8,128)(2,1)}, bf16[2,192,384]{2,1,0:T(8,128)(2,1)S(1)}, u32[]{:S(2)}, u32[]{:S(2)}) %collective-permute-start) | collective-permute-done | bytes 294944 | tf_op jit(solution)/shard_map/ppermute | solution.py:340
  12.5 0.0 copy-done.1
  12.5 0.0 copy-done.2
  12.5 0.2 pack.4
  12.7 0.0 copy-start
  12.7 1.8 %collective-permute-start.1 = (bf16[2,192,384]{2,1,0:T(8,128)(2,1)S(1)}, bf16[2,192,384]{2,1,0:T(8,128)(2,1)S(1)}, u32[]{:S(2)}, u32[]{:S(2)}) collective-permute-start(bf16[2,192,384]{2,1,0:T(8,128)(2,1)S(1)} %pack.4), channel_id=1, source_target_pairs={{0,2},{2,0},{1,3},{3,1},{4,6},{6,4},{5,7},{7,5},{8,10},{10,8},{9,1... | collective-permute-start | bytes 884744 | tf_op jit(solution)/shard_map/ppermute | solution.py:340
  14.5 0.0 copy-done.3
  14.5 0.7 collective-permute-start.4
  15.2 4.4 %collective-permute-start.3 = (bf16[2,192,384]{2,1,0:T(8,128)(2,1)S(1)}, bf16[2,192,384]{2,1,0:T(8,128)(2,1)S(1)}, u32[]{:S(2)}, u32[]{:S(2)}) collective-permute-start(bf16[2,192,384]{2,1,0:T(8,128)(2,1)S(1)} %copy-done.3), channel_id=1, source_target_pairs={{0,4},{4,0},{8,12},{12,8},{1,5},{5,1},{9,13},{13,9},{2,6},{6,2},{1... | collective-permute-start | bytes 884744 | tf_op jit(solution)/shard_map/ppermute | solution.py:348
  19.6 0.0 collective-permute-done.8.refs_2_.refs_5_
  19.6 0.0 collective-permute-done.7.refs_1_.refs_4_
  19.7 0.1 join.3
  19.8 0.7 collective-permute-start.9
  20.5 1.8 %collective-permute-start.10 = (bf16[4,192,384]{2,1,0:T(8,128)(2,1)S(1)}, bf16[4,192,384]{2,1,0:T(8,128)(2,1)S(1)}, u32[]{:S(2)}, u32[]{:S(2)}) collective-permute-start(bf16[4,192,384]{2,1,0:T(8,128)(2,1)S(1)} %get-tuple-element.38), channel_id=1, source_target_pairs={{0,4},{4,0},{8,12},{12,8},{1,5},{5,1},{9,13},{13,9},{2,6},{6,2},{1... | collective-permute-start | bytes 1769480 | tf_op jit(solution)/shard_map/ppermute | solution.py:348
  22.2 0.0 collective-permute-done.1.refs_1_.refs_0_
  22.2 0.0 copy-done
  22.2 0.1 pack.5.refs_1_
  22.3 0.0 copy-start.4
  22.4 0.0 collective-permute-done.4.refs_2_.refs_5_
  22.4 5.2 %collective-permute-done.3.refs_1_.refs_4_ = bf16[2,192,384]{2,1,0:T(8,128)(2,1)S(1)} collective-permute-done((bf16[2,192,384]{2,1,0:T(8,128)(2,1)S(1)}, bf16[2,192,384]{2,1,0:T(8,128)(2,1)S(1)}, u32[]{:S(2)}, u32[]{:S(2)}) %collective-permute-start.3) | collective-permute-done | bytes 294944 | tf_op jit(solution)/shard_map/ppermute | solution.py:348
  27.6 0.1 join.2
  27.7 0.0 copy-start.5
  27.7 0.0 copy-start.6
  27.7 0.7 collective-permute-start.5
  28.4 3.7 %collective-permute-start.6 = (bf16[4,192,384]{2,1,0:T(8,128)(2,1)S(1)}, bf16[4,192,384]{2,1,0:T(8,128)(2,1)S(1)}, u32[]{:S(2)}, u32[]{:S(2)}) collective-permute-start(bf16[4,192,384]{2,1,0:T(8,128)(2,1)S(1)} %get-tuple-element.35), channel_id=1, source_target_pairs={{0,4},{4,0},{8,12},{12,8},{1,5},{5,1},{9,13},{13,9},{2,6},{6,2},{1... | collective-permute-start | bytes 1769480 | tf_op jit(solution)/shard_map/ppermute | solution.py:348
  32.2 0.5 collective-permute-start.2
  32.7 6.2 %collective-permute-done.2.refs_1_ = bf16[192,768]{1,0:T(8,128)(2,1)S(1)} collective-permute-done((bf16[192,768]{1,0:T(8,128)(2,1)S(1)}, bf16[192,768]{1,0:T(8,128)(2,1)S(1)}, u32[]{:S(2)}, u32[]{:S(2)}) %collective-permute-start.2) | collective-permute-done | bytes 294944 | tf_op jit(solution)/shard_map/ppermute | solution.py:340
  38.9 0.0 copy-done.4
  38.9 0.0 copy-done.5
  38.9 0.0 copy-done.6
  38.9 2.2 %attend.4 = (f32[3,128,384]{2,1,0:T(8,128)S(1)}, f32[3,8,384]{2,1,0:T(8,128)S(1)}) custom-call(s32[4,4]{1,0:T(4,128)S(1)} %copy-done.5, s32[4]{0:T(128)S(1)} %copy-done.6, bf16[192,1536]{1,0:T(8,128)(2,1)S(1)} %bitcast.5, bf16[192,768]{1,0:T(8,128)(2,1)S(1)} %collective-permute-done.2.refs_1_, bf16[2,192,384]{2,1,0:T(8,128)(2,1)S(1)} %copy-done.4, ...), custom_call_target="tpu_custom_call" | custom-call | flops 452984832 | bytes 1179648 | tf_op jit(solution)/shard_map/attend/pallas_call | solution.py:250
  41.1 0.0 collective-permute-done.9.refs_0_
  41.1 0.0 collective-permute-done.10.refs_1_
  41.2 0.7 collective-permute-start.15
  41.9 3.6 %collective-permute-start.14 = (bf16[2,192,384]{2,1,0:T(8,128)(2,1)S(1)}, bf16[2,192,384]{2,1,0:T(8,128)(2,1)S(1)}, u32[]{:S(2)}, u32[]{:S(2)}) collective-permute-start(bf16[2,192,384]{2,1,0:T(8,128)(2,1)S(1)} %slice.14), channel_id=1, source_target_pairs={{0,4},{4,0},{8,12},{12,8},{1,5},{5,1},{9,13},{13,9},{2,6},{6,2},{1... | collective-permute-start | bytes 884744 | tf_op jit(solution)/shard_map/ppermute | solution.py:348
  45.5 2.3 %attend.6 = (f32[3,128,384]{2,1,0:T(8,128)S(1)}, f32[3,8,384]{2,1,0:T(8,128)S(1)}) custom-call(s32[4,4]{1,0:T(4,128)S(1)} %copy-done.5, s32[4]{0:T(128)S(1)} %copy-done.6, bf16[192,1536]{1,0:T(8,128)(2,1)S(1)} %bitcast.6, bf16[192,768]{1,0:T(8,128)(2,1)S(1)} %collective-permute-done.2.refs_1_, bf16[2,192,384]{2,1,0:T(8,128)(2,1)S(1)} %copy-done.3, ...), custom_call_target="tpu_custom_call" | custom-call | flops 452984832 | bytes 1179648 | tf_op jit(solution)/shard_map/attend/pallas_call | solution.py:250
  47.8 1.4 %attend.5 = (f32[3,128,384]{2,1,0:T(8,128)S(1)}, f32[3,8,384]{2,1,0:T(8,128)S(1)}) custom-call(s32[4,4]{1,0:T(4,128)S(1)} %copy-done.5, s32[4]{0:T(128)S(1)} %copy-done.6, bf16[192,1536]{1,0:T(8,128)(2,1)S(1)} %bitcast.7, bf16[192,768]{1,0:T(8,128)(2,1)S(1)} %collective-permute-done.2.refs_1_, bf16[4,192,384]{2,1,0:T(8,128)(2,1)S(1)} %get-tuple-element.40.refs_2_, ...), custom_call_target="tpu_custom_call" | custom-call | flops 452984832 | bytes 1179648 | tf_op jit(solution)/shard_map/attend/pallas_call | solution.py:250
  49.2 0.0 collective-permute-done.5.refs_0_
  49.2 3.6 %collective-permute-done.6.refs_1_ = bf16[4,192,384]{2,1,0:T(8,128)(2,1)S(1)} collective-permute-done((bf16[4,192,384]{2,1,0:T(8,128)(2,1)S(1)}, bf16[4,192,384]{2,1,0:T(8,128)(2,1)S(1)}, u32[]{:S(2)}, u32[]{:S(2)}) %collective-permute-start.6) | collective-permute-done | bytes 589856 | tf_op jit(solution)/shard_map/ppermute | solution.py:348
  52.9 0.7 collective-permute-start.12
  53.6 3.8 %collective-permute-start.11 = (bf16[2,192,384]{2,1,0:T(8,128)(2,1)S(1)}, bf16[2,192,384]{2,1,0:T(8,128)(2,1)S(1)}, u32[]{:S(2)}, u32[]{:S(2)}) collective-permute-start(bf16[2,192,384]{2,1,0:T(8,128)(2,1)S(1)} %slice.12), channel_id=1, source_target_pairs={{0,4},{4,0},{8,12},{12,8},{1,5},{5,1},{9,13},{13,9},{2,6},{6,2},{1... | collective-permute-start | bytes 884744 | tf_op jit(solution)/shard_map/ppermute | solution.py:348
  57.4 1.4 %attend.7 = (f32[3,128,384]{2,1,0:T(8,128)S(1)}, f32[3,8,384]{2,1,0:T(8,128)S(1)}) custom-call(s32[4,4]{1,0:T(4,128)S(1)} %copy-done.5, s32[4]{0:T(128)S(1)} %copy-done.6, bf16[192,1536]{1,0:T(8,128)(2,1)S(1)} %bitcast.8, bf16[192,768]{1,0:T(8,128)(2,1)S(1)} %collective-permute-done.2.refs_1_, bf16[4,192,384]{2,1,0:T(8,128)(2,1)S(1)} %get-tuple-element.46.refs_2_, ...), custom_call_target="tpu_custom_call" | custom-call | flops 452984832 | bytes 1179648 | tf_op jit(solution)/shard_map/attend/pallas_call | solution.py:250
  58.8 0.0 collective-permute-done.15.refs_1_
  58.8 0.4 collective-permute-done.14.refs_0_
  59.2 0.9 %attend_final.3 = (bf16[192,384]{1,0:T(8,128)(2,1)S(1)}, bf16[192,384]{1,0:T(8,128)(2,1)S(1)}) custom-call(s32[4,4]{1,0:T(4,128)S(1)} %copy-done.5, s32[4]{0:T(128)S(1)} %copy-done.6, bf16[192,1536]{1,0:T(8,128)(2,1)S(1)} %bitcast.9, bf16[192,768]{1,0:T(8,128)(2,1)S(1)} %collective-permute-done.2.refs_1_, ...), custom_call_target="tpu_custom_call" | custom-call | flops 226492416 | bytes 1179648 | tf_op jit(solution)/shard_map/attend_final/pallas_call | solution.py:250
  60.1 0.6 collective-permute-start.16
  60.7 0.0 collective-permute-done.12.refs_1_
  60.7 2.4 %collective-permute-done.11.refs_0_ = bf16[2,192,384]{2,1,0:T(8,128)(2,1)S(1)} collective-permute-done((bf16[2,192,384]{2,1,0:T(8,128)(2,1)S(1)}, bf16[2,192,384]{2,1,0:T(8,128)(2,1)S(1)}, u32[]{:S(2)}, u32[]{:S(2)}) %collective-permute-start.11) | collective-permute-done | bytes 294944 | tf_op jit(solution)/shard_map/ppermute | solution.py:348
  63.1 0.9 %attend_final.2 = (bf16[192,384]{1,0:T(8,128)(2,1)S(1)}, bf16[192,384]{1,0:T(8,128)(2,1)S(1)}) custom-call(s32[4,4]{1,0:T(4,128)S(1)} %copy-done.5, s32[4]{0:T(128)S(1)} %copy-done.6, bf16[192,1536]{1,0:T(8,128)(2,1)S(1)} %bitcast.10, bf16[192,768]{1,0:T(8,128)(2,1)S(1)} %collective-permute-done.2.refs_1_, ...), custom_call_target="tpu_custom_call" | custom-call | flops 226492416 | bytes 1179648 | tf_op jit(solution)/shard_map/attend_final/pallas_call | solution.py:250
  64.1 0.6 collective-permute-start.13
  64.7 1.5 %collective-permute-done.16.refs_2_ = bf16[192,384]{1,0:T(8,128)(2,1)S(1)} collective-permute-done((bf16[192,384]{1,0:T(8,128)(2,1)S(1)}, bf16[192,384]{1,0:T(8,128)(2,1)S(1)}, u32[]{:S(2)}, u32[]{:S(2)}) %collective-permute-start.16) | collective-permute-done | bytes 147488 | tf_op jit(solution)/shard_map/ppermute | solution.py:340
  66.1 0.8 %put.2.refs_1_ = bf16[192,1536]{1,0:T(8,128)(2,1)} custom-call(bf16[192,384]{1,0:T(8,128)(2,1)S(1)} %get-tuple-element.56.refs_0_, bf16[192,384]{1,0:T(8,128)(2,1)S(1)} %get-tuple-element.57.refs_1_, bf16[192,384]{1,0:T(8,128)(2,1)S(1)} %collective-permute-done.16.refs_2_), custom_call_target="tpu_custom_call" | custom-call | tf_op jit(solution)/shard_map/put/pallas_call | solution.py:314
  66.9 2.3 %collective-permute-done.13.refs_0_ = bf16[192,384]{1,0:T(8,128)(2,1)S(1)} collective-permute-done((bf16[192,384]{1,0:T(8,128)(2,1)S(1)}, bf16[192,384]{1,0:T(8,128)(2,1)S(1)}, u32[]{:S(2)}, u32[]{:S(2)}) %collective-permute-start.13) | collective-permute-done | bytes 147488 | tf_op jit(solution)/shard_map/ppermute | solution.py:340
  69.3 0.7 put.3
  (9 shorter events, 0.1 us)
Async XLA Ops:
  0.0 12.5 %copy-start.1 = (bf16[1,4,48,1536]{3,2,1,0:T(8,128)(2,1)S(1)}, bf16[1,4,48,1536]{3,2,1,0:T(8,128)(2,1)}, u32[]{:S(2)}) copy-start(bf16[1,4,48,1536]{3,2,1,0:T(8,128)(2,1)} %param.6) | copy-start | bytes 1769476
  0.0 12.5 %copy-start.2 = (bf16[1,4,48,1536]{3,2,1,0:T(8,128)(2,1)S(1)}, bf16[1,4,48,1536]{3,2,1,0:T(8,128)(2,1)}, u32[]{:S(2)}) copy-start(bf16[1,4,48,1536]{3,2,1,0:T(8,128)(2,1)} %param.7) | copy-start | bytes 1769476
  2.3 10.2 %collective-permute-start = (bf16[2,192,384]{2,1,0:T(8,128)(2,1)}, bf16[2,192,384]{2,1,0:T(8,128)(2,1)S(1)}, u32[]{:S(2)}, u32[]{:S(2)}) collective-permute-start(bf16[2,192,384]{2,1,0:T(8,128)(2,1)} %get-tuple-element.32), channel_id=1, source_target_pairs={{0,2},{2,0},{1,3},{3,1},{4,6},{6,4},{5,7},{7,5},{8,10},{10,8},{9,1... | collective-permute-start | bytes 884744 | tf_op jit(solution)/shard_map/ppermute | solution.py:340
  5.3 9.2 %copy-start.3 = (bf16[2,192,384]{2,1,0:T(8,128)(2,1)S(1)}, bf16[2,192,384]{2,1,0:T(8,128)(2,1)}, u32[]{:S(2)}) copy-start(bf16[2,192,384]{2,1,0:T(8,128)(2,1)} %get-tuple-element.33.refs_2_) | copy-start | bytes 884740
  5.3 14.4 %collective-permute-start.8 = (bf16[2,192,384]{2,1,0:T(8,128)(2,1)}, bf16[2,192,384]{2,1,0:T(8,128)(2,1)S(1)}, u32[]{:S(2)}, u32[]{:S(2)}) collective-permute-start(bf16[2,192,384]{2,1,0:T(8,128)(2,1)} %get-tuple-element.36.refs_2_), channel_id=1, source_target_pairs={{4,8},{8,4},{5,9},{9,5},{6,10},{10,6},{7,11},{11,7},{20,24},{24,20... | collective-permute-start | bytes 884744 | tf_op jit(solution)/shard_map/ppermute | solution.py:348
  6.1 13.6 %collective-permute-start.7 = (bf16[2,192,384]{2,1,0:T(8,128)(2,1)}, bf16[2,192,384]{2,1,0:T(8,128)(2,1)S(1)}, u32[]{:S(2)}, u32[]{:S(2)}) collective-permute-start(bf16[2,192,384]{2,1,0:T(8,128)(2,1)} %get-tuple-element.36.refs_2_), channel_id=1, source_target_pairs={{0,4},{4,0},{8,12},{12,8},{1,5},{5,1},{9,13},{13,9},{2,6},{6,2},{1... | collective-permute-start | bytes 884744 | tf_op jit(solution)/shard_map/ppermute | solution.py:348
  12.7 9.5 %copy-start = (bf16[1,4,48,1536]{3,2,1,0:T(8,128)(2,1)S(1)}, bf16[1,4,48,1536]{3,2,1,0:T(8,128)(2,1)}, u32[]{:S(2)}) copy-start(bf16[1,4,48,1536]{3,2,1,0:T(8,128)(2,1)} %param.5) | copy-start | bytes 1769476
  12.7 9.5 %collective-permute-start.1 = (bf16[2,192,384]{2,1,0:T(8,128)(2,1)S(1)}, bf16[2,192,384]{2,1,0:T(8,128)(2,1)S(1)}, u32[]{:S(2)}, u32[]{:S(2)}) collective-permute-start(bf16[2,192,384]{2,1,0:T(8,128)(2,1)S(1)} %pack.4), channel_id=1, source_target_pairs={{0,2},{2,0},{1,3},{3,1},{4,6},{6,4},{5,7},{7,5},{8,10},{10,8},{9,1... | collective-permute-start | bytes 884744 | tf_op jit(solution)/shard_map/ppermute | solution.py:340
  14.5 7.8 %collective-permute-start.4 = (bf16[2,192,384]{2,1,0:T(8,128)(2,1)S(1)}, bf16[2,192,384]{2,1,0:T(8,128)(2,1)S(1)}, u32[]{:S(2)}, u32[]{:S(2)}) collective-permute-start(bf16[2,192,384]{2,1,0:T(8,128)(2,1)S(1)} %copy-done.3), channel_id=1, source_target_pairs={{4,8},{8,4},{5,9},{9,5},{6,10},{10,6},{7,11},{11,7},{20,24},{24,20... | collective-permute-start | bytes 884744 | tf_op jit(solution)/shard_map/ppermute | solution.py:348
  15.2 12.4 %collective-permute-start.3 = (bf16[2,192,384]{2,1,0:T(8,128)(2,1)S(1)}, bf16[2,192,384]{2,1,0:T(8,128)(2,1)S(1)}, u32[]{:S(2)}, u32[]{:S(2)}) collective-permute-start(bf16[2,192,384]{2,1,0:T(8,128)(2,1)S(1)} %copy-done.3), channel_id=1, source_target_pairs={{0,4},{4,0},{8,12},{12,8},{1,5},{5,1},{9,13},{13,9},{2,6},{6,2},{1... | collective-permute-start | bytes 884744 | tf_op jit(solution)/shard_map/ppermute | solution.py:348
  19.8 21.4 %collective-permute-start.9 = (bf16[4,192,384]{2,1,0:T(8,128)(2,1)S(1)}, bf16[4,192,384]{2,1,0:T(8,128)(2,1)S(1)}, u32[]{:S(2)}, u32[]{:S(2)}) collective-permute-start(bf16[4,192,384]{2,1,0:T(8,128)(2,1)S(1)} %get-tuple-element.37), channel_id=1, source_target_pairs={{4,8},{8,4},{5,9},{9,5},{6,10},{10,6},{7,11},{11,7},{20,24},{24,20... | collective-permute-start | bytes 1769480 | tf_op jit(solution)/shard_map/ppermute | solution.py:348
  20.5 20.7 %collective-permute-start.10 = (bf16[4,192,384]{2,1,0:T(8,128)(2,1)S(1)}, bf16[4,192,384]{2,1,0:T(8,128)(2,1)S(1)}, u32[]{:S(2)}, u32[]{:S(2)}) collective-permute-start(bf16[4,192,384]{2,1,0:T(8,128)(2,1)S(1)} %get-tuple-element.38), channel_id=1, source_target_pairs={{0,4},{4,0},{8,12},{12,8},{1,5},{5,1},{9,13},{13,9},{2,6},{6,2},{1... | collective-permute-start | bytes 1769480 | tf_op jit(solution)/shard_map/ppermute | solution.py:348
  22.3 16.5 %copy-start.4 = (bf16[2,192,384]{2,1,0:T(8,128)(2,1)S(1)}, bf16[2,192,384]{2,1,0:T(8,128)(2,1)}, u32[]{:S(2)}) copy-start(bf16[2,192,384]{2,1,0:T(8,128)(2,1)} %get-tuple-element.36.refs_2_) | copy-start | bytes 884740
  27.7 11.2 %copy-start.5 = (s32[4,4]{1,0:T(4,128)S(1)}, s32[4,4]{1,0:T(4,128)}, u32[]{:S(2)}) copy-start(s32[4,4]{1,0:T(4,128)} %flags_ref.11) | copy-start | bytes 196
  27.7 11.2 %copy-start.6 = (s32[4]{0:T(128)S(1)}, s32[4]{0:T(128)}, u32[]{:S(2)}) copy-start(s32[4]{0:T(128)} %widths_ref.11) | copy-start | bytes 52
  27.7 21.5 %collective-permute-start.5 = (bf16[4,192,384]{2,1,0:T(8,128)(2,1)S(1)}, bf16[4,192,384]{2,1,0:T(8,128)(2,1)S(1)}, u32[]{:S(2)}, u32[]{:S(2)}) collective-permute-start(bf16[4,192,384]{2,1,0:T(8,128)(2,1)S(1)} %get-tuple-element.34), channel_id=1, source_target_pairs={{4,8},{8,4},{5,9},{9,5},{6,10},{10,6},{7,11},{11,7},{20,24},{24,20... | collective-permute-start | bytes 1769480 | tf_op jit(solution)/shard_map/ppermute | solution.py:348
  28.4 24.4 %collective-permute-start.6 = (bf16[4,192,384]{2,1,0:T(8,128)(2,1)S(1)}, bf16[4,192,384]{2,1,0:T(8,128)(2,1)S(1)}, u32[]{:S(2)}, u32[]{:S(2)}) collective-permute-start(bf16[4,192,384]{2,1,0:T(8,128)(2,1)S(1)} %get-tuple-element.35), channel_id=1, source_target_pairs={{0,4},{4,0},{8,12},{12,8},{1,5},{5,1},{9,13},{13,9},{2,6},{6,2},{1... | collective-permute-start | bytes 1769480 | tf_op jit(solution)/shard_map/ppermute | solution.py:348
  32.2 6.7 %collective-permute-start.2 = (bf16[192,768]{1,0:T(8,128)(2,1)S(1)}, bf16[192,768]{1,0:T(8,128)(2,1)S(1)}, u32[]{:S(2)}, u32[]{:S(2)}) collective-permute-start(bf16[192,768]{1,0:T(8,128)(2,1)S(1)} %pack.5.refs_1_), channel_id=1, source_target_pairs={{0,2},{2,0},{1,3},{3,1},{4,6},{6,4},{5,7},{7,5},{8,10},{10,8},{9,1... | collective-permute-start | bytes 884744 | tf_op jit(solution)/shard_map/ppermute | solution.py:340
  41.2 17.6 %collective-permute-start.15 = (bf16[2,192,384]{2,1,0:T(8,128)(2,1)S(1)}, bf16[2,192,384]{2,1,0:T(8,128)(2,1)S(1)}, u32[]{:S(2)}, u32[]{:S(2)}) collective-permute-start(bf16[2,192,384]{2,1,0:T(8,128)(2,1)S(1)} %slice.15), channel_id=1, source_target_pairs={{4,8},{8,4},{5,9},{9,5},{6,10},{10,6},{7,11},{11,7},{20,24},{24,20... | collective-permute-start | bytes 884744 | tf_op jit(solution)/shard_map/ppermute | solution.py:348
  41.9 17.2 %collective-permute-start.14 = (bf16[2,192,384]{2,1,0:T(8,128)(2,1)S(1)}, bf16[2,192,384]{2,1,0:T(8,128)(2,1)S(1)}, u32[]{:S(2)}, u32[]{:S(2)}) collective-permute-start(bf16[2,192,384]{2,1,0:T(8,128)(2,1)S(1)} %slice.14), channel_id=1, source_target_pairs={{0,4},{4,0},{8,12},{12,8},{1,5},{5,1},{9,13},{13,9},{2,6},{6,2},{1... | collective-permute-start | bytes 884744 | tf_op jit(solution)/shard_map/ppermute | solution.py:348
  52.9 7.8 %collective-permute-start.12 = (bf16[2,192,384]{2,1,0:T(8,128)(2,1)S(1)}, bf16[2,192,384]{2,1,0:T(8,128)(2,1)S(1)}, u32[]{:S(2)}, u32[]{:S(2)}) collective-permute-start(bf16[2,192,384]{2,1,0:T(8,128)(2,1)S(1)} %slice.13), channel_id=1, source_target_pairs={{4,8},{8,4},{5,9},{9,5},{6,10},{10,6},{7,11},{11,7},{20,24},{24,20... | collective-permute-start | bytes 884744 | tf_op jit(solution)/shard_map/ppermute | solution.py:348
  53.6 9.5 %collective-permute-start.11 = (bf16[2,192,384]{2,1,0:T(8,128)(2,1)S(1)}, bf16[2,192,384]{2,1,0:T(8,128)(2,1)S(1)}, u32[]{:S(2)}, u32[]{:S(2)}) collective-permute-start(bf16[2,192,384]{2,1,0:T(8,128)(2,1)S(1)} %slice.12), channel_id=1, source_target_pairs={{0,4},{4,0},{8,12},{12,8},{1,5},{5,1},{9,13},{13,9},{2,6},{6,2},{1... | collective-permute-start | bytes 884744 | tf_op jit(solution)/shard_map/ppermute | solution.py:348
  60.1 6.1 %collective-permute-start.16 = (bf16[192,384]{1,0:T(8,128)(2,1)S(1)}, bf16[192,384]{1,0:T(8,128)(2,1)S(1)}, u32[]{:S(2)}, u32[]{:S(2)}) collective-permute-start(bf16[192,384]{1,0:T(8,128)(2,1)S(1)} %get-tuple-element.58), channel_id=1, source_target_pairs={{0,2},{2,0},{1,3},{3,1},{4,6},{6,4},{5,7},{7,5},{8,10},{10,8},{9,1... | collective-permute-start | bytes 442376 | tf_op jit(solution)/shard_map/ppermute | solution.py:340
  64.1 5.2 %collective-permute-start.13 = (bf16[192,384]{1,0:T(8,128)(2,1)S(1)}, bf16[192,384]{1,0:T(8,128)(2,1)S(1)}, u32[]{:S(2)}, u32[]{:S(2)}) collective-permute-start(bf16[192,384]{1,0:T(8,128)(2,1)S(1)} %get-tuple-element.52), channel_id=1, source_target_pairs={{0,2},{2,0},{1,3},{3,1},{4,6},{6,4},{5,7},{7,5},{8,10},{10,8},{9,1... | collective-permute-start | bytes 442376 | tf_op jit(solution)/shard_map/ppermute | solution.py:340

commit v10 on v7

--- a/solution.py
+++ b/solution.py
@@ -88,7 +88,7 @@
 
 
 def attend_kernel(
-    spaces, frames, columns, row_band, heads, together, groups, skips, fresh, final,
+    spaces, frames, columns, row_band, heads, together, groups, query_skip, fresh, final,
     flags_ref, widths_ref, *refs,
 ):
     refs = list(refs)
@@ -151,7 +151,9 @@
                 top = jnp.maximum(top, before)
             weights = jnp.exp2(scores * scale - top)
             total = jnp.sum(weights, axis=0, keepdims=True)
-            values = jnp.concatenate([keyvals[i][r + 1, :, lanes(t)] for i, r, o in pieces], axis=0)
+            values = jnp.concatenate(
+                [keyvals[i][r + 1, :, lanes(t)] for i, r, o in pieces], axis=0
+            )
             acc = lax.dot_general(
                 values, weights.astype(jnp.bfloat16), TN, preferred_element_type=jnp.float32
             )
@@ -165,7 +167,7 @@
 
         for t in range(together):
             for offset in range(spaces):
-                skip = skips[offset] + (own_column if offset == 0 else 0)
+                skip = query_skip + (own_column if offset == 0 else 0)
                 query_ref[t, pl.ds(offset * tokens, tokens), :HEAD_DIM] = queries[offset][
                     :, lanes(t, skip)
                 ]
@@ -250,7 +252,7 @@
     return pl.pallas_call(
         functools.partial(
             attend_kernel, spaces, frames, columns, row_band, heads, together,
-            tuple(numbered), (first * HEAD_DIM,) * spaces, state is None, final,
+            tuple(numbered), first * HEAD_DIM, state is None, final,
         ),
         in_specs=[pl.BlockSpec(memory_space=pltpu.SMEM)] * 2
         + [pl.BlockSpec(memory_space=pltpu.VMEM)] * len(operands),
@@ -267,19 +269,21 @@
     )(*scalars, *operands)
 
 
-def join_kernel(parts, *refs):
-    for n, rows in enumerate(parts):
-        refs[-1][pl.ds(sum(parts[:n]), rows)] = refs[n][...]
-
-
-def join(arrays):
-    parts = tuple(x.shape[0] for x in arrays)
-    shape = (sum(parts),) + arrays[0].shape[1:]
+def join_kernel(outs_copies, *refs):
+    arrays, outs = refs[: -len(outs_copies)], refs[-len(outs_copies) :]
+    for out_ref, copies in zip(outs, outs_copies):
+        for n, lane, width, row, column in copies:
+            rows = pl.ds(row, arrays[n].shape[0])
+            out_ref[rows, :, pl.ds(column, width)] = arrays[n][:, :, pl.ds(lane, width)]
+
+
+def join(arrays, outs_copies, rows, width):
+    shape = jax.ShapeDtypeStruct((rows, arrays[0].shape[1], width), arrays[0].dtype)
     return pl.pallas_call(
-        functools.partial(join_kernel, parts),
+        functools.partial(join_kernel, outs_copies),
         in_specs=[pl.BlockSpec(memory_space=pltpu.VMEM)] * len(arrays),
-        out_specs=pl.BlockSpec(memory_space=pltpu.VMEM),
-        out_shape=jax.ShapeDtypeStruct(shape, arrays[0].dtype),
+        out_specs=[pl.BlockSpec(memory_space=pltpu.VMEM)] * len(outs_copies),
+        out_shape=[shape] * len(outs_copies),
         compiler_params=pltpu.CompilerParams(vmem_limit_bytes=SMALL_LIMIT),
         name="join",
     )(*arrays)
@@ -342,18 +346,24 @@
         second = swap(xs[1], 1)
         return [swap(xs[0], 0), second]
 
-    own, partners, arrived = [], [], []
-    for c, (first, number) in enumerate(chunks):
-        blocks = [(offset, first * HEAD_DIM, number * HEAD_DIM) for offset in offsets]
-        if c == 0:
-            mine = [(0, f * HEAD_DIM, n * HEAD_DIM) for f, n in chunks]
-            packed = pack((k, v), blocks + mine, (), spaces, True)
-            sends, own = packed[: len(blocks)], packed[len(blocks) :]
-        else:
-            sends = pack((k, v), blocks, arrived, spaces, False)
-        arrived = [along_space(x, offset) for x, offset in zip(sends, offsets)]
-        partners.append(arrived)
-    sends = pack((q,), [(offset, 0, width) for offset in offsets], arrived, spaces, False)
+    def blocks_of(chunk, which):
+        return [(offset, chunk[0] * HEAD_DIM, chunk[1] * HEAD_DIM) for offset in which]
+
+    large = heads - heads // 3
+    cuts = [(0, large), (large, heads - large)]
+    packed = pack(
+        (k, v), blocks_of(chunks[0], offsets) + [blocks_of(cut, (0,))[0] for cut in cuts],
+        (), spaces, True,
+    )
+    sends, sources = packed[: len(offsets)], packed[len(offsets) :]
+    partners = [[along_space(x, offset) for x, offset in zip(sends, offsets)]]
+    firsts = [swap_both([x, x]) for x in sources]
+    *sends, own = pack(
+        (k, v), blocks_of(chunks[1], offsets) + blocks_of(chunks[1], (0,)), partners[0], spaces, False
+    )
+    partners.append([along_space(x, offset) for x, offset in zip(sends, offsets)])
+    own = [sources[0], own]
+    sends = pack((q,), [(offset, 0, width) for offset in offsets], partners[1], spaces, False)
     query_parts = [q] + [along_space(x, offset) for x, offset in zip(sends, offsets)]
     partners[1] = list(tie(partners[1], sends))
 
@@ -368,23 +378,35 @@
             (slot, hops, [(x, 2 * (o - 1), o) for o in offsets]) for slot, x in enumerate(message)
         ]
 
-    firsts = [swap_both([x, x]) for x in own]
-    seconds = []
-    for c in range(len(chunks)):
-        ready = [join(partners[c] + [firsts[c][1 - slot]]) for slot in range(2)]
+    seconds, states = [], []
+    for c, chunk in enumerate(chunks):
+        begin, end = chunk[0], sum(chunk)
+        arrays, here = list(partners[c]), []
+        for (first, number), pair in zip(cuts, firsts):
+            low, high = max(begin, first), min(end, first + number)
+            if low < high:
+                here.append((len(arrays), low - first, high - low, low - begin))
+                arrays += pair
+        outs_copies = []
+        for slot in range(2):
+            copies = [(n, 0, chunk[1] * HEAD_DIM, 2 * n, 0) for n in range(len(offsets))]
+            copies += [
+                (n + 1 - slot, lane * HEAD_DIM, number * HEAD_DIM, behind, to * HEAD_DIM)
+                for n, lane, number, to in here
+            ]
+            outs_copies.append(tuple(copies))
+        ready = join(arrays, tuple(outs_copies), behind + 2, chunk[1] * HEAD_DIM)
         seconds.append(swap_both(ready))
-    states = []
-    for c, chunk in enumerate(chunks):
         pieces = [(own[c], 0, 0)] + [(x, 0, o) for x, o in zip(partners[c], offsets)]
-        groups = [(0, 0, pieces)] + own_band(firsts[c], 1)
+        groups = [(0, 0, pieces)] + own_band(ready[::-1], 1)
         states.append(attend(scalars, query_parts, groups, None, False, chunk, sizes))
 
     messages = seconds
     for hops in range(2, frames - 1):
         following = []
         for c, chunk in enumerate(chunks):
-            after = [state[1] for state in (states if c == 0 else states[:c])]
-            came = list(tie(messages[c], after))
+            after = [state[1] for state in states]
+            came = list(tie(messages[c][::-1], after))[::-1]
             rows = behind if hops == last else behind + 2
             following.append(swap_both([came[1 - slot][:rows] for slot in range(2)]))
             groups = partner_bands(came, hops - 1) + own_band(came, hops)

time: 70.8 us -> 69.2 us (0.977)
  starting transfers between devices: 37 us -> 36 us
  waiting for transfers between devices: 17.3 us -> 16.3 us
    ppermute x12, starting transfers between devices: 30.4 us -> 29.3 us  [swap(): return lax.ppermute(x, 'frame', pairs)]
  transfers between devices with their start and end apart: 17 -> 17, of which waited for: 9 -> 7; matrix products, arithmetic and copies ran while one was open for 0% -> 0% of each run, Pallas kernels for 18% -> 19%
where the time goes in v10:
time: 69.2 us; the launch traced here: 68.9 us
  starting transfers between devices  36 us (52%)
  waiting for transfers between devices  16.3 us (24%)
  Pallas kernels  16.2 us (23%)
    ppermute x12, starting transfers between devices, swap(): return lax.ppermute(x, 'frame', pairs)  29.3 us
    ppermute x5, waiting for transfers between devices, along_space(): lax.ppermute(x, 'space', [(s, (s + offset) % spaces) for s in range(space...  11.9 us
    pallas_call x6, Pallas kernels, attend(): pl.pallas_call(functools.partial(attend_kernel, spaces, frames, columns,...  11.8 us
    ppermute x5, starting transfers between devices, along_space(): lax.ppermute(x, 'space', [(s, (s + offset) % spaces) for s in range(space...  6.67 us
    ppermute x12, waiting for transfers between devices, swap(): return lax.ppermute(x, 'frame', pairs)  4.45 us
    pallas_call x3, Pallas kernels, pack(): pl.pallas_call(functools.partial(pack_kernel, spaces, tuple(jobs), staged...  2.75 us
    pallas_call x2, Pallas kernels, put(): pl.pallas_call(functools.partial(put_kernel, spaces, tuple(places)), in_s...  1.45 us
  transfers between devices with their start and end apart: 17, of which 7 were waited for; matrix products, arithmetic and copies ran while one was open for 0% of the time, Pallas kernels for 19%

profile of v10, /device:TPU:0, one launch (start us, length us, event | category | flops | bytes accessed | tf_op | source)
XLA Modules:
  0.0 68.9 jit_solution(14254821070318902044)
XLA Ops:
  0.0 0.0 copy-start.1
  0.0 0.0 copy-start.2
  0.0 2.3 %pack.3 = (bf16[2,192,384]{2,1,0:T(8,128)(2,1)}, bf16[2,192,512]{2,1,0:T(8,128)(2,1)}, bf16[2,192,256]{2,1,0:T(8,128)(2,1)}) custom-call(bf16[192,1536]{1,0:T(8,128)(2,1)} %bitcast.11, bf16[192,1536]{1,0:T(8,128)(2,1)} %bitcast.13), custom_call_target="tpu_custom_call" | custom-call | tf_op jit(solution)/shard_map/pack/pallas_call | solution.py:64
  2.3 3.0 %collective-permute-start = (bf16[2,192,384]{2,1,0:T(8,128)(2,1)}, bf16[2,192,384]{2,1,0:T(8,128)(2,1)S(1)}, u32[]{:S(2)}, u32[]{:S(2)}) collective-permute-start(bf16[2,192,384]{2,1,0:T(8,128)(2,1)} %get-tuple-element.34), channel_id=1, source_target_pairs={{0,2},{2,0},{1,3},{3,1},{4,6},{6,4},{5,7},{7,5},{8,10},{10,8},{9,1... | collective-permute-start | bytes 884744 | tf_op jit(solution)/shard_map/ppermute | solution.py:335
  5.3 0.0 copy-start.6
  5.3 0.8 %collective-permute-start.4 = (bf16[2,192,512]{2,1,0:T(8,128)(2,1)}, bf16[2,192,512]{2,1,0:T(8,128)(2,1)S(1)}, u32[]{:S(2)}, u32[]{:S(2)}) collective-permute-start(bf16[2,192,512]{2,1,0:T(8,128)(2,1)} %get-tuple-element.36.refs_2_), channel_id=1, source_target_pairs={{4,8},{8,4},{5,9},{9,5},{6,10},{10,6},{7,11},{11,7},{20,24},{24,20... | collective-permute-start | bytes 1179656 | tf_op jit(solution)/shard_map/ppermute | solution.py:343
  6.1 4.4 %collective-permute-start.3 = (bf16[2,192,512]{2,1,0:T(8,128)(2,1)}, bf16[2,192,512]{2,1,0:T(8,128)(2,1)S(1)}, u32[]{:S(2)}, u32[]{:S(2)}) collective-permute-start(bf16[2,192,512]{2,1,0:T(8,128)(2,1)} %get-tuple-element.36.refs_2_), channel_id=1, source_target_pairs={{0,4},{4,0},{8,12},{12,8},{1,5},{5,1},{9,13},{13,9},{2,6},{6,2},{1... | collective-permute-start | bytes 1179656 | tf_op jit(solution)/shard_map/ppermute | solution.py:343
  10.6 2.0 %collective-permute-done.refs_2_.refs_0_.refs_3_ = bf16[2,192,384]{2,1,0:T(8,128)(2,1)S(1)} collective-permute-done((bf16[2,192,384]{2,1,0:T(8,128)(2,1)}, bf16[2,192,384]{2,1,0:T(8,128)(2,1)S(1)}, u32[]{:S(2)}, u32[]{:S(2)}) %collective-permute-start) | collective-permute-done | bytes 294944 | tf_op jit(solution)/shard_map/ppermute | solution.py:335
  12.5 0.0 copy-done.1
  12.5 0.0 copy-done.2
  12.5 0.4 pack.4
  12.9 0.0 copy-start
  12.9 1.8 %collective-permute-start.1 = (bf16[2,192,384]{2,1,0:T(8,128)(2,1)S(1)}, bf16[2,192,384]{2,1,0:T(8,128)(2,1)S(1)}, u32[]{:S(2)}, u32[]{:S(2)}) collective-permute-start(bf16[2,192,384]{2,1,0:T(8,128)(2,1)S(1)} %get-tuple-element.35), channel_id=1, source_target_pairs={{0,2},{2,0},{1,3},{3,1},{4,6},{6,4},{5,7},{7,5},{8,10},{10,8},{9,1... | collective-permute-start | bytes 884744 | tf_op jit(solution)/shard_map/ppermute | solution.py:335
  14.7 0.0 copy-done.6
  14.7 0.7 collective-permute-start.6
  15.4 4.5 %collective-permute-start.5 = (bf16[2,192,256]{2,1,0:T(8,128)(2,1)S(1)}, bf16[2,192,256]{2,1,0:T(8,128)(2,1)S(1)}, u32[]{:S(2)}, u32[]{:S(2)}) collective-permute-start(bf16[2,192,256]{2,1,0:T(8,128)(2,1)S(1)} %copy-done.6), channel_id=1, source_target_pairs={{0,4},{4,0},{8,12},{12,8},{1,5},{5,1},{9,13},{13,9},{2,6},{6,2},{1... | collective-permute-start | bytes 589832 | tf_op jit(solution)/shard_map/ppermute | solution.py:343
  19.8 0.0 collective-permute-done.4.refs_2_
  19.8 0.0 collective-permute-done.3.refs_1_
  19.8 0.1 join.3
  20.0 0.7 %collective-permute-start.9 = (bf16[4,192,384]{2,1,0:T(8,128)(2,1)S(1)}, bf16[4,192,384]{2,1,0:T(8,128)(2,1)S(1)}, u32[]{:S(2)}, u32[]{:S(2)}) collective-permute-start(bf16[4,192,384]{2,1,0:T(8,128)(2,1)S(1)} %get-tuple-element.40.refs_4_), channel_id=1, source_target_pairs={{4,8},{8,4},{5,9},{9,5},{6,10},{10,6},{7,11},{11,7},{20,24},{24,20... | collective-permute-start | bytes 1769480 | tf_op jit(solution)/shard_map/ppermute | solution.py:343
  20.7 3.1 %collective-permute-start.10 = (bf16[4,192,384]{2,1,0:T(8,128)(2,1)S(1)}, bf16[4,192,384]{2,1,0:T(8,128)(2,1)S(1)}, u32[]{:S(2)}, u32[]{:S(2)}) collective-permute-start(bf16[4,192,384]{2,1,0:T(8,128)(2,1)S(1)} %get-tuple-element.41.refs_5_), channel_id=1, source_target_pairs={{0,4},{4,0},{8,12},{12,8},{1,5},{5,1},{9,13},{13,9},{2,6},{6,2},{1... | collective-permute-start | bytes 1769480 | tf_op jit(solution)/shard_map/ppermute | solution.py:343
  23.8 0.0 collective-permute-done.1.refs_1_.refs_0_
  23.8 0.0 copy-done
  23.8 0.1 pack.5.refs_1_
  23.9 0.0 copy-start.3
  23.9 0.0 collective-permute-done.6.refs_4_
  23.9 0.6 collective-permute-done.5.refs_3_
  24.5 0.1 join.2
  24.6 0.0 copy-start.4
  24.6 0.0 copy-start.5
  24.6 0.7 %collective-permute-start.7 = (bf16[4,192,384]{2,1,0:T(8,128)(2,1)S(1)}, bf16[4,192,384]{2,1,0:T(8,128)(2,1)S(1)}, u32[]{:S(2)}, u32[]{:S(2)}) collective-permute-start(bf16[4,192,384]{2,1,0:T(8,128)(2,1)S(1)} %get-tuple-element.38.refs_4_), channel_id=1, source_target_pairs={{4,8},{8,4},{5,9},{9,5},{6,10},{10,6},{7,11},{11,7},{20,24},{24,20... | collective-permute-start | bytes 1769480 | tf_op jit(solution)/shard_map/ppermute | solution.py:343
  25.3 3.5 %collective-permute-start.8 = (bf16[4,192,384]{2,1,0:T(8,128)(2,1)S(1)}, bf16[4,192,384]{2,1,0:T(8,128)(2,1)S(1)}, u32[]{:S(2)}, u32[]{:S(2)}) collective-permute-start(bf16[4,192,384]{2,1,0:T(8,128)(2,1)S(1)} %get-tuple-element.39.refs_5_), channel_id=1, source_target_pairs={{0,4},{4,0},{8,12},{12,8},{1,5},{5,1},{9,13},{13,9},{2,6},{6,2},{1... | collective-permute-start | bytes 1769480 | tf_op jit(solution)/shard_map/ppermute | solution.py:343
  28.9 0.5 collective-permute-start.2
  29.4 6.2 %collective-permute-done.2.refs_1_ = bf16[192,768]{1,0:T(8,128)(2,1)S(1)} collective-permute-done((bf16[192,768]{1,0:T(8,128)(2,1)S(1)}, bf16[192,768]{1,0:T(8,128)(2,1)S(1)}, u32[]{:S(2)}, u32[]{:S(2)}) %collective-permute-start.2) | collective-permute-done | bytes 294944 | tf_op jit(solution)/shard_map/ppermute | solution.py:335
  35.6 0.0 copy-done.3
  35.6 0.0 copy-done.4
  35.6 0.0 copy-done.5
  35.6 2.2 %attend.4 = (f32[3,128,384]{2,1,0:T(8,128)S(1)}, f32[3,8,384]{2,1,0:T(8,128)S(1)}) custom-call(s32[4,4]{1,0:T(4,128)S(1)} %copy-done.4, s32[4]{0:T(128)S(1)} %copy-done.5, bf16[192,1536]{1,0:T(8,128)(2,1)S(1)} %bitcast.5, bf16[192,768]{1,0:T(8,128)(2,1)S(1)} %collective-permute-done.2.refs_1_, bf16[2,192,512]{2,1,0:T(8,128)(2,1)S(1)} %copy-done.3, ...), custom_call_target="tpu_custom_call" | custom-call | flops 452984832 | bytes 1179648 | tf_op jit(solution)/shard_map/attend/pallas_call | solution.py:252
  37.8 2.3 %attend.5 = (f32[3,128,384]{2,1,0:T(8,128)S(1)}, f32[3,8,384]{2,1,0:T(8,128)S(1)}) custom-call(s32[4,4]{1,0:T(4,128)S(1)} %copy-done.4, s32[4]{0:T(128)S(1)} %copy-done.5, bf16[192,1536]{1,0:T(8,128)(2,1)S(1)} %bitcast.6, bf16[192,768]{1,0:T(8,128)(2,1)S(1)} %collective-permute-done.2.refs_1_, bf16[2,192,384]{2,1,0:T(8,128)(2,1)S(1)} %get-tuple-element.43.refs_2_, ...), custom_call_target="tpu_custom_call" | custom-call | flops 452984832 | bytes 1179648 | tf_op jit(solution)/shard_map/attend/pallas_call | solution.py:252
  40.1 0.0 collective-permute-done.9.refs_0_
  40.1 0.0 collective-permute-done.10.refs_1_
  40.2 0.7 collective-permute-start.15
  40.9 4.7 %collective-permute-start.14 = (bf16[2,192,384]{2,1,0:T(8,128)(2,1)S(1)}, bf16[2,192,384]{2,1,0:T(8,128)(2,1)S(1)}, u32[]{:S(2)}, u32[]{:S(2)}) collective-permute-start(bf16[2,192,384]{2,1,0:T(8,128)(2,1)S(1)} %slice.14), channel_id=1, source_target_pairs={{0,4},{4,0},{8,12},{12,8},{1,5},{5,1},{9,13},{13,9},{2,6},{6,2},{1... | collective-permute-start | bytes 884744 | tf_op jit(solution)/shard_map/ppermute | solution.py:343
  45.6 2.1 %attend.6 = (f32[3,128,384]{2,1,0:T(8,128)S(1)}, f32[3,8,384]{2,1,0:T(8,128)S(1)}) custom-call(s32[4,4]{1,0:T(4,128)S(1)} %copy-done.4, s32[4]{0:T(128)S(1)} %copy-done.5, bf16[192,1536]{1,0:T(8,128)(2,1)S(1)} %bitcast.7, bf16[192,768]{1,0:T(8,128)(2,1)S(1)} %collective-permute-done.2.refs_1_, bf16[4,192,384]{2,1,0:T(8,128)(2,1)S(1)} %get-tuple-element.45.refs_2_, ...), custom_call_target="tpu_custom_call" | custom-call | flops 452984832 | bytes 1179648 | tf_op jit(solution)/shard_map/attend/pallas_call | solution.py:252
  47.7 0.0 collective-permute-done.7.refs_0_
  47.7 3.0 %collective-permute-done.8.refs_1_ = bf16[4,192,384]{2,1,0:T(8,128)(2,1)S(1)} collective-permute-done((bf16[4,192,384]{2,1,0:T(8,128)(2,1)S(1)}, bf16[4,192,384]{2,1,0:T(8,128)(2,1)S(1)}, u32[]{:S(2)}, u32[]{:S(2)}) %collective-permute-start.8) | collective-permute-done | bytes 589856 | tf_op jit(solution)/shard_map/ppermute | solution.py:343
  50.7 0.7 collective-permute-start.12
  51.4 4.9 %collective-permute-start.11 = (bf16[2,192,384]{2,1,0:T(8,128)(2,1)S(1)}, bf16[2,192,384]{2,1,0:T(8,128)(2,1)S(1)}, u32[]{:S(2)}, u32[]{:S(2)}) collective-permute-start(bf16[2,192,384]{2,1,0:T(8,128)(2,1)S(1)} %slice.12), channel_id=1, source_target_pairs={{0,4},{4,0},{8,12},{12,8},{1,5},{5,1},{9,13},{13,9},{2,6},{6,2},{1... | collective-permute-start | bytes 884744 | tf_op jit(solution)/shard_map/ppermute | solution.py:343
  56.3 2.1 %attend.7 = (f32[3,128,384]{2,1,0:T(8,128)S(1)}, f32[3,8,384]{2,1,0:T(8,128)S(1)}) custom-call(s32[4,4]{1,0:T(4,128)S(1)} %copy-done.4, s32[4]{0:T(128)S(1)} %copy-done.5, bf16[192,1536]{1,0:T(8,128)(2,1)S(1)} %bitcast.8, bf16[192,768]{1,0:T(8,128)(2,1)S(1)} %collective-permute-done.2.refs_1_, bf16[4,192,384]{2,1,0:T(8,128)(2,1)S(1)} %get-tuple-element.50.refs_2_, ...), custom_call_target="tpu_custom_call" | custom-call | flops 452984832 | bytes 1179648 | tf_op jit(solution)/shard_map/attend/pallas_call | solution.py:252
  58.4 0.0 collective-permute-done.15.refs_1_
  58.4 0.0 collective-permute-done.14.refs_0_
  58.4 1.6 %attend_final.3 = (bf16[192,384]{1,0:T(8,128)(2,1)S(1)}, bf16[192,384]{1,0:T(8,128)(2,1)S(1)}) custom-call(s32[4,4]{1,0:T(4,128)S(1)} %copy-done.4, s32[4]{0:T(128)S(1)} %copy-done.5, bf16[192,1536]{1,0:T(8,128)(2,1)S(1)} %bitcast.9, bf16[192,768]{1,0:T(8,128)(2,1)S(1)} %collective-permute-done.2.refs_1_, ...), custom_call_target="tpu_custom_call" | custom-call | flops 226492416 | bytes 1179648 | tf_op jit(solution)/shard_map/attend_final/pallas_call | solution.py:252
  60.0 0.6 collective-permute-start.16
  60.6 0.0 collective-permute-done.12.refs_1_
  60.6 0.9 %collective-permute-done.11.refs_0_ = bf16[2,192,384]{2,1,0:T(8,128)(2,1)S(1)} collective-permute-done((bf16[2,192,384]{2,1,0:T(8,128)(2,1)S(1)}, bf16[2,192,384]{2,1,0:T(8,128)(2,1)S(1)}, u32[]{:S(2)}, u32[]{:S(2)}) %collective-permute-start.11) | collective-permute-done | bytes 294944 | tf_op jit(solution)/shard_map/ppermute | solution.py:343
  61.5 1.6 %attend_final.2 = (bf16[192,384]{1,0:T(8,128)(2,1)S(1)}, bf16[192,384]{1,0:T(8,128)(2,1)S(1)}) custom-call(s32[4,4]{1,0:T(4,128)S(1)} %copy-done.4, s32[4]{0:T(128)S(1)} %copy-done.5, bf16[192,1536]{1,0:T(8,128)(2,1)S(1)} %bitcast.10, bf16[192,768]{1,0:T(8,128)(2,1)S(1)} %collective-permute-done.2.refs_1_, ...), custom_call_target="tpu_custom_call" | custom-call | flops 226492416 | bytes 1179648 | tf_op jit(solution)/shard_map/attend_final/pallas_call | solution.py:252
  63.0 0.7 %collective-permute-start.13 = (bf16[192,384]{1,0:T(8,128)(2,1)S(1)}, bf16[192,384]{1,0:T(8,128)(2,1)S(1)}, u32[]{:S(2)}, u32[]{:S(2)}) collective-permute-start(bf16[192,384]{1,0:T(8,128)(2,1)S(1)} %get-tuple-element.56), channel_id=1, source_target_pairs={{0,2},{2,0},{1,3},{3,1},{4,6},{6,4},{5,7},{7,5},{8,10},{10,8},{9,1... | collective-permute-start | bytes 442376 | tf_op jit(solution)/shard_map/ppermute | solution.py:335
  63.7 2.5 %collective-permute-done.16.refs_2_ = bf16[192,384]{1,0:T(8,128)(2,1)S(1)} collective-permute-done((bf16[192,384]{1,0:T(8,128)(2,1)S(1)}, bf16[192,384]{1,0:T(8,128)(2,1)S(1)}, u32[]{:S(2)}, u32[]{:S(2)}) %collective-permute-start.16) | collective-permute-done | bytes 147488 | tf_op jit(solution)/shard_map/ppermute | solution.py:335
  66.2 0.8 %put.2.refs_1_ = bf16[192,1536]{1,0:T(8,128)(2,1)} custom-call(bf16[192,384]{1,0:T(8,128)(2,1)S(1)} %get-tuple-element.60.refs_0_, bf16[192,384]{1,0:T(8,128)(2,1)S(1)} %get-tuple-element.61.refs_1_, bf16[192,384]{1,0:T(8,128)(2,1)S(1)} %collective-permute-done.16.refs_2_), custom_call_target="tpu_custom_call" | custom-call | tf_op jit(solution)/shard_map/put/pallas_call | solution.py:309
  67.0 1.3 %collective-permute-done.13.refs_0_ = bf16[192,384]{1,0:T(8,128)(2,1)S(1)} collective-permute-done((bf16[192,384]{1,0:T(8,128)(2,1)S(1)}, bf16[192,384]{1,0:T(8,128)(2,1)S(1)}, u32[]{:S(2)}, u32[]{:S(2)}) %collective-permute-start.13) | collective-permute-done | bytes 147488 | tf_op jit(solution)/shard_map/ppermute | solution.py:335
  68.2 0.7 put.3
  (9 shorter events, 0.1 us)
Async XLA Ops:
  0.0 12.5 %copy-start.1 = (bf16[1,4,48,1536]{3,2,1,0:T(8,128)(2,1)S(1)}, bf16[1,4,48,1536]{3,2,1,0:T(8,128)(2,1)}, u32[]{:S(2)}) copy-start(bf16[1,4,48,1536]{3,2,1,0:T(8,128)(2,1)} %param.6) | copy-start | bytes 1769476
  0.0 12.5 %copy-start.2 = (bf16[1,4,48,1536]{3,2,1,0:T(8,128)(2,1)S(1)}, bf16[1,4,48,1536]{3,2,1,0:T(8,128)(2,1)}, u32[]{:S(2)}) copy-start(bf16[1,4,48,1536]{3,2,1,0:T(8,128)(2,1)} %param.7) | copy-start | bytes 1769476
  2.3 10.2 %collective-permute-start = (bf16[2,192,384]{2,1,0:T(8,128)(2,1)}, bf16[2,192,384]{2,1,0:T(8,128)(2,1)S(1)}, u32[]{:S(2)}, u32[]{:S(2)}) collective-permute-start(bf16[2,192,384]{2,1,0:T(8,128)(2,1)} %get-tuple-element.34), channel_id=1, source_target_pairs={{0,2},{2,0},{1,3},{3,1},{4,6},{6,4},{5,7},{7,5},{8,10},{10,8},{9,1... | collective-permute-start | bytes 884744 | tf_op jit(solution)/shard_map/ppermute | solution.py:335
  5.3 9.4 %copy-start.6 = (bf16[2,192,256]{2,1,0:T(8,128)(2,1)S(1)}, bf16[2,192,256]{2,1,0:T(8,128)(2,1)}, u32[]{:S(2)}) copy-start(bf16[2,192,256]{2,1,0:T(8,128)(2,1)} %get-tuple-element.37) | copy-start | bytes 589828
  5.3 14.5 %collective-permute-start.4 = (bf16[2,192,512]{2,1,0:T(8,128)(2,1)}, bf16[2,192,512]{2,1,0:T(8,128)(2,1)S(1)}, u32[]{:S(2)}, u32[]{:S(2)}) collective-permute-start(bf16[2,192,512]{2,1,0:T(8,128)(2,1)} %get-tuple-element.36.refs_2_), channel_id=1, source_target_pairs={{4,8},{8,4},{5,9},{9,5},{6,10},{10,6},{7,11},{11,7},{20,24},{24,20... | collective-permute-start | bytes 1179656 | tf_op jit(solution)/shard_map/ppermute | solution.py:343
  6.1 13.7 %collective-permute-start.3 = (bf16[2,192,512]{2,1,0:T(8,128)(2,1)}, bf16[2,192,512]{2,1,0:T(8,128)(2,1)S(1)}, u32[]{:S(2)}, u32[]{:S(2)}) collective-permute-start(bf16[2,192,512]{2,1,0:T(8,128)(2,1)} %get-tuple-element.36.refs_2_), channel_id=1, source_target_pairs={{0,4},{4,0},{8,12},{12,8},{1,5},{5,1},{9,13},{13,9},{2,6},{6,2},{1... | collective-permute-start | bytes 1179656 | tf_op jit(solution)/shard_map/ppermute | solution.py:343
  12.9 10.9 %copy-start = (bf16[1,4,48,1536]{3,2,1,0:T(8,128)(2,1)S(1)}, bf16[1,4,48,1536]{3,2,1,0:T(8,128)(2,1)}, u32[]{:S(2)}) copy-start(bf16[1,4,48,1536]{3,2,1,0:T(8,128)(2,1)} %param.5) | copy-start | bytes 1769476
  12.9 10.9 %collective-permute-start.1 = (bf16[2,192,384]{2,1,0:T(8,128)(2,1)S(1)}, bf16[2,192,384]{2,1,0:T(8,128)(2,1)S(1)}, u32[]{:S(2)}, u32[]{:S(2)}) collective-permute-start(bf16[2,192,384]{2,1,0:T(8,128)(2,1)S(1)} %get-tuple-element.35), channel_id=1, source_target_pairs={{0,2},{2,0},{1,3},{3,1},{4,6},{6,4},{5,7},{7,5},{8,10},{10,8},{9,1... | collective-permute-start | bytes 884744 | tf_op jit(solution)/shard_map/ppermute | solution.py:335
  14.7 9.2 %collective-permute-start.6 = (bf16[2,192,256]{2,1,0:T(8,128)(2,1)S(1)}, bf16[2,192,256]{2,1,0:T(8,128)(2,1)S(1)}, u32[]{:S(2)}, u32[]{:S(2)}) collective-permute-start(bf16[2,192,256]{2,1,0:T(8,128)(2,1)S(1)} %copy-done.6), channel_id=1, source_target_pairs={{4,8},{8,4},{5,9},{9,5},{6,10},{10,6},{7,11},{11,7},{20,24},{24,20... | collective-permute-start | bytes 589832 | tf_op jit(solution)/shard_map/ppermute | solution.py:343
  15.4 9.1 %collective-permute-start.5 = (bf16[2,192,256]{2,1,0:T(8,128)(2,1)S(1)}, bf16[2,192,256]{2,1,0:T(8,128)(2,1)S(1)}, u32[]{:S(2)}, u32[]{:S(2)}) collective-permute-start(bf16[2,192,256]{2,1,0:T(8,128)(2,1)S(1)} %copy-done.6), channel_id=1, source_target_pairs={{0,4},{4,0},{8,12},{12,8},{1,5},{5,1},{9,13},{13,9},{2,6},{6,2},{1... | collective-permute-start | bytes 589832 | tf_op jit(solution)/shard_map/ppermute | solution.py:343
  20.0 20.2 %collective-permute-start.9 = (bf16[4,192,384]{2,1,0:T(8,128)(2,1)S(1)}, bf16[4,192,384]{2,1,0:T(8,128)(2,1)S(1)}, u32[]{:S(2)}, u32[]{:S(2)}) collective-permute-start(bf16[4,192,384]{2,1,0:T(8,128)(2,1)S(1)} %get-tuple-element.40.refs_4_), channel_id=1, source_target_pairs={{4,8},{8,4},{5,9},{9,5},{6,10},{10,6},{7,11},{11,7},{20,24},{24,20... | collective-permute-start | bytes 1769480 | tf_op jit(solution)/shard_map/ppermute | solution.py:343
  20.7 19.5 %collective-permute-start.10 = (bf16[4,192,384]{2,1,0:T(8,128)(2,1)S(1)}, bf16[4,192,384]{2,1,0:T(8,128)(2,1)S(1)}, u32[]{:S(2)}, u32[]{:S(2)}) collective-permute-start(bf16[4,192,384]{2,1,0:T(8,128)(2,1)S(1)} %get-tuple-element.41.refs_5_), channel_id=1, source_target_pairs={{0,4},{4,0},{8,12},{12,8},{1,5},{5,1},{9,13},{13,9},{2,6},{6,2},{1... | collective-permute-start | bytes 1769480 | tf_op jit(solution)/shard_map/ppermute | solution.py:343
  23.9 11.7 %copy-start.3 = (bf16[2,192,512]{2,1,0:T(8,128)(2,1)S(1)}, bf16[2,192,512]{2,1,0:T(8,128)(2,1)}, u32[]{:S(2)}) copy-start(bf16[2,192,512]{2,1,0:T(8,128)(2,1)} %get-tuple-element.36.refs_2_) | copy-start | bytes 1179652
  24.6 11.0 %copy-start.4 = (s32[4,4]{1,0:T(4,128)S(1)}, s32[4,4]{1,0:T(4,128)}, u32[]{:S(2)}) copy-start(s32[4,4]{1,0:T(4,128)} %flags_ref.11) | copy-start | bytes 196
  24.6 11.0 %copy-start.5 = (s32[4]{0:T(128)S(1)}, s32[4]{0:T(128)}, u32[]{:S(2)}) copy-start(s32[4]{0:T(128)} %widths_ref.11) | copy-start | bytes 52
  24.6 23.0 %collective-permute-start.7 = (bf16[4,192,384]{2,1,0:T(8,128)(2,1)S(1)}, bf16[4,192,384]{2,1,0:T(8,128)(2,1)S(1)}, u32[]{:S(2)}, u32[]{:S(2)}) collective-permute-start(bf16[4,192,384]{2,1,0:T(8,128)(2,1)S(1)} %get-tuple-element.38.refs_4_), channel_id=1, source_target_pairs={{4,8},{8,4},{5,9},{9,5},{6,10},{10,6},{7,11},{11,7},{20,24},{24,20... | collective-permute-start | bytes 1769480 | tf_op jit(solution)/shard_map/ppermute | solution.py:343
  25.3 25.3 %collective-permute-start.8 = (bf16[4,192,384]{2,1,0:T(8,128)(2,1)S(1)}, bf16[4,192,384]{2,1,0:T(8,128)(2,1)S(1)}, u32[]{:S(2)}, u32[]{:S(2)}) collective-permute-start(bf16[4,192,384]{2,1,0:T(8,128)(2,1)S(1)} %get-tuple-element.39.refs_5_), channel_id=1, source_target_pairs={{0,4},{4,0},{8,12},{12,8},{1,5},{5,1},{9,13},{13,9},{2,6},{6,2},{1... | collective-permute-start | bytes 1769480 | tf_op jit(solution)/shard_map/ppermute | solution.py:343
  28.9 6.7 %collective-permute-start.2 = (bf16[192,768]{1,0:T(8,128)(2,1)S(1)}, bf16[192,768]{1,0:T(8,128)(2,1)S(1)}, u32[]{:S(2)}, u32[]{:S(2)}) collective-permute-start(bf16[192,768]{1,0:T(8,128)(2,1)S(1)} %pack.5.refs_1_), channel_id=1, source_target_pairs={{0,2},{2,0},{1,3},{3,1},{4,6},{6,4},{5,7},{7,5},{8,10},{10,8},{9,1... | collective-permute-start | bytes 884744 | tf_op jit(solution)/shard_map/ppermute | solution.py:335
  40.2 18.2 %collective-permute-start.15 = (bf16[2,192,384]{2,1,0:T(8,128)(2,1)S(1)}, bf16[2,192,384]{2,1,0:T(8,128)(2,1)S(1)}, u32[]{:S(2)}, u32[]{:S(2)}) collective-permute-start(bf16[2,192,384]{2,1,0:T(8,128)(2,1)S(1)} %slice.15), channel_id=1, source_target_pairs={{4,8},{8,4},{5,9},{9,5},{6,10},{10,6},{7,11},{11,7},{20,24},{24,20... | collective-permute-start | bytes 884744 | tf_op jit(solution)/shard_map/ppermute | solution.py:343
  40.9 17.5 %collective-permute-start.14 = (bf16[2,192,384]{2,1,0:T(8,128)(2,1)S(1)}, bf16[2,192,384]{2,1,0:T(8,128)(2,1)S(1)}, u32[]{:S(2)}, u32[]{:S(2)}) collective-permute-start(bf16[2,192,384]{2,1,0:T(8,128)(2,1)S(1)} %slice.14), channel_id=1, source_target_pairs={{0,4},{4,0},{8,12},{12,8},{1,5},{5,1},{9,13},{13,9},{2,6},{6,2},{1... | collective-permute-start | bytes 884744 | tf_op jit(solution)/shard_map/ppermute | solution.py:343
  50.7 9.9 %collective-permute-start.12 = (bf16[2,192,384]{2,1,0:T(8,128)(2,1)S(1)}, bf16[2,192,384]{2,1,0:T(8,128)(2,1)S(1)}, u32[]{:S(2)}, u32[]{:S(2)}) collective-permute-start(bf16[2,192,384]{2,1,0:T(8,128)(2,1)S(1)} %slice.13), channel_id=1, source_target_pairs={{4,8},{8,4},{5,9},{9,5},{6,10},{10,6},{7,11},{11,7},{20,24},{24,20... | collective-permute-start | bytes 884744 | tf_op jit(solution)/shard_map/ppermute | solution.py:343
  51.4 10.0 %collective-permute-start.11 = (bf16[2,192,384]{2,1,0:T(8,128)(2,1)S(1)}, bf16[2,192,384]{2,1,0:T(8,128)(2,1)S(1)}, u32[]{:S(2)}, u32[]{:S(2)}) collective-permute-start(bf16[2,192,384]{2,1,0:T(8,128)(2,1)S(1)} %slice.12), channel_id=1, source_target_pairs={{0,4},{4,0},{8,12},{12,8},{1,5},{5,1},{9,13},{13,9},{2,6},{6,2},{1... | collective-permute-start | bytes 884744 | tf_op jit(solution)/shard_map/ppermute | solution.py:343
  60.0 6.2 %collective-permute-start.16 = (bf16[192,384]{1,0:T(8,128)(2,1)S(1)}, bf16[192,384]{1,0:T(8,128)(2,1)S(1)}, u32[]{:S(2)}, u32[]{:S(2)}) collective-permute-start(bf16[192,384]{1,0:T(8,128)(2,1)S(1)} %get-tuple-element.62), channel_id=1, source_target_pairs={{0,2},{2,0},{1,3},{3,1},{4,6},{6,4},{5,7},{7,5},{8,10},{10,8},{9,1... | collective-permute-start | bytes 442376 | tf_op jit(solution)/shard_map/ppermute | solution.py:335
  63.0 5.2 %collective-permute-start.13 = (bf16[192,384]{1,0:T(8,128)(2,1)S(1)}, bf16[192,384]{1,0:T(8,128)(2,1)S(1)}, u32[]{:S(2)}, u32[]{:S(2)}) collective-permute-start(bf16[192,384]{1,0:T(8,128)(2,1)S(1)} %get-tuple-element.56), channel_id=1, source_target_pairs={{0,2},{2,0},{1,3},{3,1},{4,6},{6,4},{5,7},{7,5},{8,10},{10,8},{9,1... | collective-permute-start | bytes 442376 | tf_op jit(solution)/shard_map/ppermute | solution.py:335

commit v11 on v10

--- a/solution.py
+++ b/solution.py
@@ -351,18 +351,19 @@
 
     large = heads - heads // 3
     cuts = [(0, large), (large, heads - large)]
-    packed = pack(
-        (k, v), blocks_of(chunks[0], offsets) + [blocks_of(cut, (0,))[0] for cut in cuts],
-        (), spaces, True,
+    *sends, source = pack(
+        (k, v), blocks_of(chunks[0], offsets) + blocks_of(cuts[0], (0,)), (), spaces, True
     )
-    sends, sources = packed[: len(offsets)], packed[len(offsets) :]
     partners = [[along_space(x, offset) for x, offset in zip(sends, offsets)]]
-    firsts = [swap_both([x, x]) for x in sources]
-    *sends, own = pack(
-        (k, v), blocks_of(chunks[1], offsets) + blocks_of(chunks[1], (0,)), partners[0], spaces, False
+    firsts, own = [swap_both([source, source])], [source]
+    *sends, source, rest = pack(
+        (k, v),
+        blocks_of(chunks[1], offsets) + blocks_of(cuts[1], (0,)) + blocks_of(chunks[1], (0,)),
+        partners[0], spaces, False,
     )
     partners.append([along_space(x, offset) for x, offset in zip(sends, offsets)])
-    own = [sources[0], own]
+    firsts.append(swap_both([source, source]))
+    own.append(rest)
     sends = pack((q,), [(offset, 0, width) for offset in offsets], partners[1], spaces, False)
     query_parts = [q] + [along_space(x, offset) for x, offset in zip(sends, offsets)]
     partners[1] = list(tie(partners[1], sends))
@@ -405,12 +406,16 @@
     for hops in range(2, frames - 1):
         following = []
         for c, chunk in enumerate(chunks):
-            after = [state[1] for state in states]
-            came = list(tie(messages[c][::-1], after))[::-1]
+            came = messages[c]
+            if c == 0:
+                groups = partner_bands(came, hops - 1)[::-1] + own_band(came, hops)[::-1]
+                states[c] = attend(scalars, query_parts, groups, states[c], False, chunk, sizes)
+            came = list(tie(came[::-1], [state[1] for state in states]))[::-1]
             rows = behind if hops == last else behind + 2
             following.append(swap_both([came[1 - slot][:rows] for slot in range(2)]))
-            groups = partner_bands(came, hops - 1) + own_band(came, hops)
-            states[c] = attend(scalars, query_parts, groups, states[c], False, chunk, sizes)
+            if c > 0:
+                groups = partner_bands(came, hops - 1) + own_band(came, hops)
+                states[c] = attend(scalars, query_parts, groups, states[c], False, chunk, sizes)
         messages = following
     ends = []
     for message in messages:

time: 69.2 us -> 69.1 us (level)
  no operation moved by 1% of the time
where the time goes in v11:
time: 69.1 us; the launch traced here: 68.8 us
  starting transfers between devices  36 us (52%)
  Pallas kernels  16.2 us (23%)
  waiting for transfers between devices  16.2 us (23%)
    ppermute x12, starting transfers between devices, swap(): return lax.ppermute(x, 'frame', pairs)  29.4 us
    ppermute x5, waiting for transfers between devices, along_space(): lax.ppermute(x, 'space', [(s, (s + offset) % spaces) for s in range(space...  12.1 us
    pallas_call x6, Pallas kernels, attend(): pl.pallas_call(functools.partial(attend_kernel, spaces, frames, columns,...  11.8 us
    ppermute x5, starting transfers between devices, along_space(): lax.ppermute(x, 'space', [(s, (s + offset) % spaces) for s in range(space...  6.54 us
    ppermute x12, waiting for transfers between devices, swap(): return lax.ppermute(x, 'frame', pairs)  4.14 us
    pallas_call x3, Pallas kernels, pack(): pl.pallas_call(functools.partial(pack_kernel, spaces, tuple(jobs), staged...  2.71 us
    pallas_call x2, Pallas kernels, put(): pl.pallas_call(functools.partial(put_kernel, spaces, tuple(places)), in_s...  1.45 us
  transfers between devices with their start and end apart: 17, of which 7 were waited for; matrix products, arithmetic and copies ran while one was open for 0% of the time, Pallas kernels for 19%

profile of v11, /device:TPU:0, one launch (start us, length us, event | category | flops | bytes accessed | tf_op | source)
XLA Modules:
  0.0 68.8 jit_solution(2644016409318178104)
XLA Ops:
  0.0 0.0 copy-start.1
  0.0 0.0 copy-start.2
  0.0 2.1 %pack.3 = (bf16[2,192,384]{2,1,0:T(8,128)(2,1)}, bf16[2,192,512]{2,1,0:T(8,128)(2,1)}) custom-call(bf16[192,1536]{1,0:T(8,128)(2,1)} %bitcast.11, bf16[192,1536]{1,0:T(8,128)(2,1)} %bitcast.13), custom_call_target="tpu_custom_call" | custom-call | tf_op jit(solution)/shard_map/pack/pallas_call | solution.py:64
  2.1 3.0 %collective-permute-start = (bf16[2,192,384]{2,1,0:T(8,128)(2,1)}, bf16[2,192,384]{2,1,0:T(8,128)(2,1)S(1)}, u32[]{:S(2)}, u32[]{:S(2)}) collective-permute-start(bf16[2,192,384]{2,1,0:T(8,128)(2,1)} %get-tuple-element.34), channel_id=1, source_target_pairs={{0,2},{2,0},{1,3},{3,1},{4,6},{6,4},{5,7},{7,5},{8,10},{10,8},{9,1... | collective-permute-start | bytes 884744 | tf_op jit(solution)/shard_map/ppermute | solution.py:335
  5.1 0.7 collective-permute-start.4
  5.8 4.4 %collective-permute-start.3 = (bf16[2,192,512]{2,1,0:T(8,128)(2,1)}, bf16[2,192,512]{2,1,0:T(8,128)(2,1)S(1)}, u32[]{:S(2)}, u32[]{:S(2)}) collective-permute-start(bf16[2,192,512]{2,1,0:T(8,128)(2,1)} %get-tuple-element.36.refs_2_), channel_id=1, source_target_pairs={{0,4},{4,0},{8,12},{12,8},{1,5},{5,1},{9,13},{13,9},{2,6},{6,2},{1... | collective-permute-start | bytes 1179656 | tf_op jit(solution)/shard_map/ppermute | solution.py:343
  10.2 2.1 %collective-permute-done.refs_2_.refs_0_.refs_3_ = bf16[2,192,384]{2,1,0:T(8,128)(2,1)S(1)} collective-permute-done((bf16[2,192,384]{2,1,0:T(8,128)(2,1)}, bf16[2,192,384]{2,1,0:T(8,128)(2,1)S(1)}, u32[]{:S(2)}, u32[]{:S(2)}) %collective-permute-start) | collective-permute-done | bytes 294944 | tf_op jit(solution)/shard_map/ppermute | solution.py:335
  12.3 0.0 copy-done.1
  12.3 0.0 copy-done.2
  12.3 0.5 pack.4
  12.9 0.0 copy-start
  12.9 1.8 %collective-permute-start.1 = (bf16[2,192,384]{2,1,0:T(8,128)(2,1)S(1)}, bf16[2,192,384]{2,1,0:T(8,128)(2,1)S(1)}, u32[]{:S(2)}, u32[]{:S(2)}) collective-permute-start(bf16[2,192,384]{2,1,0:T(8,128)(2,1)S(1)} %get-tuple-element.35), channel_id=1, source_target_pairs={{0,2},{2,0},{1,3},{3,1},{4,6},{6,4},{5,7},{7,5},{8,10},{10,8},{9,1... | collective-permute-start | bytes 884744 | tf_op jit(solution)/shard_map/ppermute | solution.py:335
  14.7 0.7 collective-permute-start.6
  15.4 4.5 %collective-permute-start.5 = (bf16[2,192,256]{2,1,0:T(8,128)(2,1)S(1)}, bf16[2,192,256]{2,1,0:T(8,128)(2,1)S(1)}, u32[]{:S(2)}, u32[]{:S(2)}) collective-permute-start(bf16[2,192,256]{2,1,0:T(8,128)(2,1)S(1)} %get-tuple-element.37), channel_id=1, source_target_pairs={{0,4},{4,0},{8,12},{12,8},{1,5},{5,1},{9,13},{13,9},{2,6},{6,2},{1... | collective-permute-start | bytes 589832 | tf_op jit(solution)/shard_map/ppermute | solution.py:343
  19.8 0.0 collective-permute-done.4.refs_2_
  19.8 0.0 collective-permute-done.3.refs_1_
  19.8 0.1 join.3
  19.9 0.7 %collective-permute-start.9 = (bf16[4,192,384]{2,1,0:T(8,128)(2,1)S(1)}, bf16[4,192,384]{2,1,0:T(8,128)(2,1)S(1)}, u32[]{:S(2)}, u32[]{:S(2)}) collective-permute-start(bf16[4,192,384]{2,1,0:T(8,128)(2,1)S(1)} %get-tuple-element.40.refs_4_), channel_id=1, source_target_pairs={{4,8},{8,4},{5,9},{9,5},{6,10},{10,6},{7,11},{11,7},{20,24},{24,20... | collective-permute-start | bytes 1769480 | tf_op jit(solution)/shard_map/ppermute | solution.py:343
  20.6 2.6 %collective-permute-start.10 = (bf16[4,192,384]{2,1,0:T(8,128)(2,1)S(1)}, bf16[4,192,384]{2,1,0:T(8,128)(2,1)S(1)}, u32[]{:S(2)}, u32[]{:S(2)}) collective-permute-start(bf16[4,192,384]{2,1,0:T(8,128)(2,1)S(1)} %get-tuple-element.41.refs_5_), channel_id=1, source_target_pairs={{0,4},{4,0},{8,12},{12,8},{1,5},{5,1},{9,13},{13,9},{2,6},{6,2},{1... | collective-permute-start | bytes 1769480 | tf_op jit(solution)/shard_map/ppermute | solution.py:343
  23.3 0.0 collective-permute-done.1.refs_1_.refs_0_
  23.3 0.0 copy-done
  23.3 0.1 pack.5.refs_1_
  23.4 0.0 copy-start.3
  23.4 0.0 collective-permute-done.6.refs_4_
  23.4 1.3 %collective-permute-done.5.refs_3_ = bf16[2,192,256]{2,1,0:T(8,128)(2,1)S(1)} collective-permute-done((bf16[2,192,256]{2,1,0:T(8,128)(2,1)S(1)}, bf16[2,192,256]{2,1,0:T(8,128)(2,1)S(1)}, u32[]{:S(2)}, u32[]{:S(2)}) %collective-permute-start.5) | collective-permute-done | bytes 196640 | tf_op jit(solution)/shard_map/ppermute | solution.py:343
  24.7 0.1 join.2
  24.8 0.0 copy-start.4
  24.8 0.0 copy-start.5
  24.8 0.7 %collective-permute-start.7 = (bf16[4,192,384]{2,1,0:T(8,128)(2,1)S(1)}, bf16[4,192,384]{2,1,0:T(8,128)(2,1)S(1)}, u32[]{:S(2)}, u32[]{:S(2)}) collective-permute-start(bf16[4,192,384]{2,1,0:T(8,128)(2,1)S(1)} %get-tuple-element.38.refs_4_), channel_id=1, source_target_pairs={{4,8},{8,4},{5,9},{9,5},{6,10},{10,6},{7,11},{11,7},{20,24},{24,20... | collective-permute-start | bytes 1769480 | tf_op jit(solution)/shard_map/ppermute | solution.py:343
  25.5 3.6 %collective-permute-start.8 = (bf16[4,192,384]{2,1,0:T(8,128)(2,1)S(1)}, bf16[4,192,384]{2,1,0:T(8,128)(2,1)S(1)}, u32[]{:S(2)}, u32[]{:S(2)}) collective-permute-start(bf16[4,192,384]{2,1,0:T(8,128)(2,1)S(1)} %get-tuple-element.39.refs_5_), channel_id=1, source_target_pairs={{0,4},{4,0},{8,12},{12,8},{1,5},{5,1},{9,13},{13,9},{2,6},{6,2},{1... | collective-permute-start | bytes 1769480 | tf_op jit(solution)/shard_map/ppermute | solution.py:343
  29.2 0.5 collective-permute-start.2
  29.7 6.2 %collective-permute-done.2.refs_1_ = bf16[192,768]{1,0:T(8,128)(2,1)S(1)} collective-permute-done((bf16[192,768]{1,0:T(8,128)(2,1)S(1)}, bf16[192,768]{1,0:T(8,128)(2,1)S(1)}, u32[]{:S(2)}, u32[]{:S(2)}) %collective-permute-start.2) | collective-permute-done | bytes 294944 | tf_op jit(solution)/shard_map/ppermute | solution.py:335
  35.9 0.0 copy-done.3
  35.9 0.0 copy-done.4
  35.9 0.0 copy-done.5
  35.9 2.3 %attend.4 = (f32[3,128,384]{2,1,0:T(8,128)S(1)}, f32[3,8,384]{2,1,0:T(8,128)S(1)}) custom-call(s32[4,4]{1,0:T(4,128)S(1)} %copy-done.4, s32[4]{0:T(128)S(1)} %copy-done.5, bf16[192,1536]{1,0:T(8,128)(2,1)S(1)} %bitcast.5, bf16[192,768]{1,0:T(8,128)(2,1)S(1)} %collective-permute-done.2.refs_1_, bf16[2,192,512]{2,1,0:T(8,128)(2,1)S(1)} %copy-done.3, ...), custom_call_target="tpu_custom_call" | custom-call | flops 452984832 | bytes 1179648 | tf_op jit(solution)/shard_map/attend/pallas_call | solution.py:252
  38.2 2.3 %attend.6 = (f32[3,128,384]{2,1,0:T(8,128)S(1)}, f32[3,8,384]{2,1,0:T(8,128)S(1)}) custom-call(s32[4,4]{1,0:T(4,128)S(1)} %copy-done.4, s32[4]{0:T(128)S(1)} %copy-done.5, bf16[192,1536]{1,0:T(8,128)(2,1)S(1)} %bitcast.6, bf16[192,768]{1,0:T(8,128)(2,1)S(1)} %collective-permute-done.2.refs_1_, bf16[2,192,384]{2,1,0:T(8,128)(2,1)S(1)} %get-tuple-element.45.refs_2_, ...), custom_call_target="tpu_custom_call" | custom-call | flops 452984832 | bytes 1179648 | tf_op jit(solution)/shard_map/attend/pallas_call | solution.py:252
  40.4 0.0 collective-permute-done.9.refs_2_.refs_0_
  40.4 0.0 collective-permute-done.10.refs_3_.refs_1_
  40.4 2.1 %attend.5 = (f32[3,128,384]{2,1,0:T(8,128)S(1)}, f32[3,8,384]{2,1,0:T(8,128)S(1)}) custom-call(s32[4,4]{1,0:T(4,128)S(1)} %copy-done.4, s32[4]{0:T(128)S(1)} %copy-done.5, bf16[192,1536]{1,0:T(8,128)(2,1)S(1)} %bitcast.7, bf16[192,768]{1,0:T(8,128)(2,1)S(1)} %collective-permute-done.2.refs_1_, ...), custom_call_target="tpu_custom_call" | custom-call | flops 452984832 | bytes 1179648 | tf_op jit(solution)/shard_map/attend/pallas_call | solution.py:252
  42.6 0.7 collective-permute-start.15
  43.3 5.3 %collective-permute-start.14 = (bf16[2,192,384]{2,1,0:T(8,128)(2,1)S(1)}, bf16[2,192,384]{2,1,0:T(8,128)(2,1)S(1)}, u32[]{:S(2)}, u32[]{:S(2)}) collective-permute-start(bf16[2,192,384]{2,1,0:T(8,128)(2,1)S(1)} %slice.14), channel_id=1, source_target_pairs={{0,4},{4,0},{8,12},{12,8},{1,5},{5,1},{9,13},{13,9},{2,6},{6,2},{1... | collective-permute-start | bytes 884744 | tf_op jit(solution)/shard_map/ppermute | solution.py:343
  48.6 0.0 collective-permute-done.7.refs_0_
  48.6 1.6 %collective-permute-done.8.refs_1_ = bf16[4,192,384]{2,1,0:T(8,128)(2,1)S(1)} collective-permute-done((bf16[4,192,384]{2,1,0:T(8,128)(2,1)S(1)}, bf16[4,192,384]{2,1,0:T(8,128)(2,1)S(1)}, u32[]{:S(2)}, u32[]{:S(2)}) %collective-permute-start.8) | collective-permute-done | bytes 589856 | tf_op jit(solution)/shard_map/ppermute | solution.py:343
  50.2 0.7 collective-permute-start.12
  50.9 4.9 %collective-permute-start.11 = (bf16[2,192,384]{2,1,0:T(8,128)(2,1)S(1)}, bf16[2,192,384]{2,1,0:T(8,128)(2,1)S(1)}, u32[]{:S(2)}, u32[]{:S(2)}) collective-permute-start(bf16[2,192,384]{2,1,0:T(8,128)(2,1)S(1)} %slice.12), channel_id=1, source_target_pairs={{0,4},{4,0},{8,12},{12,8},{1,5},{5,1},{9,13},{13,9},{2,6},{6,2},{1... | collective-permute-start | bytes 884744 | tf_op jit(solution)/shard_map/ppermute | solution.py:343
  55.8 2.1 %attend.7 = (f32[3,128,384]{2,1,0:T(8,128)S(1)}, f32[3,8,384]{2,1,0:T(8,128)S(1)}) custom-call(s32[4,4]{1,0:T(4,128)S(1)} %copy-done.4, s32[4]{0:T(128)S(1)} %copy-done.5, bf16[192,1536]{1,0:T(8,128)(2,1)S(1)} %bitcast.8, bf16[192,768]{1,0:T(8,128)(2,1)S(1)} %collective-permute-done.2.refs_1_, bf16[4,192,384]{2,1,0:T(8,128)(2,1)S(1)} %get-tuple-element.48.refs_2_, ...), custom_call_target="tpu_custom_call" | custom-call | flops 452984832 | bytes 1179648 | tf_op jit(solution)/shard_map/attend/pallas_call | solution.py:252
  57.9 0.0 collective-permute-done.15.refs_1_
  57.9 0.0 collective-permute-done.14.refs_0_
  57.9 1.5 %attend_final.3 = (bf16[192,384]{1,0:T(8,128)(2,1)S(1)}, bf16[192,384]{1,0:T(8,128)(2,1)S(1)}) custom-call(s32[4,4]{1,0:T(4,128)S(1)} %copy-done.4, s32[4]{0:T(128)S(1)} %copy-done.5, bf16[192,1536]{1,0:T(8,128)(2,1)S(1)} %bitcast.9, bf16[192,768]{1,0:T(8,128)(2,1)S(1)} %collective-permute-done.2.refs_1_, ...), custom_call_target="tpu_custom_call" | custom-call | flops 226492416 | bytes 1179648 | tf_op jit(solution)/shard_map/attend_final/pallas_call | solution.py:252
  59.5 0.6 collective-permute-start.16
  60.1 0.0 collective-permute-done.12.refs_1_
  60.1 1.3 %collective-permute-done.11.refs_0_ = bf16[2,192,384]{2,1,0:T(8,128)(2,1)S(1)} collective-permute-done((bf16[2,192,384]{2,1,0:T(8,128)(2,1)S(1)}, bf16[2,192,384]{2,1,0:T(8,128)(2,1)S(1)}, u32[]{:S(2)}, u32[]{:S(2)}) %collective-permute-start.11) | collective-permute-done | bytes 294944 | tf_op jit(solution)/shard_map/ppermute | solution.py:343
  61.4 1.6 %attend_final.2 = (bf16[192,384]{1,0:T(8,128)(2,1)S(1)}, bf16[192,384]{1,0:T(8,128)(2,1)S(1)}) custom-call(s32[4,4]{1,0:T(4,128)S(1)} %copy-done.4, s32[4]{0:T(128)S(1)} %copy-done.5, bf16[192,1536]{1,0:T(8,128)(2,1)S(1)} %bitcast.10, bf16[192,768]{1,0:T(8,128)(2,1)S(1)} %collective-permute-done.2.refs_1_, ...), custom_call_target="tpu_custom_call" | custom-call | flops 226492416 | bytes 1179648 | tf_op jit(solution)/shard_map/attend_final/pallas_call | solution.py:252
  62.9 0.6 collective-permute-start.13
  63.5 2.5 %collective-permute-done.16.refs_2_ = bf16[192,384]{1,0:T(8,128)(2,1)S(1)} collective-permute-done((bf16[192,384]{1,0:T(8,128)(2,1)S(1)}, bf16[192,384]{1,0:T(8,128)(2,1)S(1)}, u32[]{:S(2)}, u32[]{:S(2)}) %collective-permute-start.16) | collective-permute-done | bytes 147488 | tf_op jit(solution)/shard_map/ppermute | solution.py:335
  66.0 0.8 %put.2.refs_1_ = bf16[192,1536]{1,0:T(8,128)(2,1)} custom-call(bf16[192,384]{1,0:T(8,128)(2,1)S(1)} %get-tuple-element.60.refs_0_, bf16[192,384]{1,0:T(8,128)(2,1)S(1)} %get-tuple-element.61.refs_1_, bf16[192,384]{1,0:T(8,128)(2,1)S(1)} %collective-permute-done.16.refs_2_), custom_call_target="tpu_custom_call" | custom-call | tf_op jit(solution)/shard_map/put/pallas_call | solution.py:309
  66.8 1.3 %collective-permute-done.13.refs_0_ = bf16[192,384]{1,0:T(8,128)(2,1)S(1)} collective-permute-done((bf16[192,384]{1,0:T(8,128)(2,1)S(1)}, bf16[192,384]{1,0:T(8,128)(2,1)S(1)}, u32[]{:S(2)}, u32[]{:S(2)}) %collective-permute-start.13) | collective-permute-done | bytes 147488 | tf_op jit(solution)/shard_map/ppermute | solution.py:335
  68.1 0.7 put.3
  (9 shorter events, 0.1 us)
Async XLA Ops:
  0.0 12.3 %copy-start.1 = (bf16[1,4,48,1536]{3,2,1,0:T(8,128)(2,1)S(1)}, bf16[1,4,48,1536]{3,2,1,0:T(8,128)(2,1)}, u32[]{:S(2)}) copy-start(bf16[1,4,48,1536]{3,2,1,0:T(8,128)(2,1)} %param.6) | copy-start | bytes 1769476
  0.0 12.3 %copy-start.2 = (bf16[1,4,48,1536]{3,2,1,0:T(8,128)(2,1)S(1)}, bf16[1,4,48,1536]{3,2,1,0:T(8,128)(2,1)}, u32[]{:S(2)}) copy-start(bf16[1,4,48,1536]{3,2,1,0:T(8,128)(2,1)} %param.7) | copy-start | bytes 1769476
  2.1 10.2 %collective-permute-start = (bf16[2,192,384]{2,1,0:T(8,128)(2,1)}, bf16[2,192,384]{2,1,0:T(8,128)(2,1)S(1)}, u32[]{:S(2)}, u32[]{:S(2)}) collective-permute-start(bf16[2,192,384]{2,1,0:T(8,128)(2,1)} %get-tuple-element.34), channel_id=1, source_target_pairs={{0,2},{2,0},{1,3},{3,1},{4,6},{6,4},{5,7},{7,5},{8,10},{10,8},{9,1... | collective-permute-start | bytes 884744 | tf_op jit(solution)/shard_map/ppermute | solution.py:335
  5.1 14.7 %collective-permute-start.4 = (bf16[2,192,512]{2,1,0:T(8,128)(2,1)}, bf16[2,192,512]{2,1,0:T(8,128)(2,1)S(1)}, u32[]{:S(2)}, u32[]{:S(2)}) collective-permute-start(bf16[2,192,512]{2,1,0:T(8,128)(2,1)} %get-tuple-element.36.refs_2_), channel_id=1, source_target_pairs={{4,8},{8,4},{5,9},{9,5},{6,10},{10,6},{7,11},{11,7},{20,24},{24,20... | collective-permute-start | bytes 1179656 | tf_op jit(solution)/shard_map/ppermute | solution.py:343
  5.8 14.0 %collective-permute-start.3 = (bf16[2,192,512]{2,1,0:T(8,128)(2,1)}, bf16[2,192,512]{2,1,0:T(8,128)(2,1)S(1)}, u32[]{:S(2)}, u32[]{:S(2)}) collective-permute-start(bf16[2,192,512]{2,1,0:T(8,128)(2,1)} %get-tuple-element.36.refs_2_), channel_id=1, source_target_pairs={{0,4},{4,0},{8,12},{12,8},{1,5},{5,1},{9,13},{13,9},{2,6},{6,2},{1... | collective-permute-start | bytes 1179656 | tf_op jit(solution)/shard_map/ppermute | solution.py:343
  12.9 10.4 %copy-start = (bf16[1,4,48,1536]{3,2,1,0:T(8,128)(2,1)S(1)}, bf16[1,4,48,1536]{3,2,1,0:T(8,128)(2,1)}, u32[]{:S(2)}) copy-start(bf16[1,4,48,1536]{3,2,1,0:T(8,128)(2,1)} %param.5) | copy-start | bytes 1769476
  12.9 10.4 %collective-permute-start.1 = (bf16[2,192,384]{2,1,0:T(8,128)(2,1)S(1)}, bf16[2,192,384]{2,1,0:T(8,128)(2,1)S(1)}, u32[]{:S(2)}, u32[]{:S(2)}) collective-permute-start(bf16[2,192,384]{2,1,0:T(8,128)(2,1)S(1)} %get-tuple-element.35), channel_id=1, source_target_pairs={{0,2},{2,0},{1,3},{3,1},{4,6},{6,4},{5,7},{7,5},{8,10},{10,8},{9,1... | collective-permute-start | bytes 884744 | tf_op jit(solution)/shard_map/ppermute | solution.py:335
  14.7 8.7 %collective-permute-start.6 = (bf16[2,192,256]{2,1,0:T(8,128)(2,1)S(1)}, bf16[2,192,256]{2,1,0:T(8,128)(2,1)S(1)}, u32[]{:S(2)}, u32[]{:S(2)}) collective-permute-start(bf16[2,192,256]{2,1,0:T(8,128)(2,1)S(1)} %get-tuple-element.37), channel_id=1, source_target_pairs={{4,8},{8,4},{5,9},{9,5},{6,10},{10,6},{7,11},{11,7},{20,24},{24,20... | collective-permute-start | bytes 589832 | tf_op jit(solution)/shard_map/ppermute | solution.py:343
  15.4 9.3 %collective-permute-start.5 = (bf16[2,192,256]{2,1,0:T(8,128)(2,1)S(1)}, bf16[2,192,256]{2,1,0:T(8,128)(2,1)S(1)}, u32[]{:S(2)}, u32[]{:S(2)}) collective-permute-start(bf16[2,192,256]{2,1,0:T(8,128)(2,1)S(1)} %get-tuple-element.37), channel_id=1, source_target_pairs={{0,4},{4,0},{8,12},{12,8},{1,5},{5,1},{9,13},{13,9},{2,6},{6,2},{1... | collective-permute-start | bytes 589832 | tf_op jit(solution)/shard_map/ppermute | solution.py:343
  19.9 20.5 %collective-permute-start.9 = (bf16[4,192,384]{2,1,0:T(8,128)(2,1)S(1)}, bf16[4,192,384]{2,1,0:T(8,128)(2,1)S(1)}, u32[]{:S(2)}, u32[]{:S(2)}) collective-permute-start(bf16[4,192,384]{2,1,0:T(8,128)(2,1)S(1)} %get-tuple-element.40.refs_4_), channel_id=1, source_target_pairs={{4,8},{8,4},{5,9},{9,5},{6,10},{10,6},{7,11},{11,7},{20,24},{24,20... | collective-permute-start | bytes 1769480 | tf_op jit(solution)/shard_map/ppermute | solution.py:343
  20.6 19.8 %collective-permute-start.10 = (bf16[4,192,384]{2,1,0:T(8,128)(2,1)S(1)}, bf16[4,192,384]{2,1,0:T(8,128)(2,1)S(1)}, u32[]{:S(2)}, u32[]{:S(2)}) collective-permute-start(bf16[4,192,384]{2,1,0:T(8,128)(2,1)S(1)} %get-tuple-element.41.refs_5_), channel_id=1, source_target_pairs={{0,4},{4,0},{8,12},{12,8},{1,5},{5,1},{9,13},{13,9},{2,6},{6,2},{1... | collective-permute-start | bytes 1769480 | tf_op jit(solution)/shard_map/ppermute | solution.py:343
  23.4 12.5 %copy-start.3 = (bf16[2,192,512]{2,1,0:T(8,128)(2,1)S(1)}, bf16[2,192,512]{2,1,0:T(8,128)(2,1)}, u32[]{:S(2)}) copy-start(bf16[2,192,512]{2,1,0:T(8,128)(2,1)} %get-tuple-element.36.refs_2_) | copy-start | bytes 1179652
  24.8 11.1 %copy-start.4 = (s32[4,4]{1,0:T(4,128)S(1)}, s32[4,4]{1,0:T(4,128)}, u32[]{:S(2)}) copy-start(s32[4,4]{1,0:T(4,128)} %flags_ref.11) | copy-start | bytes 196
  24.8 11.1 %copy-start.5 = (s32[4]{0:T(128)S(1)}, s32[4]{0:T(128)}, u32[]{:S(2)}) copy-start(s32[4]{0:T(128)} %widths_ref.11) | copy-start | bytes 52
  24.8 23.8 %collective-permute-start.7 = (bf16[4,192,384]{2,1,0:T(8,128)(2,1)S(1)}, bf16[4,192,384]{2,1,0:T(8,128)(2,1)S(1)}, u32[]{:S(2)}, u32[]{:S(2)}) collective-permute-start(bf16[4,192,384]{2,1,0:T(8,128)(2,1)S(1)} %get-tuple-element.38.refs_4_), channel_id=1, source_target_pairs={{4,8},{8,4},{5,9},{9,5},{6,10},{10,6},{7,11},{11,7},{20,24},{24,20... | collective-permute-start | bytes 1769480 | tf_op jit(solution)/shard_map/ppermute | solution.py:343
  25.5 24.6 %collective-permute-start.8 = (bf16[4,192,384]{2,1,0:T(8,128)(2,1)S(1)}, bf16[4,192,384]{2,1,0:T(8,128)(2,1)S(1)}, u32[]{:S(2)}, u32[]{:S(2)}) collective-permute-start(bf16[4,192,384]{2,1,0:T(8,128)(2,1)S(1)} %get-tuple-element.39.refs_5_), channel_id=1, source_target_pairs={{0,4},{4,0},{8,12},{12,8},{1,5},{5,1},{9,13},{13,9},{2,6},{6,2},{1... | collective-permute-start | bytes 1769480 | tf_op jit(solution)/shard_map/ppermute | solution.py:343
  29.2 6.7 %collective-permute-start.2 = (bf16[192,768]{1,0:T(8,128)(2,1)S(1)}, bf16[192,768]{1,0:T(8,128)(2,1)S(1)}, u32[]{:S(2)}, u32[]{:S(2)}) collective-permute-start(bf16[192,768]{1,0:T(8,128)(2,1)S(1)} %pack.5.refs_1_), channel_id=1, source_target_pairs={{0,2},{2,0},{1,3},{3,1},{4,6},{6,4},{5,7},{7,5},{8,10},{10,8},{9,1... | collective-permute-start | bytes 884744 | tf_op jit(solution)/shard_map/ppermute | solution.py:335
  42.6 15.3 %collective-permute-start.15 = (bf16[2,192,384]{2,1,0:T(8,128)(2,1)S(1)}, bf16[2,192,384]{2,1,0:T(8,128)(2,1)S(1)}, u32[]{:S(2)}, u32[]{:S(2)}) collective-permute-start(bf16[2,192,384]{2,1,0:T(8,128)(2,1)S(1)} %slice.15), channel_id=1, source_target_pairs={{4,8},{8,4},{5,9},{9,5},{6,10},{10,6},{7,11},{11,7},{20,24},{24,20... | collective-permute-start | bytes 884744 | tf_op jit(solution)/shard_map/ppermute | solution.py:343
  43.3 14.6 %collective-permute-start.14 = (bf16[2,192,384]{2,1,0:T(8,128)(2,1)S(1)}, bf16[2,192,384]{2,1,0:T(8,128)(2,1)S(1)}, u32[]{:S(2)}, u32[]{:S(2)}) collective-permute-start(bf16[2,192,384]{2,1,0:T(8,128)(2,1)S(1)} %slice.14), channel_id=1, source_target_pairs={{0,4},{4,0},{8,12},{12,8},{1,5},{5,1},{9,13},{13,9},{2,6},{6,2},{1... | collective-permute-start | bytes 884744 | tf_op jit(solution)/shard_map/ppermute | solution.py:343
  50.2 9.8 %collective-permute-start.12 = (bf16[2,192,384]{2,1,0:T(8,128)(2,1)S(1)}, bf16[2,192,384]{2,1,0:T(8,128)(2,1)S(1)}, u32[]{:S(2)}, u32[]{:S(2)}) collective-permute-start(bf16[2,192,384]{2,1,0:T(8,128)(2,1)S(1)} %slice.13), channel_id=1, source_target_pairs={{4,8},{8,4},{5,9},{9,5},{6,10},{10,6},{7,11},{11,7},{20,24},{24,20... | collective-permute-start | bytes 884744 | tf_op jit(solution)/shard_map/ppermute | solution.py:343
  50.9 10.5 %collective-permute-start.11 = (bf16[2,192,384]{2,1,0:T(8,128)(2,1)S(1)}, bf16[2,192,384]{2,1,0:T(8,128)(2,1)S(1)}, u32[]{:S(2)}, u32[]{:S(2)}) collective-permute-start(bf16[2,192,384]{2,1,0:T(8,128)(2,1)S(1)} %slice.12), channel_id=1, source_target_pairs={{0,4},{4,0},{8,12},{12,8},{1,5},{5,1},{9,13},{13,9},{2,6},{6,2},{1... | collective-permute-start | bytes 884744 | tf_op jit(solution)/shard_map/ppermute | solution.py:343
  59.5 6.6 %collective-permute-start.16 = (bf16[192,384]{1,0:T(8,128)(2,1)S(1)}, bf16[192,384]{1,0:T(8,128)(2,1)S(1)}, u32[]{:S(2)}, u32[]{:S(2)}) collective-permute-start(bf16[192,384]{1,0:T(8,128)(2,1)S(1)} %get-tuple-element.62), channel_id=1, source_target_pairs={{0,2},{2,0},{1,3},{3,1},{4,6},{6,4},{5,7},{7,5},{8,10},{10,8},{9,1... | collective-permute-start | bytes 442376 | tf_op jit(solution)/shard_map/ppermute | solution.py:335
  62.9 5.2 %collective-permute-start.13 = (bf16[192,384]{1,0:T(8,128)(2,1)S(1)}, bf16[192,384]{1,0:T(8,128)(2,1)S(1)}, u32[]{:S(2)}, u32[]{:S(2)}) collective-permute-start(bf16[192,384]{1,0:T(8,128)(2,1)S(1)} %get-tuple-element.54), channel_id=1, source_target_pairs={{0,2},{2,0},{1,3},{3,1},{4,6},{6,4},{5,7},{7,5},{8,10},{10,8},{9,1... | collective-permute-start | bytes 442376 | tf_op jit(solution)/shard_map/ppermute | solution.py:335

commit v12 on v11

--- a/solution.py
+++ b/solution.py
@@ -13,7 +13,7 @@
 VMEM_LIMIT = 16 * 1024 * 1024
 SMALL_LIMIT = 2 * 1024 * 1024
 STAGED_LIMIT = 60 * 1024 * 1024
-ROW_GROUPS = 4
+ROW_GROUPS = 2
 NT = (((1,), (1,)), ((), ()))
 TN = (((0,), (0,)), ((), ()))
 
@@ -334,17 +334,17 @@
     def along_space(x, offset):
         return lax.ppermute(x, "space", [(s, (s + offset) % spaces) for s in range(spaces)])
 
-    def swap(x, slot):
+    def swap(x, slot, brought=0):
         pairs = []
         for f in range(frames):
             side = 1 if (f + slot) % 2 == 0 else -1
-            if 0 <= f + side < frames:
+            if 0 <= f + side < frames and 0 <= f - side * brought < frames:
                 pairs.append((f, f + side))
         return lax.ppermute(x, "frame", pairs)
 
-    def swap_both(xs):
-        second = swap(xs[1], 1)
-        return [swap(xs[0], 0), second]
+    def swap_both(xs, brought=0):
+        second = swap(xs[1], 1, brought)
+        return [swap(xs[0], 0, brought), second]
 
     def blocks_of(chunk, which):
         return [(offset, chunk[0] * HEAD_DIM, chunk[1] * HEAD_DIM) for offset in which]
@@ -412,7 +412,8 @@
                 states[c] = attend(scalars, query_parts, groups, states[c], False, chunk, sizes)
             came = list(tie(came[::-1], [state[1] for state in states]))[::-1]
             rows = behind if hops == last else behind + 2
-            following.append(swap_both([came[1 - slot][:rows] for slot in range(2)]))
+            sent = [came[1 - slot][:rows] for slot in range(2)]
+            following.append(swap_both(sent, hops - 1))
             if c > 0:
                 groups = partner_bands(came, hops - 1) + own_band(came, hops)
                 states[c] = attend(scalars, query_parts, groups, states[c], False, chunk, sizes)

time: 69.1 us -> 68.9 us (level)
  waiting for transfers between devices: 16.2 us -> 23.6 us
  starting transfers between devices: 36 us -> 28.7 us
    ppermute x12, waiting for transfers between devices: 4.14 us -> 11.5 us  [swap(): return lax.ppermute(x, 'frame', pairs)]
    ppermute x12, starting transfers between devices: 29.4 us -> 22.1 us  [swap(): return lax.ppermute(x, 'frame', pairs)]
where the time goes in v12:
time: 68.9 us; the launch traced here: 68.6 us
  starting transfers between devices  28.7 us (42%)
  waiting for transfers between devices  23.6 us (34%)
  Pallas kernels  15.9 us (23%)
    ppermute x12, starting transfers between devices, swap(): return lax.ppermute(x, 'frame', pairs)  22.1 us
    ppermute x5, waiting for transfers between devices, along_space(): lax.ppermute(x, 'space', [(s, (s + offset) % spaces) for s in range(space...  12.1 us
    pallas_call x6, Pallas kernels, attend(): pl.pallas_call(functools.partial(attend_kernel, spaces, frames, columns,...  11.8 us
    ppermute x12, waiting for transfers between devices, swap(): return lax.ppermute(x, 'frame', pairs)  11.5 us
    ppermute x5, starting transfers between devices, along_space(): lax.ppermute(x, 'space', [(s, (s + offset) % spaces) for s in range(space...  6.54 us
    pallas_call x3, Pallas kernels, pack(): pl.pallas_call(functools.partial(pack_kernel, spaces, tuple(jobs), staged...  2.43 us
    pallas_call x2, Pallas kernels, put(): pl.pallas_call(functools.partial(put_kernel, spaces, tuple(places)), in_s...  1.45 us
  transfers between devices with their start and end apart: 17, of which 7 were waited for; matrix products, arithmetic and copies ran while one was open for 0% of the time, Pallas kernels for 19%

profile of v12, /device:TPU:0, one launch (start us, length us, event | category | flops | bytes accessed | tf_op | source)
XLA Modules:
  0.0 68.6 jit_solution(10618258954650668603)
XLA Ops:
  0.0 0.0 copy-start.1
  0.0 0.0 copy-start.2
  0.0 2.1 %pack.3 = (bf16[2,192,384]{2,1,0:T(8,128)(2,1)}, bf16[2,192,512]{2,1,0:T(8,128)(2,1)}) custom-call(bf16[192,1536]{1,0:T(8,128)(2,1)} %bitcast.11, bf16[192,1536]{1,0:T(8,128)(2,1)} %bitcast.13), custom_call_target="tpu_custom_call" | custom-call | tf_op jit(solution)/shard_map/pack/pallas_call | solution.py:64
  2.1 3.0 %collective-permute-start = (bf16[2,192,384]{2,1,0:T(8,128)(2,1)}, bf16[2,192,384]{2,1,0:T(8,128)(2,1)S(1)}, u32[]{:S(2)}, u32[]{:S(2)}) collective-permute-start(bf16[2,192,384]{2,1,0:T(8,128)(2,1)} %get-tuple-element.34), channel_id=1, source_target_pairs={{0,2},{2,0},{1,3},{3,1},{4,6},{6,4},{5,7},{7,5},{8,10},{10,8},{9,1... | collective-permute-start | bytes 884744 | tf_op jit(solution)/shard_map/ppermute | solution.py:335
  5.1 0.7 collective-permute-start.4
  5.8 4.4 %collective-permute-start.3 = (bf16[2,192,512]{2,1,0:T(8,128)(2,1)}, bf16[2,192,512]{2,1,0:T(8,128)(2,1)S(1)}, u32[]{:S(2)}, u32[]{:S(2)}) collective-permute-start(bf16[2,192,512]{2,1,0:T(8,128)(2,1)} %get-tuple-element.36.refs_2_), channel_id=1, source_target_pairs={{0,4},{4,0},{8,12},{12,8},{1,5},{5,1},{9,13},{13,9},{2,6},{6,2},{1... | collective-permute-start | bytes 1179656 | tf_op jit(solution)/shard_map/ppermute | solution.py:343
  10.2 2.1 %collective-permute-done.refs_2_.refs_0_.refs_3_ = bf16[2,192,384]{2,1,0:T(8,128)(2,1)S(1)} collective-permute-done((bf16[2,192,384]{2,1,0:T(8,128)(2,1)}, bf16[2,192,384]{2,1,0:T(8,128)(2,1)S(1)}, u32[]{:S(2)}, u32[]{:S(2)}) %collective-permute-start) | collective-permute-done | bytes 294944 | tf_op jit(solution)/shard_map/ppermute | solution.py:335
  12.3 0.0 copy-done.1
  12.3 0.0 copy-done.2
  12.3 0.3 pack.4
  12.6 0.0 copy-start
  12.6 1.8 %collective-permute-start.1 = (bf16[2,192,384]{2,1,0:T(8,128)(2,1)S(1)}, bf16[2,192,384]{2,1,0:T(8,128)(2,1)S(1)}, u32[]{:S(2)}, u32[]{:S(2)}) collective-permute-start(bf16[2,192,384]{2,1,0:T(8,128)(2,1)S(1)} %get-tuple-element.35), channel_id=1, source_target_pairs={{0,2},{2,0},{1,3},{3,1},{4,6},{6,4},{5,7},{7,5},{8,10},{10,8},{9,1... | collective-permute-start | bytes 884744 | tf_op jit(solution)/shard_map/ppermute | solution.py:335
  14.4 0.7 collective-permute-start.6
  15.1 4.5 %collective-permute-start.5 = (bf16[2,192,256]{2,1,0:T(8,128)(2,1)S(1)}, bf16[2,192,256]{2,1,0:T(8,128)(2,1)S(1)}, u32[]{:S(2)}, u32[]{:S(2)}) collective-permute-start(bf16[2,192,256]{2,1,0:T(8,128)(2,1)S(1)} %get-tuple-element.37), channel_id=1, source_target_pairs={{0,4},{4,0},{8,12},{12,8},{1,5},{5,1},{9,13},{13,9},{2,6},{6,2},{1... | collective-permute-start | bytes 589832 | tf_op jit(solution)/shard_map/ppermute | solution.py:343
  19.6 0.0 collective-permute-done.4.refs_2_
  19.6 0.0 collective-permute-done.3.refs_1_
  19.6 0.1 join.3
  19.7 0.7 %collective-permute-start.9 = (bf16[4,192,384]{2,1,0:T(8,128)(2,1)S(1)}, bf16[4,192,384]{2,1,0:T(8,128)(2,1)S(1)}, u32[]{:S(2)}, u32[]{:S(2)}) collective-permute-start(bf16[4,192,384]{2,1,0:T(8,128)(2,1)S(1)} %get-tuple-element.40.refs_4_), channel_id=1, source_target_pairs={{4,8},{8,4},{5,9},{9,5},{6,10},{10,6},{7,11},{11,7},{20,24},{24,20... | collective-permute-start | bytes 1769480 | tf_op jit(solution)/shard_map/ppermute | solution.py:343
  20.4 2.9 %collective-permute-start.10 = (bf16[4,192,384]{2,1,0:T(8,128)(2,1)S(1)}, bf16[4,192,384]{2,1,0:T(8,128)(2,1)S(1)}, u32[]{:S(2)}, u32[]{:S(2)}) collective-permute-start(bf16[4,192,384]{2,1,0:T(8,128)(2,1)S(1)} %get-tuple-element.41.refs_5_), channel_id=1, source_target_pairs={{0,4},{4,0},{8,12},{12,8},{1,5},{5,1},{9,13},{13,9},{2,6},{6,2},{1... | collective-permute-start | bytes 1769480 | tf_op jit(solution)/shard_map/ppermute | solution.py:343
  23.3 0.0 collective-permute-done.1.refs_1_.refs_0_
  23.3 0.0 copy-done
  23.3 0.1 pack.5.refs_1_
  23.4 0.0 copy-start.3
  23.4 0.0 collective-permute-done.6.refs_4_
  23.4 0.8 %collective-permute-done.5.refs_3_ = bf16[2,192,256]{2,1,0:T(8,128)(2,1)S(1)} collective-permute-done((bf16[2,192,256]{2,1,0:T(8,128)(2,1)S(1)}, bf16[2,192,256]{2,1,0:T(8,128)(2,1)S(1)}, u32[]{:S(2)}, u32[]{:S(2)}) %collective-permute-start.5) | collective-permute-done | bytes 196640 | tf_op jit(solution)/shard_map/ppermute | solution.py:343
  24.2 0.1 join.2
  24.3 0.0 copy-start.4
  24.3 0.0 copy-start.5
  24.3 0.7 %collective-permute-start.7 = (bf16[4,192,384]{2,1,0:T(8,128)(2,1)S(1)}, bf16[4,192,384]{2,1,0:T(8,128)(2,1)S(1)}, u32[]{:S(2)}, u32[]{:S(2)}) collective-permute-start(bf16[4,192,384]{2,1,0:T(8,128)(2,1)S(1)} %get-tuple-element.38.refs_4_), channel_id=1, source_target_pairs={{4,8},{8,4},{5,9},{9,5},{6,10},{10,6},{7,11},{11,7},{20,24},{24,20... | collective-permute-start | bytes 1769480 | tf_op jit(solution)/shard_map/ppermute | solution.py:343
  25.0 3.6 %collective-permute-start.8 = (bf16[4,192,384]{2,1,0:T(8,128)(2,1)S(1)}, bf16[4,192,384]{2,1,0:T(8,128)(2,1)S(1)}, u32[]{:S(2)}, u32[]{:S(2)}) collective-permute-start(bf16[4,192,384]{2,1,0:T(8,128)(2,1)S(1)} %get-tuple-element.39.refs_5_), channel_id=1, source_target_pairs={{0,4},{4,0},{8,12},{12,8},{1,5},{5,1},{9,13},{13,9},{2,6},{6,2},{1... | collective-permute-start | bytes 1769480 | tf_op jit(solution)/shard_map/ppermute | solution.py:343
  28.7 0.5 collective-permute-start.2
  29.2 6.2 %collective-permute-done.2.refs_1_ = bf16[192,768]{1,0:T(8,128)(2,1)S(1)} collective-permute-done((bf16[192,768]{1,0:T(8,128)(2,1)S(1)}, bf16[192,768]{1,0:T(8,128)(2,1)S(1)}, u32[]{:S(2)}, u32[]{:S(2)}) %collective-permute-start.2) | collective-permute-done | bytes 294944 | tf_op jit(solution)/shard_map/ppermute | solution.py:335
  35.4 0.0 copy-done.3
  35.4 0.0 copy-done.4
  35.4 0.0 copy-done.5
  35.4 2.3 %attend.4 = (f32[3,128,384]{2,1,0:T(8,128)S(1)}, f32[3,8,384]{2,1,0:T(8,128)S(1)}) custom-call(s32[4,4]{1,0:T(4,128)S(1)} %copy-done.4, s32[4]{0:T(128)S(1)} %copy-done.5, bf16[192,1536]{1,0:T(8,128)(2,1)S(1)} %bitcast.5, bf16[192,768]{1,0:T(8,128)(2,1)S(1)} %collective-permute-done.2.refs_1_, bf16[2,192,512]{2,1,0:T(8,128)(2,1)S(1)} %copy-done.3, ...), custom_call_target="tpu_custom_call" | custom-call | flops 452984832 | bytes 1179648 | tf_op jit(solution)/shard_map/attend/pallas_call | solution.py:252
  37.7 2.3 %attend.6 = (f32[3,128,384]{2,1,0:T(8,128)S(1)}, f32[3,8,384]{2,1,0:T(8,128)S(1)}) custom-call(s32[4,4]{1,0:T(4,128)S(1)} %copy-done.4, s32[4]{0:T(128)S(1)} %copy-done.5, bf16[192,1536]{1,0:T(8,128)(2,1)S(1)} %bitcast.6, bf16[192,768]{1,0:T(8,128)(2,1)S(1)} %collective-permute-done.2.refs_1_, bf16[2,192,384]{2,1,0:T(8,128)(2,1)S(1)} %get-tuple-element.45.refs_2_, ...), custom_call_target="tpu_custom_call" | custom-call | flops 452984832 | bytes 1179648 | tf_op jit(solution)/shard_map/attend/pallas_call | solution.py:252
  39.9 0.0 collective-permute-done.9.refs_2_.refs_0_
  39.9 0.0 collective-permute-done.10.refs_3_.refs_1_
  40.0 2.1 %attend.5 = (f32[3,128,384]{2,1,0:T(8,128)S(1)}, f32[3,8,384]{2,1,0:T(8,128)S(1)}) custom-call(s32[4,4]{1,0:T(4,128)S(1)} %copy-done.4, s32[4]{0:T(128)S(1)} %copy-done.5, bf16[192,1536]{1,0:T(8,128)(2,1)S(1)} %bitcast.7, bf16[192,768]{1,0:T(8,128)(2,1)S(1)} %collective-permute-done.2.refs_1_, ...), custom_call_target="tpu_custom_call" | custom-call | flops 452984832 | bytes 1179648 | tf_op jit(solution)/shard_map/attend/pallas_call | solution.py:252
  42.1 0.7 collective-permute-start.15
  42.8 1.3 %collective-permute-start.14 = (bf16[2,192,384]{2,1,0:T(8,128)(2,1)S(1)}, bf16[2,192,384]{2,1,0:T(8,128)(2,1)S(1)}, u32[]{:S(2)}, u32[]{:S(2)}) collective-permute-start(bf16[2,192,384]{2,1,0:T(8,128)(2,1)S(1)} %slice.14), channel_id=1, source_target_pairs={{4,0},{8,12},{5,1},{9,13},{6,2},{10,14},{7,3},{11,15},{20,16},{24,... | collective-permute-start | bytes 884744 | tf_op jit(solution)/shard_map/ppermute | solution.py:343
  44.1 0.0 collective-permute-done.7.refs_0_
  44.1 6.1 %collective-permute-done.8.refs_1_ = bf16[4,192,384]{2,1,0:T(8,128)(2,1)S(1)} collective-permute-done((bf16[4,192,384]{2,1,0:T(8,128)(2,1)S(1)}, bf16[4,192,384]{2,1,0:T(8,128)(2,1)S(1)}, u32[]{:S(2)}, u32[]{:S(2)}) %collective-permute-start.8) | collective-permute-done | bytes 589856 | tf_op jit(solution)/shard_map/ppermute | solution.py:343
  50.3 0.7 collective-permute-start.12
  51.0 1.3 %collective-permute-start.11 = (bf16[2,192,384]{2,1,0:T(8,128)(2,1)S(1)}, bf16[2,192,384]{2,1,0:T(8,128)(2,1)S(1)}, u32[]{:S(2)}, u32[]{:S(2)}) collective-permute-start(bf16[2,192,384]{2,1,0:T(8,128)(2,1)S(1)} %slice.12), channel_id=1, source_target_pairs={{4,0},{8,12},{5,1},{9,13},{6,2},{10,14},{7,3},{11,15},{20,16},{24,... | collective-permute-start | bytes 884744 | tf_op jit(solution)/shard_map/ppermute | solution.py:343
  52.3 2.1 %attend.7 = (f32[3,128,384]{2,1,0:T(8,128)S(1)}, f32[3,8,384]{2,1,0:T(8,128)S(1)}) custom-call(s32[4,4]{1,0:T(4,128)S(1)} %copy-done.4, s32[4]{0:T(128)S(1)} %copy-done.5, bf16[192,1536]{1,0:T(8,128)(2,1)S(1)} %bitcast.8, bf16[192,768]{1,0:T(8,128)(2,1)S(1)} %collective-permute-done.2.refs_1_, bf16[4,192,384]{2,1,0:T(8,128)(2,1)S(1)} %get-tuple-element.48.refs_2_, ...), custom_call_target="tpu_custom_call" | custom-call | flops 452984832 | bytes 1179648 | tf_op jit(solution)/shard_map/attend/pallas_call | solution.py:252
  54.3 0.0 collective-permute-done.15.refs_1_
  54.4 2.2 %collective-permute-done.14.refs_0_ = bf16[2,192,384]{2,1,0:T(8,128)(2,1)S(1)} collective-permute-done((bf16[2,192,384]{2,1,0:T(8,128)(2,1)S(1)}, bf16[2,192,384]{2,1,0:T(8,128)(2,1)S(1)}, u32[]{:S(2)}, u32[]{:S(2)}) %collective-permute-start.14) | collective-permute-done | bytes 294944 | tf_op jit(solution)/shard_map/ppermute | solution.py:343
  56.5 1.5 %attend_final.3 = (bf16[192,384]{1,0:T(8,128)(2,1)S(1)}, bf16[192,384]{1,0:T(8,128)(2,1)S(1)}) custom-call(s32[4,4]{1,0:T(4,128)S(1)} %copy-done.4, s32[4]{0:T(128)S(1)} %copy-done.5, bf16[192,1536]{1,0:T(8,128)(2,1)S(1)} %bitcast.9, bf16[192,768]{1,0:T(8,128)(2,1)S(1)} %collective-permute-done.2.refs_1_, ...), custom_call_target="tpu_custom_call" | custom-call | flops 226492416 | bytes 1179648 | tf_op jit(solution)/shard_map/attend_final/pallas_call | solution.py:252
  58.1 0.6 collective-permute-start.16
  58.7 0.0 collective-permute-done.12.refs_1_
  58.7 2.5 %collective-permute-done.11.refs_0_ = bf16[2,192,384]{2,1,0:T(8,128)(2,1)S(1)} collective-permute-done((bf16[2,192,384]{2,1,0:T(8,128)(2,1)S(1)}, bf16[2,192,384]{2,1,0:T(8,128)(2,1)S(1)}, u32[]{:S(2)}, u32[]{:S(2)}) %collective-permute-start.11) | collective-permute-done | bytes 294944 | tf_op jit(solution)/shard_map/ppermute | solution.py:343
  61.1 1.6 %attend_final.2 = (bf16[192,384]{1,0:T(8,128)(2,1)S(1)}, bf16[192,384]{1,0:T(8,128)(2,1)S(1)}) custom-call(s32[4,4]{1,0:T(4,128)S(1)} %copy-done.4, s32[4]{0:T(128)S(1)} %copy-done.5, bf16[192,1536]{1,0:T(8,128)(2,1)S(1)} %bitcast.10, bf16[192,768]{1,0:T(8,128)(2,1)S(1)} %collective-permute-done.2.refs_1_, ...), custom_call_target="tpu_custom_call" | custom-call | flops 226492416 | bytes 1179648 | tf_op jit(solution)/shard_map/attend_final/pallas_call | solution.py:252
  62.7 0.6 collective-permute-start.13
  63.3 0.0 collective-permute-done.16.refs_2_
  63.3 0.8 %put.2.refs_1_ = bf16[192,1536]{1,0:T(8,128)(2,1)} custom-call(bf16[192,384]{1,0:T(8,128)(2,1)S(1)} %get-tuple-element.60.refs_0_, bf16[192,384]{1,0:T(8,128)(2,1)S(1)} %get-tuple-element.61.refs_1_, bf16[192,384]{1,0:T(8,128)(2,1)S(1)} %collective-permute-done.16.refs_2_), custom_call_target="tpu_custom_call" | custom-call | tf_op jit(solution)/shard_map/put/pallas_call | solution.py:309
  64.1 3.8 %collective-permute-done.13.refs_0_ = bf16[192,384]{1,0:T(8,128)(2,1)S(1)} collective-permute-done((bf16[192,384]{1,0:T(8,128)(2,1)S(1)}, bf16[192,384]{1,0:T(8,128)(2,1)S(1)}, u32[]{:S(2)}, u32[]{:S(2)}) %collective-permute-start.13) | collective-permute-done | bytes 147488 | tf_op jit(solution)/shard_map/ppermute | solution.py:335
  67.9 0.7 put.3
  (9 shorter events, 0.1 us)
Async XLA Ops:
  0.0 12.3 %copy-start.1 = (bf16[1,4,48,1536]{3,2,1,0:T(8,128)(2,1)S(1)}, bf16[1,4,48,1536]{3,2,1,0:T(8,128)(2,1)}, u32[]{:S(2)}) copy-start(bf16[1,4,48,1536]{3,2,1,0:T(8,128)(2,1)} %param.6) | copy-start | bytes 1769476
  0.0 12.3 %copy-start.2 = (bf16[1,4,48,1536]{3,2,1,0:T(8,128)(2,1)S(1)}, bf16[1,4,48,1536]{3,2,1,0:T(8,128)(2,1)}, u32[]{:S(2)}) copy-start(bf16[1,4,48,1536]{3,2,1,0:T(8,128)(2,1)} %param.7) | copy-start | bytes 1769476
  2.1 10.2 %collective-permute-start = (bf16[2,192,384]{2,1,0:T(8,128)(2,1)}, bf16[2,192,384]{2,1,0:T(8,128)(2,1)S(1)}, u32[]{:S(2)}, u32[]{:S(2)}) collective-permute-start(bf16[2,192,384]{2,1,0:T(8,128)(2,1)} %get-tuple-element.34), channel_id=1, source_target_pairs={{0,2},{2,0},{1,3},{3,1},{4,6},{6,4},{5,7},{7,5},{8,10},{10,8},{9,1... | collective-permute-start | bytes 884744 | tf_op jit(solution)/shard_map/ppermute | solution.py:335
  5.1 14.5 %collective-permute-start.4 = (bf16[2,192,512]{2,1,0:T(8,128)(2,1)}, bf16[2,192,512]{2,1,0:T(8,128)(2,1)S(1)}, u32[]{:S(2)}, u32[]{:S(2)}) collective-permute-start(bf16[2,192,512]{2,1,0:T(8,128)(2,1)} %get-tuple-element.36.refs_2_), channel_id=1, source_target_pairs={{4,8},{8,4},{5,9},{9,5},{6,10},{10,6},{7,11},{11,7},{20,24},{24,20... | collective-permute-start | bytes 1179656 | tf_op jit(solution)/shard_map/ppermute | solution.py:343
  5.8 13.8 %collective-permute-start.3 = (bf16[2,192,512]{2,1,0:T(8,128)(2,1)}, bf16[2,192,512]{2,1,0:T(8,128)(2,1)S(1)}, u32[]{:S(2)}, u32[]{:S(2)}) collective-permute-start(bf16[2,192,512]{2,1,0:T(8,128)(2,1)} %get-tuple-element.36.refs_2_), channel_id=1, source_target_pairs={{0,4},{4,0},{8,12},{12,8},{1,5},{5,1},{9,13},{13,9},{2,6},{6,2},{1... | collective-permute-start | bytes 1179656 | tf_op jit(solution)/shard_map/ppermute | solution.py:343
  12.6 10.7 %copy-start = (bf16[1,4,48,1536]{3,2,1,0:T(8,128)(2,1)S(1)}, bf16[1,4,48,1536]{3,2,1,0:T(8,128)(2,1)}, u32[]{:S(2)}) copy-start(bf16[1,4,48,1536]{3,2,1,0:T(8,128)(2,1)} %param.5) | copy-start | bytes 1769476
  12.6 10.7 %collective-permute-start.1 = (bf16[2,192,384]{2,1,0:T(8,128)(2,1)S(1)}, bf16[2,192,384]{2,1,0:T(8,128)(2,1)S(1)}, u32[]{:S(2)}, u32[]{:S(2)}) collective-permute-start(bf16[2,192,384]{2,1,0:T(8,128)(2,1)S(1)} %get-tuple-element.35), channel_id=1, source_target_pairs={{0,2},{2,0},{1,3},{3,1},{4,6},{6,4},{5,7},{7,5},{8,10},{10,8},{9,1... | collective-permute-start | bytes 884744 | tf_op jit(solution)/shard_map/ppermute | solution.py:335
  14.4 9.0 %collective-permute-start.6 = (bf16[2,192,256]{2,1,0:T(8,128)(2,1)S(1)}, bf16[2,192,256]{2,1,0:T(8,128)(2,1)S(1)}, u32[]{:S(2)}, u32[]{:S(2)}) collective-permute-start(bf16[2,192,256]{2,1,0:T(8,128)(2,1)S(1)} %get-tuple-element.37), channel_id=1, source_target_pairs={{4,8},{8,4},{5,9},{9,5},{6,10},{10,6},{7,11},{11,7},{20,24},{24,20... | collective-permute-start | bytes 589832 | tf_op jit(solution)/shard_map/ppermute | solution.py:343
  15.1 9.1 %collective-permute-start.5 = (bf16[2,192,256]{2,1,0:T(8,128)(2,1)S(1)}, bf16[2,192,256]{2,1,0:T(8,128)(2,1)S(1)}, u32[]{:S(2)}, u32[]{:S(2)}) collective-permute-start(bf16[2,192,256]{2,1,0:T(8,128)(2,1)S(1)} %get-tuple-element.37), channel_id=1, source_target_pairs={{0,4},{4,0},{8,12},{12,8},{1,5},{5,1},{9,13},{13,9},{2,6},{6,2},{1... | collective-permute-start | bytes 589832 | tf_op jit(solution)/shard_map/ppermute | solution.py:343
  19.7 20.3 %collective-permute-start.9 = (bf16[4,192,384]{2,1,0:T(8,128)(2,1)S(1)}, bf16[4,192,384]{2,1,0:T(8,128)(2,1)S(1)}, u32[]{:S(2)}, u32[]{:S(2)}) collective-permute-start(bf16[4,192,384]{2,1,0:T(8,128)(2,1)S(1)} %get-tuple-element.40.refs_4_), channel_id=1, source_target_pairs={{4,8},{8,4},{5,9},{9,5},{6,10},{10,6},{7,11},{11,7},{20,24},{24,20... | collective-permute-start | bytes 1769480 | tf_op jit(solution)/shard_map/ppermute | solution.py:343
  20.4 19.6 %collective-permute-start.10 = (bf16[4,192,384]{2,1,0:T(8,128)(2,1)S(1)}, bf16[4,192,384]{2,1,0:T(8,128)(2,1)S(1)}, u32[]{:S(2)}, u32[]{:S(2)}) collective-permute-start(bf16[4,192,384]{2,1,0:T(8,128)(2,1)S(1)} %get-tuple-element.41.refs_5_), channel_id=1, source_target_pairs={{0,4},{4,0},{8,12},{12,8},{1,5},{5,1},{9,13},{13,9},{2,6},{6,2},{1... | collective-permute-start | bytes 1769480 | tf_op jit(solution)/shard_map/ppermute | solution.py:343
  23.4 12.0 %copy-start.3 = (bf16[2,192,512]{2,1,0:T(8,128)(2,1)S(1)}, bf16[2,192,512]{2,1,0:T(8,128)(2,1)}, u32[]{:S(2)}) copy-start(bf16[2,192,512]{2,1,0:T(8,128)(2,1)} %get-tuple-element.36.refs_2_) | copy-start | bytes 1179652
  24.3 11.1 %copy-start.4 = (s32[4,4]{1,0:T(4,128)S(1)}, s32[4,4]{1,0:T(4,128)}, u32[]{:S(2)}) copy-start(s32[4,4]{1,0:T(4,128)} %flags_ref.11) | copy-start | bytes 196
  24.3 11.1 %copy-start.5 = (s32[4]{0:T(128)S(1)}, s32[4]{0:T(128)}, u32[]{:S(2)}) copy-start(s32[4]{0:T(128)} %widths_ref.11) | copy-start | bytes 52
  24.3 19.8 %collective-permute-start.7 = (bf16[4,192,384]{2,1,0:T(8,128)(2,1)S(1)}, bf16[4,192,384]{2,1,0:T(8,128)(2,1)S(1)}, u32[]{:S(2)}, u32[]{:S(2)}) collective-permute-start(bf16[4,192,384]{2,1,0:T(8,128)(2,1)S(1)} %get-tuple-element.38.refs_4_), channel_id=1, source_target_pairs={{4,8},{8,4},{5,9},{9,5},{6,10},{10,6},{7,11},{11,7},{20,24},{24,20... | collective-permute-start | bytes 1769480 | tf_op jit(solution)/shard_map/ppermute | solution.py:343
  25.0 25.2 %collective-permute-start.8 = (bf16[4,192,384]{2,1,0:T(8,128)(2,1)S(1)}, bf16[4,192,384]{2,1,0:T(8,128)(2,1)S(1)}, u32[]{:S(2)}, u32[]{:S(2)}) collective-permute-start(bf16[4,192,384]{2,1,0:T(8,128)(2,1)S(1)} %get-tuple-element.39.refs_5_), channel_id=1, source_target_pairs={{0,4},{4,0},{8,12},{12,8},{1,5},{5,1},{9,13},{13,9},{2,6},{6,2},{1... | collective-permute-start | bytes 1769480 | tf_op jit(solution)/shard_map/ppermute | solution.py:343
  28.7 6.7 %collective-permute-start.2 = (bf16[192,768]{1,0:T(8,128)(2,1)S(1)}, bf16[192,768]{1,0:T(8,128)(2,1)S(1)}, u32[]{:S(2)}, u32[]{:S(2)}) collective-permute-start(bf16[192,768]{1,0:T(8,128)(2,1)S(1)} %pack.5.refs_1_), channel_id=1, source_target_pairs={{0,2},{2,0},{1,3},{3,1},{4,6},{6,4},{5,7},{7,5},{8,10},{10,8},{9,1... | collective-permute-start | bytes 884744 | tf_op jit(solution)/shard_map/ppermute | solution.py:335
  42.1 12.2 %collective-permute-start.15 = (bf16[2,192,384]{2,1,0:T(8,128)(2,1)S(1)}, bf16[2,192,384]{2,1,0:T(8,128)(2,1)S(1)}, u32[]{:S(2)}, u32[]{:S(2)}) collective-permute-start(bf16[2,192,384]{2,1,0:T(8,128)(2,1)S(1)} %slice.15), channel_id=1, source_target_pairs={{4,8},{8,4},{5,9},{9,5},{6,10},{10,6},{7,11},{11,7},{20,24},{24,20... | collective-permute-start | bytes 884744 | tf_op jit(solution)/shard_map/ppermute | solution.py:343
  42.8 13.7 %collective-permute-start.14 = (bf16[2,192,384]{2,1,0:T(8,128)(2,1)S(1)}, bf16[2,192,384]{2,1,0:T(8,128)(2,1)S(1)}, u32[]{:S(2)}, u32[]{:S(2)}) collective-permute-start(bf16[2,192,384]{2,1,0:T(8,128)(2,1)S(1)} %slice.14), channel_id=1, source_target_pairs={{4,0},{8,12},{5,1},{9,13},{6,2},{10,14},{7,3},{11,15},{20,16},{24,... | collective-permute-start | bytes 884744 | tf_op jit(solution)/shard_map/ppermute | solution.py:343
  50.3 8.4 %collective-permute-start.12 = (bf16[2,192,384]{2,1,0:T(8,128)(2,1)S(1)}, bf16[2,192,384]{2,1,0:T(8,128)(2,1)S(1)}, u32[]{:S(2)}, u32[]{:S(2)}) collective-permute-start(bf16[2,192,384]{2,1,0:T(8,128)(2,1)S(1)} %slice.13), channel_id=1, source_target_pairs={{4,8},{8,4},{5,9},{9,5},{6,10},{10,6},{7,11},{11,7},{20,24},{24,20... | collective-permute-start | bytes 884744 | tf_op jit(solution)/shard_map/ppermute | solution.py:343
  51.0 10.2 %collective-permute-start.11 = (bf16[2,192,384]{2,1,0:T(8,128)(2,1)S(1)}, bf16[2,192,384]{2,1,0:T(8,128)(2,1)S(1)}, u32[]{:S(2)}, u32[]{:S(2)}) collective-permute-start(bf16[2,192,384]{2,1,0:T(8,128)(2,1)S(1)} %slice.12), channel_id=1, source_target_pairs={{4,0},{8,12},{5,1},{9,13},{6,2},{10,14},{7,3},{11,15},{20,16},{24,... | collective-permute-start | bytes 884744 | tf_op jit(solution)/shard_map/ppermute | solution.py:343
  58.1 5.2 %collective-permute-start.16 = (bf16[192,384]{1,0:T(8,128)(2,1)S(1)}, bf16[192,384]{1,0:T(8,128)(2,1)S(1)}, u32[]{:S(2)}, u32[]{:S(2)}) collective-permute-start(bf16[192,384]{1,0:T(8,128)(2,1)S(1)} %get-tuple-element.62), channel_id=1, source_target_pairs={{0,2},{2,0},{1,3},{3,1},{4,6},{6,4},{5,7},{7,5},{8,10},{10,8},{9,1... | collective-permute-start | bytes 442376 | tf_op jit(solution)/shard_map/ppermute | solution.py:335
  62.7 5.2 %collective-permute-start.13 = (bf16[192,384]{1,0:T(8,128)(2,1)S(1)}, bf16[192,384]{1,0:T(8,128)(2,1)S(1)}, u32[]{:S(2)}, u32[]{:S(2)}) collective-permute-start(bf16[192,384]{1,0:T(8,128)(2,1)S(1)} %get-tuple-element.54), channel_id=1, source_target_pairs={{0,2},{2,0},{1,3},{3,1},{4,6},{6,4},{5,7},{7,5},{8,10},{10,8},{9,1... | collective-permute-start | bytes 442376 | tf_op jit(solution)/shard_map/ppermute | solution.py:335

commit v13 on v12

--- a/solution.py
+++ b/solution.py
@@ -420,7 +420,7 @@
         messages = following
     ends = []
     for message in messages:
-        came = list(tie(message, [state[1] for state in states]))
+        came = [*tie(message[:1], [state[1] for state in states]), message[1]]
         ends.append(partner_bands(came, last))
 
     own, returned = [], []

time: 68.9 us -> 68.2 us (0.990)
  Pallas kernels: 15.9 us -> 13.3 us
  waiting for transfers between devices: 23.6 us -> 25.5 us
    pallas_call x6, Pallas kernels: 11.8 us -> 9.21 us  [attend(): pl.pallas_call(functools.partial(attend_kernel, spaces, frames, columns,...]
    ppermute x12, waiting for transfers between devices: 11.5 us -> 13.4 us  [swap(): return lax.ppermute(x, 'frame', pairs)]
  transfers between devices with their start and end apart: 17 -> 17, of which waited for: 7 -> 7; matrix products, arithmetic and copies ran while one was open for 0% -> 0% of each run, Pallas kernels for 19% -> 16%
where the time goes in v13:
time: 68.2 us; the launch traced here: 67.9 us
  starting transfers between devices  28.7 us (42%)
  waiting for transfers between devices  25.5 us (37%)
  Pallas kernels  13.3 us (20%)
    ppermute x12, starting transfers between devices, swap(): return lax.ppermute(x, 'frame', pairs)  22.1 us
    ppermute x12, waiting for transfers between devices, swap(): return lax.ppermute(x, 'frame', pairs)  13.4 us
    ppermute x5, waiting for transfers between devices, along_space(): lax.ppermute(x, 'space', [(s, (s + offset) % spaces) for s in range(space...  12.1 us
    pallas_call x6, Pallas kernels, attend(): pl.pallas_call(functools.partial(attend_kernel, spaces, frames, columns,...  9.21 us
    ppermute x5, starting transfers between devices, along_space(): lax.ppermute(x, 'space', [(s, (s + offset) % spaces) for s in range(space...  6.54 us
    pallas_call x3, Pallas kernels, pack(): pl.pallas_call(functools.partial(pack_kernel, spaces, tuple(jobs), staged...  2.43 us
    pallas_call x2, Pallas kernels, put(): pl.pallas_call(functools.partial(put_kernel, spaces, tuple(places)), in_s...  1.45 us
  transfers between devices with their start and end apart: 17, of which 7 were waited for; matrix products, arithmetic and copies ran while one was open for 0% of the time, Pallas kernels for 16%

profile of v13, /device:TPU:0, one launch (start us, length us, event | category | flops | bytes accessed | tf_op | source)
XLA Modules:
  0.0 67.9 jit_solution(2949444607249095044)
XLA Ops:
  0.0 0.0 copy-start.1
  0.0 0.0 copy-start.2
  0.0 2.1 %pack.3 = (bf16[2,192,384]{2,1,0:T(8,128)(2,1)}, bf16[2,192,512]{2,1,0:T(8,128)(2,1)}) custom-call(bf16[192,1536]{1,0:T(8,128)(2,1)} %bitcast.11, bf16[192,1536]{1,0:T(8,128)(2,1)} %bitcast.13), custom_call_target="tpu_custom_call" | custom-call | tf_op jit(solution)/shard_map/pack/pallas_call | solution.py:64
  2.1 3.0 %collective-permute-start = (bf16[2,192,384]{2,1,0:T(8,128)(2,1)}, bf16[2,192,384]{2,1,0:T(8,128)(2,1)S(1)}, u32[]{:S(2)}, u32[]{:S(2)}) collective-permute-start(bf16[2,192,384]{2,1,0:T(8,128)(2,1)} %get-tuple-element.30), channel_id=1, source_target_pairs={{0,2},{2,0},{1,3},{3,1},{4,6},{6,4},{5,7},{7,5},{8,10},{10,8},{9,1... | collective-permute-start | bytes 884744 | tf_op jit(solution)/shard_map/ppermute | solution.py:335
  5.1 0.7 collective-permute-start.4
  5.8 4.4 %collective-permute-start.3 = (bf16[2,192,512]{2,1,0:T(8,128)(2,1)}, bf16[2,192,512]{2,1,0:T(8,128)(2,1)S(1)}, u32[]{:S(2)}, u32[]{:S(2)}) collective-permute-start(bf16[2,192,512]{2,1,0:T(8,128)(2,1)} %get-tuple-element.32.refs_2_), channel_id=1, source_target_pairs={{0,4},{4,0},{8,12},{12,8},{1,5},{5,1},{9,13},{13,9},{2,6},{6,2},{1... | collective-permute-start | bytes 1179656 | tf_op jit(solution)/shard_map/ppermute | solution.py:343
  10.2 2.1 %collective-permute-done.refs_2_.refs_0_.refs_3_ = bf16[2,192,384]{2,1,0:T(8,128)(2,1)S(1)} collective-permute-done((bf16[2,192,384]{2,1,0:T(8,128)(2,1)}, bf16[2,192,384]{2,1,0:T(8,128)(2,1)S(1)}, u32[]{:S(2)}, u32[]{:S(2)}) %collective-permute-start) | collective-permute-done | bytes 294944 | tf_op jit(solution)/shard_map/ppermute | solution.py:335
  12.3 0.0 copy-done.1
  12.3 0.0 copy-done.2
  12.3 0.3 pack.4
  12.6 0.0 copy-start
  12.6 1.8 %collective-permute-start.1 = (bf16[2,192,384]{2,1,0:T(8,128)(2,1)S(1)}, bf16[2,192,384]{2,1,0:T(8,128)(2,1)S(1)}, u32[]{:S(2)}, u32[]{:S(2)}) collective-permute-start(bf16[2,192,384]{2,1,0:T(8,128)(2,1)S(1)} %get-tuple-element.31), channel_id=1, source_target_pairs={{0,2},{2,0},{1,3},{3,1},{4,6},{6,4},{5,7},{7,5},{8,10},{10,8},{9,1... | collective-permute-start | bytes 884744 | tf_op jit(solution)/shard_map/ppermute | solution.py:335
  14.4 0.7 collective-permute-start.6
  15.1 4.5 %collective-permute-start.5 = (bf16[2,192,256]{2,1,0:T(8,128)(2,1)S(1)}, bf16[2,192,256]{2,1,0:T(8,128)(2,1)S(1)}, u32[]{:S(2)}, u32[]{:S(2)}) collective-permute-start(bf16[2,192,256]{2,1,0:T(8,128)(2,1)S(1)} %get-tuple-element.33), channel_id=1, source_target_pairs={{0,4},{4,0},{8,12},{12,8},{1,5},{5,1},{9,13},{13,9},{2,6},{6,2},{1... | collective-permute-start | bytes 589832 | tf_op jit(solution)/shard_map/ppermute | solution.py:343
  19.6 0.0 collective-permute-done.4.refs_2_
  19.6 0.0 collective-permute-done.3.refs_1_
  19.6 0.1 join.3
  19.7 0.7 %collective-permute-start.9 = (bf16[4,192,384]{2,1,0:T(8,128)(2,1)S(1)}, bf16[4,192,384]{2,1,0:T(8,128)(2,1)S(1)}, u32[]{:S(2)}, u32[]{:S(2)}) collective-permute-start(bf16[4,192,384]{2,1,0:T(8,128)(2,1)S(1)} %get-tuple-element.36.refs_4_), channel_id=1, source_target_pairs={{4,8},{8,4},{5,9},{9,5},{6,10},{10,6},{7,11},{11,7},{20,24},{24,20... | collective-permute-start | bytes 1769480 | tf_op jit(solution)/shard_map/ppermute | solution.py:343
  20.4 2.9 %collective-permute-start.10 = (bf16[4,192,384]{2,1,0:T(8,128)(2,1)S(1)}, bf16[4,192,384]{2,1,0:T(8,128)(2,1)S(1)}, u32[]{:S(2)}, u32[]{:S(2)}) collective-permute-start(bf16[4,192,384]{2,1,0:T(8,128)(2,1)S(1)} %get-tuple-element.37.refs_5_), channel_id=1, source_target_pairs={{0,4},{4,0},{8,12},{12,8},{1,5},{5,1},{9,13},{13,9},{2,6},{6,2},{1... | collective-permute-start | bytes 1769480 | tf_op jit(solution)/shard_map/ppermute | solution.py:343
  23.3 0.0 collective-permute-done.1.refs_1_.refs_0_
  23.3 0.0 copy-done
  23.3 0.1 pack.5.refs_1_
  23.4 0.0 copy-start.3
  23.4 0.0 collective-permute-done.6.refs_4_
  23.4 0.8 %collective-permute-done.5.refs_3_ = bf16[2,192,256]{2,1,0:T(8,128)(2,1)S(1)} collective-permute-done((bf16[2,192,256]{2,1,0:T(8,128)(2,1)S(1)}, bf16[2,192,256]{2,1,0:T(8,128)(2,1)S(1)}, u32[]{:S(2)}, u32[]{:S(2)}) %collective-permute-start.5) | collective-permute-done | bytes 196640 | tf_op jit(solution)/shard_map/ppermute | solution.py:343
  24.2 0.1 join.2
  24.3 0.0 copy-start.4
  24.3 0.0 copy-start.5
  24.3 0.7 %collective-permute-start.7 = (bf16[4,192,384]{2,1,0:T(8,128)(2,1)S(1)}, bf16[4,192,384]{2,1,0:T(8,128)(2,1)S(1)}, u32[]{:S(2)}, u32[]{:S(2)}) collective-permute-start(bf16[4,192,384]{2,1,0:T(8,128)(2,1)S(1)} %get-tuple-element.34.refs_4_), channel_id=1, source_target_pairs={{4,8},{8,4},{5,9},{9,5},{6,10},{10,6},{7,11},{11,7},{20,24},{24,20... | collective-permute-start | bytes 1769480 | tf_op jit(solution)/shard_map/ppermute | solution.py:343
  25.0 3.6 %collective-permute-start.8 = (bf16[4,192,384]{2,1,0:T(8,128)(2,1)S(1)}, bf16[4,192,384]{2,1,0:T(8,128)(2,1)S(1)}, u32[]{:S(2)}, u32[]{:S(2)}) collective-permute-start(bf16[4,192,384]{2,1,0:T(8,128)(2,1)S(1)} %get-tuple-element.35.refs_5_), channel_id=1, source_target_pairs={{0,4},{4,0},{8,12},{12,8},{1,5},{5,1},{9,13},{13,9},{2,6},{6,2},{1... | collective-permute-start | bytes 1769480 | tf_op jit(solution)/shard_map/ppermute | solution.py:343
  28.7 0.5 collective-permute-start.2
  29.2 6.2 %collective-permute-done.2.refs_1_ = bf16[192,768]{1,0:T(8,128)(2,1)S(1)} collective-permute-done((bf16[192,768]{1,0:T(8,128)(2,1)S(1)}, bf16[192,768]{1,0:T(8,128)(2,1)S(1)}, u32[]{:S(2)}, u32[]{:S(2)}) %collective-permute-start.2) | collective-permute-done | bytes 294944 | tf_op jit(solution)/shard_map/ppermute | solution.py:335
  35.4 0.0 copy-done.3
  35.4 0.0 copy-done.4
  35.4 0.0 copy-done.5
  35.4 2.2 %attend.4 = (f32[3,128,384]{2,1,0:T(8,128)S(1)}, f32[3,8,384]{2,1,0:T(8,128)S(1)}) custom-call(s32[4,4]{1,0:T(4,128)S(1)} %copy-done.4, s32[4]{0:T(128)S(1)} %copy-done.5, bf16[192,1536]{1,0:T(8,128)(2,1)S(1)} %bitcast.5, bf16[192,768]{1,0:T(8,128)(2,1)S(1)} %collective-permute-done.2.refs_1_, bf16[2,192,512]{2,1,0:T(8,128)(2,1)S(1)} %copy-done.3, ...), custom_call_target="tpu_custom_call" | custom-call | flops 452984832 | bytes 1179648 | tf_op jit(solution)/shard_map/attend/pallas_call | solution.py:252
  37.6 2.3 %attend.6 = (f32[3,128,384]{2,1,0:T(8,128)S(1)}, f32[3,8,384]{2,1,0:T(8,128)S(1)}) custom-call(s32[4,4]{1,0:T(4,128)S(1)} %copy-done.4, s32[4]{0:T(128)S(1)} %copy-done.5, bf16[192,1536]{1,0:T(8,128)(2,1)S(1)} %bitcast.6, bf16[192,768]{1,0:T(8,128)(2,1)S(1)} %collective-permute-done.2.refs_1_, bf16[2,192,384]{2,1,0:T(8,128)(2,1)S(1)} %get-tuple-element.41.refs_2_, ...), custom_call_target="tpu_custom_call" | custom-call | flops 452984832 | bytes 1179648 | tf_op jit(solution)/shard_map/attend/pallas_call | solution.py:252
  39.9 0.0 collective-permute-done.9.refs_2_.refs_0_
  39.9 0.0 collective-permute-done.10.refs_3_.refs_1_
  39.9 1.4 %attend.5 = (f32[3,128,384]{2,1,0:T(8,128)S(1)}, f32[3,8,384]{2,1,0:T(8,128)S(1)}) custom-call(s32[4,4]{1,0:T(4,128)S(1)} %copy-done.4, s32[4]{0:T(128)S(1)} %copy-done.5, bf16[192,1536]{1,0:T(8,128)(2,1)S(1)} %bitcast.7, bf16[192,768]{1,0:T(8,128)(2,1)S(1)} %collective-permute-done.2.refs_1_, ...), custom_call_target="tpu_custom_call" | custom-call | flops 452984832 | bytes 1179648 | tf_op jit(solution)/shard_map/attend/pallas_call | solution.py:252
  41.4 1.3 %collective-permute-start.14 = (bf16[2,192,384]{2,1,0:T(8,128)(2,1)S(1)}, bf16[2,192,384]{2,1,0:T(8,128)(2,1)S(1)}, u32[]{:S(2)}, u32[]{:S(2)}) collective-permute-start(bf16[2,192,384]{2,1,0:T(8,128)(2,1)S(1)} %slice.14), channel_id=1, source_target_pairs={{4,0},{8,12},{5,1},{9,13},{6,2},{10,14},{7,3},{11,15},{20,16},{24,... | collective-permute-start | bytes 884744 | tf_op jit(solution)/shard_map/ppermute | solution.py:343
  42.8 0.7 %collective-permute-start.15 = (bf16[2,192,384]{2,1,0:T(8,128)(2,1)S(1)}, bf16[2,192,384]{2,1,0:T(8,128)(2,1)S(1)}, u32[]{:S(2)}, u32[]{:S(2)}) collective-permute-start(bf16[2,192,384]{2,1,0:T(8,128)(2,1)S(1)} %slice.15), channel_id=1, source_target_pairs={{4,8},{8,4},{5,9},{9,5},{6,10},{10,6},{7,11},{11,7},{20,24},{24,20... | collective-permute-start | bytes 884744 | tf_op jit(solution)/shard_map/ppermute | solution.py:343
  43.5 0.0 collective-permute-done.7.refs_0_
  43.5 6.7 %collective-permute-done.8.refs_1_ = bf16[4,192,384]{2,1,0:T(8,128)(2,1)S(1)} collective-permute-done((bf16[4,192,384]{2,1,0:T(8,128)(2,1)S(1)}, bf16[4,192,384]{2,1,0:T(8,128)(2,1)S(1)}, u32[]{:S(2)}, u32[]{:S(2)}) %collective-permute-start.8) | collective-permute-done | bytes 589856 | tf_op jit(solution)/shard_map/ppermute | solution.py:343
  50.2 1.3 %collective-permute-start.11 = (bf16[2,192,384]{2,1,0:T(8,128)(2,1)S(1)}, bf16[2,192,384]{2,1,0:T(8,128)(2,1)S(1)}, u32[]{:S(2)}, u32[]{:S(2)}) collective-permute-start(bf16[2,192,384]{2,1,0:T(8,128)(2,1)S(1)} %slice.12), channel_id=1, source_target_pairs={{4,0},{8,12},{5,1},{9,13},{6,2},{10,14},{7,3},{11,15},{20,16},{24,... | collective-permute-start | bytes 884744 | tf_op jit(solution)/shard_map/ppermute | solution.py:343
  51.6 0.7 %collective-permute-start.12 = (bf16[2,192,384]{2,1,0:T(8,128)(2,1)S(1)}, bf16[2,192,384]{2,1,0:T(8,128)(2,1)S(1)}, u32[]{:S(2)}, u32[]{:S(2)}) collective-permute-start(bf16[2,192,384]{2,1,0:T(8,128)(2,1)S(1)} %slice.13), channel_id=1, source_target_pairs={{4,8},{8,4},{5,9},{9,5},{6,10},{10,6},{7,11},{11,7},{20,24},{24,20... | collective-permute-start | bytes 884744 | tf_op jit(solution)/shard_map/ppermute | solution.py:343
  52.3 1.4 %attend.7 = (f32[3,128,384]{2,1,0:T(8,128)S(1)}, f32[3,8,384]{2,1,0:T(8,128)S(1)}) custom-call(s32[4,4]{1,0:T(4,128)S(1)} %copy-done.4, s32[4]{0:T(128)S(1)} %copy-done.5, bf16[192,1536]{1,0:T(8,128)(2,1)S(1)} %bitcast.8, bf16[192,768]{1,0:T(8,128)(2,1)S(1)} %collective-permute-done.2.refs_1_, bf16[4,192,384]{2,1,0:T(8,128)(2,1)S(1)} %get-tuple-element.44.refs_2_, ...), custom_call_target="tpu_custom_call" | custom-call | flops 452984832 | bytes 1179648 | tf_op jit(solution)/shard_map/attend/pallas_call | solution.py:252
  53.7 2.8 %collective-permute-done.14.refs_0_ = bf16[2,192,384]{2,1,0:T(8,128)(2,1)S(1)} collective-permute-done((bf16[2,192,384]{2,1,0:T(8,128)(2,1)S(1)}, bf16[2,192,384]{2,1,0:T(8,128)(2,1)S(1)}, u32[]{:S(2)}, u32[]{:S(2)}) %collective-permute-start.14) | collective-permute-done | bytes 294944 | tf_op jit(solution)/shard_map/ppermute | solution.py:343
  56.5 0.0 collective-permute-done.15.refs_3_
  56.5 0.9 %attend_final.3 = (bf16[192,384]{1,0:T(8,128)(2,1)S(1)}, bf16[192,384]{1,0:T(8,128)(2,1)S(1)}) custom-call(s32[4,4]{1,0:T(4,128)S(1)} %copy-done.4, s32[4]{0:T(128)S(1)} %copy-done.5, bf16[192,1536]{1,0:T(8,128)(2,1)S(1)} %bitcast.9, bf16[192,768]{1,0:T(8,128)(2,1)S(1)} %collective-permute-done.2.refs_1_, bf16[2,192,384]{2,1,0:T(8,128)(2,1)S(1)} %tie.9.refs_2_, ...), custom_call_target="tpu_custom_call" | custom-call | flops 226492416 | bytes 1179648 | tf_op jit(solution)/shard_map/attend_final/pallas_call | solution.py:252
  57.5 0.6 collective-permute-start.16
  58.1 3.1 %collective-permute-done.11.refs_0_ = bf16[2,192,384]{2,1,0:T(8,128)(2,1)S(1)} collective-permute-done((bf16[2,192,384]{2,1,0:T(8,128)(2,1)S(1)}, bf16[2,192,384]{2,1,0:T(8,128)(2,1)S(1)}, u32[]{:S(2)}, u32[]{:S(2)}) %collective-permute-start.11) | collective-permute-done | bytes 294944 | tf_op jit(solution)/shard_map/ppermute | solution.py:343
  61.1 0.0 collective-permute-done.12.refs_3_
  61.1 0.9 %attend_final.2 = (bf16[192,384]{1,0:T(8,128)(2,1)S(1)}, bf16[192,384]{1,0:T(8,128)(2,1)S(1)}) custom-call(s32[4,4]{1,0:T(4,128)S(1)} %copy-done.4, s32[4]{0:T(128)S(1)} %copy-done.5, bf16[192,1536]{1,0:T(8,128)(2,1)S(1)} %bitcast.10, bf16[192,768]{1,0:T(8,128)(2,1)S(1)} %collective-permute-done.2.refs_1_, bf16[2,192,384]{2,1,0:T(8,128)(2,1)S(1)} %tie.7.refs_2_, ...), custom_call_target="tpu_custom_call" | custom-call | flops 226492416 | bytes 1179648 | tf_op jit(solution)/shard_map/attend_final/pallas_call | solution.py:252
  62.1 0.6 collective-permute-start.13
  62.7 0.0 collective-permute-done.16.refs_2_
  62.7 0.8 %put.2.refs_1_ = bf16[192,1536]{1,0:T(8,128)(2,1)} custom-call(bf16[192,384]{1,0:T(8,128)(2,1)S(1)} %get-tuple-element.52.refs_0_, bf16[192,384]{1,0:T(8,128)(2,1)S(1)} %get-tuple-element.53.refs_1_, bf16[192,384]{1,0:T(8,128)(2,1)S(1)} %collective-permute-done.16.refs_2_), custom_call_target="tpu_custom_call" | custom-call | tf_op jit(solution)/shard_map/put/pallas_call | solution.py:309
  63.5 3.8 %collective-permute-done.13.refs_0_ = bf16[192,384]{1,0:T(8,128)(2,1)S(1)} collective-permute-done((bf16[192,384]{1,0:T(8,128)(2,1)S(1)}, bf16[192,384]{1,0:T(8,128)(2,1)S(1)}, u32[]{:S(2)}, u32[]{:S(2)}) %collective-permute-start.13) | collective-permute-done | bytes 147488 | tf_op jit(solution)/shard_map/ppermute | solution.py:335
  67.3 0.7 put.3
  (9 shorter events, 0.1 us)
Async XLA Ops:
  0.0 12.3 %copy-start.1 = (bf16[1,4,48,1536]{3,2,1,0:T(8,128)(2,1)S(1)}, bf16[1,4,48,1536]{3,2,1,0:T(8,128)(2,1)}, u32[]{:S(2)}) copy-start(bf16[1,4,48,1536]{3,2,1,0:T(8,128)(2,1)} %param.6) | copy-start | bytes 1769476
  0.0 12.3 %copy-start.2 = (bf16[1,4,48,1536]{3,2,1,0:T(8,128)(2,1)S(1)}, bf16[1,4,48,1536]{3,2,1,0:T(8,128)(2,1)}, u32[]{:S(2)}) copy-start(bf16[1,4,48,1536]{3,2,1,0:T(8,128)(2,1)} %param.7) | copy-start | bytes 1769476
  2.1 10.2 %collective-permute-start = (bf16[2,192,384]{2,1,0:T(8,128)(2,1)}, bf16[2,192,384]{2,1,0:T(8,128)(2,1)S(1)}, u32[]{:S(2)}, u32[]{:S(2)}) collective-permute-start(bf16[2,192,384]{2,1,0:T(8,128)(2,1)} %get-tuple-element.30), channel_id=1, source_target_pairs={{0,2},{2,0},{1,3},{3,1},{4,6},{6,4},{5,7},{7,5},{8,10},{10,8},{9,1... | collective-permute-start | bytes 884744 | tf_op jit(solution)/shard_map/ppermute | solution.py:335
  5.1 14.5 %collective-permute-start.4 = (bf16[2,192,512]{2,1,0:T(8,128)(2,1)}, bf16[2,192,512]{2,1,0:T(8,128)(2,1)S(1)}, u32[]{:S(2)}, u32[]{:S(2)}) collective-permute-start(bf16[2,192,512]{2,1,0:T(8,128)(2,1)} %get-tuple-element.32.refs_2_), channel_id=1, source_target_pairs={{4,8},{8,4},{5,9},{9,5},{6,10},{10,6},{7,11},{11,7},{20,24},{24,20... | collective-permute-start | bytes 1179656 | tf_op jit(solution)/shard_map/ppermute | solution.py:343
  5.8 13.8 %collective-permute-start.3 = (bf16[2,192,512]{2,1,0:T(8,128)(2,1)}, bf16[2,192,512]{2,1,0:T(8,128)(2,1)S(1)}, u32[]{:S(2)}, u32[]{:S(2)}) collective-permute-start(bf16[2,192,512]{2,1,0:T(8,128)(2,1)} %get-tuple-element.32.refs_2_), channel_id=1, source_target_pairs={{0,4},{4,0},{8,12},{12,8},{1,5},{5,1},{9,13},{13,9},{2,6},{6,2},{1... | collective-permute-start | bytes 1179656 | tf_op jit(solution)/shard_map/ppermute | solution.py:343
  12.6 10.7 %copy-start = (bf16[1,4,48,1536]{3,2,1,0:T(8,128)(2,1)S(1)}, bf16[1,4,48,1536]{3,2,1,0:T(8,128)(2,1)}, u32[]{:S(2)}) copy-start(bf16[1,4,48,1536]{3,2,1,0:T(8,128)(2,1)} %param.5) | copy-start | bytes 1769476
  12.6 10.7 %collective-permute-start.1 = (bf16[2,192,384]{2,1,0:T(8,128)(2,1)S(1)}, bf16[2,192,384]{2,1,0:T(8,128)(2,1)S(1)}, u32[]{:S(2)}, u32[]{:S(2)}) collective-permute-start(bf16[2,192,384]{2,1,0:T(8,128)(2,1)S(1)} %get-tuple-element.31), channel_id=1, source_target_pairs={{0,2},{2,0},{1,3},{3,1},{4,6},{6,4},{5,7},{7,5},{8,10},{10,8},{9,1... | collective-permute-start | bytes 884744 | tf_op jit(solution)/shard_map/ppermute | solution.py:335
  14.4 9.0 %collective-permute-start.6 = (bf16[2,192,256]{2,1,0:T(8,128)(2,1)S(1)}, bf16[2,192,256]{2,1,0:T(8,128)(2,1)S(1)}, u32[]{:S(2)}, u32[]{:S(2)}) collective-permute-start(bf16[2,192,256]{2,1,0:T(8,128)(2,1)S(1)} %get-tuple-element.33), channel_id=1, source_target_pairs={{4,8},{8,4},{5,9},{9,5},{6,10},{10,6},{7,11},{11,7},{20,24},{24,20... | collective-permute-start | bytes 589832 | tf_op jit(solution)/shard_map/ppermute | solution.py:343
  15.1 9.1 %collective-permute-start.5 = (bf16[2,192,256]{2,1,0:T(8,128)(2,1)S(1)}, bf16[2,192,256]{2,1,0:T(8,128)(2,1)S(1)}, u32[]{:S(2)}, u32[]{:S(2)}) collective-permute-start(bf16[2,192,256]{2,1,0:T(8,128)(2,1)S(1)} %get-tuple-element.33), channel_id=1, source_target_pairs={{0,4},{4,0},{8,12},{12,8},{1,5},{5,1},{9,13},{13,9},{2,6},{6,2},{1... | collective-permute-start | bytes 589832 | tf_op jit(solution)/shard_map/ppermute | solution.py:343
  19.7 20.3 %collective-permute-start.9 = (bf16[4,192,384]{2,1,0:T(8,128)(2,1)S(1)}, bf16[4,192,384]{2,1,0:T(8,128)(2,1)S(1)}, u32[]{:S(2)}, u32[]{:S(2)}) collective-permute-start(bf16[4,192,384]{2,1,0:T(8,128)(2,1)S(1)} %get-tuple-element.36.refs_4_), channel_id=1, source_target_pairs={{4,8},{8,4},{5,9},{9,5},{6,10},{10,6},{7,11},{11,7},{20,24},{24,20... | collective-permute-start | bytes 1769480 | tf_op jit(solution)/shard_map/ppermute | solution.py:343
  20.4 19.6 %collective-permute-start.10 = (bf16[4,192,384]{2,1,0:T(8,128)(2,1)S(1)}, bf16[4,192,384]{2,1,0:T(8,128)(2,1)S(1)}, u32[]{:S(2)}, u32[]{:S(2)}) collective-permute-start(bf16[4,192,384]{2,1,0:T(8,128)(2,1)S(1)} %get-tuple-element.37.refs_5_), channel_id=1, source_target_pairs={{0,4},{4,0},{8,12},{12,8},{1,5},{5,1},{9,13},{13,9},{2,6},{6,2},{1... | collective-permute-start | bytes 1769480 | tf_op jit(solution)/shard_map/ppermute | solution.py:343
  23.4 12.0 %copy-start.3 = (bf16[2,192,512]{2,1,0:T(8,128)(2,1)S(1)}, bf16[2,192,512]{2,1,0:T(8,128)(2,1)}, u32[]{:S(2)}) copy-start(bf16[2,192,512]{2,1,0:T(8,128)(2,1)} %get-tuple-element.32.refs_2_) | copy-start | bytes 1179652
  24.3 11.1 %copy-start.4 = (s32[4,4]{1,0:T(4,128)S(1)}, s32[4,4]{1,0:T(4,128)}, u32[]{:S(2)}) copy-start(s32[4,4]{1,0:T(4,128)} %flags_ref.11) | copy-start | bytes 196
  24.3 11.1 %copy-start.5 = (s32[4]{0:T(128)S(1)}, s32[4]{0:T(128)}, u32[]{:S(2)}) copy-start(s32[4]{0:T(128)} %widths_ref.11) | copy-start | bytes 52
  24.3 19.1 %collective-permute-start.7 = (bf16[4,192,384]{2,1,0:T(8,128)(2,1)S(1)}, bf16[4,192,384]{2,1,0:T(8,128)(2,1)S(1)}, u32[]{:S(2)}, u32[]{:S(2)}) collective-permute-start(bf16[4,192,384]{2,1,0:T(8,128)(2,1)S(1)} %get-tuple-element.34.refs_4_), channel_id=1, source_target_pairs={{4,8},{8,4},{5,9},{9,5},{6,10},{10,6},{7,11},{11,7},{20,24},{24,20... | collective-permute-start | bytes 1769480 | tf_op jit(solution)/shard_map/ppermute | solution.py:343
  25.0 25.2 %collective-permute-start.8 = (bf16[4,192,384]{2,1,0:T(8,128)(2,1)S(1)}, bf16[4,192,384]{2,1,0:T(8,128)(2,1)S(1)}, u32[]{:S(2)}, u32[]{:S(2)}) collective-permute-start(bf16[4,192,384]{2,1,0:T(8,128)(2,1)S(1)} %get-tuple-element.35.refs_5_), channel_id=1, source_target_pairs={{0,4},{4,0},{8,12},{12,8},{1,5},{5,1},{9,13},{13,9},{2,6},{6,2},{1... | collective-permute-start | bytes 1769480 | tf_op jit(solution)/shard_map/ppermute | solution.py:343
  28.7 6.7 %collective-permute-start.2 = (bf16[192,768]{1,0:T(8,128)(2,1)S(1)}, bf16[192,768]{1,0:T(8,128)(2,1)S(1)}, u32[]{:S(2)}, u32[]{:S(2)}) collective-permute-start(bf16[192,768]{1,0:T(8,128)(2,1)S(1)} %pack.5.refs_1_), channel_id=1, source_target_pairs={{0,2},{2,0},{1,3},{3,1},{4,6},{6,4},{5,7},{7,5},{8,10},{10,8},{9,1... | collective-permute-start | bytes 884744 | tf_op jit(solution)/shard_map/ppermute | solution.py:335
  41.4 15.1 %collective-permute-start.14 = (bf16[2,192,384]{2,1,0:T(8,128)(2,1)S(1)}, bf16[2,192,384]{2,1,0:T(8,128)(2,1)S(1)}, u32[]{:S(2)}, u32[]{:S(2)}) collective-permute-start(bf16[2,192,384]{2,1,0:T(8,128)(2,1)S(1)} %slice.14), channel_id=1, source_target_pairs={{4,0},{8,12},{5,1},{9,13},{6,2},{10,14},{7,3},{11,15},{20,16},{24,... | collective-permute-start | bytes 884744 | tf_op jit(solution)/shard_map/ppermute | solution.py:343
  42.8 13.8 %collective-permute-start.15 = (bf16[2,192,384]{2,1,0:T(8,128)(2,1)S(1)}, bf16[2,192,384]{2,1,0:T(8,128)(2,1)S(1)}, u32[]{:S(2)}, u32[]{:S(2)}) collective-permute-start(bf16[2,192,384]{2,1,0:T(8,128)(2,1)S(1)} %slice.15), channel_id=1, source_target_pairs={{4,8},{8,4},{5,9},{9,5},{6,10},{10,6},{7,11},{11,7},{20,24},{24,20... | collective-permute-start | bytes 884744 | tf_op jit(solution)/shard_map/ppermute | solution.py:343
  50.2 10.9 %collective-permute-start.11 = (bf16[2,192,384]{2,1,0:T(8,128)(2,1)S(1)}, bf16[2,192,384]{2,1,0:T(8,128)(2,1)S(1)}, u32[]{:S(2)}, u32[]{:S(2)}) collective-permute-start(bf16[2,192,384]{2,1,0:T(8,128)(2,1)S(1)} %slice.12), channel_id=1, source_target_pairs={{4,0},{8,12},{5,1},{9,13},{6,2},{10,14},{7,3},{11,15},{20,16},{24,... | collective-permute-start | bytes 884744 | tf_op jit(solution)/shard_map/ppermute | solution.py:343
  51.6 9.6 %collective-permute-start.12 = (bf16[2,192,384]{2,1,0:T(8,128)(2,1)S(1)}, bf16[2,192,384]{2,1,0:T(8,128)(2,1)S(1)}, u32[]{:S(2)}, u32[]{:S(2)}) collective-permute-start(bf16[2,192,384]{2,1,0:T(8,128)(2,1)S(1)} %slice.13), channel_id=1, source_target_pairs={{4,8},{8,4},{5,9},{9,5},{6,10},{10,6},{7,11},{11,7},{20,24},{24,20... | collective-permute-start | bytes 884744 | tf_op jit(solution)/shard_map/ppermute | solution.py:343
  57.5 5.2 %collective-permute-start.16 = (bf16[192,384]{1,0:T(8,128)(2,1)S(1)}, bf16[192,384]{1,0:T(8,128)(2,1)S(1)}, u32[]{:S(2)}, u32[]{:S(2)}) collective-permute-start(bf16[192,384]{1,0:T(8,128)(2,1)S(1)} %get-tuple-element.54), channel_id=1, source_target_pairs={{0,2},{2,0},{1,3},{3,1},{4,6},{6,4},{5,7},{7,5},{8,10},{10,8},{9,1... | collective-permute-start | bytes 442376 | tf_op jit(solution)/shard_map/ppermute | solution.py:335
  62.1 5.2 %collective-permute-start.13 = (bf16[192,384]{1,0:T(8,128)(2,1)S(1)}, bf16[192,384]{1,0:T(8,128)(2,1)S(1)}, u32[]{:S(2)}, u32[]{:S(2)}) collective-permute-start(bf16[192,384]{1,0:T(8,128)(2,1)S(1)} %get-tuple-element.48), channel_id=1, source_target_pairs={{0,2},{2,0},{1,3},{3,1},{4,6},{6,4},{5,7},{7,5},{8,10},{10,8},{9,1... | collective-permute-start | bytes 442376 | tf_op jit(solution)/shard_map/ppermute | solution.py:335

commit v14 on v12

--- a/solution.py
+++ b/solution.py
@@ -407,16 +407,12 @@
         following = []
         for c, chunk in enumerate(chunks):
             came = messages[c]
-            if c == 0:
-                groups = partner_bands(came, hops - 1)[::-1] + own_band(came, hops)[::-1]
-                states[c] = attend(scalars, query_parts, groups, states[c], False, chunk, sizes)
             came = list(tie(came[::-1], [state[1] for state in states]))[::-1]
             rows = behind if hops == last else behind + 2
             sent = [came[1 - slot][:rows] for slot in range(2)]
             following.append(swap_both(sent, hops - 1))
-            if c > 0:
-                groups = partner_bands(came, hops - 1) + own_band(came, hops)
-                states[c] = attend(scalars, query_parts, groups, states[c], False, chunk, sizes)
+            groups = partner_bands(came, hops - 1) + own_band(came, hops)
+            states[c] = attend(scalars, query_parts, groups, states[c], False, chunk, sizes)
         messages = following
     ends = []
     for message in messages:

time: 68.9 us -> 68.2 us (0.990)
  Pallas kernels: 15.9 us -> 13.3 us
  waiting for transfers between devices: 23.6 us -> 25.5 us
    pallas_call x6, Pallas kernels: 11.8 us -> 9.21 us  [attend(): pl.pallas_call(functools.partial(attend_kernel, spaces, frames, columns,...]
    ppermute x12, waiting for transfers between devices: 11.5 us -> 13.4 us  [swap(): return lax.ppermute(x, 'frame', pairs)]
  transfers between devices with their start and end apart: 17 -> 17, of which waited for: 7 -> 7; matrix products, arithmetic and copies ran while one was open for 0% -> 0% of each run, Pallas kernels for 19% -> 16%
where the time goes in v14:
time: 68.2 us; the launch traced here: 67.9 us
  starting transfers between devices  28.7 us (42%)
  waiting for transfers between devices  25.5 us (37%)
  Pallas kernels  13.3 us (20%)
    ppermute x12, starting transfers between devices, swap(): return lax.ppermute(x, 'frame', pairs)  22.1 us
    ppermute x12, waiting for transfers between devices, swap(): return lax.ppermute(x, 'frame', pairs)  13.4 us
    ppermute x5, waiting for transfers between devices, along_space(): lax.ppermute(x, 'space', [(s, (s + offset) % spaces) for s in range(space...  12.1 us
    pallas_call x6, Pallas kernels, attend(): pl.pallas_call(functools.partial(attend_kernel, spaces, frames, columns,...  9.21 us
    ppermute x5, starting transfers between devices, along_space(): lax.ppermute(x, 'space', [(s, (s + offset) % spaces) for s in range(space...  6.54 us
    pallas_call x3, Pallas kernels, pack(): pl.pallas_call(functools.partial(pack_kernel, spaces, tuple(jobs), staged...  2.43 us
    pallas_call x2, Pallas kernels, put(): pl.pallas_call(functools.partial(put_kernel, spaces, tuple(places)), in_s...  1.45 us
  transfers between devices with their start and end apart: 17, of which 7 were waited for; matrix products, arithmetic and copies ran while one was open for 0% of the time, Pallas kernels for 16%

profile of v14, /device:TPU:0, one launch (start us, length us, event | category | flops | bytes accessed | tf_op | source)
XLA Modules:
  0.0 67.9 jit_solution(861551476788849496)
XLA Ops:
  0.0 0.0 copy-start.1
  0.0 0.0 copy-start.2
  0.0 2.1 %pack.3 = (bf16[2,192,384]{2,1,0:T(8,128)(2,1)}, bf16[2,192,512]{2,1,0:T(8,128)(2,1)}) custom-call(bf16[192,1536]{1,0:T(8,128)(2,1)} %bitcast.11, bf16[192,1536]{1,0:T(8,128)(2,1)} %bitcast.13), custom_call_target="tpu_custom_call" | custom-call | tf_op jit(solution)/shard_map/pack/pallas_call | solution.py:64
  2.1 3.0 %collective-permute-start = (bf16[2,192,384]{2,1,0:T(8,128)(2,1)}, bf16[2,192,384]{2,1,0:T(8,128)(2,1)S(1)}, u32[]{:S(2)}, u32[]{:S(2)}) collective-permute-start(bf16[2,192,384]{2,1,0:T(8,128)(2,1)} %get-tuple-element.34), channel_id=1, source_target_pairs={{0,2},{2,0},{1,3},{3,1},{4,6},{6,4},{5,7},{7,5},{8,10},{10,8},{9,1... | collective-permute-start | bytes 884744 | tf_op jit(solution)/shard_map/ppermute | solution.py:335
  5.1 0.7 collective-permute-start.4
  5.8 4.4 %collective-permute-start.3 = (bf16[2,192,512]{2,1,0:T(8,128)(2,1)}, bf16[2,192,512]{2,1,0:T(8,128)(2,1)S(1)}, u32[]{:S(2)}, u32[]{:S(2)}) collective-permute-start(bf16[2,192,512]{2,1,0:T(8,128)(2,1)} %get-tuple-element.36.refs_2_), channel_id=1, source_target_pairs={{0,4},{4,0},{8,12},{12,8},{1,5},{5,1},{9,13},{13,9},{2,6},{6,2},{1... | collective-permute-start | bytes 1179656 | tf_op jit(solution)/shard_map/ppermute | solution.py:343
  10.2 2.1 %collective-permute-done.refs_2_.refs_0_.refs_3_ = bf16[2,192,384]{2,1,0:T(8,128)(2,1)S(1)} collective-permute-done((bf16[2,192,384]{2,1,0:T(8,128)(2,1)}, bf16[2,192,384]{2,1,0:T(8,128)(2,1)S(1)}, u32[]{:S(2)}, u32[]{:S(2)}) %collective-permute-start) | collective-permute-done | bytes 294944 | tf_op jit(solution)/shard_map/ppermute | solution.py:335
  12.3 0.0 copy-done.1
  12.3 0.0 copy-done.2
  12.3 0.3 pack.4
  12.6 0.0 copy-start
  12.6 1.8 %collective-permute-start.1 = (bf16[2,192,384]{2,1,0:T(8,128)(2,1)S(1)}, bf16[2,192,384]{2,1,0:T(8,128)(2,1)S(1)}, u32[]{:S(2)}, u32[]{:S(2)}) collective-permute-start(bf16[2,192,384]{2,1,0:T(8,128)(2,1)S(1)} %get-tuple-element.35), channel_id=1, source_target_pairs={{0,2},{2,0},{1,3},{3,1},{4,6},{6,4},{5,7},{7,5},{8,10},{10,8},{9,1... | collective-permute-start | bytes 884744 | tf_op jit(solution)/shard_map/ppermute | solution.py:335
  14.4 0.7 collective-permute-start.6
  15.1 4.5 %collective-permute-start.5 = (bf16[2,192,256]{2,1,0:T(8,128)(2,1)S(1)}, bf16[2,192,256]{2,1,0:T(8,128)(2,1)S(1)}, u32[]{:S(2)}, u32[]{:S(2)}) collective-permute-start(bf16[2,192,256]{2,1,0:T(8,128)(2,1)S(1)} %get-tuple-element.37), channel_id=1, source_target_pairs={{0,4},{4,0},{8,12},{12,8},{1,5},{5,1},{9,13},{13,9},{2,6},{6,2},{1... | collective-permute-start | bytes 589832 | tf_op jit(solution)/shard_map/ppermute | solution.py:343
  19.6 0.0 collective-permute-done.4.refs_2_
  19.6 0.0 collective-permute-done.3.refs_1_
  19.6 0.1 join.3
  19.7 0.7 %collective-permute-start.9 = (bf16[4,192,384]{2,1,0:T(8,128)(2,1)S(1)}, bf16[4,192,384]{2,1,0:T(8,128)(2,1)S(1)}, u32[]{:S(2)}, u32[]{:S(2)}) collective-permute-start(bf16[4,192,384]{2,1,0:T(8,128)(2,1)S(1)} %get-tuple-element.40.refs_4_), channel_id=1, source_target_pairs={{4,8},{8,4},{5,9},{9,5},{6,10},{10,6},{7,11},{11,7},{20,24},{24,20... | collective-permute-start | bytes 1769480 | tf_op jit(solution)/shard_map/ppermute | solution.py:343
  20.4 2.9 %collective-permute-start.10 = (bf16[4,192,384]{2,1,0:T(8,128)(2,1)S(1)}, bf16[4,192,384]{2,1,0:T(8,128)(2,1)S(1)}, u32[]{:S(2)}, u32[]{:S(2)}) collective-permute-start(bf16[4,192,384]{2,1,0:T(8,128)(2,1)S(1)} %get-tuple-element.41.refs_5_), channel_id=1, source_target_pairs={{0,4},{4,0},{8,12},{12,8},{1,5},{5,1},{9,13},{13,9},{2,6},{6,2},{1... | collective-permute-start | bytes 1769480 | tf_op jit(solution)/shard_map/ppermute | solution.py:343
  23.3 0.0 collective-permute-done.1.refs_1_.refs_0_
  23.3 0.0 copy-done
  23.3 0.1 pack.5.refs_1_
  23.4 0.0 copy-start.3
  23.4 0.0 collective-permute-done.6.refs_4_
  23.4 0.8 %collective-permute-done.5.refs_3_ = bf16[2,192,256]{2,1,0:T(8,128)(2,1)S(1)} collective-permute-done((bf16[2,192,256]{2,1,0:T(8,128)(2,1)S(1)}, bf16[2,192,256]{2,1,0:T(8,128)(2,1)S(1)}, u32[]{:S(2)}, u32[]{:S(2)}) %collective-permute-start.5) | collective-permute-done | bytes 196640 | tf_op jit(solution)/shard_map/ppermute | solution.py:343
  24.2 0.1 join.2
  24.3 0.0 copy-start.4
  24.3 0.0 copy-start.5
  24.3 0.7 %collective-permute-start.7 = (bf16[4,192,384]{2,1,0:T(8,128)(2,1)S(1)}, bf16[4,192,384]{2,1,0:T(8,128)(2,1)S(1)}, u32[]{:S(2)}, u32[]{:S(2)}) collective-permute-start(bf16[4,192,384]{2,1,0:T(8,128)(2,1)S(1)} %get-tuple-element.38.refs_4_), channel_id=1, source_target_pairs={{4,8},{8,4},{5,9},{9,5},{6,10},{10,6},{7,11},{11,7},{20,24},{24,20... | collective-permute-start | bytes 1769480 | tf_op jit(solution)/shard_map/ppermute | solution.py:343
  25.0 3.6 %collective-permute-start.8 = (bf16[4,192,384]{2,1,0:T(8,128)(2,1)S(1)}, bf16[4,192,384]{2,1,0:T(8,128)(2,1)S(1)}, u32[]{:S(2)}, u32[]{:S(2)}) collective-permute-start(bf16[4,192,384]{2,1,0:T(8,128)(2,1)S(1)} %get-tuple-element.39.refs_5_), channel_id=1, source_target_pairs={{0,4},{4,0},{8,12},{12,8},{1,5},{5,1},{9,13},{13,9},{2,6},{6,2},{1... | collective-permute-start | bytes 1769480 | tf_op jit(solution)/shard_map/ppermute | solution.py:343
  28.7 0.5 collective-permute-start.2
  29.2 6.2 %collective-permute-done.2.refs_1_ = bf16[192,768]{1,0:T(8,128)(2,1)S(1)} collective-permute-done((bf16[192,768]{1,0:T(8,128)(2,1)S(1)}, bf16[192,768]{1,0:T(8,128)(2,1)S(1)}, u32[]{:S(2)}, u32[]{:S(2)}) %collective-permute-start.2) | collective-permute-done | bytes 294944 | tf_op jit(solution)/shard_map/ppermute | solution.py:335
  35.4 0.0 copy-done.3
  35.4 0.0 copy-done.4
  35.4 0.0 copy-done.5
  35.4 2.2 %attend.4 = (f32[3,128,384]{2,1,0:T(8,128)S(1)}, f32[3,8,384]{2,1,0:T(8,128)S(1)}) custom-call(s32[4,4]{1,0:T(4,128)S(1)} %copy-done.4, s32[4]{0:T(128)S(1)} %copy-done.5, bf16[192,1536]{1,0:T(8,128)(2,1)S(1)} %bitcast.5, bf16[192,768]{1,0:T(8,128)(2,1)S(1)} %collective-permute-done.2.refs_1_, bf16[2,192,512]{2,1,0:T(8,128)(2,1)S(1)} %copy-done.3, ...), custom_call_target="tpu_custom_call" | custom-call | flops 452984832 | bytes 1179648 | tf_op jit(solution)/shard_map/attend/pallas_call | solution.py:252
  37.6 2.3 %attend.5 = (f32[3,128,384]{2,1,0:T(8,128)S(1)}, f32[3,8,384]{2,1,0:T(8,128)S(1)}) custom-call(s32[4,4]{1,0:T(4,128)S(1)} %copy-done.4, s32[4]{0:T(128)S(1)} %copy-done.5, bf16[192,1536]{1,0:T(8,128)(2,1)S(1)} %bitcast.6, bf16[192,768]{1,0:T(8,128)(2,1)S(1)} %collective-permute-done.2.refs_1_, bf16[2,192,384]{2,1,0:T(8,128)(2,1)S(1)} %get-tuple-element.43.refs_2_, ...), custom_call_target="tpu_custom_call" | custom-call | flops 452984832 | bytes 1179648 | tf_op jit(solution)/shard_map/attend/pallas_call | solution.py:252
  39.9 0.0 collective-permute-done.9.refs_0_
  39.9 0.0 collective-permute-done.10.refs_1_
  40.0 0.7 %collective-permute-start.15 = (bf16[2,192,384]{2,1,0:T(8,128)(2,1)S(1)}, bf16[2,192,384]{2,1,0:T(8,128)(2,1)S(1)}, u32[]{:S(2)}, u32[]{:S(2)}) collective-permute-start(bf16[2,192,384]{2,1,0:T(8,128)(2,1)S(1)} %slice.15), channel_id=1, source_target_pairs={{4,8},{8,4},{5,9},{9,5},{6,10},{10,6},{7,11},{11,7},{20,24},{24,20... | collective-permute-start | bytes 884744 | tf_op jit(solution)/shard_map/ppermute | solution.py:343
  40.7 1.3 %collective-permute-start.14 = (bf16[2,192,384]{2,1,0:T(8,128)(2,1)S(1)}, bf16[2,192,384]{2,1,0:T(8,128)(2,1)S(1)}, u32[]{:S(2)}, u32[]{:S(2)}) collective-permute-start(bf16[2,192,384]{2,1,0:T(8,128)(2,1)S(1)} %slice.14), channel_id=1, source_target_pairs={{4,0},{8,12},{5,1},{9,13},{6,2},{10,14},{7,3},{11,15},{20,16},{24,... | collective-permute-start | bytes 884744 | tf_op jit(solution)/shard_map/ppermute | solution.py:343
  42.0 1.4 %attend.6 = (f32[3,128,384]{2,1,0:T(8,128)S(1)}, f32[3,8,384]{2,1,0:T(8,128)S(1)}) custom-call(s32[4,4]{1,0:T(4,128)S(1)} %copy-done.4, s32[4]{0:T(128)S(1)} %copy-done.5, bf16[192,1536]{1,0:T(8,128)(2,1)S(1)} %bitcast.7, bf16[192,768]{1,0:T(8,128)(2,1)S(1)} %collective-permute-done.2.refs_1_, bf16[4,192,384]{2,1,0:T(8,128)(2,1)S(1)} %get-tuple-element.45.refs_2_, ...), custom_call_target="tpu_custom_call" | custom-call | flops 452984832 | bytes 1179648 | tf_op jit(solution)/shard_map/attend/pallas_call | solution.py:252
  43.5 0.0 collective-permute-done.7.refs_0_
  43.5 6.7 %collective-permute-done.8.refs_1_ = bf16[4,192,384]{2,1,0:T(8,128)(2,1)S(1)} collective-permute-done((bf16[4,192,384]{2,1,0:T(8,128)(2,1)S(1)}, bf16[4,192,384]{2,1,0:T(8,128)(2,1)S(1)}, u32[]{:S(2)}, u32[]{:S(2)}) %collective-permute-start.8) | collective-permute-done | bytes 589856 | tf_op jit(solution)/shard_map/ppermute | solution.py:343
  50.3 0.7 %collective-permute-start.12 = (bf16[2,192,384]{2,1,0:T(8,128)(2,1)S(1)}, bf16[2,192,384]{2,1,0:T(8,128)(2,1)S(1)}, u32[]{:S(2)}, u32[]{:S(2)}) collective-permute-start(bf16[2,192,384]{2,1,0:T(8,128)(2,1)S(1)} %slice.13), channel_id=1, source_target_pairs={{4,8},{8,4},{5,9},{9,5},{6,10},{10,6},{7,11},{11,7},{20,24},{24,20... | collective-permute-start | bytes 884744 | tf_op jit(solution)/shard_map/ppermute | solution.py:343
  51.0 1.3 %collective-permute-start.11 = (bf16[2,192,384]{2,1,0:T(8,128)(2,1)S(1)}, bf16[2,192,384]{2,1,0:T(8,128)(2,1)S(1)}, u32[]{:S(2)}, u32[]{:S(2)}) collective-permute-start(bf16[2,192,384]{2,1,0:T(8,128)(2,1)S(1)} %slice.12), channel_id=1, source_target_pairs={{4,0},{8,12},{5,1},{9,13},{6,2},{10,14},{7,3},{11,15},{20,16},{24,... | collective-permute-start | bytes 884744 | tf_op jit(solution)/shard_map/ppermute | solution.py:343
  52.3 1.4 %attend.7 = (f32[3,128,384]{2,1,0:T(8,128)S(1)}, f32[3,8,384]{2,1,0:T(8,128)S(1)}) custom-call(s32[4,4]{1,0:T(4,128)S(1)} %copy-done.4, s32[4]{0:T(128)S(1)} %copy-done.5, bf16[192,1536]{1,0:T(8,128)(2,1)S(1)} %bitcast.8, bf16[192,768]{1,0:T(8,128)(2,1)S(1)} %collective-permute-done.2.refs_1_, bf16[4,192,384]{2,1,0:T(8,128)(2,1)S(1)} %get-tuple-element.50.refs_2_, ...), custom_call_target="tpu_custom_call" | custom-call | flops 452984832 | bytes 1179648 | tf_op jit(solution)/shard_map/attend/pallas_call | solution.py:252
  53.7 0.0 collective-permute-done.15.refs_1_
  53.7 2.8 %collective-permute-done.14.refs_0_ = bf16[2,192,384]{2,1,0:T(8,128)(2,1)S(1)} collective-permute-done((bf16[2,192,384]{2,1,0:T(8,128)(2,1)S(1)}, bf16[2,192,384]{2,1,0:T(8,128)(2,1)S(1)}, u32[]{:S(2)}, u32[]{:S(2)}) %collective-permute-start.14) | collective-permute-done | bytes 294944 | tf_op jit(solution)/shard_map/ppermute | solution.py:343
  56.5 0.9 %attend_final.3 = (bf16[192,384]{1,0:T(8,128)(2,1)S(1)}, bf16[192,384]{1,0:T(8,128)(2,1)S(1)}) custom-call(s32[4,4]{1,0:T(4,128)S(1)} %copy-done.4, s32[4]{0:T(128)S(1)} %copy-done.5, bf16[192,1536]{1,0:T(8,128)(2,1)S(1)} %bitcast.9, bf16[192,768]{1,0:T(8,128)(2,1)S(1)} %collective-permute-done.2.refs_1_, ...), custom_call_target="tpu_custom_call" | custom-call | flops 226492416 | bytes 1179648 | tf_op jit(solution)/shard_map/attend_final/pallas_call | solution.py:252
  57.4 0.6 collective-permute-start.16
  58.0 0.0 collective-permute-done.12.refs_1_
  58.1 3.1 %collective-permute-done.11.refs_0_ = bf16[2,192,384]{2,1,0:T(8,128)(2,1)S(1)} collective-permute-done((bf16[2,192,384]{2,1,0:T(8,128)(2,1)S(1)}, bf16[2,192,384]{2,1,0:T(8,128)(2,1)S(1)}, u32[]{:S(2)}, u32[]{:S(2)}) %collective-permute-start.11) | collective-permute-done | bytes 294944 | tf_op jit(solution)/shard_map/ppermute | solution.py:343
  61.1 0.9 %attend_final.2 = (bf16[192,384]{1,0:T(8,128)(2,1)S(1)}, bf16[192,384]{1,0:T(8,128)(2,1)S(1)}) custom-call(s32[4,4]{1,0:T(4,128)S(1)} %copy-done.4, s32[4]{0:T(128)S(1)} %copy-done.5, bf16[192,1536]{1,0:T(8,128)(2,1)S(1)} %bitcast.10, bf16[192,768]{1,0:T(8,128)(2,1)S(1)} %collective-permute-done.2.refs_1_, ...), custom_call_target="tpu_custom_call" | custom-call | flops 226492416 | bytes 1179648 | tf_op jit(solution)/shard_map/attend_final/pallas_call | solution.py:252
  62.0 0.6 collective-permute-start.13
  62.6 0.0 collective-permute-done.16.refs_2_
  62.7 0.8 %put.2.refs_1_ = bf16[192,1536]{1,0:T(8,128)(2,1)} custom-call(bf16[192,384]{1,0:T(8,128)(2,1)S(1)} %get-tuple-element.60.refs_0_, bf16[192,384]{1,0:T(8,128)(2,1)S(1)} %get-tuple-element.61.refs_1_, bf16[192,384]{1,0:T(8,128)(2,1)S(1)} %collective-permute-done.16.refs_2_), custom_call_target="tpu_custom_call" | custom-call | tf_op jit(solution)/shard_map/put/pallas_call | solution.py:309
  63.4 3.8 %collective-permute-done.13.refs_0_ = bf16[192,384]{1,0:T(8,128)(2,1)S(1)} collective-permute-done((bf16[192,384]{1,0:T(8,128)(2,1)S(1)}, bf16[192,384]{1,0:T(8,128)(2,1)S(1)}, u32[]{:S(2)}, u32[]{:S(2)}) %collective-permute-start.13) | collective-permute-done | bytes 147488 | tf_op jit(solution)/shard_map/ppermute | solution.py:335
  67.3 0.7 put.3
  (9 shorter events, 0.1 us)
Async XLA Ops:
  0.0 12.3 %copy-start.1 = (bf16[1,4,48,1536]{3,2,1,0:T(8,128)(2,1)S(1)}, bf16[1,4,48,1536]{3,2,1,0:T(8,128)(2,1)}, u32[]{:S(2)}) copy-start(bf16[1,4,48,1536]{3,2,1,0:T(8,128)(2,1)} %param.6) | copy-start | bytes 1769476
  0.0 12.3 %copy-start.2 = (bf16[1,4,48,1536]{3,2,1,0:T(8,128)(2,1)S(1)}, bf16[1,4,48,1536]{3,2,1,0:T(8,128)(2,1)}, u32[]{:S(2)}) copy-start(bf16[1,4,48,1536]{3,2,1,0:T(8,128)(2,1)} %param.7) | copy-start | bytes 1769476
  2.1 10.2 %collective-permute-start = (bf16[2,192,384]{2,1,0:T(8,128)(2,1)}, bf16[2,192,384]{2,1,0:T(8,128)(2,1)S(1)}, u32[]{:S(2)}, u32[]{:S(2)}) collective-permute-start(bf16[2,192,384]{2,1,0:T(8,128)(2,1)} %get-tuple-element.34), channel_id=1, source_target_pairs={{0,2},{2,0},{1,3},{3,1},{4,6},{6,4},{5,7},{7,5},{8,10},{10,8},{9,1... | collective-permute-start | bytes 884744 | tf_op jit(solution)/shard_map/ppermute | solution.py:335
  5.1 14.5 %collective-permute-start.4 = (bf16[2,192,512]{2,1,0:T(8,128)(2,1)}, bf16[2,192,512]{2,1,0:T(8,128)(2,1)S(1)}, u32[]{:S(2)}, u32[]{:S(2)}) collective-permute-start(bf16[2,192,512]{2,1,0:T(8,128)(2,1)} %get-tuple-element.36.refs_2_), channel_id=1, source_target_pairs={{4,8},{8,4},{5,9},{9,5},{6,10},{10,6},{7,11},{11,7},{20,24},{24,20... | collective-permute-start | bytes 1179656 | tf_op jit(solution)/shard_map/ppermute | solution.py:343
  5.8 13.8 %collective-permute-start.3 = (bf16[2,192,512]{2,1,0:T(8,128)(2,1)}, bf16[2,192,512]{2,1,0:T(8,128)(2,1)S(1)}, u32[]{:S(2)}, u32[]{:S(2)}) collective-permute-start(bf16[2,192,512]{2,1,0:T(8,128)(2,1)} %get-tuple-element.36.refs_2_), channel_id=1, source_target_pairs={{0,4},{4,0},{8,12},{12,8},{1,5},{5,1},{9,13},{13,9},{2,6},{6,2},{1... | collective-permute-start | bytes 1179656 | tf_op jit(solution)/shard_map/ppermute | solution.py:343
  12.6 10.7 %copy-start = (bf16[1,4,48,1536]{3,2,1,0:T(8,128)(2,1)S(1)}, bf16[1,4,48,1536]{3,2,1,0:T(8,128)(2,1)}, u32[]{:S(2)}) copy-start(bf16[1,4,48,1536]{3,2,1,0:T(8,128)(2,1)} %param.5) | copy-start | bytes 1769476
  12.6 10.7 %collective-permute-start.1 = (bf16[2,192,384]{2,1,0:T(8,128)(2,1)S(1)}, bf16[2,192,384]{2,1,0:T(8,128)(2,1)S(1)}, u32[]{:S(2)}, u32[]{:S(2)}) collective-permute-start(bf16[2,192,384]{2,1,0:T(8,128)(2,1)S(1)} %get-tuple-element.35), channel_id=1, source_target_pairs={{0,2},{2,0},{1,3},{3,1},{4,6},{6,4},{5,7},{7,5},{8,10},{10,8},{9,1... | collective-permute-start | bytes 884744 | tf_op jit(solution)/shard_map/ppermute | solution.py:335
  14.4 9.0 %collective-permute-start.6 = (bf16[2,192,256]{2,1,0:T(8,128)(2,1)S(1)}, bf16[2,192,256]{2,1,0:T(8,128)(2,1)S(1)}, u32[]{:S(2)}, u32[]{:S(2)}) collective-permute-start(bf16[2,192,256]{2,1,0:T(8,128)(2,1)S(1)} %get-tuple-element.37), channel_id=1, source_target_pairs={{4,8},{8,4},{5,9},{9,5},{6,10},{10,6},{7,11},{11,7},{20,24},{24,20... | collective-permute-start | bytes 589832 | tf_op jit(solution)/shard_map/ppermute | solution.py:343
  15.1 9.1 %collective-permute-start.5 = (bf16[2,192,256]{2,1,0:T(8,128)(2,1)S(1)}, bf16[2,192,256]{2,1,0:T(8,128)(2,1)S(1)}, u32[]{:S(2)}, u32[]{:S(2)}) collective-permute-start(bf16[2,192,256]{2,1,0:T(8,128)(2,1)S(1)} %get-tuple-element.37), channel_id=1, source_target_pairs={{0,4},{4,0},{8,12},{12,8},{1,5},{5,1},{9,13},{13,9},{2,6},{6,2},{1... | collective-permute-start | bytes 589832 | tf_op jit(solution)/shard_map/ppermute | solution.py:343
  19.7 20.2 %collective-permute-start.9 = (bf16[4,192,384]{2,1,0:T(8,128)(2,1)S(1)}, bf16[4,192,384]{2,1,0:T(8,128)(2,1)S(1)}, u32[]{:S(2)}, u32[]{:S(2)}) collective-permute-start(bf16[4,192,384]{2,1,0:T(8,128)(2,1)S(1)} %get-tuple-element.40.refs_4_), channel_id=1, source_target_pairs={{4,8},{8,4},{5,9},{9,5},{6,10},{10,6},{7,11},{11,7},{20,24},{24,20... | collective-permute-start | bytes 1769480 | tf_op jit(solution)/shard_map/ppermute | solution.py:343
  20.4 19.5 %collective-permute-start.10 = (bf16[4,192,384]{2,1,0:T(8,128)(2,1)S(1)}, bf16[4,192,384]{2,1,0:T(8,128)(2,1)S(1)}, u32[]{:S(2)}, u32[]{:S(2)}) collective-permute-start(bf16[4,192,384]{2,1,0:T(8,128)(2,1)S(1)} %get-tuple-element.41.refs_5_), channel_id=1, source_target_pairs={{0,4},{4,0},{8,12},{12,8},{1,5},{5,1},{9,13},{13,9},{2,6},{6,2},{1... | collective-permute-start | bytes 1769480 | tf_op jit(solution)/shard_map/ppermute | solution.py:343
  23.4 12.0 %copy-start.3 = (bf16[2,192,512]{2,1,0:T(8,128)(2,1)S(1)}, bf16[2,192,512]{2,1,0:T(8,128)(2,1)}, u32[]{:S(2)}) copy-start(bf16[2,192,512]{2,1,0:T(8,128)(2,1)} %get-tuple-element.36.refs_2_) | copy-start | bytes 1179652
  24.3 11.1 %copy-start.4 = (s32[4,4]{1,0:T(4,128)S(1)}, s32[4,4]{1,0:T(4,128)}, u32[]{:S(2)}) copy-start(s32[4,4]{1,0:T(4,128)} %flags_ref.11) | copy-start | bytes 196
  24.3 11.1 %copy-start.5 = (s32[4]{0:T(128)S(1)}, s32[4]{0:T(128)}, u32[]{:S(2)}) copy-start(s32[4]{0:T(128)} %widths_ref.11) | copy-start | bytes 52
  24.3 19.1 %collective-permute-start.7 = (bf16[4,192,384]{2,1,0:T(8,128)(2,1)S(1)}, bf16[4,192,384]{2,1,0:T(8,128)(2,1)S(1)}, u32[]{:S(2)}, u32[]{:S(2)}) collective-permute-start(bf16[4,192,384]{2,1,0:T(8,128)(2,1)S(1)} %get-tuple-element.38.refs_4_), channel_id=1, source_target_pairs={{4,8},{8,4},{5,9},{9,5},{6,10},{10,6},{7,11},{11,7},{20,24},{24,20... | collective-permute-start | bytes 1769480 | tf_op jit(solution)/shard_map/ppermute | solution.py:343
  25.0 25.2 %collective-permute-start.8 = (bf16[4,192,384]{2,1,0:T(8,128)(2,1)S(1)}, bf16[4,192,384]{2,1,0:T(8,128)(2,1)S(1)}, u32[]{:S(2)}, u32[]{:S(2)}) collective-permute-start(bf16[4,192,384]{2,1,0:T(8,128)(2,1)S(1)} %get-tuple-element.39.refs_5_), channel_id=1, source_target_pairs={{0,4},{4,0},{8,12},{12,8},{1,5},{5,1},{9,13},{13,9},{2,6},{6,2},{1... | collective-permute-start | bytes 1769480 | tf_op jit(solution)/shard_map/ppermute | solution.py:343
  28.7 6.7 %collective-permute-start.2 = (bf16[192,768]{1,0:T(8,128)(2,1)S(1)}, bf16[192,768]{1,0:T(8,128)(2,1)S(1)}, u32[]{:S(2)}, u32[]{:S(2)}) collective-permute-start(bf16[192,768]{1,0:T(8,128)(2,1)S(1)} %pack.5.refs_1_), channel_id=1, source_target_pairs={{0,2},{2,0},{1,3},{3,1},{4,6},{6,4},{5,7},{7,5},{8,10},{10,8},{9,1... | collective-permute-start | bytes 884744 | tf_op jit(solution)/shard_map/ppermute | solution.py:335
  40.0 13.7 %collective-permute-start.15 = (bf16[2,192,384]{2,1,0:T(8,128)(2,1)S(1)}, bf16[2,192,384]{2,1,0:T(8,128)(2,1)S(1)}, u32[]{:S(2)}, u32[]{:S(2)}) collective-permute-start(bf16[2,192,384]{2,1,0:T(8,128)(2,1)S(1)} %slice.15), channel_id=1, source_target_pairs={{4,8},{8,4},{5,9},{9,5},{6,10},{10,6},{7,11},{11,7},{20,24},{24,20... | collective-permute-start | bytes 884744 | tf_op jit(solution)/shard_map/ppermute | solution.py:343
  40.7 15.8 %collective-permute-start.14 = (bf16[2,192,384]{2,1,0:T(8,128)(2,1)S(1)}, bf16[2,192,384]{2,1,0:T(8,128)(2,1)S(1)}, u32[]{:S(2)}, u32[]{:S(2)}) collective-permute-start(bf16[2,192,384]{2,1,0:T(8,128)(2,1)S(1)} %slice.14), channel_id=1, source_target_pairs={{4,0},{8,12},{5,1},{9,13},{6,2},{10,14},{7,3},{11,15},{20,16},{24,... | collective-permute-start | bytes 884744 | tf_op jit(solution)/shard_map/ppermute | solution.py:343
  50.3 7.8 %collective-permute-start.12 = (bf16[2,192,384]{2,1,0:T(8,128)(2,1)S(1)}, bf16[2,192,384]{2,1,0:T(8,128)(2,1)S(1)}, u32[]{:S(2)}, u32[]{:S(2)}) collective-permute-start(bf16[2,192,384]{2,1,0:T(8,128)(2,1)S(1)} %slice.13), channel_id=1, source_target_pairs={{4,8},{8,4},{5,9},{9,5},{6,10},{10,6},{7,11},{11,7},{20,24},{24,20... | collective-permute-start | bytes 884744 | tf_op jit(solution)/shard_map/ppermute | solution.py:343
  51.0 10.2 %collective-permute-start.11 = (bf16[2,192,384]{2,1,0:T(8,128)(2,1)S(1)}, bf16[2,192,384]{2,1,0:T(8,128)(2,1)S(1)}, u32[]{:S(2)}, u32[]{:S(2)}) collective-permute-start(bf16[2,192,384]{2,1,0:T(8,128)(2,1)S(1)} %slice.12), channel_id=1, source_target_pairs={{4,0},{8,12},{5,1},{9,13},{6,2},{10,14},{7,3},{11,15},{20,16},{24,... | collective-permute-start | bytes 884744 | tf_op jit(solution)/shard_map/ppermute | solution.py:343
  57.4 5.2 %collective-permute-start.16 = (bf16[192,384]{1,0:T(8,128)(2,1)S(1)}, bf16[192,384]{1,0:T(8,128)(2,1)S(1)}, u32[]{:S(2)}, u32[]{:S(2)}) collective-permute-start(bf16[192,384]{1,0:T(8,128)(2,1)S(1)} %get-tuple-element.62), channel_id=1, source_target_pairs={{0,2},{2,0},{1,3},{3,1},{4,6},{6,4},{5,7},{7,5},{8,10},{10,8},{9,1... | collective-permute-start | bytes 442376 | tf_op jit(solution)/shard_map/ppermute | solution.py:335
  62.0 5.2 %collective-permute-start.13 = (bf16[192,384]{1,0:T(8,128)(2,1)S(1)}, bf16[192,384]{1,0:T(8,128)(2,1)S(1)}, u32[]{:S(2)}, u32[]{:S(2)}) collective-permute-start(bf16[192,384]{1,0:T(8,128)(2,1)S(1)} %get-tuple-element.56), channel_id=1, source_target_pairs={{0,2},{2,0},{1,3},{3,1},{4,6},{6,4},{5,7},{7,5},{8,10},{10,8},{9,1... | collective-permute-start | bytes 442376 | tf_op jit(solution)/shard_map/ppermute | solution.py:335

commit v15 on v14

--- a/solution.py
+++ b/solution.py
@@ -415,8 +415,9 @@
             states[c] = attend(scalars, query_parts, groups, states[c], False, chunk, sizes)
         messages = following
     ends = []
-    for message in messages:
-        came = list(tie(message, [state[1] for state in states]))
+    for c, message in enumerate(messages):
+        turn = -1 if c == 0 else 1
+        came = list(tie(message[::turn], [state[1] for state in states]))[::turn]
         ends.append(partner_bands(came, last))
 
     own, returned = [], []

time: 68.2 us -> 68.9 us (1.010)
  Pallas kernels: 13.3 us -> 15.9 us
  waiting for transfers between devices: 25.5 us -> 23.6 us
    pallas_call x6, Pallas kernels: 9.21 us -> 11.8 us  [attend(): pl.pallas_call(functools.partial(attend_kernel, spaces, frames, columns,...]
    ppermute x12, waiting for transfers between devices: 13.4 us -> 11.5 us  [swap(): return lax.ppermute(x, 'frame', pairs)]
  transfers between devices with their start and end apart: 17 -> 17, of which waited for: 7 -> 7; matrix products, arithmetic and copies ran while one was open for 0% -> 0% of each run, Pallas kernels for 16% -> 19%
where the time goes in v15:
time: 68.9 us; the launch traced here: 68.6 us
  starting transfers between devices  28.7 us (42%)
  waiting for transfers between devices  23.6 us (34%)
  Pallas kernels  15.9 us (23%)
    ppermute x12, starting transfers between devices, swap(): return lax.ppermute(x, 'frame', pairs)  22.1 us
    ppermute x5, waiting for transfers between devices, along_space(): lax.ppermute(x, 'space', [(s, (s + offset) % spaces) for s in range(space...  12.1 us
    pallas_call x6, Pallas kernels, attend(): pl.pallas_call(functools.partial(attend_kernel, spaces, frames, columns,...  11.8 us
    ppermute x12, waiting for transfers between devices, swap(): return lax.ppermute(x, 'frame', pairs)  11.5 us
    ppermute x5, starting transfers between devices, along_space(): lax.ppermute(x, 'space', [(s, (s + offset) % spaces) for s in range(space...  6.54 us
    pallas_call x3, Pallas kernels, pack(): pl.pallas_call(functools.partial(pack_kernel, spaces, tuple(jobs), staged...  2.43 us
    pallas_call x2, Pallas kernels, put(): pl.pallas_call(functools.partial(put_kernel, spaces, tuple(places)), in_s...  1.45 us
  transfers between devices with their start and end apart: 17, of which 7 were waited for; matrix products, arithmetic and copies ran while one was open for 0% of the time, Pallas kernels for 19%

profile of v15, /device:TPU:0, one launch (start us, length us, event | category | flops | bytes accessed | tf_op | source)
XLA Modules:
  0.0 68.6 jit_solution(5632590960311430806)
XLA Ops:
  0.0 0.0 copy-start.1
  0.0 0.0 copy-start.2
  0.0 2.1 %pack.3 = (bf16[2,192,384]{2,1,0:T(8,128)(2,1)}, bf16[2,192,512]{2,1,0:T(8,128)(2,1)}) custom-call(bf16[192,1536]{1,0:T(8,128)(2,1)} %bitcast.11, bf16[192,1536]{1,0:T(8,128)(2,1)} %bitcast.13), custom_call_target="tpu_custom_call" | custom-call | tf_op jit(solution)/shard_map/pack/pallas_call | solution.py:64
  2.1 3.0 %collective-permute-start = (bf16[2,192,384]{2,1,0:T(8,128)(2,1)}, bf16[2,192,384]{2,1,0:T(8,128)(2,1)S(1)}, u32[]{:S(2)}, u32[]{:S(2)}) collective-permute-start(bf16[2,192,384]{2,1,0:T(8,128)(2,1)} %get-tuple-element.34), channel_id=1, source_target_pairs={{0,2},{2,0},{1,3},{3,1},{4,6},{6,4},{5,7},{7,5},{8,10},{10,8},{9,1... | collective-permute-start | bytes 884744 | tf_op jit(solution)/shard_map/ppermute | solution.py:335
  5.1 0.7 collective-permute-start.4
  5.8 4.4 %collective-permute-start.3 = (bf16[2,192,512]{2,1,0:T(8,128)(2,1)}, bf16[2,192,512]{2,1,0:T(8,128)(2,1)S(1)}, u32[]{:S(2)}, u32[]{:S(2)}) collective-permute-start(bf16[2,192,512]{2,1,0:T(8,128)(2,1)} %get-tuple-element.36.refs_2_), channel_id=1, source_target_pairs={{0,4},{4,0},{8,12},{12,8},{1,5},{5,1},{9,13},{13,9},{2,6},{6,2},{1... | collective-permute-start | bytes 1179656 | tf_op jit(solution)/shard_map/ppermute | solution.py:343
  10.2 2.1 %collective-permute-done.refs_2_.refs_0_.refs_3_ = bf16[2,192,384]{2,1,0:T(8,128)(2,1)S(1)} collective-permute-done((bf16[2,192,384]{2,1,0:T(8,128)(2,1)}, bf16[2,192,384]{2,1,0:T(8,128)(2,1)S(1)}, u32[]{:S(2)}, u32[]{:S(2)}) %collective-permute-start) | collective-permute-done | bytes 294944 | tf_op jit(solution)/shard_map/ppermute | solution.py:335
  12.3 0.0 copy-done.1
  12.3 0.0 copy-done.2
  12.3 0.3 pack.4
  12.6 0.0 copy-start
  12.6 1.8 %collective-permute-start.1 = (bf16[2,192,384]{2,1,0:T(8,128)(2,1)S(1)}, bf16[2,192,384]{2,1,0:T(8,128)(2,1)S(1)}, u32[]{:S(2)}, u32[]{:S(2)}) collective-permute-start(bf16[2,192,384]{2,1,0:T(8,128)(2,1)S(1)} %get-tuple-element.35), channel_id=1, source_target_pairs={{0,2},{2,0},{1,3},{3,1},{4,6},{6,4},{5,7},{7,5},{8,10},{10,8},{9,1... | collective-permute-start | bytes 884744 | tf_op jit(solution)/shard_map/ppermute | solution.py:335
  14.4 0.7 collective-permute-start.6
  15.1 4.5 %collective-permute-start.5 = (bf16[2,192,256]{2,1,0:T(8,128)(2,1)S(1)}, bf16[2,192,256]{2,1,0:T(8,128)(2,1)S(1)}, u32[]{:S(2)}, u32[]{:S(2)}) collective-permute-start(bf16[2,192,256]{2,1,0:T(8,128)(2,1)S(1)} %get-tuple-element.37), channel_id=1, source_target_pairs={{0,4},{4,0},{8,12},{12,8},{1,5},{5,1},{9,13},{13,9},{2,6},{6,2},{1... | collective-permute-start | bytes 589832 | tf_op jit(solution)/shard_map/ppermute | solution.py:343
  19.6 0.0 collective-permute-done.4.refs_2_
  19.6 0.0 collective-permute-done.3.refs_1_
  19.6 0.1 join.3
  19.7 0.7 %collective-permute-start.9 = (bf16[4,192,384]{2,1,0:T(8,128)(2,1)S(1)}, bf16[4,192,384]{2,1,0:T(8,128)(2,1)S(1)}, u32[]{:S(2)}, u32[]{:S(2)}) collective-permute-start(bf16[4,192,384]{2,1,0:T(8,128)(2,1)S(1)} %get-tuple-element.40.refs_4_), channel_id=1, source_target_pairs={{4,8},{8,4},{5,9},{9,5},{6,10},{10,6},{7,11},{11,7},{20,24},{24,20... | collective-permute-start | bytes 1769480 | tf_op jit(solution)/shard_map/ppermute | solution.py:343
  20.4 2.9 %collective-permute-start.10 = (bf16[4,192,384]{2,1,0:T(8,128)(2,1)S(1)}, bf16[4,192,384]{2,1,0:T(8,128)(2,1)S(1)}, u32[]{:S(2)}, u32[]{:S(2)}) collective-permute-start(bf16[4,192,384]{2,1,0:T(8,128)(2,1)S(1)} %get-tuple-element.41.refs_5_), channel_id=1, source_target_pairs={{0,4},{4,0},{8,12},{12,8},{1,5},{5,1},{9,13},{13,9},{2,6},{6,2},{1... | collective-permute-start | bytes 1769480 | tf_op jit(solution)/shard_map/ppermute | solution.py:343
  23.3 0.0 collective-permute-done.1.refs_1_.refs_0_
  23.3 0.0 copy-done
  23.3 0.1 pack.5.refs_1_
  23.4 0.0 copy-start.3
  23.4 0.0 collective-permute-done.6.refs_4_
  23.4 0.8 %collective-permute-done.5.refs_3_ = bf16[2,192,256]{2,1,0:T(8,128)(2,1)S(1)} collective-permute-done((bf16[2,192,256]{2,1,0:T(8,128)(2,1)S(1)}, bf16[2,192,256]{2,1,0:T(8,128)(2,1)S(1)}, u32[]{:S(2)}, u32[]{:S(2)}) %collective-permute-start.5) | collective-permute-done | bytes 196640 | tf_op jit(solution)/shard_map/ppermute | solution.py:343
  24.2 0.1 join.2
  24.3 0.0 copy-start.4
  24.3 0.0 copy-start.5
  24.3 0.7 %collective-permute-start.7 = (bf16[4,192,384]{2,1,0:T(8,128)(2,1)S(1)}, bf16[4,192,384]{2,1,0:T(8,128)(2,1)S(1)}, u32[]{:S(2)}, u32[]{:S(2)}) collective-permute-start(bf16[4,192,384]{2,1,0:T(8,128)(2,1)S(1)} %get-tuple-element.38.refs_4_), channel_id=1, source_target_pairs={{4,8},{8,4},{5,9},{9,5},{6,10},{10,6},{7,11},{11,7},{20,24},{24,20... | collective-permute-start | bytes 1769480 | tf_op jit(solution)/shard_map/ppermute | solution.py:343
  25.0 3.6 %collective-permute-start.8 = (bf16[4,192,384]{2,1,0:T(8,128)(2,1)S(1)}, bf16[4,192,384]{2,1,0:T(8,128)(2,1)S(1)}, u32[]{:S(2)}, u32[]{:S(2)}) collective-permute-start(bf16[4,192,384]{2,1,0:T(8,128)(2,1)S(1)} %get-tuple-element.39.refs_5_), channel_id=1, source_target_pairs={{0,4},{4,0},{8,12},{12,8},{1,5},{5,1},{9,13},{13,9},{2,6},{6,2},{1... | collective-permute-start | bytes 1769480 | tf_op jit(solution)/shard_map/ppermute | solution.py:343
  28.7 0.5 collective-permute-start.2
  29.2 6.2 %collective-permute-done.2.refs_1_ = bf16[192,768]{1,0:T(8,128)(2,1)S(1)} collective-permute-done((bf16[192,768]{1,0:T(8,128)(2,1)S(1)}, bf16[192,768]{1,0:T(8,128)(2,1)S(1)}, u32[]{:S(2)}, u32[]{:S(2)}) %collective-permute-start.2) | collective-permute-done | bytes 294944 | tf_op jit(solution)/shard_map/ppermute | solution.py:335
  35.4 0.0 copy-done.3
  35.4 0.0 copy-done.4
  35.4 0.0 copy-done.5
  35.4 2.2 %attend.4 = (f32[3,128,384]{2,1,0:T(8,128)S(1)}, f32[3,8,384]{2,1,0:T(8,128)S(1)}) custom-call(s32[4,4]{1,0:T(4,128)S(1)} %copy-done.4, s32[4]{0:T(128)S(1)} %copy-done.5, bf16[192,1536]{1,0:T(8,128)(2,1)S(1)} %bitcast.5, bf16[192,768]{1,0:T(8,128)(2,1)S(1)} %collective-permute-done.2.refs_1_, bf16[2,192,512]{2,1,0:T(8,128)(2,1)S(1)} %copy-done.3, ...), custom_call_target="tpu_custom_call" | custom-call | flops 452984832 | bytes 1179648 | tf_op jit(solution)/shard_map/attend/pallas_call | solution.py:252
  37.6 2.3 %attend.5 = (f32[3,128,384]{2,1,0:T(8,128)S(1)}, f32[3,8,384]{2,1,0:T(8,128)S(1)}) custom-call(s32[4,4]{1,0:T(4,128)S(1)} %copy-done.4, s32[4]{0:T(128)S(1)} %copy-done.5, bf16[192,1536]{1,0:T(8,128)(2,1)S(1)} %bitcast.6, bf16[192,768]{1,0:T(8,128)(2,1)S(1)} %collective-permute-done.2.refs_1_, bf16[2,192,384]{2,1,0:T(8,128)(2,1)S(1)} %get-tuple-element.43.refs_2_, ...), custom_call_target="tpu_custom_call" | custom-call | flops 452984832 | bytes 1179648 | tf_op jit(solution)/shard_map/attend/pallas_call | solution.py:252
  39.9 0.0 collective-permute-done.9.refs_0_
  39.9 0.0 collective-permute-done.10.refs_1_
  40.0 0.7 collective-permute-start.14
  40.7 1.3 %collective-permute-start.15 = (bf16[2,192,384]{2,1,0:T(8,128)(2,1)S(1)}, bf16[2,192,384]{2,1,0:T(8,128)(2,1)S(1)}, u32[]{:S(2)}, u32[]{:S(2)}) collective-permute-start(bf16[2,192,384]{2,1,0:T(8,128)(2,1)S(1)} %slice.15), channel_id=1, source_target_pairs={{4,0},{8,12},{5,1},{9,13},{6,2},{10,14},{7,3},{11,15},{20,16},{24,... | collective-permute-start | bytes 884744 | tf_op jit(solution)/shard_map/ppermute | solution.py:343
  42.0 2.1 %attend.6 = (f32[3,128,384]{2,1,0:T(8,128)S(1)}, f32[3,8,384]{2,1,0:T(8,128)S(1)}) custom-call(s32[4,4]{1,0:T(4,128)S(1)} %copy-done.4, s32[4]{0:T(128)S(1)} %copy-done.5, bf16[192,1536]{1,0:T(8,128)(2,1)S(1)} %bitcast.7, bf16[192,768]{1,0:T(8,128)(2,1)S(1)} %collective-permute-done.2.refs_1_, bf16[4,192,384]{2,1,0:T(8,128)(2,1)S(1)} %get-tuple-element.45.refs_2_, ...), custom_call_target="tpu_custom_call" | custom-call | flops 452984832 | bytes 1179648 | tf_op jit(solution)/shard_map/attend/pallas_call | solution.py:252
  44.1 0.0 collective-permute-done.7.refs_0_
  44.1 6.1 %collective-permute-done.8.refs_1_ = bf16[4,192,384]{2,1,0:T(8,128)(2,1)S(1)} collective-permute-done((bf16[4,192,384]{2,1,0:T(8,128)(2,1)S(1)}, bf16[4,192,384]{2,1,0:T(8,128)(2,1)S(1)}, u32[]{:S(2)}, u32[]{:S(2)}) %collective-permute-start.8) | collective-permute-done | bytes 589856 | tf_op jit(solution)/shard_map/ppermute | solution.py:343
  50.3 0.7 collective-permute-start.12
  51.0 1.3 %collective-permute-start.11 = (bf16[2,192,384]{2,1,0:T(8,128)(2,1)S(1)}, bf16[2,192,384]{2,1,0:T(8,128)(2,1)S(1)}, u32[]{:S(2)}, u32[]{:S(2)}) collective-permute-start(bf16[2,192,384]{2,1,0:T(8,128)(2,1)S(1)} %slice.12), channel_id=1, source_target_pairs={{4,0},{8,12},{5,1},{9,13},{6,2},{10,14},{7,3},{11,15},{20,16},{24,... | collective-permute-start | bytes 884744 | tf_op jit(solution)/shard_map/ppermute | solution.py:343
  52.3 2.1 %attend.7 = (f32[3,128,384]{2,1,0:T(8,128)S(1)}, f32[3,8,384]{2,1,0:T(8,128)S(1)}) custom-call(s32[4,4]{1,0:T(4,128)S(1)} %copy-done.4, s32[4]{0:T(128)S(1)} %copy-done.5, bf16[192,1536]{1,0:T(8,128)(2,1)S(1)} %bitcast.8, bf16[192,768]{1,0:T(8,128)(2,1)S(1)} %collective-permute-done.2.refs_1_, bf16[4,192,384]{2,1,0:T(8,128)(2,1)S(1)} %get-tuple-element.50.refs_2_, ...), custom_call_target="tpu_custom_call" | custom-call | flops 452984832 | bytes 1179648 | tf_op jit(solution)/shard_map/attend/pallas_call | solution.py:252
  54.3 0.0 collective-permute-done.14.refs_0_
  54.4 2.2 %collective-permute-done.15.refs_1_ = bf16[2,192,384]{2,1,0:T(8,128)(2,1)S(1)} collective-permute-done((bf16[2,192,384]{2,1,0:T(8,128)(2,1)S(1)}, bf16[2,192,384]{2,1,0:T(8,128)(2,1)S(1)}, u32[]{:S(2)}, u32[]{:S(2)}) %collective-permute-start.15) | collective-permute-done | bytes 294944 | tf_op jit(solution)/shard_map/ppermute | solution.py:343
  56.5 1.6 %attend_final.3 = (bf16[192,384]{1,0:T(8,128)(2,1)S(1)}, bf16[192,384]{1,0:T(8,128)(2,1)S(1)}) custom-call(s32[4,4]{1,0:T(4,128)S(1)} %copy-done.4, s32[4]{0:T(128)S(1)} %copy-done.5, bf16[192,1536]{1,0:T(8,128)(2,1)S(1)} %bitcast.9, bf16[192,768]{1,0:T(8,128)(2,1)S(1)} %collective-permute-done.2.refs_1_, ...), custom_call_target="tpu_custom_call" | custom-call | flops 226492416 | bytes 1179648 | tf_op jit(solution)/shard_map/attend_final/pallas_call | solution.py:252
  58.1 0.6 collective-permute-start.16
  58.7 0.0 collective-permute-done.12.refs_1_
  58.7 2.4 %collective-permute-done.11.refs_0_ = bf16[2,192,384]{2,1,0:T(8,128)(2,1)S(1)} collective-permute-done((bf16[2,192,384]{2,1,0:T(8,128)(2,1)S(1)}, bf16[2,192,384]{2,1,0:T(8,128)(2,1)S(1)}, u32[]{:S(2)}, u32[]{:S(2)}) %collective-permute-start.11) | collective-permute-done | bytes 294944 | tf_op jit(solution)/shard_map/ppermute | solution.py:343
  61.1 1.6 %attend_final.2 = (bf16[192,384]{1,0:T(8,128)(2,1)S(1)}, bf16[192,384]{1,0:T(8,128)(2,1)S(1)}) custom-call(s32[4,4]{1,0:T(4,128)S(1)} %copy-done.4, s32[4]{0:T(128)S(1)} %copy-done.5, bf16[192,1536]{1,0:T(8,128)(2,1)S(1)} %bitcast.10, bf16[192,768]{1,0:T(8,128)(2,1)S(1)} %collective-permute-done.2.refs_1_, ...), custom_call_target="tpu_custom_call" | custom-call | flops 226492416 | bytes 1179648 | tf_op jit(solution)/shard_map/attend_final/pallas_call | solution.py:252
  62.7 0.6 collective-permute-start.13
  63.3 0.0 collective-permute-done.16.refs_2_
  63.3 0.8 %put.2.refs_1_ = bf16[192,1536]{1,0:T(8,128)(2,1)} custom-call(bf16[192,384]{1,0:T(8,128)(2,1)S(1)} %get-tuple-element.60.refs_0_, bf16[192,384]{1,0:T(8,128)(2,1)S(1)} %get-tuple-element.61.refs_1_, bf16[192,384]{1,0:T(8,128)(2,1)S(1)} %collective-permute-done.16.refs_2_), custom_call_target="tpu_custom_call" | custom-call | tf_op jit(solution)/shard_map/put/pallas_call | solution.py:309
  64.1 3.8 %collective-permute-done.13.refs_0_ = bf16[192,384]{1,0:T(8,128)(2,1)S(1)} collective-permute-done((bf16[192,384]{1,0:T(8,128)(2,1)S(1)}, bf16[192,384]{1,0:T(8,128)(2,1)S(1)}, u32[]{:S(2)}, u32[]{:S(2)}) %collective-permute-start.13) | collective-permute-done | bytes 147488 | tf_op jit(solution)/shard_map/ppermute | solution.py:335
  67.9 0.7 put.3
  (9 shorter events, 0.1 us)
Async XLA Ops:
  0.0 12.3 %copy-start.1 = (bf16[1,4,48,1536]{3,2,1,0:T(8,128)(2,1)S(1)}, bf16[1,4,48,1536]{3,2,1,0:T(8,128)(2,1)}, u32[]{:S(2)}) copy-start(bf16[1,4,48,1536]{3,2,1,0:T(8,128)(2,1)} %param.6) | copy-start | bytes 1769476
  0.0 12.3 %copy-start.2 = (bf16[1,4,48,1536]{3,2,1,0:T(8,128)(2,1)S(1)}, bf16[1,4,48,1536]{3,2,1,0:T(8,128)(2,1)}, u32[]{:S(2)}) copy-start(bf16[1,4,48,1536]{3,2,1,0:T(8,128)(2,1)} %param.7) | copy-start | bytes 1769476
  2.1 10.2 %collective-permute-start = (bf16[2,192,384]{2,1,0:T(8,128)(2,1)}, bf16[2,192,384]{2,1,0:T(8,128)(2,1)S(1)}, u32[]{:S(2)}, u32[]{:S(2)}) collective-permute-start(bf16[2,192,384]{2,1,0:T(8,128)(2,1)} %get-tuple-element.34), channel_id=1, source_target_pairs={{0,2},{2,0},{1,3},{3,1},{4,6},{6,4},{5,7},{7,5},{8,10},{10,8},{9,1... | collective-permute-start | bytes 884744 | tf_op jit(solution)/shard_map/ppermute | solution.py:335
  5.1 14.5 %collective-permute-start.4 = (bf16[2,192,512]{2,1,0:T(8,128)(2,1)}, bf16[2,192,512]{2,1,0:T(8,128)(2,1)S(1)}, u32[]{:S(2)}, u32[]{:S(2)}) collective-permute-start(bf16[2,192,512]{2,1,0:T(8,128)(2,1)} %get-tuple-element.36.refs_2_), channel_id=1, source_target_pairs={{4,8},{8,4},{5,9},{9,5},{6,10},{10,6},{7,11},{11,7},{20,24},{24,20... | collective-permute-start | bytes 1179656 | tf_op jit(solution)/shard_map/ppermute | solution.py:343
  5.8 13.8 %collective-permute-start.3 = (bf16[2,192,512]{2,1,0:T(8,128)(2,1)}, bf16[2,192,512]{2,1,0:T(8,128)(2,1)S(1)}, u32[]{:S(2)}, u32[]{:S(2)}) collective-permute-start(bf16[2,192,512]{2,1,0:T(8,128)(2,1)} %get-tuple-element.36.refs_2_), channel_id=1, source_target_pairs={{0,4},{4,0},{8,12},{12,8},{1,5},{5,1},{9,13},{13,9},{2,6},{6,2},{1... | collective-permute-start | bytes 1179656 | tf_op jit(solution)/shard_map/ppermute | solution.py:343
  12.6 10.7 %copy-start = (bf16[1,4,48,1536]{3,2,1,0:T(8,128)(2,1)S(1)}, bf16[1,4,48,1536]{3,2,1,0:T(8,128)(2,1)}, u32[]{:S(2)}) copy-start(bf16[1,4,48,1536]{3,2,1,0:T(8,128)(2,1)} %param.5) | copy-start | bytes 1769476
  12.6 10.7 %collective-permute-start.1 = (bf16[2,192,384]{2,1,0:T(8,128)(2,1)S(1)}, bf16[2,192,384]{2,1,0:T(8,128)(2,1)S(1)}, u32[]{:S(2)}, u32[]{:S(2)}) collective-permute-start(bf16[2,192,384]{2,1,0:T(8,128)(2,1)S(1)} %get-tuple-element.35), channel_id=1, source_target_pairs={{0,2},{2,0},{1,3},{3,1},{4,6},{6,4},{5,7},{7,5},{8,10},{10,8},{9,1... | collective-permute-start | bytes 884744 | tf_op jit(solution)/shard_map/ppermute | solution.py:335
  14.4 9.0 %collective-permute-start.6 = (bf16[2,192,256]{2,1,0:T(8,128)(2,1)S(1)}, bf16[2,192,256]{2,1,0:T(8,128)(2,1)S(1)}, u32[]{:S(2)}, u32[]{:S(2)}) collective-permute-start(bf16[2,192,256]{2,1,0:T(8,128)(2,1)S(1)} %get-tuple-element.37), channel_id=1, source_target_pairs={{4,8},{8,4},{5,9},{9,5},{6,10},{10,6},{7,11},{11,7},{20,24},{24,20... | collective-permute-start | bytes 589832 | tf_op jit(solution)/shard_map/ppermute | solution.py:343
  15.1 9.1 %collective-permute-start.5 = (bf16[2,192,256]{2,1,0:T(8,128)(2,1)S(1)}, bf16[2,192,256]{2,1,0:T(8,128)(2,1)S(1)}, u32[]{:S(2)}, u32[]{:S(2)}) collective-permute-start(bf16[2,192,256]{2,1,0:T(8,128)(2,1)S(1)} %get-tuple-element.37), channel_id=1, source_target_pairs={{0,4},{4,0},{8,12},{12,8},{1,5},{5,1},{9,13},{13,9},{2,6},{6,2},{1... | collective-permute-start | bytes 589832 | tf_op jit(solution)/shard_map/ppermute | solution.py:343
  19.7 20.2 %collective-permute-start.9 = (bf16[4,192,384]{2,1,0:T(8,128)(2,1)S(1)}, bf16[4,192,384]{2,1,0:T(8,128)(2,1)S(1)}, u32[]{:S(2)}, u32[]{:S(2)}) collective-permute-start(bf16[4,192,384]{2,1,0:T(8,128)(2,1)S(1)} %get-tuple-element.40.refs_4_), channel_id=1, source_target_pairs={{4,8},{8,4},{5,9},{9,5},{6,10},{10,6},{7,11},{11,7},{20,24},{24,20... | collective-permute-start | bytes 1769480 | tf_op jit(solution)/shard_map/ppermute | solution.py:343
  20.4 19.5 %collective-permute-start.10 = (bf16[4,192,384]{2,1,0:T(8,128)(2,1)S(1)}, bf16[4,192,384]{2,1,0:T(8,128)(2,1)S(1)}, u32[]{:S(2)}, u32[]{:S(2)}) collective-permute-start(bf16[4,192,384]{2,1,0:T(8,128)(2,1)S(1)} %get-tuple-element.41.refs_5_), channel_id=1, source_target_pairs={{0,4},{4,0},{8,12},{12,8},{1,5},{5,1},{9,13},{13,9},{2,6},{6,2},{1... | collective-permute-start | bytes 1769480 | tf_op jit(solution)/shard_map/ppermute | solution.py:343
  23.4 12.0 %copy-start.3 = (bf16[2,192,512]{2,1,0:T(8,128)(2,1)S(1)}, bf16[2,192,512]{2,1,0:T(8,128)(2,1)}, u32[]{:S(2)}) copy-start(bf16[2,192,512]{2,1,0:T(8,128)(2,1)} %get-tuple-element.36.refs_2_) | copy-start | bytes 1179652
  24.3 11.1 %copy-start.4 = (s32[4,4]{1,0:T(4,128)S(1)}, s32[4,4]{1,0:T(4,128)}, u32[]{:S(2)}) copy-start(s32[4,4]{1,0:T(4,128)} %flags_ref.11) | copy-start | bytes 196
  24.3 11.1 %copy-start.5 = (s32[4]{0:T(128)S(1)}, s32[4]{0:T(128)}, u32[]{:S(2)}) copy-start(s32[4]{0:T(128)} %widths_ref.11) | copy-start | bytes 52
  24.3 19.8 %collective-permute-start.7 = (bf16[4,192,384]{2,1,0:T(8,128)(2,1)S(1)}, bf16[4,192,384]{2,1,0:T(8,128)(2,1)S(1)}, u32[]{:S(2)}, u32[]{:S(2)}) collective-permute-start(bf16[4,192,384]{2,1,0:T(8,128)(2,1)S(1)} %get-tuple-element.38.refs_4_), channel_id=1, source_target_pairs={{4,8},{8,4},{5,9},{9,5},{6,10},{10,6},{7,11},{11,7},{20,24},{24,20... | collective-permute-start | bytes 1769480 | tf_op jit(solution)/shard_map/ppermute | solution.py:343
  25.0 25.2 %collective-permute-start.8 = (bf16[4,192,384]{2,1,0:T(8,128)(2,1)S(1)}, bf16[4,192,384]{2,1,0:T(8,128)(2,1)S(1)}, u32[]{:S(2)}, u32[]{:S(2)}) collective-permute-start(bf16[4,192,384]{2,1,0:T(8,128)(2,1)S(1)} %get-tuple-element.39.refs_5_), channel_id=1, source_target_pairs={{0,4},{4,0},{8,12},{12,8},{1,5},{5,1},{9,13},{13,9},{2,6},{6,2},{1... | collective-permute-start | bytes 1769480 | tf_op jit(solution)/shard_map/ppermute | solution.py:343
  28.7 6.7 %collective-permute-start.2 = (bf16[192,768]{1,0:T(8,128)(2,1)S(1)}, bf16[192,768]{1,0:T(8,128)(2,1)S(1)}, u32[]{:S(2)}, u32[]{:S(2)}) collective-permute-start(bf16[192,768]{1,0:T(8,128)(2,1)S(1)} %pack.5.refs_1_), channel_id=1, source_target_pairs={{0,2},{2,0},{1,3},{3,1},{4,6},{6,4},{5,7},{7,5},{8,10},{10,8},{9,1... | collective-permute-start | bytes 884744 | tf_op jit(solution)/shard_map/ppermute | solution.py:335
  40.0 14.3 %collective-permute-start.14 = (bf16[2,192,384]{2,1,0:T(8,128)(2,1)S(1)}, bf16[2,192,384]{2,1,0:T(8,128)(2,1)S(1)}, u32[]{:S(2)}, u32[]{:S(2)}) collective-permute-start(bf16[2,192,384]{2,1,0:T(8,128)(2,1)S(1)} %slice.14), channel_id=1, source_target_pairs={{4,8},{8,4},{5,9},{9,5},{6,10},{10,6},{7,11},{11,7},{20,24},{24,20... | collective-permute-start | bytes 884744 | tf_op jit(solution)/shard_map/ppermute | solution.py:343
  40.7 15.8 %collective-permute-start.15 = (bf16[2,192,384]{2,1,0:T(8,128)(2,1)S(1)}, bf16[2,192,384]{2,1,0:T(8,128)(2,1)S(1)}, u32[]{:S(2)}, u32[]{:S(2)}) collective-permute-start(bf16[2,192,384]{2,1,0:T(8,128)(2,1)S(1)} %slice.15), channel_id=1, source_target_pairs={{4,0},{8,12},{5,1},{9,13},{6,2},{10,14},{7,3},{11,15},{20,16},{24,... | collective-permute-start | bytes 884744 | tf_op jit(solution)/shard_map/ppermute | solution.py:343
  50.3 8.4 %collective-permute-start.12 = (bf16[2,192,384]{2,1,0:T(8,128)(2,1)S(1)}, bf16[2,192,384]{2,1,0:T(8,128)(2,1)S(1)}, u32[]{:S(2)}, u32[]{:S(2)}) collective-permute-start(bf16[2,192,384]{2,1,0:T(8,128)(2,1)S(1)} %slice.13), channel_id=1, source_target_pairs={{4,8},{8,4},{5,9},{9,5},{6,10},{10,6},{7,11},{11,7},{20,24},{24,20... | collective-permute-start | bytes 884744 | tf_op jit(solution)/shard_map/ppermute | solution.py:343
  51.0 10.2 %collective-permute-start.11 = (bf16[2,192,384]{2,1,0:T(8,128)(2,1)S(1)}, bf16[2,192,384]{2,1,0:T(8,128)(2,1)S(1)}, u32[]{:S(2)}, u32[]{:S(2)}) collective-permute-start(bf16[2,192,384]{2,1,0:T(8,128)(2,1)S(1)} %slice.12), channel_id=1, source_target_pairs={{4,0},{8,12},{5,1},{9,13},{6,2},{10,14},{7,3},{11,15},{20,16},{24,... | collective-permute-start | bytes 884744 | tf_op jit(solution)/shard_map/ppermute | solution.py:343
  58.1 5.2 %collective-permute-start.16 = (bf16[192,384]{1,0:T(8,128)(2,1)S(1)}, bf16[192,384]{1,0:T(8,128)(2,1)S(1)}, u32[]{:S(2)}, u32[]{:S(2)}) collective-permute-start(bf16[192,384]{1,0:T(8,128)(2,1)S(1)} %get-tuple-element.62), channel_id=1, source_target_pairs={{0,2},{2,0},{1,3},{3,1},{4,6},{6,4},{5,7},{7,5},{8,10},{10,8},{9,1... | collective-permute-start | bytes 442376 | tf_op jit(solution)/shard_map/ppermute | solution.py:335
  62.7 5.2 %collective-permute-start.13 = (bf16[192,384]{1,0:T(8,128)(2,1)S(1)}, bf16[192,384]{1,0:T(8,128)(2,1)S(1)}, u32[]{:S(2)}, u32[]{:S(2)}) collective-permute-start(bf16[192,384]{1,0:T(8,128)(2,1)S(1)} %get-tuple-element.56), channel_id=1, source_target_pairs={{0,2},{2,0},{1,3},{3,1},{4,6},{6,4},{5,7},{7,5},{8,10},{10,8},{9,1... | collective-permute-start | bytes 442376 | tf_op jit(solution)/shard_map/ppermute | solution.py:335
